TPU v7x, 32 devices: a whole 2x2x4 slice. The times are simulated.
32 devices in a mesh: parts: 2 (over x), blk: 16 (over z, y, core).
Axes of the slice: x: 2, y: 2, z: 4, core: 2. Of those that a mesh axis runs over, the one named last changes fastest.
Arguments:
- observed: bfloat16 [24576, 1024], P(('parts', 'blk')), parts along dimension 0, may hold values from -6 to 6
- sharpness: float32 [24576], P(('parts', 'blk')), parts along dimension 0, may hold values from 0.03 to 0.15
- obs_class: int32 [24576], P(('parts', 'blk')), parts along dimension 0, may hold values from 0 to 7
- pattern: int32 [192, 16], P(('parts', 'blk')), parts along dimension 0, may hold values from 0 to 1, as said below
- evolved: bfloat16 [4096, 1024], P(('parts', 'blk')), parts along dimension 0, may hold values from -6 to 6
- sim_params: bfloat16 [4, 4096], P(None, ('parts', 'blk')), parts along dimension 1, may hold values from -6 to 6
- sim_class: int32 [4096], P(('parts', 'blk')), parts along dimension 0, may hold values from 0 to 7, as said below
Outputs:
- posterior_mean: float32 [4, 24576], P(None, ('parts', 'blk')), parts along dimension 1
- log_evidence: float32 [24576], P(('parts', 'blk')), parts along dimension 0
There are 2 independent parts, one for each index of `parts`. A program takes and returns all parts, laid end to end along the dimension named above; each array names one. Nothing has to cross between parts.
Inputs may be any that keep to these rules, and one draw needn't show every extreme that they name: `sim_class`: every block of 128 evolved profiles holds every class, at its first 8 positions. `pattern`: every block of observed profiles is compared with at least one block of evolved profiles; the share of compared blocks differs from one observed block to another.
All inputs are finite; a program needn't handle non-finite values.
Results may differ from a plain program's by a relative error of at most 0.0045.
Values may be sent and summed in bfloat16 or wider, within the bound.
No kernel may reach another device: no remote copies, remote signals or barrier semaphores. Data moves between devices by JAX's collectives and lax.ppermute only.
A program may use at most 64 MiB of HBM per device.

v0:
```python
import jax
import jax.numpy as jnp
from jax import lax
from jax.sharding import PartitionSpec as P

NEG_START = -1e30


def from_behind(array, axis, by):
    count = lax.axis_size(axis)
    return lax.ppermute(array, axis, [(i, (i + by) % count) for i in range(count)])


def visit_block(
    observed,
    obs_sq,
    sharpness,
    obs_class,
    rows_open,
    sims,
    sims_sq,
    params,
    sims_class,
    running_max,
    weight_total,
    param_sums,
):
    inner = lax.dot_general(
        observed, sims, (((1,), (1,)), ((), ())), preferred_element_type=jnp.float32
    )
    distance = obs_sq[:, None] + sims_sq[None, :] - 2.0 * inner
    score = sharpness[:, None] * (2.0 * observed.shape[1] - distance)
    active = rows_open[:, None] & (obs_class[:, None] == sims_class[None, :])
    new_max = jnp.maximum(running_max, jnp.max(jnp.where(active, score, NEG_START), axis=1))
    factor = jnp.exp(running_max - new_max)
    weights = jnp.where(active, jnp.exp(score - new_max[:, None]), 0.0)
    weight_total = weight_total * factor + jnp.sum(weights, axis=1)
    weight_low = weights.astype(jnp.bfloat16)
    added = lax.dot_general(
        params, weight_low, (((1,), (1,)), ((), ())), preferred_element_type=jnp.float32
    )
    param_sums = param_sums * factor[None, :] + added
    return (new_max, weight_total, param_sums)


def on_device(observed, sharpness, obs_class, pattern, evolved, sim_params, sim_class):
    cycle_size = lax.axis_size("blk")
    position = lax.axis_index("blk")
    row_count = observed.shape[0]
    tile_count = pattern.shape[0]
    tile_rows = row_count // tile_count
    obs_sq = jnp.sum(jnp.square(observed.astype(jnp.float32)), axis=1)

    def absorb(state, packet, block_id):
        sims, params, class_low = packet
        sims_class = class_low.astype(jnp.int32)
        sims_sq = jnp.sum(jnp.square(sims.astype(jnp.float32)), axis=1)
        column = lax.dynamic_slice_in_dim(pattern, block_id, 1, 1)[:, 0] == 1
        rows_open = jnp.repeat(column, tile_rows)
        return visit_block(
            observed,
            obs_sq,
            sharpness,
            obs_class,
            rows_open,
            sims,
            sims_sq,
            params,
            sims_class,
            state[0],
            state[1],
            state[2],
        )

    packet = (evolved, sim_params, sim_class.astype(jnp.bfloat16))
    state = (
        jnp.full((row_count,), NEG_START, jnp.float32),
        jnp.zeros((row_count,), jnp.float32),
        jnp.zeros((sim_params.shape[0], row_count), jnp.float32),
    )
    state = absorb(state, packet, position)

    def turn(turn_index, carry):
        state_now, moving = carry
        moving = from_behind((moving[0], moving[1], moving[2]), "blk", 1)
        state_now = absorb(state_now, moving, (position - turn_index) % cycle_size)
        return (state_now, moving)

    state, packet_end = lax.fori_loop(1, cycle_size, turn, (state, packet))
    running_max, weight_total, param_sums = state
    return (param_sums / weight_total[None, :], running_max + jnp.log(weight_total))


def solution(mesh):
    placed = (
        P(("parts", "blk"), None),
        P(("parts", "blk")),
        P(("parts", "blk")),
        P(("parts", "blk"), None),
        P(("parts", "blk"), None),
        P(None, ("parts", "blk")),
        P(("parts", "blk")),
    )
    return jax.shard_map(
        on_device,
        mesh=mesh,
        in_specs=placed,
        out_specs=(P(None, ("parts", "blk")), P(("parts", "blk"))),
        check_vma=False,
    )
```

profile of v0, /device:TPU:0, one launch (start us, length us, event | category | flops | bytes accessed | tf_op | source)
XLA Modules:
  0.0 161.7 jit_solution(7447141425702174597)
XLA Ops:
  0.7 1.1 copy.33
  2.4 0.9 fusion.12
  4.2 1.8 %multiply_reduce_fusion.1 = f32[768]{0:T(1024)S(1)} fusion(bf16[768,1024]{1,0:T(8,128)(2,1)} %param.9), kind=kLoop, calls=%fused_computation.14 | loop fusion | flops 2358528 | bytes 1575936 | tf_op jit(solution)/shard_map/reduce_sum | solution.py:52
  7.2 153.3 %while.25 = (s32[]{:T(128)}, f32[768]{0:T(1024)S(1)}, f32[768]{0:T(1024)S(1)}, f32[4,768]{1,0:T(4,128)S(1)}, bf16[128,1024]{1,0:T(8,128)(2,1)S(1)}, /*index=5*/b...) while((s32[]{:T(128)}, f32[768]{0:T(1024)S(1)}, ...), condition=%wide.region_8.9_spmd, body=%wide.region_4.8_spmd.sunk | while | flops 205168144 | bytes 4967640 | solution.py:89
  7.7 2.6 %collective-permute-start.1 = (bf16[128]{0:T(256)(128)(2,1)S(1)}, bf16[128]{0:T(256)(128)(2,1)S(1)}, u32[]{:S(2)}, u32[]{:S(2)}) collective-permute-start(bf16[128]{0:T(256)(128)(2,1)S(1)} %get-tuple-element.475), channel_id=1, source_target_pairs={{0,1},{1,2},{2,3},{3,4},{4,5},{5,6},{6,7},{7,8},{8,9},{9,10},{10,1... | collective-permute-start | bytes 776 | tf_op jit(solution)/shard_map/while/body/eval_jaxpr/ppermute | solution.py:11
  10.4 6.3 %collective-permute-done.1 = bf16[128]{0:T(256)(128)(2,1)S(1)} collective-permute-done((bf16[128]{0:T(256)(128)(2,1)S(1)}, bf16[128]{0:T(256)(128)(2,1)S(1)}, u32[]{:S(2)}, u32[]{:S(2)}) %collective-permute-start.1) | collective-permute-done | bytes 288 | tf_op jit(solution)/shard_map/while/body/eval_jaxpr/ppermute | solution.py:11
  17.0 0.7 select_reduce_fusion.3
  18.6 8.3 %collective-permute-done.1 = bf16[128]{0:T(256)(128)(2,1)S(1)} collective-permute-done((bf16[128]{0:T(256)(128)(2,1)S(1)}, bf16[128]{0:T(256)(128)(2,1)S(1)}, u32[]{:S(2)}, u32[]{:S(2)}) %collective-permute-start.1) | collective-permute-done | bytes 288 | tf_op jit(solution)/shard_map/while/body/eval_jaxpr/ppermute | solution.py:11
  27.1 0.7 select_reduce_fusion.3
  28.8 8.3 %collective-permute-done.1 = bf16[128]{0:T(256)(128)(2,1)S(1)} collective-permute-done((bf16[128]{0:T(256)(128)(2,1)S(1)}, bf16[128]{0:T(256)(128)(2,1)S(1)}, u32[]{:S(2)}, u32[]{:S(2)}) %collective-permute-start.1) | collective-permute-done | bytes 288 | tf_op jit(solution)/shard_map/while/body/eval_jaxpr/ppermute | solution.py:11
  37.3 0.7 select_reduce_fusion.3
  39.0 8.3 %collective-permute-done.1 = bf16[128]{0:T(256)(128)(2,1)S(1)} collective-permute-done((bf16[128]{0:T(256)(128)(2,1)S(1)}, bf16[128]{0:T(256)(128)(2,1)S(1)}, u32[]{:S(2)}, u32[]{:S(2)}) %collective-permute-start.1) | collective-permute-done | bytes 288 | tf_op jit(solution)/shard_map/while/body/eval_jaxpr/ppermute | solution.py:11
  47.4 0.7 select_reduce_fusion.3
  49.1 8.3 %collective-permute-done.1 = bf16[128]{0:T(256)(128)(2,1)S(1)} collective-permute-done((bf16[128]{0:T(256)(128)(2,1)S(1)}, bf16[128]{0:T(256)(128)(2,1)S(1)}, u32[]{:S(2)}, u32[]{:S(2)}) %collective-permute-start.1) | collective-permute-done | bytes 288 | tf_op jit(solution)/shard_map/while/body/eval_jaxpr/ppermute | solution.py:11
  59.3 8.3 %collective-permute-done.1 = bf16[128]{0:T(256)(128)(2,1)S(1)} collective-permute-done((bf16[128]{0:T(256)(128)(2,1)S(1)}, bf16[128]{0:T(256)(128)(2,1)S(1)}, u32[]{:S(2)}, u32[]{:S(2)}) %collective-permute-start.1) | collective-permute-done | bytes 288 | tf_op jit(solution)/shard_map/while/body/eval_jaxpr/ppermute | solution.py:11
  69.4 8.3 %collective-permute-done.1 = bf16[128]{0:T(256)(128)(2,1)S(1)} collective-permute-done((bf16[128]{0:T(256)(128)(2,1)S(1)}, bf16[128]{0:T(256)(128)(2,1)S(1)}, u32[]{:S(2)}, u32[]{:S(2)}) %collective-permute-start.1) | collective-permute-done | bytes 288 | tf_op jit(solution)/shard_map/while/body/eval_jaxpr/ppermute | solution.py:11
  79.6 8.3 %collective-permute-done.1 = bf16[128]{0:T(256)(128)(2,1)S(1)} collective-permute-done((bf16[128]{0:T(256)(128)(2,1)S(1)}, bf16[128]{0:T(256)(128)(2,1)S(1)}, u32[]{:S(2)}, u32[]{:S(2)}) %collective-permute-start.1) | collective-permute-done | bytes 288 | tf_op jit(solution)/shard_map/while/body/eval_jaxpr/ppermute | solution.py:11
  89.7 8.3 %collective-permute-done.1 = bf16[128]{0:T(256)(128)(2,1)S(1)} collective-permute-done((bf16[128]{0:T(256)(128)(2,1)S(1)}, bf16[128]{0:T(256)(128)(2,1)S(1)}, u32[]{:S(2)}, u32[]{:S(2)}) %collective-permute-start.1) | collective-permute-done | bytes 288 | tf_op jit(solution)/shard_map/while/body/eval_jaxpr/ppermute | solution.py:11
  99.9 8.3 %collective-permute-done.1 = bf16[128]{0:T(256)(128)(2,1)S(1)} collective-permute-done((bf16[128]{0:T(256)(128)(2,1)S(1)}, bf16[128]{0:T(256)(128)(2,1)S(1)}, u32[]{:S(2)}, u32[]{:S(2)}) %collective-permute-start.1) | collective-permute-done | bytes 288 | tf_op jit(solution)/shard_map/while/body/eval_jaxpr/ppermute | solution.py:11
  110.0 8.3 %collective-permute-done.1 = bf16[128]{0:T(256)(128)(2,1)S(1)} collective-permute-done((bf16[128]{0:T(256)(128)(2,1)S(1)}, bf16[128]{0:T(256)(128)(2,1)S(1)}, u32[]{:S(2)}, u32[]{:S(2)}) %collective-permute-start.1) | collective-permute-done | bytes 288 | tf_op jit(solution)/shard_map/while/body/eval_jaxpr/ppermute | solution.py:11
  120.2 8.3 %collective-permute-done.1 = bf16[128]{0:T(256)(128)(2,1)S(1)} collective-permute-done((bf16[128]{0:T(256)(128)(2,1)S(1)}, bf16[128]{0:T(256)(128)(2,1)S(1)}, u32[]{:S(2)}, u32[]{:S(2)}) %collective-permute-start.1) | collective-permute-done | bytes 288 | tf_op jit(solution)/shard_map/while/body/eval_jaxpr/ppermute | solution.py:11
  130.4 8.3 %collective-permute-done.1 = bf16[128]{0:T(256)(128)(2,1)S(1)} collective-permute-done((bf16[128]{0:T(256)(128)(2,1)S(1)}, bf16[128]{0:T(256)(128)(2,1)S(1)}, u32[]{:S(2)}, u32[]{:S(2)}) %collective-permute-start.1) | collective-permute-done | bytes 288 | tf_op jit(solution)/shard_map/while/body/eval_jaxpr/ppermute | solution.py:11
  140.5 8.3 %collective-permute-done.1 = bf16[128]{0:T(256)(128)(2,1)S(1)} collective-permute-done((bf16[128]{0:T(256)(128)(2,1)S(1)}, bf16[128]{0:T(256)(128)(2,1)S(1)}, u32[]{:S(2)}, u32[]{:S(2)}) %collective-permute-start.1) | collective-permute-done | bytes 288 | tf_op jit(solution)/shard_map/while/body/eval_jaxpr/ppermute | solution.py:11
  150.7 8.3 %collective-permute-done.1 = bf16[128]{0:T(256)(128)(2,1)S(1)} collective-permute-done((bf16[128]{0:T(256)(128)(2,1)S(1)}, bf16[128]{0:T(256)(128)(2,1)S(1)}, u32[]{:S(2)}, u32[]{:S(2)}) %collective-permute-start.1) | collective-permute-done | bytes 288 | tf_op jit(solution)/shard_map/while/body/eval_jaxpr/ppermute | solution.py:11
  (285 shorter events, 27.6 us)
Async XLA Ops:
  7.2 9.6 %collective-permute-start = (bf16[128,1024]{1,0:T(8,128)(2,1)S(1)}, bf16[128,1024]{1,0:T(8,128)(2,1)S(1)}, u32[]{:S(2)}, u32[]{:S(2)}) collective-permute-start(bf16[128,1024]{1,0:T(8,128)(2,1)S(1)} %get-tuple-element.473), channel_id=1, source_target_pairs={{0,1},{1,2},{2,3},{3,4},{4,5},{5,6},{6,7},{7,8},{8,9},{9,10},{10,1... | collective-permute-start | bytes 786440 | tf_op jit(solution)/shard_map/while/body/eval_jaxpr/ppermute | solution.py:11
  7.7 9.1 %collective-permute-start.1 = (bf16[128]{0:T(256)(128)(2,1)S(1)}, bf16[128]{0:T(256)(128)(2,1)S(1)}, u32[]{:S(2)}, u32[]{:S(2)}) collective-permute-start(bf16[128]{0:T(256)(128)(2,1)S(1)} %get-tuple-element.475), channel_id=1, source_target_pairs={{0,1},{1,2},{2,3},{3,4},{4,5},{5,6},{6,7},{7,8},{8,9},{9,10},{10,1... | collective-permute-start | bytes 776 | tf_op jit(solution)/shard_map/while/body/eval_jaxpr/ppermute | solution.py:11
  18.3 8.6 %collective-permute-start = (bf16[128,1024]{1,0:T(8,128)(2,1)S(1)}, bf16[128,1024]{1,0:T(8,128)(2,1)S(1)}, u32[]{:S(2)}, u32[]{:S(2)}) collective-permute-start(bf16[128,1024]{1,0:T(8,128)(2,1)S(1)} %get-tuple-element.473), channel_id=1, source_target_pairs={{0,1},{1,2},{2,3},{3,4},{4,5},{5,6},{6,7},{7,8},{8,9},{9,10},{10,1... | collective-permute-start | bytes 786440 | tf_op jit(solution)/shard_map/while/body/eval_jaxpr/ppermute | solution.py:11
  18.4 8.5 %collective-permute-start.1 = (bf16[128]{0:T(256)(128)(2,1)S(1)}, bf16[128]{0:T(256)(128)(2,1)S(1)}, u32[]{:S(2)}, u32[]{:S(2)}) collective-permute-start(bf16[128]{0:T(256)(128)(2,1)S(1)} %get-tuple-element.475), channel_id=1, source_target_pairs={{0,1},{1,2},{2,3},{3,4},{4,5},{5,6},{6,7},{7,8},{8,9},{9,10},{10,1... | collective-permute-start | bytes 776 | tf_op jit(solution)/shard_map/while/body/eval_jaxpr/ppermute | solution.py:11
  28.5 8.6 %collective-permute-start = (bf16[128,1024]{1,0:T(8,128)(2,1)S(1)}, bf16[128,1024]{1,0:T(8,128)(2,1)S(1)}, u32[]{:S(2)}, u32[]{:S(2)}) collective-permute-start(bf16[128,1024]{1,0:T(8,128)(2,1)S(1)} %get-tuple-element.473), channel_id=1, source_target_pairs={{0,1},{1,2},{2,3},{3,4},{4,5},{5,6},{6,7},{7,8},{8,9},{9,10},{10,1... | collective-permute-start | bytes 786440 | tf_op jit(solution)/shard_map/while/body/eval_jaxpr/ppermute | solution.py:11
  28.6 8.5 %collective-permute-start.1 = (bf16[128]{0:T(256)(128)(2,1)S(1)}, bf16[128]{0:T(256)(128)(2,1)S(1)}, u32[]{:S(2)}, u32[]{:S(2)}) collective-permute-start(bf16[128]{0:T(256)(128)(2,1)S(1)} %get-tuple-element.475), channel_id=1, source_target_pairs={{0,1},{1,2},{2,3},{3,4},{4,5},{5,6},{6,7},{7,8},{8,9},{9,10},{10,1... | collective-permute-start | bytes 776 | tf_op jit(solution)/shard_map/while/body/eval_jaxpr/ppermute | solution.py:11
  38.6 8.6 %collective-permute-start = (bf16[128,1024]{1,0:T(8,128)(2,1)S(1)}, bf16[128,1024]{1,0:T(8,128)(2,1)S(1)}, u32[]{:S(2)}, u32[]{:S(2)}) collective-permute-start(bf16[128,1024]{1,0:T(8,128)(2,1)S(1)} %get-tuple-element.473), channel_id=1, source_target_pairs={{0,1},{1,2},{2,3},{3,4},{4,5},{5,6},{6,7},{7,8},{8,9},{9,10},{10,1... | collective-permute-start | bytes 786440 | tf_op jit(solution)/shard_map/while/body/eval_jaxpr/ppermute | solution.py:11
  38.7 8.5 %collective-permute-start.1 = (bf16[128]{0:T(256)(128)(2,1)S(1)}, bf16[128]{0:T(256)(128)(2,1)S(1)}, u32[]{:S(2)}, u32[]{:S(2)}) collective-permute-start(bf16[128]{0:T(256)(128)(2,1)S(1)} %get-tuple-element.475), channel_id=1, source_target_pairs={{0,1},{1,2},{2,3},{3,4},{4,5},{5,6},{6,7},{7,8},{8,9},{9,10},{10,1... | collective-permute-start | bytes 776 | tf_op jit(solution)/shard_map/while/body/eval_jaxpr/ppermute | solution.py:11
  48.8 8.6 %collective-permute-start = (bf16[128,1024]{1,0:T(8,128)(2,1)S(1)}, bf16[128,1024]{1,0:T(8,128)(2,1)S(1)}, u32[]{:S(2)}, u32[]{:S(2)}) collective-permute-start(bf16[128,1024]{1,0:T(8,128)(2,1)S(1)} %get-tuple-element.473), channel_id=1, source_target_pairs={{0,1},{1,2},{2,3},{3,4},{4,5},{5,6},{6,7},{7,8},{8,9},{9,10},{10,1... | collective-permute-start | bytes 786440 | tf_op jit(solution)/shard_map/while/body/eval_jaxpr/ppermute | solution.py:11
  48.9 8.5 %collective-permute-start.1 = (bf16[128]{0:T(256)(128)(2,1)S(1)}, bf16[128]{0:T(256)(128)(2,1)S(1)}, u32[]{:S(2)}, u32[]{:S(2)}) collective-permute-start(bf16[128]{0:T(256)(128)(2,1)S(1)} %get-tuple-element.475), channel_id=1, source_target_pairs={{0,1},{1,2},{2,3},{3,4},{4,5},{5,6},{6,7},{7,8},{8,9},{9,10},{10,1... | collective-permute-start | bytes 776 | tf_op jit(solution)/shard_map/while/body/eval_jaxpr/ppermute | solution.py:11
  59.0 8.6 %collective-permute-start = (bf16[128,1024]{1,0:T(8,128)(2,1)S(1)}, bf16[128,1024]{1,0:T(8,128)(2,1)S(1)}, u32[]{:S(2)}, u32[]{:S(2)}) collective-permute-start(bf16[128,1024]{1,0:T(8,128)(2,1)S(1)} %get-tuple-element.473), channel_id=1, source_target_pairs={{0,1},{1,2},{2,3},{3,4},{4,5},{5,6},{6,7},{7,8},{8,9},{9,10},{10,1... | collective-permute-start | bytes 786440 | tf_op jit(solution)/shard_map/while/body/eval_jaxpr/ppermute | solution.py:11
  59.0 8.5 %collective-permute-start.1 = (bf16[128]{0:T(256)(128)(2,1)S(1)}, bf16[128]{0:T(256)(128)(2,1)S(1)}, u32[]{:S(2)}, u32[]{:S(2)}) collective-permute-start(bf16[128]{0:T(256)(128)(2,1)S(1)} %get-tuple-element.475), channel_id=1, source_target_pairs={{0,1},{1,2},{2,3},{3,4},{4,5},{5,6},{6,7},{7,8},{8,9},{9,10},{10,1... | collective-permute-start | bytes 776 | tf_op jit(solution)/shard_map/while/body/eval_jaxpr/ppermute | solution.py:11
  69.1 8.6 %collective-permute-start = (bf16[128,1024]{1,0:T(8,128)(2,1)S(1)}, bf16[128,1024]{1,0:T(8,128)(2,1)S(1)}, u32[]{:S(2)}, u32[]{:S(2)}) collective-permute-start(bf16[128,1024]{1,0:T(8,128)(2,1)S(1)} %get-tuple-element.473), channel_id=1, source_target_pairs={{0,1},{1,2},{2,3},{3,4},{4,5},{5,6},{6,7},{7,8},{8,9},{9,10},{10,1... | collective-permute-start | bytes 786440 | tf_op jit(solution)/shard_map/while/body/eval_jaxpr/ppermute | solution.py:11
  69.2 8.5 %collective-permute-start.1 = (bf16[128]{0:T(256)(128)(2,1)S(1)}, bf16[128]{0:T(256)(128)(2,1)S(1)}, u32[]{:S(2)}, u32[]{:S(2)}) collective-permute-start(bf16[128]{0:T(256)(128)(2,1)S(1)} %get-tuple-element.475), channel_id=1, source_target_pairs={{0,1},{1,2},{2,3},{3,4},{4,5},{5,6},{6,7},{7,8},{8,9},{9,10},{10,1... | collective-permute-start | bytes 776 | tf_op jit(solution)/shard_map/while/body/eval_jaxpr/ppermute | solution.py:11
  79.3 8.6 %collective-permute-start = (bf16[128,1024]{1,0:T(8,128)(2,1)S(1)}, bf16[128,1024]{1,0:T(8,128)(2,1)S(1)}, u32[]{:S(2)}, u32[]{:S(2)}) collective-permute-start(bf16[128,1024]{1,0:T(8,128)(2,1)S(1)} %get-tuple-element.473), channel_id=1, source_target_pairs={{0,1},{1,2},{2,3},{3,4},{4,5},{5,6},{6,7},{7,8},{8,9},{9,10},{10,1... | collective-permute-start | bytes 786440 | tf_op jit(solution)/shard_map/while/body/eval_jaxpr/ppermute | solution.py:11
  79.3 8.5 %collective-permute-start.1 = (bf16[128]{0:T(256)(128)(2,1)S(1)}, bf16[128]{0:T(256)(128)(2,1)S(1)}, u32[]{:S(2)}, u32[]{:S(2)}) collective-permute-start(bf16[128]{0:T(256)(128)(2,1)S(1)} %get-tuple-element.475), channel_id=1, source_target_pairs={{0,1},{1,2},{2,3},{3,4},{4,5},{5,6},{6,7},{7,8},{8,9},{9,10},{10,1... | collective-permute-start | bytes 776 | tf_op jit(solution)/shard_map/while/body/eval_jaxpr/ppermute | solution.py:11
  89.4 8.6 %collective-permute-start = (bf16[128,1024]{1,0:T(8,128)(2,1)S(1)}, bf16[128,1024]{1,0:T(8,128)(2,1)S(1)}, u32[]{:S(2)}, u32[]{:S(2)}) collective-permute-start(bf16[128,1024]{1,0:T(8,128)(2,1)S(1)} %get-tuple-element.473), channel_id=1, source_target_pairs={{0,1},{1,2},{2,3},{3,4},{4,5},{5,6},{6,7},{7,8},{8,9},{9,10},{10,1... | collective-permute-start | bytes 786440 | tf_op jit(solution)/shard_map/while/body/eval_jaxpr/ppermute | solution.py:11
  99.6 8.6 %collective-permute-start = (bf16[128,1024]{1,0:T(8,128)(2,1)S(1)}, bf16[128,1024]{1,0:T(8,128)(2,1)S(1)}, u32[]{:S(2)}, u32[]{:S(2)}) collective-permute-start(bf16[128,1024]{1,0:T(8,128)(2,1)S(1)} %get-tuple-element.473), channel_id=1, source_target_pairs={{0,1},{1,2},{2,3},{3,4},{4,5},{5,6},{6,7},{7,8},{8,9},{9,10},{10,1... | collective-permute-start | bytes 786440 | tf_op jit(solution)/shard_map/while/body/eval_jaxpr/ppermute | solution.py:11
  109.7 8.6 %collective-permute-start = (bf16[128,1024]{1,0:T(8,128)(2,1)S(1)}, bf16[128,1024]{1,0:T(8,128)(2,1)S(1)}, u32[]{:S(2)}, u32[]{:S(2)}) collective-permute-start(bf16[128,1024]{1,0:T(8,128)(2,1)S(1)} %get-tuple-element.473), channel_id=1, source_target_pairs={{0,1},{1,2},{2,3},{3,4},{4,5},{5,6},{6,7},{7,8},{8,9},{9,10},{10,1... | collective-permute-start | bytes 786440 | tf_op jit(solution)/shard_map/while/body/eval_jaxpr/ppermute | solution.py:11
  119.9 8.6 %collective-permute-start = (bf16[128,1024]{1,0:T(8,128)(2,1)S(1)}, bf16[128,1024]{1,0:T(8,128)(2,1)S(1)}, u32[]{:S(2)}, u32[]{:S(2)}) collective-permute-start(bf16[128,1024]{1,0:T(8,128)(2,1)S(1)} %get-tuple-element.473), channel_id=1, source_target_pairs={{0,1},{1,2},{2,3},{3,4},{4,5},{5,6},{6,7},{7,8},{8,9},{9,10},{10,1... | collective-permute-start | bytes 786440 | tf_op jit(solution)/shard_map/while/body/eval_jaxpr/ppermute | solution.py:11
  130.0 8.6 %collective-permute-start = (bf16[128,1024]{1,0:T(8,128)(2,1)S(1)}, bf16[128,1024]{1,0:T(8,128)(2,1)S(1)}, u32[]{:S(2)}, u32[]{:S(2)}) collective-permute-start(bf16[128,1024]{1,0:T(8,128)(2,1)S(1)} %get-tuple-element.473), channel_id=1, source_target_pairs={{0,1},{1,2},{2,3},{3,4},{4,5},{5,6},{6,7},{7,8},{8,9},{9,10},{10,1... | collective-permute-start | bytes 786440 | tf_op jit(solution)/shard_map/while/body/eval_jaxpr/ppermute | solution.py:11
  140.2 8.6 %collective-permute-start = (bf16[128,1024]{1,0:T(8,128)(2,1)S(1)}, bf16[128,1024]{1,0:T(8,128)(2,1)S(1)}, u32[]{:S(2)}, u32[]{:S(2)}) collective-permute-start(bf16[128,1024]{1,0:T(8,128)(2,1)S(1)} %get-tuple-element.473), channel_id=1, source_target_pairs={{0,1},{1,2},{2,3},{3,4},{4,5},{5,6},{6,7},{7,8},{8,9},{9,10},{10,1... | collective-permute-start | bytes 786440 | tf_op jit(solution)/shard_map/while/body/eval_jaxpr/ppermute | solution.py:11
  150.4 8.6 %collective-permute-start = (bf16[128,1024]{1,0:T(8,128)(2,1)S(1)}, bf16[128,1024]{1,0:T(8,128)(2,1)S(1)}, u32[]{:S(2)}, u32[]{:S(2)}) collective-permute-start(bf16[128,1024]{1,0:T(8,128)(2,1)S(1)} %get-tuple-element.473), channel_id=1, source_target_pairs={{0,1},{1,2},{2,3},{3,4},{4,5},{5,6},{6,7},{7,8},{8,9},{9,10},{10,1... | collective-permute-start | bytes 786440 | tf_op jit(solution)/shard_map/while/body/eval_jaxpr/ppermute | solution.py:11
  150.4 8.5 %collective-permute-start.1 = (bf16[128]{0:T(256)(128)(2,1)S(1)}, bf16[128]{0:T(256)(128)(2,1)S(1)}, u32[]{:S(2)}, u32[]{:S(2)}) collective-permute-start(bf16[128]{0:T(256)(128)(2,1)S(1)} %get-tuple-element.475), channel_id=1, source_target_pairs={{0,1},{1,2},{2,3},{3,4},{4,5},{5,6},{6,7},{7,8},{8,9},{9,10},{10,1... | collective-permute-start | bytes 776 | tf_op jit(solution)/shard_map/while/body/eval_jaxpr/ppermute | solution.py:11
  (25 other events, 193.7 us)
where the time goes:
time: 162 us
  waiting for transfers between devices  123 us (76%)
  matrix products  16.7 us (10%)
  other arithmetic  11.1 us (7%)
  starting transfers between devices  5.54 us (3%)
  local copies, waits for them, and re-layouts  3.43 us (2%)
  loops' own time  1.73 us (1%)
    ppermute x45, waiting for transfers between devices, from_behind(): lax.ppermute(array, axis, [(i, (i + by) % count) for i in range(count)])  123 us
    dot_general x16, matrix products, visit_block(): lax.dot_general(observed, sims, (((1,), (1,)), ((), ())), preferred_eleme...  11.4 us
    ppermute x45, starting transfers between devices, from_behind(): lax.ppermute(array, axis, [(i, (i + by) % count) for i in range(count)])  5.54 us
    dot_general x16, matrix products, visit_block(): lax.dot_general(params, weight_low, (((1,), (1,)), ((), ())), preferred_e...  5.37 us
    reduce_sum x16, other arithmetic, visit_block(): weight_total = weight_total * factor + jnp.sum(weights, axis=1)  3.88 us
  transfers between devices with their start and end apart: 45, of which 15 were waited for; matrix products, arithmetic and copies ran while one was open for 1% of the time, Pallas kernels for 0%

commit v1 on v0

v1 whole, which is shorter than its diff:
```python
import functools
import math

import jax
import jax.numpy as jnp
from jax import lax
from jax.experimental import pallas as pl
from jax.experimental.pallas import tpu as pltpu
from jax.sharding import PartitionSpec as P

NEG_START = -1e30
LOG2E = math.log2(math.e)
LANES = 256
SUBLANES = 8
VMEM_LIMIT = 40 * 1024 * 1024


def ring_of(chips, grid):
    if grid and chips % 2 == 0:
        return [2 * z for z in range(chips // 2)] + [2 * z + 1 for z in reversed(range(chips // 2))]
    return list(range(chips))


def plan(size, grid):
    chips = size // 2
    ring = ring_of(chips, grid)
    place = {chip: at for at, chip in enumerate(ring)}

    def beside(device, by):
        return ring[(place[device // 2] + by) % chips] * 2 + device % 2

    ways = [[1 if device % 2 == kind else -1 for device in range(size)] for kind in range(2)]
    pairs = [[(device, beside(device, ways[kind][device])) for device in range(size)] for kind in range(2)]
    order = [
        [device] + [beside(device, -ways[step % 2][device] * (step // 2 + 1)) for step in range(chips - 1)]
        for device in range(size)
    ]
    return pairs, order


def row(values):
    return values.reshape(1, values.shape[-1])


def prepare_kernel(
    at_ref, order_ref, pattern_ref, class_ref, sharp_ref, observed_ref, params_ref, sim_class_ref,
    own_ref, sib_ref, meta_ref, square_ref,
):
    steps = order_ref.shape[1]
    tiles = pattern_ref.shape[0]
    rows = class_ref.shape[-1]
    tile = rows // tiles
    at = at_ref[0]
    classes = row(class_ref[...]).astype(jnp.float32)
    scale = row(sharp_ref[...]) * (2.0 * LOG2E)
    own_ref[...] = jnp.zeros_like(own_ref)
    sib_ref[...] = jnp.zeros_like(sib_ref)
    own_ref[0:1, :] = scale
    sib_ref[0:1, :] = scale
    for step in range(steps):
        for out_ref, device in ((own_ref, at), (sib_ref, at ^ 1)):
            block = order_ref[device, step]
            for i in range(tiles):
                columns = slice(i * tile, (i + 1) * tile)
                is_open = pattern_ref[i, block] == 1
                out_ref[step + 1 : step + 2, columns] = jnp.where(is_open, classes[:, columns], -1.0)
    meta_ref[...] = jnp.zeros_like(meta_ref)
    meta_ref[0 : params_ref.shape[0], :] = params_ref[...].astype(jnp.float32)
    meta_ref[SUBLANES - 1 : SUBLANES, :] = row(sim_class_ref[...]).astype(jnp.float32)
    ones = jnp.ones((SUBLANES, observed_ref.shape[1]), jnp.bfloat16)
    for i in range(rows // LANES):
        part = observed_ref[i * LANES : (i + 1) * LANES, :].astype(jnp.float32)
        square = part * part
        high = square.astype(jnp.bfloat16)
        low = (square - high.astype(jnp.float32)).astype(jnp.bfloat16)
        total = lax.dot_general(ones, high, (((1,), (1,)), ((), ())), preferred_element_type=jnp.float32)
        total += lax.dot_general(ones, low, (((1,), (1,)), ((), ())), preferred_element_type=jnp.float32)
        square_ref[:, i * LANES : (i + 1) * LANES] = total


def absorb_kernel(step, own_ref, sib_ref, own_aux_ref, sib_aux_ref, block_ref, meta_ref, state_ref, out_ref):
    block = block_ref[...]
    wide = block.astype(jnp.float32)
    half_square = 0.5 * jnp.sum(wide * wide, axis=1, keepdims=True)
    meta = meta_ref[...]
    params = meta.astype(jnp.bfloat16)
    count = meta.shape[1]
    square_meta = jnp.concatenate([meta] + [jnp.zeros_like(meta)] * (count // SUBLANES - 1), axis=0)
    sim_class = square_meta.T[:, SUBLANES - 1 : SUBLANES]
    rows = own_ref.shape[0]
    for half, (obs_ref, aux_ref) in enumerate(((own_ref, own_aux_ref), (sib_ref, sib_aux_ref))):
        for i in range(rows // LANES):
            columns = slice(i * LANES, (i + 1) * LANES)
            inner = lax.dot_general(
                block, obs_ref[columns, :], (((1,), (1,)), ((), ())), preferred_element_type=jnp.float32
            )
            scale = aux_ref[0:1, columns]
            active = sim_class == aux_ref[step + 1 : step + 2, columns]
            score = jnp.where(active, inner - half_square, -jnp.inf)
            old = state_ref[half, 0:1, columns]
            top = jnp.maximum(old, jnp.max(score, axis=0, keepdims=True))
            factor = jnp.exp2((old - top) * scale)
            weights = jnp.exp2((score - top) * scale)
            total = state_ref[half, 1:2, columns] * factor + jnp.sum(weights, axis=0, keepdims=True)
            added = lax.dot_general(
                params, weights.astype(jnp.bfloat16), (((1,), (0,)), ((), ())), preferred_element_type=jnp.float32
            )
            out_ref[half, 0:1, columns] = top
            out_ref[half, 1:2, columns] = total
            out_ref[half, 2:6, columns] = state_ref[half, 2:6, columns] * factor + added[0:4]
            out_ref[half, 6:8, columns] = state_ref[half, 6:8, columns]


def finish_kernel(size, mine_ref, other_ref, aux_ref, square_ref, mean_ref, evidence_ref):
    scale = aux_ref[0:1, :]
    top_a, top_b = mine_ref[0:1, :], other_ref[0:1, :]
    top = jnp.maximum(top_a, top_b)
    factor_a = jnp.exp2((top_a - top) * scale)
    factor_b = jnp.exp2((top_b - top) * scale)
    total = mine_ref[1:2, :] * factor_a + other_ref[1:2, :] * factor_b
    sums = mine_ref[2:6, :] * factor_a + other_ref[2:6, :] * factor_b
    mean_ref[...] = sums / total
    sharp = scale * (0.5 / LOG2E)
    evidence = sharp * (2.0 * size - square_ref[0:1, :] + 2.0 * top) + jnp.log(total)
    evidence_ref[...] = evidence.reshape(evidence_ref.shape)


def on_device(pairs, order, observed, sharpness, obs_class, pattern, evolved, sim_params, sim_class):
    rows, size = observed.shape
    count = evolved.shape[0]
    steps = len(order[0])
    aux_rows = -(-(steps + 1) // SUBLANES) * SUBLANES
    vmem = pl.BlockSpec(memory_space=pltpu.VMEM)
    smem = pl.BlockSpec(memory_space=pltpu.SMEM)
    params = pltpu.CompilerParams(vmem_limit_bytes=VMEM_LIMIT)
    f32 = jnp.float32
    core = [(i, i ^ 1) for i in range(len(order))]

    observed_sib = lax.ppermute(observed, "blk", core)
    own_aux, sib_aux, meta, square = pl.pallas_call(
        prepare_kernel,
        out_shape=(
            jax.ShapeDtypeStruct((aux_rows, rows), f32),
            jax.ShapeDtypeStruct((aux_rows, rows), f32),
            jax.ShapeDtypeStruct((SUBLANES, count), f32),
            jax.ShapeDtypeStruct((SUBLANES, rows), f32),
        ),
        in_specs=[smem, smem, smem, vmem, vmem, vmem, vmem, vmem],
        out_specs=(vmem,) * 4,
        compiler_params=params,
        name="prepare",
    )(
        lax.axis_index("blk").reshape(1), jnp.array(order, jnp.int32), pattern, obs_class, sharpness, observed,
        sim_params, sim_class,
    )
    sib_aux = lax.ppermute(sib_aux, "blk", core)

    state = jnp.zeros((2, SUBLANES, rows), f32).at[:, 0].set(NEG_START)

    def absorb(step, block, about, state):
        return pl.pallas_call(
            functools.partial(absorb_kernel, step),
            out_shape=jax.ShapeDtypeStruct(state.shape, f32),
            in_specs=[vmem] * 7,
            out_specs=vmem,
            compiler_params=params,
            cost_estimate=pl.CostEstimate(
                flops=4 * rows * count * size, bytes_accessed=4 * rows * size, transcendentals=2 * rows * count
            ),
            name="absorb",
        )(observed, observed_sib, own_aux, sib_aux, block, about, state)

    held = [(evolved, meta), (evolved, meta)]
    state = absorb(0, evolved, meta, state)
    for step in range(steps - 1):
        kind = step % 2
        held[kind] = tuple(lax.ppermute(part, "blk", pairs[kind]) for part in held[kind])
        state = absorb(step + 1, *held[kind], state)

    other = lax.ppermute(state[1], "blk", core)
    mean, evidence = pl.pallas_call(
        functools.partial(finish_kernel, size),
        out_shape=(jax.ShapeDtypeStruct((sim_params.shape[0], rows), f32), jax.ShapeDtypeStruct((rows,), f32)),
        in_specs=[vmem] * 4,
        out_specs=(vmem,) * 2,
        compiler_params=params,
        name="finish",
    )(state[0], other, own_aux, square)
    return mean, evidence


def solution(mesh):
    placed = (
        P(("parts", "blk"), None),
        P(("parts", "blk")),
        P(("parts", "blk")),
        P(("parts", "blk"), None),
        P(("parts", "blk"), None),
        P(None, ("parts", "blk")),
        P(("parts", "blk")),
    )
    pairs, order = plan(mesh.shape["blk"], mesh.shape["parts"] == 2)
    return jax.shard_map(
        functools.partial(on_device, pairs, order),
        mesh=mesh,
        in_specs=placed,
        out_specs=(P(None, ("parts", "blk")), P(("parts", "blk"))),
        check_vma=False,
    )
```

time: 162 us -> 74.6 us (0.46)
  waiting for transfers between devices: 123 us -> 24.3 us
  Pallas kernels: 0 us -> 22.9 us
  matrix products: 16.7 us -> 0 us
  starting transfers between devices: 5.54 us -> 19 us
  other arithmetic: 11.1 us -> 0 us
  local copies, waits for them, and re-layouts: 3.43 us -> 7.25 us
  loops' own time: 1.73 us -> 0 us
    ppermute x45 -> x17, waiting for transfers between devices: 123 us -> 24.3 us  [the longest x14 23.1 us: on_device(): lax.ppermute(part, 'blk', pairs[kind])]
    pallas_call x0 -> x10, Pallas kernels: none -> 22.9 us  [the longest x8 20.6 us: absorb(): pl.pallas_call(functools.partial(absorb_kernel, step), out_shape=jax.Shap...]
    dot_general x32 -> x0, matrix products: 16.7 us -> none  [the longest x16 11.4 us: visit_block(): lax.dot_general(observed, sims, (((1,), (1,)), ((), ())), preferred_eleme...]
    ppermute x45 -> x17, starting transfers between devices: 5.54 us -> 19 us  [the longest x14 18.5 us: on_device(): lax.ppermute(part, 'blk', pairs[kind])]
    reduce_sum x33 -> x0, other arithmetic: 7.81 us -> none  [the longest x16 3.88 us: visit_block(): weight_total = weight_total * factor + jnp.sum(weights, axis=1)]
    unnamed x10 -> x20, local copies, waits for them, and re-layouts: 1.77 us -> 7.25 us
    another operation x1 -> x0, loops' own time: 1.73 us -> none  [on_device(): state, packet_end = lax.fori_loop(1, cycle_size, turn, (state, packet))]
  transfers between devices with their start and end apart: 45 -> 17, of which waited for: 15 -> 8; matrix products, arithmetic and copies ran while one was open for 1% -> 0% of each run, Pallas kernels for 0% -> 27%
where the time goes in v1:
time: 74.6 us; the launch traced here: 74.2 us
  waiting for transfers between devices  24.3 us (33%)
  Pallas kernels  22.9 us (31%)
  starting transfers between devices  19 us (25%)
  local copies, waits for them, and re-layouts  7.25 us (10%)
    ppermute x14, waiting for transfers between devices, on_device(): lax.ppermute(part, 'blk', pairs[kind])  23.1 us
    pallas_call x8, Pallas kernels, absorb(): pl.pallas_call(functools.partial(absorb_kernel, step), out_shape=jax.Shap...  20.6 us
    ppermute x14, starting transfers between devices, on_device(): lax.ppermute(part, 'blk', pairs[kind])  18.5 us
    unnamed x20, local copies, waits for them, and re-layouts  7.25 us
    pallas_call x1, Pallas kernels, on_device(): pl.pallas_call(prepare_kernel, out_shape=(jax.ShapeDtypeStruct((aux_rows,...  1.66 us
  transfers between devices with their start and end apart: 17, of which 8 were waited for; matrix products, arithmetic and copies ran while one was open for 0% of the time, Pallas kernels for 27%

profile of v1, /device:TPU:0, one launch (start us, length us, event | category | flops | bytes accessed | tf_op | source)
XLA Modules:
  0.0 74.2 jit_solution(8835728124493432707)
XLA Ops:
  1.1 2.6 %collective-permute-start.2 = (bf16[128,1024]{1,0:T(8,128)(2,1)}, bf16[128,1024]{1,0:T(8,128)(2,1)S(1)}, u32[]{:S(2)}, u32[]{:S(2)}) collective-permute-start(bf16[128,1024]{1,0:T(8,128)(2,1)} %block_ref.1), channel_id=1, source_target_pairs={{0,4},{1,3},{2,0},{3,7},{4,8},{5,1},{6,2},{7,11},{8,12},{9,5},{10,... | collective-permute-start | bytes 786440 | tf_op jit(solution)/shard_map/ppermute | solution.py:177
  3.8 6.5 %collective-permute-done.2.block_ref = bf16[128,1024]{1,0:T(8,128)(2,1)S(1)} collective-permute-done((bf16[128,1024]{1,0:T(8,128)(2,1)}, bf16[128,1024]{1,0:T(8,128)(2,1)S(1)}, u32[]{:S(2)}, u32[]{:S(2)}) %collective-permute-start.2) | collective-permute-done | bytes 262176 | tf_op jit(solution)/shard_map/ppermute | solution.py:177
  10.3 2.4 %collective-permute-start.3 = (bf16[128,1024]{1,0:T(8,128)(2,1)S(1)}, bf16[128,1024]{1,0:T(8,128)(2,1)S(1)}, u32[]{:S(2)}, u32[]{:S(2)}) collective-permute-start(bf16[128,1024]{1,0:T(8,128)(2,1)S(1)} %collective-permute-done.2.block_ref), channel_id=1, source_target_pairs={{0,4},{1,3},{2,0},{3,7},{4,8},{5,1},{6,2},{7,11},{8,12},{9,5},{10,... | collective-permute-start | bytes 786440 | tf_op jit(solution)/shard_map/ppermute | solution.py:177
  12.7 6.4 %collective-permute-done.3.block_ref = bf16[128,1024]{1,0:T(8,128)(2,1)S(1)} collective-permute-done((bf16[128,1024]{1,0:T(8,128)(2,1)S(1)}, bf16[128,1024]{1,0:T(8,128)(2,1)S(1)}, u32[]{:S(2)}, u32[]{:S(2)}) %collective-permute-start.3) | collective-permute-done | bytes 262176 | tf_op jit(solution)/shard_map/ppermute | solution.py:177
  19.1 1.5 %collective-permute-start.4 = (bf16[128,1024]{1,0:T(8,128)(2,1)S(1)}, bf16[128,1024]{1,0:T(8,128)(2,1)S(1)}, u32[]{:S(2)}, u32[]{:S(2)}) collective-permute-start(bf16[128,1024]{1,0:T(8,128)(2,1)S(1)} %collective-permute-done.3.block_ref), channel_id=1, source_target_pairs={{0,4},{1,3},{2,0},{3,7},{4,8},{5,1},{6,2},{7,11},{8,12},{9,5},{10,... | collective-permute-start | bytes 786440 | tf_op jit(solution)/shard_map/ppermute | solution.py:177
  20.6 1.4 %copy-done = bf16[768,1024]{1,0:T(8,128)(2,1)S(1)} copy-done((bf16[768,1024]{1,0:T(8,128)(2,1)S(1)}, bf16[768,1024]{1,0:T(8,128)(2,1)}, u32[]{:S(2)}) %copy-start) | copy-done | bytes 1572888
  26.1 1.7 %prepare.1 = (f32[16,768]{1,0:T(8,128)S(1)}, f32[16,768]{1,0:T(8,128)S(1)}, f32[8,128]{1,0:T(8,128)S(1)}, f32[8,768]{1,0:T(8,128)S(1)}) custom-call(s32[1]{0:T(128)} %bitcast.at_ref, s32[16,8]{1,0:T(8,128)S(1)} %copy-done.4, s32[6,16]{1,0:T(8,128)S(1)} %copy-done.5, s32[768]{0:T(1024)S(1)} %copy-done.6, f32[768]{0:T(1024)S(1)} %copy-done.7, ...), custom_call_target="tpu_custom_call" | custom-call | tf_op jit(solution)/shard_map/prepare/pallas_call | solution.py:140
  28.5 1.3 %collective-permute-start.6 = (f32[8,128]{1,0:T(8,128)S(1)}, f32[8,128]{1,0:T(8,128)S(1)}, u32[]{:S(2)}, u32[]{:S(2)}) collective-permute-start(f32[8,128]{1,0:T(8,128)S(1)} %get-tuple-element.20.meta_ref), channel_id=1, source_target_pairs={{0,4},{1,3},{2,0},{3,7},{4,8},{5,1},{6,2},{7,11},{8,12},{9,5},{10,... | collective-permute-start | bytes 12296 | tf_op jit(solution)/shard_map/ppermute | solution.py:177
  29.8 2.3 %collective-permute-done.6.meta_ref = f32[8,128]{1,0:T(8,128)S(1)} collective-permute-done((f32[8,128]{1,0:T(8,128)S(1)}, f32[8,128]{1,0:T(8,128)S(1)}, u32[]{:S(2)}, u32[]{:S(2)}) %collective-permute-start.6) | collective-permute-done | bytes 4128 | tf_op jit(solution)/shard_map/ppermute | solution.py:177
  32.2 2.1 %collective-permute-start.13 = (f32[8,128]{1,0:T(8,128)S(1)}, f32[8,128]{1,0:T(8,128)S(1)}, u32[]{:S(2)}, u32[]{:S(2)}) collective-permute-start(f32[8,128]{1,0:T(8,128)S(1)} %get-tuple-element.20.meta_ref), channel_id=1, source_target_pairs={{0,2},{1,5},{2,6},{3,1},{4,0},{5,9},{6,10},{7,3},{8,4},{9,13},{10,... | collective-permute-start | bytes 12296 | tf_op jit(solution)/shard_map/ppermute | solution.py:177
  34.2 1.5 %collective-permute-done.13.meta_ref = f32[8,128]{1,0:T(8,128)S(1)} collective-permute-done((f32[8,128]{1,0:T(8,128)S(1)}, f32[8,128]{1,0:T(8,128)S(1)}, u32[]{:S(2)}, u32[]{:S(2)}) %collective-permute-start.13) | collective-permute-done | bytes 4128 | tf_op jit(solution)/shard_map/ppermute | solution.py:177
  37.1 2.4 %collective-permute-done.7.meta_ref = f32[8,128]{1,0:T(8,128)S(1)} collective-permute-done((f32[8,128]{1,0:T(8,128)S(1)}, f32[8,128]{1,0:T(8,128)S(1)}, u32[]{:S(2)}, u32[]{:S(2)}) %collective-permute-start.7) | collective-permute-done | bytes 4128 | tf_op jit(solution)/shard_map/ppermute | solution.py:177
  39.4 2.0 %collective-permute-start.14 = (f32[8,128]{1,0:T(8,128)S(1)}, f32[8,128]{1,0:T(8,128)S(1)}, u32[]{:S(2)}, u32[]{:S(2)}) collective-permute-start(f32[8,128]{1,0:T(8,128)S(1)} %collective-permute-done.13.meta_ref), channel_id=1, source_target_pairs={{0,2},{1,5},{2,6},{3,1},{4,0},{5,9},{6,10},{7,3},{8,4},{9,13},{10,... | collective-permute-start | bytes 12296 | tf_op jit(solution)/shard_map/ppermute | solution.py:177
  41.5 1.6 %collective-permute-done.14.meta_ref = f32[8,128]{1,0:T(8,128)S(1)} collective-permute-done((f32[8,128]{1,0:T(8,128)S(1)}, f32[8,128]{1,0:T(8,128)S(1)}, u32[]{:S(2)}, u32[]{:S(2)}) %collective-permute-start.14) | collective-permute-done | bytes 4128 | tf_op jit(solution)/shard_map/ppermute | solution.py:177
  44.3 2.4 %collective-permute-done.8.meta_ref = f32[8,128]{1,0:T(8,128)S(1)} collective-permute-done((f32[8,128]{1,0:T(8,128)S(1)}, f32[8,128]{1,0:T(8,128)S(1)}, u32[]{:S(2)}, u32[]{:S(2)}) %collective-permute-start.8) | collective-permute-done | bytes 4128 | tf_op jit(solution)/shard_map/ppermute | solution.py:177
  46.6 2.0 %collective-permute-start.15 = (f32[8,128]{1,0:T(8,128)S(1)}, f32[8,128]{1,0:T(8,128)S(1)}, u32[]{:S(2)}, u32[]{:S(2)}) collective-permute-start(f32[8,128]{1,0:T(8,128)S(1)} %collective-permute-done.14.meta_ref), channel_id=1, source_target_pairs={{0,2},{1,5},{2,6},{3,1},{4,0},{5,9},{6,10},{7,3},{8,4},{9,13},{10,... | collective-permute-start | bytes 12296 | tf_op jit(solution)/shard_map/ppermute | solution.py:177
  51.7 2.6 %absorb.8.state_ref = f32[2,8,768]{2,1,0:T(8,128)S(1)} custom-call(bf16[768,1024]{1,0:T(8,128)(2,1)S(1)} %copy-done.1, bf16[768,1024]{1,0:T(8,128)(2,1)S(1)} %collective-permute-done.sib_ref, f32[16,768]{1,0:T(8,128)S(1)} %get-tuple-element.18.own_aux_ref.aux_ref, f32[16,768]{1,0:T(8,128)S(1)} %collective-permute-done.1.sib_aux_ref, ...), custom_call_target="tpu_custom_call" | custom-call | flops 402653184 | bytes 3145728 | tf_op jit(solution)/shard_map/absorb/pallas_call | solution.py:161
  54.3 2.6 %absorb.9.state_ref = f32[2,8,768]{2,1,0:T(8,128)S(1)} custom-call(bf16[768,1024]{1,0:T(8,128)(2,1)S(1)} %copy-done.1, bf16[768,1024]{1,0:T(8,128)(2,1)S(1)} %collective-permute-done.sib_ref, f32[16,768]{1,0:T(8,128)S(1)} %get-tuple-element.18.own_aux_ref.aux_ref, f32[16,768]{1,0:T(8,128)S(1)} %collective-permute-done.1.sib_aux_ref, ...), custom_call_target="tpu_custom_call" | custom-call | flops 402653184 | bytes 3145728 | tf_op jit(solution)/shard_map/absorb/pallas_call | solution.py:161
  56.8 2.6 %absorb.10.state_ref = f32[2,8,768]{2,1,0:T(8,128)S(1)} custom-call(bf16[768,1024]{1,0:T(8,128)(2,1)S(1)} %copy-done.1, bf16[768,1024]{1,0:T(8,128)(2,1)S(1)} %collective-permute-done.sib_ref, f32[16,768]{1,0:T(8,128)S(1)} %get-tuple-element.18.own_aux_ref.aux_ref, f32[16,768]{1,0:T(8,128)S(1)} %collective-permute-done.1.sib_aux_ref, ...), custom_call_target="tpu_custom_call" | custom-call | flops 402653184 | bytes 3145728 | tf_op jit(solution)/shard_map/absorb/pallas_call | solution.py:161
  59.4 2.6 %absorb.11.state_ref = f32[2,8,768]{2,1,0:T(8,128)S(1)} custom-call(bf16[768,1024]{1,0:T(8,128)(2,1)S(1)} %copy-done.1, bf16[768,1024]{1,0:T(8,128)(2,1)S(1)} %collective-permute-done.sib_ref, f32[16,768]{1,0:T(8,128)S(1)} %get-tuple-element.18.own_aux_ref.aux_ref, f32[16,768]{1,0:T(8,128)S(1)} %collective-permute-done.1.sib_aux_ref, ...), custom_call_target="tpu_custom_call" | custom-call | flops 402653184 | bytes 3145728 | tf_op jit(solution)/shard_map/absorb/pallas_call | solution.py:161
  62.0 2.6 %absorb.12.state_ref = f32[2,8,768]{2,1,0:T(8,128)S(1)} custom-call(bf16[768,1024]{1,0:T(8,128)(2,1)S(1)} %copy-done.1, bf16[768,1024]{1,0:T(8,128)(2,1)S(1)} %collective-permute-done.sib_ref, f32[16,768]{1,0:T(8,128)S(1)} %get-tuple-element.18.own_aux_ref.aux_ref, f32[16,768]{1,0:T(8,128)S(1)} %collective-permute-done.1.sib_aux_ref, ...), custom_call_target="tpu_custom_call" | custom-call | flops 402653184 | bytes 3145728 | tf_op jit(solution)/shard_map/absorb/pallas_call | solution.py:161
  64.6 2.6 %absorb.13.state_ref = f32[2,8,768]{2,1,0:T(8,128)S(1)} custom-call(bf16[768,1024]{1,0:T(8,128)(2,1)S(1)} %copy-done.1, bf16[768,1024]{1,0:T(8,128)(2,1)S(1)} %collective-permute-done.sib_ref, f32[16,768]{1,0:T(8,128)S(1)} %get-tuple-element.18.own_aux_ref.aux_ref, f32[16,768]{1,0:T(8,128)S(1)} %collective-permute-done.1.sib_aux_ref, ...), custom_call_target="tpu_custom_call" | custom-call | flops 402653184 | bytes 3145728 | tf_op jit(solution)/shard_map/absorb/pallas_call | solution.py:161
  67.2 2.6 %absorb.14.state_ref = f32[2,8,768]{2,1,0:T(8,128)S(1)} custom-call(bf16[768,1024]{1,0:T(8,128)(2,1)S(1)} %copy-done.1, bf16[768,1024]{1,0:T(8,128)(2,1)S(1)} %collective-permute-done.sib_ref, f32[16,768]{1,0:T(8,128)S(1)} %get-tuple-element.18.own_aux_ref.aux_ref, f32[16,768]{1,0:T(8,128)S(1)} %collective-permute-done.1.sib_aux_ref, ...), custom_call_target="tpu_custom_call" | custom-call | flops 402653184 | bytes 3145728 | tf_op jit(solution)/shard_map/absorb/pallas_call | solution.py:161
  69.7 2.6 %absorb.15 = f32[2,8,768]{2,1,0:T(8,128)S(1)} custom-call(bf16[768,1024]{1,0:T(8,128)(2,1)S(1)} %copy-done.1, bf16[768,1024]{1,0:T(8,128)(2,1)S(1)} %collective-permute-done.sib_ref, f32[16,768]{1,0:T(8,128)S(1)} %get-tuple-element.18.own_aux_ref.aux_ref, f32[16,768]{1,0:T(8,128)S(1)} %collective-permute-done.1.sib_aux_ref, ...), custom_call_target="tpu_custom_call" | custom-call | flops 402653184 | bytes 3145728 | tf_op jit(solution)/shard_map/absorb/pallas_call | solution.py:161
  (41 shorter events, 12.8 us)
Async XLA Ops:
  0.6 49.3 %collective-permute-start = (bf16[768,1024]{1,0:T(8,128)(2,1)}, bf16[768,1024]{1,0:T(8,128)(2,1)S(1)}, u32[]{:S(2)}, u32[]{:S(2)}) collective-permute-start(bf16[768,1024]{1,0:T(8,128)(2,1)} %own_ref.15), channel_id=1, source_target_pairs={{0,1},{1,0},{2,3},{3,2},{4,5},{5,4},{6,7},{7,6},{8,9},{9,8},{10,11... | collective-permute-start | bytes 4718600 | tf_op jit(solution)/shard_map/ppermute | solution.py:139
  1.1 9.1 %collective-permute-start.2 = (bf16[128,1024]{1,0:T(8,128)(2,1)}, bf16[128,1024]{1,0:T(8,128)(2,1)S(1)}, u32[]{:S(2)}, u32[]{:S(2)}) collective-permute-start(bf16[128,1024]{1,0:T(8,128)(2,1)} %block_ref.1), channel_id=1, source_target_pairs={{0,4},{1,3},{2,0},{3,7},{4,8},{5,1},{6,2},{7,11},{8,12},{9,5},{10,... | collective-permute-start | bytes 786440 | tf_op jit(solution)/shard_map/ppermute | solution.py:177
  3.8 8.9 %collective-permute-start.10 = (bf16[128,1024]{1,0:T(8,128)(2,1)}, bf16[128,1024]{1,0:T(8,128)(2,1)S(1)}, u32[]{:S(2)}, u32[]{:S(2)}) collective-permute-start(bf16[128,1024]{1,0:T(8,128)(2,1)} %block_ref.1), channel_id=1, source_target_pairs={{0,2},{1,5},{2,6},{3,1},{4,0},{5,9},{6,10},{7,3},{8,4},{9,13},{10,... | collective-permute-start | bytes 786440 | tf_op jit(solution)/shard_map/ppermute | solution.py:177
  10.3 8.8 %collective-permute-start.3 = (bf16[128,1024]{1,0:T(8,128)(2,1)S(1)}, bf16[128,1024]{1,0:T(8,128)(2,1)S(1)}, u32[]{:S(2)}, u32[]{:S(2)}) collective-permute-start(bf16[128,1024]{1,0:T(8,128)(2,1)S(1)} %collective-permute-done.2.block_ref), channel_id=1, source_target_pairs={{0,4},{1,3},{2,0},{3,7},{4,8},{5,1},{6,2},{7,11},{8,12},{9,5},{10,... | collective-permute-start | bytes 786440 | tf_op jit(solution)/shard_map/ppermute | solution.py:177
  12.7 15.1 %collective-permute-start.11 = (bf16[128,1024]{1,0:T(8,128)(2,1)S(1)}, bf16[128,1024]{1,0:T(8,128)(2,1)S(1)}, u32[]{:S(2)}, u32[]{:S(2)}) collective-permute-start(bf16[128,1024]{1,0:T(8,128)(2,1)S(1)} %collective-permute-done.10.block_ref), channel_id=1, source_target_pairs={{0,2},{1,5},{2,6},{3,1},{4,0},{5,9},{6,10},{7,3},{8,4},{9,13},{10,... | collective-permute-start | bytes 786440 | tf_op jit(solution)/shard_map/ppermute | solution.py:177
  19.1 29.6 %collective-permute-start.4 = (bf16[128,1024]{1,0:T(8,128)(2,1)S(1)}, bf16[128,1024]{1,0:T(8,128)(2,1)S(1)}, u32[]{:S(2)}, u32[]{:S(2)}) collective-permute-start(bf16[128,1024]{1,0:T(8,128)(2,1)S(1)} %collective-permute-done.3.block_ref), channel_id=1, source_target_pairs={{0,4},{1,3},{2,0},{3,7},{4,8},{5,1},{6,2},{7,11},{8,12},{9,5},{10,... | collective-permute-start | bytes 786440 | tf_op jit(solution)/shard_map/ppermute | solution.py:177
  20.6 1.4 %copy-start = (bf16[768,1024]{1,0:T(8,128)(2,1)S(1)}, bf16[768,1024]{1,0:T(8,128)(2,1)}, u32[]{:S(2)}) copy-start(bf16[768,1024]{1,0:T(8,128)(2,1)} %own_ref.15) | copy-start | bytes 4718596
  22.0 0.7 copy-start.4
  22.7 0.7 copy-start.5
  23.4 0.7 copy-start.6
  26.1 23.9 %copy-start.1 = (bf16[768,1024]{1,0:T(8,128)(2,1)S(1)}, bf16[768,1024]{1,0:T(8,128)(2,1)}, u32[]{:S(2)}) copy-start(bf16[768,1024]{1,0:T(8,128)(2,1)} %own_ref.15) | copy-start | bytes 4718596
  27.7 20.9 %collective-permute-start.1 = (f32[16,768]{1,0:T(8,128)S(1)}, f32[16,768]{1,0:T(8,128)S(1)}, u32[]{:S(2)}, u32[]{:S(2)}) collective-permute-start(f32[16,768]{1,0:T(8,128)S(1)} %get-tuple-element.19), channel_id=1, source_target_pairs={{0,1},{1,0},{2,3},{3,2},{4,5},{5,4},{6,7},{7,6},{8,9},{9,8},{10,11... | collective-permute-start | bytes 147464 | tf_op jit(solution)/shard_map/ppermute | solution.py:156
  27.8 39.4 %collective-permute-start.12 = (bf16[128,1024]{1,0:T(8,128)(2,1)S(1)}, bf16[128,1024]{1,0:T(8,128)(2,1)S(1)}, u32[]{:S(2)}, u32[]{:S(2)}) collective-permute-start(bf16[128,1024]{1,0:T(8,128)(2,1)S(1)} %collective-permute-done.11.block_ref), channel_id=1, source_target_pairs={{0,2},{1,5},{2,6},{3,1},{4,0},{5,9},{6,10},{7,3},{8,4},{9,13},{10,... | collective-permute-start | bytes 786440 | tf_op jit(solution)/shard_map/ppermute | solution.py:177
  28.5 3.7 %collective-permute-start.6 = (f32[8,128]{1,0:T(8,128)S(1)}, f32[8,128]{1,0:T(8,128)S(1)}, u32[]{:S(2)}, u32[]{:S(2)}) collective-permute-start(f32[8,128]{1,0:T(8,128)S(1)} %get-tuple-element.20.meta_ref), channel_id=1, source_target_pairs={{0,4},{1,3},{2,0},{3,7},{4,8},{5,1},{6,2},{7,11},{8,12},{9,5},{10,... | collective-permute-start | bytes 12296 | tf_op jit(solution)/shard_map/ppermute | solution.py:177
  32.2 3.6 %collective-permute-start.13 = (f32[8,128]{1,0:T(8,128)S(1)}, f32[8,128]{1,0:T(8,128)S(1)}, u32[]{:S(2)}, u32[]{:S(2)}) collective-permute-start(f32[8,128]{1,0:T(8,128)S(1)} %get-tuple-element.20.meta_ref), channel_id=1, source_target_pairs={{0,2},{1,5},{2,6},{3,1},{4,0},{5,9},{6,10},{7,3},{8,4},{9,13},{10,... | collective-permute-start | bytes 12296 | tf_op jit(solution)/shard_map/ppermute | solution.py:177
  35.8 3.6 %collective-permute-start.7 = (f32[8,128]{1,0:T(8,128)S(1)}, f32[8,128]{1,0:T(8,128)S(1)}, u32[]{:S(2)}, u32[]{:S(2)}) collective-permute-start(f32[8,128]{1,0:T(8,128)S(1)} %collective-permute-done.6.meta_ref), channel_id=1, source_target_pairs={{0,4},{1,3},{2,0},{3,7},{4,8},{5,1},{6,2},{7,11},{8,12},{9,5},{10,... | collective-permute-start | bytes 12296 | tf_op jit(solution)/shard_map/ppermute | solution.py:177
  39.4 3.6 %collective-permute-start.14 = (f32[8,128]{1,0:T(8,128)S(1)}, f32[8,128]{1,0:T(8,128)S(1)}, u32[]{:S(2)}, u32[]{:S(2)}) collective-permute-start(f32[8,128]{1,0:T(8,128)S(1)} %collective-permute-done.13.meta_ref), channel_id=1, source_target_pairs={{0,2},{1,5},{2,6},{3,1},{4,0},{5,9},{6,10},{7,3},{8,4},{9,13},{10,... | collective-permute-start | bytes 12296 | tf_op jit(solution)/shard_map/ppermute | solution.py:177
  43.0 3.6 %collective-permute-start.8 = (f32[8,128]{1,0:T(8,128)S(1)}, f32[8,128]{1,0:T(8,128)S(1)}, u32[]{:S(2)}, u32[]{:S(2)}) collective-permute-start(f32[8,128]{1,0:T(8,128)S(1)} %collective-permute-done.7.meta_ref), channel_id=1, source_target_pairs={{0,4},{1,3},{2,0},{3,7},{4,8},{5,1},{6,2},{7,11},{8,12},{9,5},{10,... | collective-permute-start | bytes 12296 | tf_op jit(solution)/shard_map/ppermute | solution.py:177
  46.6 20.5 %collective-permute-start.15 = (f32[8,128]{1,0:T(8,128)S(1)}, f32[8,128]{1,0:T(8,128)S(1)}, u32[]{:S(2)}, u32[]{:S(2)}) collective-permute-start(f32[8,128]{1,0:T(8,128)S(1)} %collective-permute-done.14.meta_ref), channel_id=1, source_target_pairs={{0,2},{1,5},{2,6},{3,1},{4,0},{5,9},{6,10},{7,3},{8,4},{9,13},{10,... | collective-permute-start | bytes 12296 | tf_op jit(solution)/shard_map/ppermute | solution.py:177
  48.7 21.1 %collective-permute-start.9 = (f32[8,128]{1,0:T(8,128)S(1)}, f32[8,128]{1,0:T(8,128)S(1)}, u32[]{:S(2)}, u32[]{:S(2)}) collective-permute-start(f32[8,128]{1,0:T(8,128)S(1)} %collective-permute-done.8.meta_ref), channel_id=1, source_target_pairs={{0,4},{1,3},{2,0},{3,7},{4,8},{5,1},{6,2},{7,11},{8,12},{9,5},{10,... | collective-permute-start | bytes 12296 | tf_op jit(solution)/shard_map/ppermute | solution.py:177
  48.7 21.1 %collective-permute-start.5 = (bf16[128,1024]{1,0:T(8,128)(2,1)S(1)}, bf16[128,1024]{1,0:T(8,128)(2,1)S(1)}, u32[]{:S(2)}, u32[]{:S(2)}) collective-permute-start(bf16[128,1024]{1,0:T(8,128)(2,1)S(1)} %collective-permute-done.4.block_ref), channel_id=1, source_target_pairs={{0,4},{1,3},{2,0},{3,7},{4,8},{5,1},{6,2},{7,11},{8,12},{9,5},{10,... | collective-permute-start | bytes 786440 | tf_op jit(solution)/shard_map/ppermute | solution.py:177
  49.9 1.0 %copy-start.2 = (bf16[128,1024]{1,0:T(8,128)(2,1)S(1)}, bf16[128,1024]{1,0:T(8,128)(2,1)}, u32[]{:S(2)}) copy-start(bf16[128,1024]{1,0:T(8,128)(2,1)} %block_ref.1) | copy-start | bytes 786436
  50.9 0.8 %copy-start.3 = (f32[2,8,768]{2,1,0:T(8,128)S(1)}, f32[2,8,768]{2,1,0:T(8,128)}, u32[]{:S(2)}) copy-start(f32[2,8,768]{2,1,0:T(8,128)} %constant.35.clone.1.state_ref) | copy-start | bytes 147460
  72.3 1.2 %collective-permute-start.16 = (f32[8,768]{1,0:T(8,128)S(1)}, f32[8,768]{1,0:T(8,128)S(1)}, u32[]{:S(2)}, u32[]{:S(2)}) collective-permute-start(f32[8,768]{1,0:T(8,128)S(1)} %get-tuple-element.22), channel_id=1, source_target_pairs={{0,1},{1,0},{2,3},{3,2},{4,5},{5,4},{6,7},{7,6},{8,9},{9,8},{10,11... | collective-permute-start | bytes 73736 | tf_op jit(solution)/shard_map/ppermute | solution.py:180
  (3 other events, 2.0 us)

commit v2 on v0

v2 whole, which is shorter than its diff:
```python
import functools
import math

import jax
import jax.numpy as jnp
import numpy as np
from jax import lax
from jax.experimental import pallas as pl
from jax.experimental.pallas import tpu as pltpu
from jax.sharding import PartitionSpec as P

NEG_START = -1e30
LOG2E = math.log2(math.e)
SUBLANES = 8
VMEM_LIMIT = 40 * 1024 * 1024


def plan(size, grid):
    chips = size // 2

    def ring(place):
        if not grid:
            return place
        return jnp.where(place < chips // 2, 2 * place, 2 * (chips - 1 - place) + 1)

    def place_of(chip):
        if not grid:
            return chip
        return jnp.where(chip % 2 == 0, chip // 2, chips - 1 - chip // 2)

    def beside(device, by):
        return ring((place_of(device // 2) + by + chips) % chips) * 2 + device % 2

    def way(device, kind):
        return 1 - 2 * ((device + kind) % 2)

    def block_of(device, step):
        if step == 0:
            return device
        return beside(device, -way(device, (step - 1) % 2) * ((step + 1) // 2))

    all_devices = np.arange(size)
    with jax.ensure_compile_time_eval():
        targets = [np.asarray(beside(all_devices, way(all_devices, kind))).tolist() for kind in range(2)]
    return [list(enumerate(target)) for target in targets], block_of


def joined(parts, axis):
    return parts[0] if len(parts) == 1 else jnp.concatenate(parts, axis=axis)


def lanes_of(aux_ref, at):
    return jnp.concatenate([aux_ref[i, pl.ds(at, 1), :] for i in range(aux_ref.shape[0])], axis=1)


def norms(observed):
    wide = observed.astype(jnp.float32)
    square = wide * wide
    high = square.astype(jnp.bfloat16)
    low = (square - high.astype(jnp.float32)).astype(jnp.bfloat16)
    ones = jnp.ones((SUBLANES, observed.shape[1]), jnp.bfloat16)
    return sum(
        lax.dot_general(ones, part, (((1,), (1,)), ((), ())), preferred_element_type=jnp.float32)[0:1]
        for part in (high, low)
    )


def absorb_kernel(steps, block_of, half, first, at_ref, observed_ref, aux_ref, *refs):
    count = len(steps)
    block_refs, meta_refs, out_ref = refs[:count], refs[count : 2 * count], refs[-1]
    inner = lax.dot_general(
        joined([ref[...] for ref in block_refs], 0), observed_ref[...],
        (((1,), (1,)), ((), ())), preferred_element_type=jnp.float32,
    )
    scale = lanes_of(aux_ref, aux_ref.shape[1] - 1) * (2.0 * LOG2E)
    metas = [ref[...] for ref in meta_refs]
    if first:
        top = jnp.full(scale.shape, NEG_START, jnp.float32)
    else:
        state_ref = refs[2 * count]
        top = old = state_ref[0:1, :]
    scores = []
    for i, (step, block_ref, meta) in enumerate(zip(steps, block_refs, metas)):
        rows = block_ref.shape[0]
        wide = block_ref[...].astype(jnp.float32)
        half_square = 0.5 * jnp.sum(wide * wide, axis=1, keepdims=True)
        padded = jnp.concatenate([meta] + [jnp.zeros_like(meta)] * (rows // SUBLANES - 1), axis=0)
        active = padded.T[:, SUBLANES - 1 : SUBLANES] == lanes_of(aux_ref, block_of(at_ref[0], step))
        score = jnp.where(active, inner[i * rows : (i + 1) * rows] - half_square, -jnp.inf)
        top = jnp.maximum(top, jnp.max(score, axis=0, keepdims=True))
        scores.append(score)
    weights = [jnp.exp2((score - top) * scale) for score in scores]
    total = sum(jnp.sum(weight, axis=0, keepdims=True) for weight in weights)
    sums = lax.dot_general(
        joined([meta.astype(jnp.bfloat16) for meta in metas], 1),
        joined([weight.astype(jnp.bfloat16) for weight in weights], 0),
        (((1,), (0,)), ((), ())), preferred_element_type=jnp.float32,
    )[0:4]
    if not first:
        factor = jnp.exp2((old - top) * scale)
        total += state_ref[1:2, :] * factor
        sums += state_ref[2:6, :] * factor
    out_ref[0:1, :] = top
    out_ref[1:2, :] = total
    out_ref[2:6, :] = sums
    if half == 1:
        out_ref[6:8, :] = jnp.zeros_like(out_ref[6:8, :])
    elif first:
        out_ref[6:8, :] = jnp.broadcast_to(norms(observed_ref[...]), out_ref[6:8, :].shape)
    else:
        out_ref[6:8, :] = state_ref[6:8, :]


def finish_kernel(size, mine_ref, other_ref, aux_ref, mean_ref, evidence_ref):
    sharp = lanes_of(aux_ref, aux_ref.shape[1] - 1)
    scale = sharp * (2.0 * LOG2E)
    top_a, top_b = mine_ref[0:1, :], other_ref[0:1, :]
    top = jnp.maximum(top_a, top_b)
    factor_a = jnp.exp2((top_a - top) * scale)
    factor_b = jnp.exp2((top_b - top) * scale)
    total = mine_ref[1:2, :] * factor_a + other_ref[1:2, :] * factor_b
    sums = mine_ref[2:6, :] * factor_a + other_ref[2:6, :] * factor_b
    mean_ref[...] = sums / total
    evidence = sharp * (2.0 * size - mine_ref[6:7, :] + 2.0 * top) + jnp.log(total)
    evidence_ref[...] = evidence.reshape(evidence_ref.shape)


def after(values, *earlier):
    return lax.optimization_barrier((values, earlier))[0]


def on_device(pairs, block_of, observed, sharpness, obs_class, pattern, evolved, sim_params, sim_class):
    rows, size = observed.shape
    count = evolved.shape[0]
    tiles, devices = pattern.shape
    steps = devices // 2
    tile = rows // tiles
    vmem = pl.BlockSpec(memory_space=pltpu.VMEM)
    smem = pl.BlockSpec(memory_space=pltpu.SMEM)
    compiler_params = pltpu.CompilerParams(vmem_limit_bytes=VMEM_LIMIT)
    f32 = jnp.float32
    core = [(i, i ^ 1) for i in range(devices)]
    at = lax.axis_index("blk").astype(jnp.int32).reshape(1)

    blocks = [evolved]
    moving = [evolved, evolved]

    def send(step):
        kind = step % 2
        moving[kind] = lax.ppermute(moving[kind], "blk", pairs[kind])
        blocks.append(moving[kind])

    send(0)
    observed_sib = lax.ppermute(observed, "blk", core)
    classes = obs_class.astype(f32).reshape(tiles, 1, tile)
    own_aux = jnp.concatenate(
        [
            jnp.where(pattern[:, :, None] == 1, classes, -1.0),
            jnp.broadcast_to(sharpness.reshape(tiles, 1, tile), (tiles, SUBLANES, tile)),
        ],
        axis=1,
    )
    meta = jnp.concatenate(
        [
            sim_params.astype(f32),
            jnp.broadcast_to(sim_class.astype(f32)[None, :], (SUBLANES - sim_params.shape[0], count)),
        ],
        axis=0,
    )
    sib_aux = lax.ppermute(own_aux, "blk", core)
    metas = [meta]
    moving_meta = [meta, meta]

    def absorb(work, half, state):
        observed_half, aux = ((observed, own_aux), (observed_sib, sib_aux))[half]
        before = () if state is None else (state,)
        return pl.pallas_call(
            functools.partial(absorb_kernel, work, block_of, half, state is None),
            out_shape=jax.ShapeDtypeStruct((SUBLANES, rows), f32),
            in_specs=[smem] + [vmem] * (2 + 2 * len(work) + len(before)),
            out_specs=vmem,
            compiler_params=compiler_params,
            cost_estimate=pl.CostEstimate(
                flops=2 * len(work) * rows * count * size,
                bytes_accessed=2 * (rows + len(work) * count) * size,
                transcendentals=len(work) * rows * count,
            ),
            name="absorb",
        )(at, observed_half, aux, *(blocks[i] for i in work), *(metas[i] for i in work), *before)

    def send_meta(step):
        kind = step % 2
        moving_meta[kind] = lax.ppermute(moving_meta[kind], "blk", pairs[kind])
        metas.append(moving_meta[kind])

    send_meta(0)
    moving[1] = after(moving[1], meta, own_aux)
    send(1)
    send_meta(1)
    states = [None, None]
    works = []
    for first in range(0, steps, 2):
        work = tuple(range(first, min(first + 2, steps)))
        works += [(work, half) for half in ((0, 1) if first + 2 < steps else (1, 0))]
    done = []
    for step in range(steps - 1):
        ahead = step + 2
        if ahead < steps - 1:
            kind = ahead % 2
            if done:
                moving[kind], moving_meta[kind] = after((moving[kind], moving_meta[kind]), done[-1])
            send(ahead)
            send_meta(ahead)
        if step < len(works):
            work, half = works[step]
            states[half] = absorb(work, half, states[half])
            done.append(states[half])
    for work, half in works[steps - 1 : -1]:
        states[half] = absorb(work, half, states[half])
    other = lax.ppermute(states[1], "blk", core)
    work, half = works[-1]
    states[half] = absorb(work, half, states[half])
    mean, evidence = pl.pallas_call(
        functools.partial(finish_kernel, size),
        out_shape=(jax.ShapeDtypeStruct((sim_params.shape[0], rows), f32), jax.ShapeDtypeStruct((rows,), f32)),
        in_specs=[vmem] * 3,
        out_specs=(vmem,) * 2,
        compiler_params=compiler_params,
        name="finish",
    )(states[0], other, own_aux)
    return mean, evidence


def solution(mesh):
    placed = (
        P(("parts", "blk"), None),
        P(("parts", "blk")),
        P(("parts", "blk")),
        P(("parts", "blk"), None),
        P(("parts", "blk"), None),
        P(None, ("parts", "blk")),
        P(("parts", "blk")),
    )
    pairs, block_of = plan(mesh.shape["blk"], mesh.shape["parts"] == 2)
    return jax.shard_map(
        functools.partial(on_device, pairs, block_of),
        mesh=mesh,
        in_specs=placed,
        out_specs=(P(None, ("parts", "blk")), P(("parts", "blk"))),
        check_vma=False,
    )
```

time: 162 us -> 46.6 us (0.29)
  waiting for transfers between devices: 123 us -> 12.2 us
  matrix products: 16.7 us -> 0 us
  starting transfers between devices: 5.54 us -> 17.1 us
  Pallas kernels: 0 us -> 10.4 us
  other arithmetic: 11.1 us -> 2.81 us
  loops' own time: 1.73 us -> 0 us
    ppermute x45 -> x17, waiting for transfers between devices: 123 us -> 12.2 us  [the longest x7 11.2 us: send_meta(): moving_meta[kind] = lax.ppermute(moving_meta[kind], 'blk', pairs[kind])]
    dot_general x32 -> x0, matrix products: 16.7 us -> none  [the longest x16 11.4 us: visit_block(): lax.dot_general(observed, sims, (((1,), (1,)), ((), ())), preferred_eleme...]
    ppermute x45 -> x17, starting transfers between devices: 5.54 us -> 17.1 us  [the longest x7 9.28 us: send(): moving[kind] = lax.ppermute(moving[kind], 'blk', pairs[kind])]
    pallas_call x0 -> x9, Pallas kernels: none -> 10.4 us  [the longest x8 9.76 us: absorb(): pl.pallas_call(functools.partial(absorb_kernel, work, block_of, half, sta...]
    reduce_sum x33 -> x0, other arithmetic: 7.81 us -> none  [the longest x16 3.88 us: visit_block(): weight_total = weight_total * factor + jnp.sum(weights, axis=1)]
    another operation x1 -> x0, loops' own time: 1.73 us -> none  [on_device(): state, packet_end = lax.fori_loop(1, cycle_size, turn, (state, packet))]
  transfers between devices with their start and end apart: 45 -> 17, of which waited for: 15 -> 7; matrix products, arithmetic and copies ran while one was open for 1% -> 8% of each run, Pallas kernels for 0% -> 19%
where the time goes in v2:
time: 46.6 us; the launch traced here: 46.3 us
  starting transfers between devices  17.1 us (37%)
  waiting for transfers between devices  12.2 us (26%)
  Pallas kernels  10.4 us (22%)
  local copies, waits for them, and re-layouts  3.05 us (7%)
  other arithmetic  2.81 us (6%)
  between operations  0.7 us (2%)
    ppermute x7, waiting for transfers between devices, send_meta(): moving_meta[kind] = lax.ppermute(moving_meta[kind], 'blk', pairs[kind])  11.2 us
    pallas_call x8, Pallas kernels, absorb(): pl.pallas_call(functools.partial(absorb_kernel, work, block_of, half, sta...  9.76 us
    ppermute x7, starting transfers between devices, send(): moving[kind] = lax.ppermute(moving[kind], 'blk', pairs[kind])  9.28 us
    ppermute x7, starting transfers between devices, send_meta(): moving_meta[kind] = lax.ppermute(moving_meta[kind], 'blk', pairs[kind])  7.24 us
    unnamed x6, local copies, waits for them, and re-layouts  2.36 us
  transfers between devices with their start and end apart: 17, of which 7 were waited for; matrix products, arithmetic and copies ran while one was open for 8% of the time, Pallas kernels for 19%

profile of v2, /device:TPU:0, one launch (start us, length us, event | category | flops | bytes accessed | tf_op | source)
XLA Modules:
  0.0 46.3 jit_solution(9715887451429986069)
XLA Ops:
  1.1 2.6 %collective-permute-start.2 = (bf16[128,1024]{1,0:T(8,128)(2,1)}, bf16[128,1024]{1,0:T(8,128)(2,1)S(1)}, u32[]{:S(2)}, u32[]{:S(2)}) collective-permute-start(bf16[128,1024]{1,0:T(8,128)(2,1)} %refs_0_.3), channel_id=1, source_target_pairs={{0,4},{1,3},{2,0},{3,7},{4,8},{5,1},{6,2},{7,11},{8,12},{9,5},{10,... | collective-permute-start | bytes 786440 | tf_op jit(solution)/shard_map/ppermute | solution.py:150
  6.6 0.7 %broadcast_in_dim.41 = f32[6,8,128]{2,1,0:T(8,128)S(1)} broadcast(f32[6,128]{1,0:T(8,128)} %bitcast.4), dimensions={0,2} | broadcast | bytes 27648 | tf_op jit(solution)/shard_map/broadcast_in_dim | solution.py:159
  7.4 0.9 %collective-permute-done.2.refs_1_ = bf16[128,1024]{1,0:T(8,128)(2,1)S(1)} collective-permute-done((bf16[128,1024]{1,0:T(8,128)(2,1)}, bf16[128,1024]{1,0:T(8,128)(2,1)S(1)}, u32[]{:S(2)}, u32[]{:S(2)}) %collective-permute-start.2) | collective-permute-done | bytes 262176 | tf_op jit(solution)/shard_map/ppermute | solution.py:150
  8.3 2.1 %collective-permute-start.6 = (bf16[128,1024]{1,0:T(8,128)(2,1)S(1)}, bf16[128,1024]{1,0:T(8,128)(2,1)S(1)}, u32[]{:S(2)}, u32[]{:S(2)}) collective-permute-start(bf16[128,1024]{1,0:T(8,128)(2,1)S(1)} %collective-permute-done.2.refs_1_), channel_id=1, source_target_pairs={{0,4},{1,3},{2,0},{3,7},{4,8},{5,1},{6,2},{7,11},{8,12},{9,5},{10,... | collective-permute-start | bytes 786440 | tf_op jit(solution)/shard_map/ppermute | solution.py:150
  10.4 1.6 %collective-permute-start.3 = (f32[8,128]{1,0:T(8,128)S(1)}, f32[8,128]{1,0:T(8,128)S(1)}, u32[]{:S(2)}, u32[]{:S(2)}) collective-permute-start(f32[8,128]{1,0:T(8,128)S(1)} %pad_maximum_fusion.1.refs_2_), channel_id=1, source_target_pairs={{0,4},{1,3},{2,0},{3,7},{4,8},{5,1},{6,2},{7,11},{8,12},{9,5},{10,... | collective-permute-start | bytes 12296 | tf_op jit(solution)/shard_map/ppermute | solution.py:193
  11.9 4.0 %collective-permute-done.3.refs_3_ = f32[8,128]{1,0:T(8,128)S(1)} collective-permute-done((f32[8,128]{1,0:T(8,128)S(1)}, f32[8,128]{1,0:T(8,128)S(1)}, u32[]{:S(2)}, u32[]{:S(2)}) %collective-permute-start.3) | collective-permute-done | bytes 4128 | tf_op jit(solution)/shard_map/ppermute | solution.py:193
  15.9 1.6 %collective-permute-start.1 = (f32[8,128]{1,0:T(8,128)S(1)}, f32[8,128]{1,0:T(8,128)S(1)}, u32[]{:S(2)}, u32[]{:S(2)}) collective-permute-start(f32[8,128]{1,0:T(8,128)S(1)} %pad_maximum_fusion.1.refs_2_), channel_id=1, source_target_pairs={{0,2},{1,5},{2,6},{3,1},{4,0},{5,9},{6,10},{7,3},{8,4},{9,13},{10,... | collective-permute-start | bytes 12296 | tf_op jit(solution)/shard_map/ppermute | solution.py:193
  17.5 1.4 %copy-done = bf16[768,1024]{1,0:T(8,128)(2,1)S(1)} copy-done((bf16[768,1024]{1,0:T(8,128)(2,1)S(1)}, bf16[768,1024]{1,0:T(8,128)(2,1)}, u32[]{:S(2)}) %copy-start) | copy-done | bytes 1572888
  18.9 0.9 %copy-done.2 = bf16[128,1024]{1,0:T(8,128)(2,1)S(1)} copy-done((bf16[128,1024]{1,0:T(8,128)(2,1)S(1)}, bf16[128,1024]{1,0:T(8,128)(2,1)}, u32[]{:S(2)}) %copy-start.2) | copy-done | bytes 262168
  19.9 2.3 %absorb.8.refs_4_ = f32[8,768]{1,0:T(8,128)S(1)} custom-call(s32[1]{0:T(128)} %bitcast.at_ref, bf16[768,1024]{1,0:T(8,128)(2,1)S(1)} %copy-done, f32[6,24,128]{2,1,0:T(8,128)S(1)} %pad_maximum_fusion.aux_ref, bf16[128,1024]{1,0:T(8,128)(2,1)S(1)} %copy-done.2, bf16[128,1024]{1,0:T(8,128)(2,1)S(1)} %collective-permute-done.2.refs_1_, ...), custom_call_target="tpu_custom_call" | custom-call | flops 402653184 | bytes 2097152 | tf_op jit(solution)/shard_map/absorb/pallas_call | solution.py:177
  22.6 1.6 %collective-permute-start.4 = (bf16[128,1024]{1,0:T(8,128)(2,1)S(1)}, bf16[128,1024]{1,0:T(8,128)(2,1)S(1)}, u32[]{:S(2)}, u32[]{:S(2)}) collective-permute-start(bf16[128,1024]{1,0:T(8,128)(2,1)S(1)} %collective-permute-done.refs_0_), channel_id=1, source_target_pairs={{0,2},{1,5},{2,6},{3,1},{4,0},{5,9},{6,10},{7,3},{8,4},{9,13},{10,... | collective-permute-start | bytes 786440 | tf_op jit(solution)/shard_map/ppermute | solution.py:150
  24.2 0.9 %absorb.10.refs_4_ = f32[8,768]{1,0:T(8,128)S(1)} custom-call(s32[1]{0:T(128)} %bitcast.at_ref, bf16[768,1024]{1,0:T(8,128)(2,1)S(1)} %collective-permute-done.9.observed_ref, f32[6,24,128]{2,1,0:T(8,128)S(1)} %collective-permute-done.10.aux_ref, bf16[128,1024]{1,0:T(8,128)(2,1)S(1)} %copy-done.2, bf16[128,1024]{1,0:T(8,128)(2,1)S(1)} %collective-permute-done.2.refs_1_, ...), custom_call_target="tpu_custom_call" | custom-call | flops 402653184 | bytes 2097152 | tf_op jit(solution)/shard_map/absorb/pallas_call | solution.py:177
  26.2 1.6 %collective-permute-start.5 = (f32[8,128]{1,0:T(8,128)S(1)}, f32[8,128]{1,0:T(8,128)S(1)}, u32[]{:S(2)}, u32[]{:S(2)}) collective-permute-start(f32[8,128]{1,0:T(8,128)S(1)} %collective-permute-done.1.refs_2_), channel_id=1, source_target_pairs={{0,2},{1,5},{2,6},{3,1},{4,0},{5,9},{6,10},{7,3},{8,4},{9,13},{10,... | collective-permute-start | bytes 12296 | tf_op jit(solution)/shard_map/ppermute | solution.py:193
  27.8 1.1 %absorb.9.refs_4_ = f32[8,768]{1,0:T(8,128)S(1)} custom-call(s32[1]{0:T(128)} %bitcast.at_ref, bf16[768,1024]{1,0:T(8,128)(2,1)S(1)} %copy-done.1, f32[6,24,128]{2,1,0:T(8,128)S(1)} %pad_maximum_fusion.aux_ref, bf16[128,1024]{1,0:T(8,128)(2,1)S(1)} %collective-permute-done.refs_0_, bf16[128,1024]{1,0:T(8,128)(2,1)S(1)} %collective-permute-done.6.refs_1_, ...), custom_call_target="tpu_custom_call" | custom-call | flops 402653184 | bytes 2097152 | tf_op jit(solution)/shard_map/absorb/pallas_call | solution.py:177
  28.9 1.9 %collective-permute-done.5.refs_2_ = f32[8,128]{1,0:T(8,128)S(1)} collective-permute-done((f32[8,128]{1,0:T(8,128)S(1)}, f32[8,128]{1,0:T(8,128)S(1)}, u32[]{:S(2)}, u32[]{:S(2)}) %collective-permute-start.5) | collective-permute-done | bytes 4128 | tf_op jit(solution)/shard_map/ppermute | solution.py:193
  30.8 2.5 %collective-permute-start.8 = (bf16[128,1024]{1,0:T(8,128)(2,1)S(1)}, bf16[128,1024]{1,0:T(8,128)(2,1)S(1)}, u32[]{:S(2)}, u32[]{:S(2)}) collective-permute-start(bf16[128,1024]{1,0:T(8,128)(2,1)S(1)} %collective-permute-done.4.refs_0_), channel_id=1, source_target_pairs={{0,2},{1,5},{2,6},{3,1},{4,0},{5,9},{6,10},{7,3},{8,4},{9,13},{10,... | collective-permute-start | bytes 786440 | tf_op jit(solution)/shard_map/ppermute | solution.py:150
  33.3 1.1 %absorb.11.refs_4_ = f32[8,768]{1,0:T(8,128)S(1)} custom-call(s32[1]{0:T(128)} %bitcast.at_ref, bf16[768,1024]{1,0:T(8,128)(2,1)S(1)} %collective-permute-done.9.observed_ref, f32[6,24,128]{2,1,0:T(8,128)S(1)} %collective-permute-done.10.aux_ref, bf16[128,1024]{1,0:T(8,128)(2,1)S(1)} %collective-permute-done.refs_0_, ...), custom_call_target="tpu_custom_call" | custom-call | flops 402653184 | bytes 2097152 | tf_op jit(solution)/shard_map/absorb/pallas_call | solution.py:177
  34.4 2.5 %collective-permute-done.12.refs_3_ = f32[8,128]{1,0:T(8,128)S(1)} collective-permute-done((f32[8,128]{1,0:T(8,128)S(1)}, f32[8,128]{1,0:T(8,128)S(1)}, u32[]{:S(2)}, u32[]{:S(2)}) %collective-permute-start.12) | collective-permute-done | bytes 4128 | tf_op jit(solution)/shard_map/ppermute | solution.py:193
  36.9 2.0 %collective-permute-start.14 = (f32[8,128]{1,0:T(8,128)S(1)}, f32[8,128]{1,0:T(8,128)S(1)}, u32[]{:S(2)}, u32[]{:S(2)}) collective-permute-start(f32[8,128]{1,0:T(8,128)S(1)} %collective-permute-done.5.refs_2_), channel_id=1, source_target_pairs={{0,2},{1,5},{2,6},{3,1},{4,0},{5,9},{6,10},{7,3},{8,4},{9,13},{10,... | collective-permute-start | bytes 12296 | tf_op jit(solution)/shard_map/ppermute | solution.py:193
  38.9 1.1 %absorb.12.refs_4_ = f32[8,768]{1,0:T(8,128)S(1)} custom-call(s32[1]{0:T(128)} %bitcast.at_ref, bf16[768,1024]{1,0:T(8,128)(2,1)S(1)} %copy-done.1, f32[6,24,128]{2,1,0:T(8,128)S(1)} %pad_maximum_fusion.aux_ref, bf16[128,1024]{1,0:T(8,128)(2,1)S(1)} %collective-permute-done.4.refs_0_, bf16[128,1024]{1,0:T(8,128)(2,1)S(1)} %collective-permute-done.11.refs_1_, ...), custom_call_target="tpu_custom_call" | custom-call | flops 402653184 | bytes 2097152 | tf_op jit(solution)/shard_map/absorb/pallas_call | solution.py:177
  40.0 1.1 %absorb.14.refs_4_ = f32[8,768]{1,0:T(8,128)S(1)} custom-call(s32[1]{0:T(128)} %bitcast.at_ref, bf16[768,1024]{1,0:T(8,128)(2,1)S(1)} %collective-permute-done.9.observed_ref, f32[6,24,128]{2,1,0:T(8,128)S(1)} %collective-permute-done.10.aux_ref, bf16[128,1024]{1,0:T(8,128)(2,1)S(1)} %collective-permute-done.4.refs_0_, ...), custom_call_target="tpu_custom_call" | custom-call | flops 402653184 | bytes 2097152 | tf_op jit(solution)/shard_map/absorb/pallas_call | solution.py:177
  41.1 2.2 %collective-permute-done.15.refs_3_ = f32[8,128]{1,0:T(8,128)S(1)} collective-permute-done((f32[8,128]{1,0:T(8,128)S(1)}, f32[8,128]{1,0:T(8,128)S(1)}, u32[]{:S(2)}, u32[]{:S(2)}) %collective-permute-start.15) | collective-permute-done | bytes 4128 | tf_op jit(solution)/shard_map/ppermute | solution.py:193
  43.3 1.1 %absorb.15 = f32[8,768]{1,0:T(8,128)S(1)} custom-call(s32[1]{0:T(128)} %bitcast.at_ref, bf16[768,1024]{1,0:T(8,128)(2,1)S(1)} %collective-permute-done.9.observed_ref, f32[6,24,128]{2,1,0:T(8,128)S(1)} %collective-permute-done.10.aux_ref, bf16[128,1024]{1,0:T(8,128)(2,1)S(1)} %collective-permute-done.8.refs_0_, ...), custom_call_target="tpu_custom_call" | custom-call | flops 402653184 | bytes 2097152 | tf_op jit(solution)/shard_map/absorb/pallas_call | solution.py:177
  44.4 1.1 %absorb.13.mine_ref = f32[8,768]{1,0:T(8,128)S(1)} custom-call(s32[1]{0:T(128)} %bitcast.at_ref, bf16[768,1024]{1,0:T(8,128)(2,1)S(1)} %copy-done.1, f32[6,24,128]{2,1,0:T(8,128)S(1)} %pad_maximum_fusion.aux_ref, bf16[128,1024]{1,0:T(8,128)(2,1)S(1)} %collective-permute-done.8.refs_0_, bf16[128,1024]{1,0:T(8,128)(2,1)S(1)} %collective-permute-done.13.refs_1_, ...), custom_call_target="tpu_custom_call" | custom-call | flops 402653184 | bytes 2097152 | tf_op jit(solution)/shard_map/absorb/pallas_call | solution.py:177
  (34 shorter events, 5.7 us)
Async XLA Ops:
  0.6 23.6 %collective-permute-start.9 = (bf16[768,1024]{1,0:T(8,128)(2,1)}, bf16[768,1024]{1,0:T(8,128)(2,1)S(1)}, u32[]{:S(2)}, u32[]{:S(2)}) collective-permute-start(bf16[768,1024]{1,0:T(8,128)(2,1)} %observed_ref.7), channel_id=1, source_target_pairs={{0,1},{1,0},{2,3},{3,2},{4,5},{5,4},{6,7},{7,6},{8,9},{9,8},{10,11... | collective-permute-start | bytes 4718600 | tf_op jit(solution)/shard_map/ppermute | solution.py:154
  1.1 7.1 %collective-permute-start.2 = (bf16[128,1024]{1,0:T(8,128)(2,1)}, bf16[128,1024]{1,0:T(8,128)(2,1)S(1)}, u32[]{:S(2)}, u32[]{:S(2)}) collective-permute-start(bf16[128,1024]{1,0:T(8,128)(2,1)} %refs_0_.3), channel_id=1, source_target_pairs={{0,4},{1,3},{2,0},{3,7},{4,8},{5,1},{6,2},{7,11},{8,12},{9,5},{10,... | collective-permute-start | bytes 786440 | tf_op jit(solution)/shard_map/ppermute | solution.py:150
  7.3 15.3 %collective-permute-start = (bf16[128,1024]{1,0:T(8,128)(2,1)}, bf16[128,1024]{1,0:T(8,128)(2,1)S(1)}, u32[]{:S(2)}, u32[]{:S(2)}) collective-permute-start(bf16[128,1024]{1,0:T(8,128)(2,1)} %refs_0_.3), channel_id=1, source_target_pairs={{0,2},{1,5},{2,6},{3,1},{4,0},{5,9},{6,10},{7,3},{8,4},{9,13},{10,... | collective-permute-start | bytes 786440 | tf_op jit(solution)/shard_map/ppermute | solution.py:150
  8.3 17.5 %collective-permute-start.6 = (bf16[128,1024]{1,0:T(8,128)(2,1)S(1)}, bf16[128,1024]{1,0:T(8,128)(2,1)S(1)}, u32[]{:S(2)}, u32[]{:S(2)}) collective-permute-start(bf16[128,1024]{1,0:T(8,128)(2,1)S(1)} %collective-permute-done.2.refs_1_), channel_id=1, source_target_pairs={{0,4},{1,3},{2,0},{3,7},{4,8},{5,1},{6,2},{7,11},{8,12},{9,5},{10,... | collective-permute-start | bytes 786440 | tf_op jit(solution)/shard_map/ppermute | solution.py:150
  10.4 13.8 %collective-permute-start.10 = (f32[6,24,128]{2,1,0:T(8,128)S(1)}, f32[6,24,128]{2,1,0:T(8,128)S(1)}, u32[]{:S(2)}, u32[]{:S(2)}) collective-permute-start(f32[6,24,128]{2,1,0:T(8,128)S(1)} %pad_maximum_fusion.aux_ref), channel_id=1, source_target_pairs={{0,1},{1,0},{2,3},{3,2},{4,5},{5,4},{6,7},{7,6},{8,9},{9,8},{10,11... | collective-permute-start | bytes 221192 | tf_op jit(solution)/shard_map/ppermute | solution.py:170
  10.4 5.6 %collective-permute-start.3 = (f32[8,128]{1,0:T(8,128)S(1)}, f32[8,128]{1,0:T(8,128)S(1)}, u32[]{:S(2)}, u32[]{:S(2)}) collective-permute-start(f32[8,128]{1,0:T(8,128)S(1)} %pad_maximum_fusion.1.refs_2_), channel_id=1, source_target_pairs={{0,4},{1,3},{2,0},{3,7},{4,8},{5,1},{6,2},{7,11},{8,12},{9,5},{10,... | collective-permute-start | bytes 12296 | tf_op jit(solution)/shard_map/ppermute | solution.py:193
  15.9 6.2 %collective-permute-start.1 = (f32[8,128]{1,0:T(8,128)S(1)}, f32[8,128]{1,0:T(8,128)S(1)}, u32[]{:S(2)}, u32[]{:S(2)}) collective-permute-start(f32[8,128]{1,0:T(8,128)S(1)} %pad_maximum_fusion.1.refs_2_), channel_id=1, source_target_pairs={{0,2},{1,5},{2,6},{3,1},{4,0},{5,9},{6,10},{7,3},{8,4},{9,13},{10,... | collective-permute-start | bytes 12296 | tf_op jit(solution)/shard_map/ppermute | solution.py:193
  17.5 1.4 %copy-start = (bf16[768,1024]{1,0:T(8,128)(2,1)S(1)}, bf16[768,1024]{1,0:T(8,128)(2,1)}, u32[]{:S(2)}) copy-start(bf16[768,1024]{1,0:T(8,128)(2,1)} %observed_ref.7) | copy-start | bytes 4718596
  18.9 0.9 %copy-start.2 = (bf16[128,1024]{1,0:T(8,128)(2,1)S(1)}, bf16[128,1024]{1,0:T(8,128)(2,1)}, u32[]{:S(2)}) copy-start(bf16[128,1024]{1,0:T(8,128)(2,1)} %refs_0_.3) | copy-start | bytes 786436
  22.1 5.7 %copy-start.1 = (bf16[768,1024]{1,0:T(8,128)(2,1)S(1)}, bf16[768,1024]{1,0:T(8,128)(2,1)}, u32[]{:S(2)}) copy-start(bf16[768,1024]{1,0:T(8,128)(2,1)} %observed_ref.7) | copy-start | bytes 4718596
  22.1 3.6 %collective-permute-start.7 = (f32[8,128]{1,0:T(8,128)S(1)}, f32[8,128]{1,0:T(8,128)S(1)}, u32[]{:S(2)}, u32[]{:S(2)}) collective-permute-start(f32[8,128]{1,0:T(8,128)S(1)} %collective-permute-done.3.refs_3_), channel_id=1, source_target_pairs={{0,4},{1,3},{2,0},{3,7},{4,8},{5,1},{6,2},{7,11},{8,12},{9,5},{10,... | collective-permute-start | bytes 12296 | tf_op jit(solution)/shard_map/ppermute | solution.py:193
  22.6 8.2 %collective-permute-start.4 = (bf16[128,1024]{1,0:T(8,128)(2,1)S(1)}, bf16[128,1024]{1,0:T(8,128)(2,1)S(1)}, u32[]{:S(2)}, u32[]{:S(2)}) collective-permute-start(bf16[128,1024]{1,0:T(8,128)(2,1)S(1)} %collective-permute-done.refs_0_), channel_id=1, source_target_pairs={{0,2},{1,5},{2,6},{3,1},{4,0},{5,9},{6,10},{7,3},{8,4},{9,13},{10,... | collective-permute-start | bytes 786440 | tf_op jit(solution)/shard_map/ppermute | solution.py:150
  25.8 11.1 %collective-permute-start.11 = (bf16[128,1024]{1,0:T(8,128)(2,1)S(1)}, bf16[128,1024]{1,0:T(8,128)(2,1)S(1)}, u32[]{:S(2)}, u32[]{:S(2)}) collective-permute-start(bf16[128,1024]{1,0:T(8,128)(2,1)S(1)} %collective-permute-done.6.refs_1_), channel_id=1, source_target_pairs={{0,4},{1,3},{2,0},{3,7},{4,8},{5,1},{6,2},{7,11},{8,12},{9,5},{10,... | collective-permute-start | bytes 786440 | tf_op jit(solution)/shard_map/ppermute | solution.py:150
  26.2 4.6 %collective-permute-start.5 = (f32[8,128]{1,0:T(8,128)S(1)}, f32[8,128]{1,0:T(8,128)S(1)}, u32[]{:S(2)}, u32[]{:S(2)}) collective-permute-start(f32[8,128]{1,0:T(8,128)S(1)} %collective-permute-done.1.refs_2_), channel_id=1, source_target_pairs={{0,2},{1,5},{2,6},{3,1},{4,0},{5,9},{6,10},{7,3},{8,4},{9,13},{10,... | collective-permute-start | bytes 12296 | tf_op jit(solution)/shard_map/ppermute | solution.py:193
  30.8 10.3 %collective-permute-start.8 = (bf16[128,1024]{1,0:T(8,128)(2,1)S(1)}, bf16[128,1024]{1,0:T(8,128)(2,1)S(1)}, u32[]{:S(2)}, u32[]{:S(2)}) collective-permute-start(bf16[128,1024]{1,0:T(8,128)(2,1)S(1)} %collective-permute-done.4.refs_0_), channel_id=1, source_target_pairs={{0,2},{1,5},{2,6},{3,1},{4,0},{5,9},{6,10},{7,3},{8,4},{9,13},{10,... | collective-permute-start | bytes 786440 | tf_op jit(solution)/shard_map/ppermute | solution.py:150
  33.3 3.6 %collective-permute-start.12 = (f32[8,128]{1,0:T(8,128)S(1)}, f32[8,128]{1,0:T(8,128)S(1)}, u32[]{:S(2)}, u32[]{:S(2)}) collective-permute-start(f32[8,128]{1,0:T(8,128)S(1)} %collective-permute-done.7.refs_3_), channel_id=1, source_target_pairs={{0,4},{1,3},{2,0},{3,7},{4,8},{5,1},{6,2},{7,11},{8,12},{9,5},{10,... | collective-permute-start | bytes 12296 | tf_op jit(solution)/shard_map/ppermute | solution.py:193
  36.9 6.4 %collective-permute-start.13 = (bf16[128,1024]{1,0:T(8,128)(2,1)S(1)}, bf16[128,1024]{1,0:T(8,128)(2,1)S(1)}, u32[]{:S(2)}, u32[]{:S(2)}) collective-permute-start(bf16[128,1024]{1,0:T(8,128)(2,1)S(1)} %collective-permute-done.11.refs_1_), channel_id=1, source_target_pairs={{0,4},{1,3},{2,0},{3,7},{4,8},{5,1},{6,2},{7,11},{8,12},{9,5},{10,... | collective-permute-start | bytes 786440 | tf_op jit(solution)/shard_map/ppermute | solution.py:150
  36.9 4.2 %collective-permute-start.14 = (f32[8,128]{1,0:T(8,128)S(1)}, f32[8,128]{1,0:T(8,128)S(1)}, u32[]{:S(2)}, u32[]{:S(2)}) collective-permute-start(f32[8,128]{1,0:T(8,128)S(1)} %collective-permute-done.5.refs_2_), channel_id=1, source_target_pairs={{0,2},{1,5},{2,6},{3,1},{4,0},{5,9},{6,10},{7,3},{8,4},{9,13},{10,... | collective-permute-start | bytes 12296 | tf_op jit(solution)/shard_map/ppermute | solution.py:193
  38.9 4.4 %collective-permute-start.15 = (f32[8,128]{1,0:T(8,128)S(1)}, f32[8,128]{1,0:T(8,128)S(1)}, u32[]{:S(2)}, u32[]{:S(2)}) collective-permute-start(f32[8,128]{1,0:T(8,128)S(1)} %collective-permute-done.12.refs_3_), channel_id=1, source_target_pairs={{0,4},{1,3},{2,0},{3,7},{4,8},{5,1},{6,2},{7,11},{8,12},{9,5},{10,... | collective-permute-start | bytes 12296 | tf_op jit(solution)/shard_map/ppermute | solution.py:193
  44.4 1.2 %collective-permute-start.16 = (f32[8,768]{1,0:T(8,128)S(1)}, f32[8,768]{1,0:T(8,128)S(1)}, u32[]{:S(2)}, u32[]{:S(2)}) collective-permute-start(f32[8,768]{1,0:T(8,128)S(1)} %absorb.15), channel_id=1, source_target_pairs={{0,1},{1,0},{2,3},{3,2},{4,5},{5,4},{6,7},{7,6},{8,9},{9,8},{10,11... | collective-permute-start | bytes 73736 | tf_op jit(solution)/shard_map/ppermute | solution.py:220

commit v3 on v2

v3 whole, which is shorter than its diff:
```python
import functools
import math

import jax
import jax.numpy as jnp
import numpy as np
from jax import lax
from jax.experimental import pallas as pl
from jax.experimental.pallas import tpu as pltpu
from jax.sharding import PartitionSpec as P

NEG_START = -1e30
LOG2E = math.log2(math.e)
SUBLANES = 8
LANES = 128
META_ROWS = 16
VMEM_LIMIT = 40 * 1024 * 1024


def plan(size, grid):
    chips = size // 2

    def ring(place):
        if not grid:
            return place
        return jnp.where(place < chips // 2, 2 * place, 2 * (chips - 1 - place) + 1)

    def place_of(chip):
        if not grid:
            return chip
        return jnp.where(chip % 2 == 0, chip // 2, chips - 1 - chip // 2)

    def beside(device, by):
        return ring((place_of(device // 2) + by + chips) % chips) * 2 + device % 2

    def way(device, kind):
        return 1 - 2 * ((device + kind) % 2)

    def block_of(device, step):
        if step == 0:
            return device
        return beside(device, -way(device, (step - 1) % 2) * ((step + 1) // 2))

    all_devices = np.arange(size)
    with jax.ensure_compile_time_eval():
        targets = [np.asarray(beside(all_devices, way(all_devices, kind))).tolist() for kind in range(2)]
    return [list(enumerate(target)) for target in targets], block_of


def joined(parts, axis):
    return parts[0] if len(parts) == 1 else jnp.concatenate(parts, axis=axis)


def row(values):
    return values.reshape(1, values.shape[-1])


def pack_kernel(params_hbm, class_hbm, evolved_hbm, packet_ref, params_ref, class_ref, arrived):
    rows, size = evolved_hbm.shape
    panels = size // LANES
    copies = [
        pltpu.make_async_copy(params_hbm, params_ref, arrived.at[0]),
        pltpu.make_async_copy(class_hbm, class_ref, arrived.at[1]),
    ]
    for i in range(panels):
        panel = packet_ref.at[pl.ds(i * rows, rows), :]
        source = evolved_hbm.at[:, pl.ds(i * LANES, LANES)]
        copies.append(pltpu.make_async_copy(source, panel, arrived.at[i + 2]))
    for copy in copies:
        copy.start()
    for copy in copies[:2]:
        copy.wait()
    params = params_ref[...].astype(jnp.float32)
    classes = row(class_ref[...]).astype(jnp.float32)
    rest = jnp.broadcast_to(classes, (META_ROWS - params.shape[0], classes.shape[1]))
    packet_ref[panels * rows :, :] = jnp.concatenate([params, rest], axis=0).astype(packet_ref.dtype)
    for copy in copies[2:]:
        copy.wait()


def norms(observed):
    wide = observed.astype(jnp.float32)
    square = wide * wide
    high = square.astype(jnp.bfloat16)
    low = (square - high.astype(jnp.float32)).astype(jnp.bfloat16)
    ones = jnp.ones((SUBLANES, observed.shape[1]), jnp.bfloat16)
    return sum(
        lax.dot_general(ones, part, (((1,), (1,)), ((), ())), preferred_element_type=jnp.float32)[0:1]
        for part in (high, low)
    )


def prepare_kernel(
    block_of, at_ref, pattern_hbm, class_hbm, sharp_hbm, observed_hbm,
    own_ref, sib_ref, observed_ref, pattern_ref, class_ref, sharp_ref, arrived,
):
    sources = (pattern_hbm, class_hbm, sharp_hbm, observed_hbm)
    targets = (pattern_ref, class_ref, sharp_ref, observed_ref)
    copies = [
        pltpu.make_async_copy(source, target, arrived.at[i])
        for i, (source, target) in enumerate(zip(sources, targets))
    ]
    for copy in copies:
        copy.start()
    for copy in copies[:3]:
        copy.wait()
    tiles, devices = pattern_ref.shape
    tile = class_ref.shape[0] // tiles
    classes = row(class_ref[...]).astype(jnp.float32)
    scale = row(sharp_ref[...]) * (2.0 * LOG2E)
    for out_ref, device in ((own_ref, at_ref[0]), (sib_ref, at_ref[0] ^ 1)):
        for step in range(devices // 2):
            block = block_of(device, step)
            opened = [
                jnp.where(pattern_ref[i, block] == 1, classes[:, i * tile : (i + 1) * tile], -1.0) for i in range(tiles)
            ]
            out_ref[step : step + 1, :] = jnp.concatenate(opened, axis=1)
        out_ref[devices // 2 : devices // 2 + 1, :] = scale
    copies[3].wait()
    own_ref[devices // 2 + 1 : devices // 2 + 2, :] = norms(observed_ref[...])
    sib_ref[devices // 2 + 1 : devices // 2 + 2, :] = scale


def absorb_kernel(steps, count, first, observed_ref, aux_ref, *refs):
    packet_refs, out_ref = refs[: len(steps)], refs[-1]
    panels = observed_ref.shape[1] // LANES
    blocks = [jnp.concatenate([ref[i * count : (i + 1) * count, :] for i in range(panels)], axis=1) for ref in packet_refs]
    inner = lax.dot_general(
        joined(blocks, 0), observed_ref[...], (((1,), (1,)), ((), ())), preferred_element_type=jnp.float32
    )
    metas = [ref[panels * count :, :] for ref in packet_refs]
    after_steps = aux_ref.shape[0] - 2
    scale = aux_ref[after_steps : after_steps + 1, :]
    if first:
        top = jnp.full(scale.shape, NEG_START, jnp.float32)
    else:
        state_ref = refs[len(steps)]
        top = old = state_ref[0:1, :]
    scores = []
    for i, (step, block, meta) in enumerate(zip(steps, blocks, metas)):
        wide = block.astype(jnp.float32)
        half_square = 0.5 * jnp.sum(wide * wide, axis=1, keepdims=True)
        classes = meta[META_ROWS // 2 :].astype(jnp.float32)
        column = jnp.concatenate([classes] * (count // SUBLANES), axis=0).T[:, 0:1]
        active = column == aux_ref[step : step + 1, :]
        score = jnp.where(active, inner[i * count : (i + 1) * count] - half_square, -jnp.inf)
        top = jnp.maximum(top, jnp.max(score, axis=0, keepdims=True))
        scores.append(score)
    weights = [jnp.exp2((score - top) * scale) for score in scores]
    total = sum(jnp.sum(weight, axis=0, keepdims=True) for weight in weights)
    sums = lax.dot_general(
        joined(metas, 1), joined([weight.astype(jnp.bfloat16) for weight in weights], 0),
        (((1,), (0,)), ((), ())), preferred_element_type=jnp.float32,
    )[0:4]
    if not first:
        factor = jnp.exp2((old - top) * scale)
        total += state_ref[1:2, :] * factor
        sums += state_ref[2:6, :] * factor
    out_ref[0:1, :] = top
    out_ref[1:2, :] = total
    out_ref[2:6, :] = sums
    out_ref[6:8, :] = jnp.zeros_like(out_ref[6:8, :])


def finish_kernel(size, mine_ref, other_ref, aux_ref, mean_ref, evidence_ref):
    after_steps = aux_ref.shape[0] - 2
    scale = aux_ref[after_steps : after_steps + 1, :]
    top_a, top_b = mine_ref[0:1, :], other_ref[0:1, :]
    top = jnp.maximum(top_a, top_b)
    factor_a = jnp.exp2((top_a - top) * scale)
    factor_b = jnp.exp2((top_b - top) * scale)
    total = mine_ref[1:2, :] * factor_a + other_ref[1:2, :] * factor_b
    sums = mine_ref[2:6, :] * factor_a + other_ref[2:6, :] * factor_b
    mean_ref[...] = sums / total
    sharp = scale * (0.5 / LOG2E)
    evidence = sharp * (2.0 * size - aux_ref[after_steps + 1 : after_steps + 2, :] + 2.0 * top) + jnp.log(total)
    evidence_ref[...] = evidence.reshape(evidence_ref.shape)


def after(values, *earlier):
    return lax.optimization_barrier((values, earlier))[0]


def in_hbm(*arrays):
    return [pltpu.with_memory_space_constraint(array, pltpu.HBM) for array in arrays]


def on_device(pairs, block_of, observed, sharpness, obs_class, pattern, evolved, sim_params, sim_class):
    rows, size = observed.shape
    count = evolved.shape[0]
    devices = pattern.shape[1]
    steps = devices // 2
    vmem = pl.BlockSpec(memory_space=pltpu.VMEM)
    smem = pl.BlockSpec(memory_space=pltpu.SMEM)
    hbm = pl.BlockSpec(memory_space=pltpu.HBM)
    compiler_params = pltpu.CompilerParams(vmem_limit_bytes=VMEM_LIMIT)
    f32 = jnp.float32
    core = [(i, i ^ 1) for i in range(devices)]
    at = lax.axis_index("blk").astype(jnp.int32).reshape(1)

    packet = pl.pallas_call(
        pack_kernel,
        out_shape=jax.ShapeDtypeStruct((count * size // LANES + META_ROWS, LANES), evolved.dtype),
        in_specs=[hbm] * 3,
        out_specs=vmem,
        scratch_shapes=[
            pltpu.VMEM(sim_params.shape, sim_params.dtype),
            pltpu.VMEM(sim_class.shape, sim_class.dtype),
            pltpu.SemaphoreType.DMA((size // LANES + 2,)),
        ],
        compiler_params=compiler_params,
        name="pack",
    )(*in_hbm(sim_params, sim_class, evolved))
    packets = [packet]
    moving = [packet, packet]

    def send(step):
        kind = step % 2
        moving[kind] = lax.ppermute(moving[kind], "blk", pairs[kind])
        packets.append(moving[kind])

    send(0)
    own_aux, sib_aux, observed_own = pl.pallas_call(
        functools.partial(prepare_kernel, block_of),
        out_shape=(
            jax.ShapeDtypeStruct((steps + 2, rows), f32),
            jax.ShapeDtypeStruct((steps + 2, rows), f32),
            jax.ShapeDtypeStruct(observed.shape, observed.dtype),
        ),
        in_specs=[smem] + [hbm] * 4,
        out_specs=(vmem,) * 3,
        scratch_shapes=[
            pltpu.SMEM(pattern.shape, pattern.dtype),
            pltpu.VMEM(obs_class.shape, obs_class.dtype),
            pltpu.VMEM(sharpness.shape, sharpness.dtype),
            pltpu.SemaphoreType.DMA((4,)),
        ],
        compiler_params=compiler_params,
        cost_estimate=pl.CostEstimate(flops=8 * rows * size, bytes_accessed=4 * rows * size, transcendentals=0),
        name="prepare",
    )(after(at, packet), *in_hbm(pattern, obs_class, sharpness, observed))
    observed_sib = lax.ppermute(observed, "blk", core)
    sib_aux = lax.ppermute(sib_aux, "blk", core)
    moving[1] = after(moving[1], own_aux)
    send(1)

    def absorb(work, half, state):
        observed_half, aux = ((observed_own, own_aux), (observed_sib, sib_aux))[half]
        before = () if state is None else (state,)
        return pl.pallas_call(
            functools.partial(absorb_kernel, work, count, state is None),
            out_shape=jax.ShapeDtypeStruct((SUBLANES, rows), f32),
            in_specs=[vmem] * (2 + len(work) + len(before)),
            out_specs=vmem,
            compiler_params=compiler_params,
            cost_estimate=pl.CostEstimate(
                flops=2 * len(work) * rows * count * size,
                bytes_accessed=2 * (rows + len(work) * count) * size,
                transcendentals=len(work) * rows * count,
            ),
            name="absorb",
        )(observed_half, aux, *(packets[i] for i in work), *before)

    states = [None, None]
    works = []
    for first in range(0, steps, 2):
        work = tuple(range(first, min(first + 2, steps)))
        works += [(work, half) for half in ((0, 1) if first + 2 < steps else (1, 0))]
    done = []
    for step in range(steps - 1):
        ahead = step + 2
        if ahead < steps - 1:
            if done:
                moving[ahead % 2] = after(moving[ahead % 2], done[-1])
            send(ahead)
        if step < len(works):
            work, half = works[step]
            states[half] = absorb(work, half, states[half])
            done.append(states[half])
    for work, half in works[steps - 1 : -1]:
        states[half] = absorb(work, half, states[half])
    other = lax.ppermute(states[1], "blk", core)
    work, half = works[-1]
    states[half] = absorb(work, half, states[half])
    mean, evidence = pl.pallas_call(
        functools.partial(finish_kernel, size),
        out_shape=(jax.ShapeDtypeStruct((sim_params.shape[0], rows), f32), jax.ShapeDtypeStruct((rows,), f32)),
        in_specs=[vmem] * 3,
        out_specs=(vmem,) * 2,
        compiler_params=compiler_params,
        name="finish",
    )(states[0], other, own_aux)
    return mean, evidence


def solution(mesh):
    placed = (
        P(("parts", "blk"), None),
        P(("parts", "blk")),
        P(("parts", "blk")),
        P(("parts", "blk"), None),
        P(("parts", "blk"), None),
        P(None, ("parts", "blk")),
        P(("parts", "blk")),
    )
    pairs, block_of = plan(mesh.shape["blk"], mesh.shape["parts"] == 2)
    return jax.shard_map(
        functools.partial(on_device, pairs, block_of),
        mesh=mesh,
        in_specs=placed,
        out_specs=(P(None, ("parts", "blk")), P(("parts", "blk"))),
        check_vma=False,
    )
```

time: 46.6 us -> 36.2 us (0.78)
  starting transfers between devices: 17.1 us -> 10.3 us
  local copies, waits for them, and re-layouts: 3.05 us -> 0 us
  other arithmetic: 2.81 us -> 0 us
  Pallas kernels: 10.4 us -> 12.6 us
    ppermute x7, waiting for transfers between devices: 0.93 us -> 12.3 us  [send(): moving[kind] = lax.ppermute(moving[kind], 'blk', pairs[kind])]
    ppermute x8 -> x1, waiting for transfers between devices: 11.2 us -> 0.01 us  [on_device(): sib_aux = lax.ppermute(sib_aux, 'blk', core)]
    ppermute x8 -> x1, starting transfers between devices: 7.24 us -> 0.01 us  [on_device(): sib_aux = lax.ppermute(sib_aux, 'blk', core)]
    unnamed x6 -> x0, local copies, waits for them, and re-layouts: 2.36 us -> none
    pallas_call x8 -> x10, Pallas kernels: 9.76 us -> 12 us  [the longest x8 8.59 us: absorb(): pl.pallas_call(functools.partial(absorb_kernel, work, count, state is Non...]
    convert_element_type x2 -> x0, other arithmetic: 1.34 us -> none  [the longest x1 0.68 us: on_device(): sim_params.astype(f32)]
    broadcast_in_dim x2 -> x0, local copies, waits for them, and re-layouts: 0.69 us -> none  [the longest x1 0.69 us: on_device(): jnp.broadcast_to(sharpness.reshape(tiles, 1, tile), (tiles, SUBLANES, tile))]
    eq x1 -> x0, other arithmetic: 0.69 us -> none  [on_device(): pattern[:, :, None] == 1]
  transfers between devices with their start and end apart: 17 -> 10, of which waited for: 7 -> 6; matrix products, arithmetic and copies ran while one was open for 8% -> 0% of each run, Pallas kernels for 19% -> 30%
where the time goes in v3:
time: 36.2 us; the launch traced here: 36 us
  Pallas kernels  12.6 us (35%)
  waiting for transfers between devices  12.4 us (34%)
  starting transfers between devices  10.3 us (28%)
  between operations  0.68 us (2%)
    ppermute x7, waiting for transfers between devices, send(): moving[kind] = lax.ppermute(moving[kind], 'blk', pairs[kind])  12.3 us
    ppermute x7, starting transfers between devices, send(): moving[kind] = lax.ppermute(moving[kind], 'blk', pairs[kind])  9.72 us
    pallas_call x8, Pallas kernels, absorb(): pl.pallas_call(functools.partial(absorb_kernel, work, count, state is Non...  8.59 us
    pallas_call x1, Pallas kernels, on_device(): pl.pallas_call(functools.partial(prepare_kernel, block_of), out_shape=(ja...  2.42 us
    pallas_call x1, Pallas kernels, on_device(): pl.pallas_call(pack_kernel, out_shape=jax.ShapeDtypeStruct((count * size...  0.99 us
  transfers between devices with their start and end apart: 10, of which 6 were waited for; matrix products, arithmetic and copies ran while one was open for 0% of the time, Pallas kernels for 30%

profile of v3, /device:TPU:0, one launch (start us, length us, event | category | flops | bytes accessed | tf_op | source)
XLA Modules:
  0.0 36.0 jit_solution(13846388101633479770)
XLA Ops:
  0.6 0.5 %collective-permute-start.5 = (bf16[768,1024]{1,0:T(8,128)(2,1)}, bf16[768,1024]{1,0:T(8,128)(2,1)S(1)}, u32[]{:S(2)}, u32[]{:S(2)}) collective-permute-start(bf16[768,1024]{1,0:T(8,128)(2,1)} %observed_hbm.1), channel_id=1, source_target_pairs={{0,1},{1,0},{2,3},{3,2},{4,5},{5,4},{6,7},{7,6},{8,9},{9,8},{10,11... | collective-permute-start | bytes 4718600 | tf_op jit(solution)/shard_map/ppermute | solution.py:242
  1.1 1.0 %pack.1.refs_0_ = bf16[1040,128]{1,0:T(8,128)(2,1)S(1)} custom-call(bf16[4,128]{1,0:T(4,128)(2,1)} %params_hbm.1, s32[128]{0:T(128)} %class_hbm.2, bf16[128,1024]{1,0:T(8,128)(2,1)} %evolved_hbm.1), custom_call_target="tpu_custom_call" | custom-call | tf_op jit(solution)/shard_map/pack/pallas_call | solution.py:201
  2.1 2.6 %collective-permute-start.1 = (bf16[1040,128]{1,0:T(8,128)(2,1)S(1)}, bf16[1040,128]{1,0:T(8,128)(2,1)S(1)}, u32[]{:S(2)}, u32[]{:S(2)}) collective-permute-start(bf16[1040,128]{1,0:T(8,128)(2,1)S(1)} %pack.1.refs_0_), channel_id=1, source_target_pairs={{0,4},{1,3},{2,0},{3,7},{4,8},{5,1},{6,2},{7,11},{8,12},{9,5},{10,... | collective-permute-start | bytes 798728 | tf_op jit(solution)/shard_map/ppermute | solution.py:219
  4.8 2.4 %prepare.1 = (f32[10,768]{1,0:T(8,128)S(1)}, f32[10,768]{1,0:T(8,128)S(1)}, bf16[768,1024]{1,0:T(8,128)(2,1)S(1)}) custom-call(s32[1]{0:T(128)} %bitcast.at_ref, s32[6,16]{1,0:T(8,128)} %pattern_hbm.1, s32[768]{0:T(1024)} %class_hbm.3, f32[768]{0:T(1024)} %sharp_hbm.1, bf16[768,1024]{1,0:T(8,128)(2,1)} %observed_hbm.1), custom_call_target="tpu_custom_call" | custom-call | flops 6291456 | bytes 3145728 | tf_op jit(solution)/shard_map/prepare/pallas_call | solution.py:223
  7.2 0.1 collective-permute-start
  7.3 2.2 %collective-permute-done.1.refs_1_ = bf16[1040,128]{1,0:T(8,128)(2,1)S(1)} collective-permute-done((bf16[1040,128]{1,0:T(8,128)(2,1)S(1)}, bf16[1040,128]{1,0:T(8,128)(2,1)S(1)}, u32[]{:S(2)}, u32[]{:S(2)}) %collective-permute-start.1) | collective-permute-done | bytes 266272 | tf_op jit(solution)/shard_map/ppermute | solution.py:219
  9.5 2.5 %collective-permute-start.3 = (bf16[1040,128]{1,0:T(8,128)(2,1)S(1)}, bf16[1040,128]{1,0:T(8,128)(2,1)S(1)}, u32[]{:S(2)}, u32[]{:S(2)}) collective-permute-start(bf16[1040,128]{1,0:T(8,128)(2,1)S(1)} %collective-permute-done.1.refs_1_), channel_id=1, source_target_pairs={{0,4},{1,3},{2,0},{3,7},{4,8},{5,1},{6,2},{7,11},{8,12},{9,5},{10,... | collective-permute-start | bytes 798728 | tf_op jit(solution)/shard_map/ppermute | solution.py:219
  12.0 1.0 %absorb.8.refs_2_ = f32[8,768]{1,0:T(8,128)S(1)} custom-call(bf16[768,1024]{1,0:T(8,128)(2,1)S(1)} %get-tuple-element.12.observed_ref, f32[10,768]{1,0:T(8,128)S(1)} %get-tuple-element.13.aux_ref, bf16[1040,128]{1,0:T(8,128)(2,1)S(1)} %pack.1.refs_0_, bf16[1040,128]{1,0:T(8,128)(2,1)S(1)} %collective-permute-done.1.refs_1_), custom_call_target="tpu_custom_call" | custom-call | flops 402653184 | bytes 2097152 | tf_op jit(solution)/shard_map/absorb/pallas_call | solution.py:250
  12.9 2.8 %collective-permute-done.refs_0_ = bf16[1040,128]{1,0:T(8,128)(2,1)S(1)} collective-permute-done((bf16[1040,128]{1,0:T(8,128)(2,1)S(1)}, bf16[1040,128]{1,0:T(8,128)(2,1)S(1)}, u32[]{:S(2)}, u32[]{:S(2)}) %collective-permute-start) | collective-permute-done | bytes 266272 | tf_op jit(solution)/shard_map/ppermute | solution.py:219
  15.7 1.0 %absorb.10.refs_2_ = f32[8,768]{1,0:T(8,128)S(1)} custom-call(bf16[768,1024]{1,0:T(8,128)(2,1)S(1)} %collective-permute-done.5.observed_ref, f32[10,768]{1,0:T(8,128)S(1)} %collective-permute-done.6.aux_ref, bf16[1040,128]{1,0:T(8,128)(2,1)S(1)} %pack.1.refs_0_, bf16[1040,128]{1,0:T(8,128)(2,1)S(1)} %collective-permute-done.1.refs_1_), custom_call_target="tpu_custom_call" | custom-call | flops 402653184 | bytes 2097152 | tf_op jit(solution)/shard_map/absorb/pallas_call | solution.py:250
  16.7 0.1 collective-permute-done.3.refs_1_
  16.7 2.5 %collective-permute-start.7 = (bf16[1040,128]{1,0:T(8,128)(2,1)S(1)}, bf16[1040,128]{1,0:T(8,128)(2,1)S(1)}, u32[]{:S(2)}, u32[]{:S(2)}) collective-permute-start(bf16[1040,128]{1,0:T(8,128)(2,1)S(1)} %collective-permute-done.3.refs_1_), channel_id=1, source_target_pairs={{0,4},{1,3},{2,0},{3,7},{4,8},{5,1},{6,2},{7,11},{8,12},{9,5},{10,... | collective-permute-start | bytes 798728 | tf_op jit(solution)/shard_map/ppermute | solution.py:219
  19.2 1.1 %absorb.9.refs_2_ = f32[8,768]{1,0:T(8,128)S(1)} custom-call(bf16[768,1024]{1,0:T(8,128)(2,1)S(1)} %get-tuple-element.12.observed_ref, f32[10,768]{1,0:T(8,128)S(1)} %get-tuple-element.13.aux_ref, bf16[1040,128]{1,0:T(8,128)(2,1)S(1)} %collective-permute-done.refs_0_, bf16[1040,128]{1,0:T(8,128)(2,1)S(1)} %collective-permute-done.3.refs_1_, ...), custom_call_target="tpu_custom_call" | custom-call | flops 402653184 | bytes 2097152 | tf_op jit(solution)/shard_map/absorb/pallas_call | solution.py:250
  20.3 4.5 %collective-permute-done.2.refs_0_ = bf16[1040,128]{1,0:T(8,128)(2,1)S(1)} collective-permute-done((bf16[1040,128]{1,0:T(8,128)(2,1)S(1)}, bf16[1040,128]{1,0:T(8,128)(2,1)S(1)}, u32[]{:S(2)}, u32[]{:S(2)}) %collective-permute-start.2) | collective-permute-done | bytes 266272 | tf_op jit(solution)/shard_map/ppermute | solution.py:219
  24.8 0.2 collective-permute-start.4
  25.0 1.1 %absorb.11.refs_2_ = f32[8,768]{1,0:T(8,128)S(1)} custom-call(bf16[768,1024]{1,0:T(8,128)(2,1)S(1)} %collective-permute-done.5.observed_ref, f32[10,768]{1,0:T(8,128)S(1)} %collective-permute-done.6.aux_ref, bf16[1040,128]{1,0:T(8,128)(2,1)S(1)} %collective-permute-done.refs_0_, bf16[1040,128]{1,0:T(8,128)(2,1)S(1)} %collective-permute-done.3.refs_1_, ...), custom_call_target="tpu_custom_call" | custom-call | flops 402653184 | bytes 2097152 | tf_op jit(solution)/shard_map/absorb/pallas_call | solution.py:250
  26.1 1.9 %collective-permute-start.8 = (bf16[1040,128]{1,0:T(8,128)(2,1)S(1)}, bf16[1040,128]{1,0:T(8,128)(2,1)S(1)}, u32[]{:S(2)}, u32[]{:S(2)}) collective-permute-start(bf16[1040,128]{1,0:T(8,128)(2,1)S(1)} %collective-permute-done.7.refs_1_), channel_id=1, source_target_pairs={{0,4},{1,3},{2,0},{3,7},{4,8},{5,1},{6,2},{7,11},{8,12},{9,5},{10,... | collective-permute-start | bytes 798728 | tf_op jit(solution)/shard_map/ppermute | solution.py:219
  28.0 1.1 %absorb.14.refs_2_ = f32[8,768]{1,0:T(8,128)S(1)} custom-call(bf16[768,1024]{1,0:T(8,128)(2,1)S(1)} %collective-permute-done.5.observed_ref, f32[10,768]{1,0:T(8,128)S(1)} %collective-permute-done.6.aux_ref, bf16[1040,128]{1,0:T(8,128)(2,1)S(1)} %collective-permute-done.2.refs_0_, bf16[1040,128]{1,0:T(8,128)(2,1)S(1)} %collective-permute-done.7.refs_1_, ...), custom_call_target="tpu_custom_call" | custom-call | flops 402653184 | bytes 2097152 | tf_op jit(solution)/shard_map/absorb/pallas_call | solution.py:250
  29.1 1.1 %absorb.12.refs_2_ = f32[8,768]{1,0:T(8,128)S(1)} custom-call(bf16[768,1024]{1,0:T(8,128)(2,1)S(1)} %get-tuple-element.12.observed_ref, f32[10,768]{1,0:T(8,128)S(1)} %get-tuple-element.13.aux_ref, bf16[1040,128]{1,0:T(8,128)(2,1)S(1)} %collective-permute-done.2.refs_0_, bf16[1040,128]{1,0:T(8,128)(2,1)S(1)} %collective-permute-done.7.refs_1_, ...), custom_call_target="tpu_custom_call" | custom-call | flops 402653184 | bytes 2097152 | tf_op jit(solution)/shard_map/absorb/pallas_call | solution.py:250
  30.2 2.8 %collective-permute-done.4.refs_0_ = bf16[1040,128]{1,0:T(8,128)(2,1)S(1)} collective-permute-done((bf16[1040,128]{1,0:T(8,128)(2,1)S(1)}, bf16[1040,128]{1,0:T(8,128)(2,1)S(1)}, u32[]{:S(2)}, u32[]{:S(2)}) %collective-permute-start.4) | collective-permute-done | bytes 266272 | tf_op jit(solution)/shard_map/ppermute | solution.py:219
  33.0 1.1 %absorb.15 = f32[8,768]{1,0:T(8,128)S(1)} custom-call(bf16[768,1024]{1,0:T(8,128)(2,1)S(1)} %collective-permute-done.5.observed_ref, f32[10,768]{1,0:T(8,128)S(1)} %collective-permute-done.6.aux_ref, bf16[1040,128]{1,0:T(8,128)(2,1)S(1)} %collective-permute-done.4.refs_0_, bf16[1040,128]{1,0:T(8,128)(2,1)S(1)} %collective-permute-done.8.refs_1_, ...), custom_call_target="tpu_custom_call" | custom-call | flops 402653184 | bytes 2097152 | tf_op jit(solution)/shard_map/absorb/pallas_call | solution.py:250
  34.2 1.1 %absorb.13.mine_ref = f32[8,768]{1,0:T(8,128)S(1)} custom-call(bf16[768,1024]{1,0:T(8,128)(2,1)S(1)} %get-tuple-element.12.observed_ref, f32[10,768]{1,0:T(8,128)S(1)} %get-tuple-element.13.aux_ref, bf16[1040,128]{1,0:T(8,128)(2,1)S(1)} %collective-permute-done.4.refs_0_, bf16[1040,128]{1,0:T(8,128)(2,1)S(1)} %collective-permute-done.8.refs_1_, ...), custom_call_target="tpu_custom_call" | custom-call | flops 402653184 | bytes 2097152 | tf_op jit(solution)/shard_map/absorb/pallas_call | solution.py:250
  35.3 0.1 collective-permute-done.9.other_ref
  35.3 0.6 %finish.1 = (f32[4,768]{1,0:T(4,128)}, f32[768]{0:T(1024)}) custom-call(f32[8,768]{1,0:T(8,128)S(1)} %absorb.13.mine_ref, f32[8,768]{1,0:T(8,128)S(1)} %collective-permute-done.9.other_ref, f32[10,768]{1,0:T(8,128)S(1)} %get-tuple-element.13.aux_ref), custom_call_target="tpu_custom_call" | custom-call | tf_op jit(solution)/shard_map/finish/pallas_call | solution.py:285
  (7 shorter events, 0.0 us)
Async XLA Ops:
  0.6 15.1 %collective-permute-start.5 = (bf16[768,1024]{1,0:T(8,128)(2,1)}, bf16[768,1024]{1,0:T(8,128)(2,1)S(1)}, u32[]{:S(2)}, u32[]{:S(2)}) collective-permute-start(bf16[768,1024]{1,0:T(8,128)(2,1)} %observed_hbm.1), channel_id=1, source_target_pairs={{0,1},{1,0},{2,3},{3,2},{4,5},{5,4},{6,7},{7,6},{8,9},{9,8},{10,11... | collective-permute-start | bytes 4718600 | tf_op jit(solution)/shard_map/ppermute | solution.py:242
  2.1 7.3 %collective-permute-start.1 = (bf16[1040,128]{1,0:T(8,128)(2,1)S(1)}, bf16[1040,128]{1,0:T(8,128)(2,1)S(1)}, u32[]{:S(2)}, u32[]{:S(2)}) collective-permute-start(bf16[1040,128]{1,0:T(8,128)(2,1)S(1)} %pack.1.refs_0_), channel_id=1, source_target_pairs={{0,4},{1,3},{2,0},{3,7},{4,8},{5,1},{6,2},{7,11},{8,12},{9,5},{10,... | collective-permute-start | bytes 798728 | tf_op jit(solution)/shard_map/ppermute | solution.py:219
  7.2 8.5 %collective-permute-start = (bf16[1040,128]{1,0:T(8,128)(2,1)S(1)}, bf16[1040,128]{1,0:T(8,128)(2,1)S(1)}, u32[]{:S(2)}, u32[]{:S(2)}) collective-permute-start(bf16[1040,128]{1,0:T(8,128)(2,1)S(1)} %pack.1.refs_0_), channel_id=1, source_target_pairs={{0,2},{1,5},{2,6},{3,1},{4,0},{5,9},{6,10},{7,3},{8,4},{9,13},{10,... | collective-permute-start | bytes 798728 | tf_op jit(solution)/shard_map/ppermute | solution.py:219
  9.5 7.2 %collective-permute-start.3 = (bf16[1040,128]{1,0:T(8,128)(2,1)S(1)}, bf16[1040,128]{1,0:T(8,128)(2,1)S(1)}, u32[]{:S(2)}, u32[]{:S(2)}) collective-permute-start(bf16[1040,128]{1,0:T(8,128)(2,1)S(1)} %collective-permute-done.1.refs_1_), channel_id=1, source_target_pairs={{0,4},{1,3},{2,0},{3,7},{4,8},{5,1},{6,2},{7,11},{8,12},{9,5},{10,... | collective-permute-start | bytes 798728 | tf_op jit(solution)/shard_map/ppermute | solution.py:219
  12.0 3.8 %collective-permute-start.6 = (f32[10,768]{1,0:T(8,128)S(1)}, f32[10,768]{1,0:T(8,128)S(1)}, u32[]{:S(2)}, u32[]{:S(2)}) collective-permute-start(f32[10,768]{1,0:T(8,128)S(1)} %get-tuple-element.17), channel_id=1, source_target_pairs={{0,1},{1,0},{2,3},{3,2},{4,5},{5,4},{6,7},{7,6},{8,9},{9,8},{10,11... | collective-permute-start | bytes 92168 | tf_op jit(solution)/shard_map/ppermute | solution.py:243
  15.7 9.1 %collective-permute-start.2 = (bf16[1040,128]{1,0:T(8,128)(2,1)S(1)}, bf16[1040,128]{1,0:T(8,128)(2,1)S(1)}, u32[]{:S(2)}, u32[]{:S(2)}) collective-permute-start(bf16[1040,128]{1,0:T(8,128)(2,1)S(1)} %collective-permute-done.refs_0_), channel_id=1, source_target_pairs={{0,2},{1,5},{2,6},{3,1},{4,0},{5,9},{6,10},{7,3},{8,4},{9,13},{10,... | collective-permute-start | bytes 798728 | tf_op jit(solution)/shard_map/ppermute | solution.py:219
  16.7 9.3 %collective-permute-start.7 = (bf16[1040,128]{1,0:T(8,128)(2,1)S(1)}, bf16[1040,128]{1,0:T(8,128)(2,1)S(1)}, u32[]{:S(2)}, u32[]{:S(2)}) collective-permute-start(bf16[1040,128]{1,0:T(8,128)(2,1)S(1)} %collective-permute-done.3.refs_1_), channel_id=1, source_target_pairs={{0,4},{1,3},{2,0},{3,7},{4,8},{5,1},{6,2},{7,11},{8,12},{9,5},{10,... | collective-permute-start | bytes 798728 | tf_op jit(solution)/shard_map/ppermute | solution.py:219
  24.8 8.2 %collective-permute-start.4 = (bf16[1040,128]{1,0:T(8,128)(2,1)S(1)}, bf16[1040,128]{1,0:T(8,128)(2,1)S(1)}, u32[]{:S(2)}, u32[]{:S(2)}) collective-permute-start(bf16[1040,128]{1,0:T(8,128)(2,1)S(1)} %collective-permute-done.2.refs_0_), channel_id=1, source_target_pairs={{0,2},{1,5},{2,6},{3,1},{4,0},{5,9},{6,10},{7,3},{8,4},{9,13},{10,... | collective-permute-start | bytes 798728 | tf_op jit(solution)/shard_map/ppermute | solution.py:219
  26.1 7.0 %collective-permute-start.8 = (bf16[1040,128]{1,0:T(8,128)(2,1)S(1)}, bf16[1040,128]{1,0:T(8,128)(2,1)S(1)}, u32[]{:S(2)}, u32[]{:S(2)}) collective-permute-start(bf16[1040,128]{1,0:T(8,128)(2,1)S(1)} %collective-permute-done.7.refs_1_), channel_id=1, source_target_pairs={{0,4},{1,3},{2,0},{3,7},{4,8},{5,1},{6,2},{7,11},{8,12},{9,5},{10,... | collective-permute-start | bytes 798728 | tf_op jit(solution)/shard_map/ppermute | solution.py:219
  34.1 1.2 %collective-permute-start.9 = (f32[8,768]{1,0:T(8,128)S(1)}, f32[8,768]{1,0:T(8,128)S(1)}, u32[]{:S(2)}, u32[]{:S(2)}) collective-permute-start(f32[8,768]{1,0:T(8,128)S(1)} %absorb.15), channel_id=1, source_target_pairs={{0,1},{1,0},{2,3},{3,2},{4,5},{5,4},{6,7},{7,6},{8,9},{9,8},{10,11... | collective-permute-start | bytes 73736 | tf_op jit(solution)/shard_map/ppermute | solution.py:282

commit v4 on v3

--- a/solution.py
+++ b/solution.py
@@ -33,17 +33,12 @@
     def beside(device, by):
         return ring((place_of(device // 2) + by + chips) % chips) * 2 + device % 2
 
-    def way(device, kind):
-        return 1 - 2 * ((device + kind) % 2)
-
     def block_of(device, step):
-        if step == 0:
-            return device
-        return beside(device, -way(device, (step - 1) % 2) * ((step + 1) // 2))
+        return beside(device, step // 2 if step % 2 == 0 else -(step + 1) // 2)
 
     all_devices = np.arange(size)
     with jax.ensure_compile_time_eval():
-        targets = [np.asarray(beside(all_devices, way(all_devices, kind))).tolist() for kind in range(2)]
+        targets = [np.asarray(beside(all_devices, way)).tolist() for way in (1, -1, 1 - 2 * (all_devices % 2))]
     return [list(enumerate(target)) for target in targets], block_of
 
 
@@ -55,7 +50,7 @@
     return values.reshape(1, values.shape[-1])
 
 
-def pack_kernel(params_hbm, class_hbm, evolved_hbm, packet_ref, params_ref, class_ref, arrived):
+def pack_kernel(params_hbm, class_hbm, evolved_hbm, observed_hbm, packet_ref, observed_ref, params_ref, class_ref, arrived):
     rows, size = evolved_hbm.shape
     panels = size // LANES
     copies = [
@@ -66,6 +61,7 @@
         panel = packet_ref.at[pl.ds(i * rows, rows), :]
         source = evolved_hbm.at[:, pl.ds(i * LANES, LANES)]
         copies.append(pltpu.make_async_copy(source, panel, arrived.at[i + 2]))
+    copies.append(pltpu.make_async_copy(observed_hbm, observed_ref, arrived.at[panels + 2]))
     for copy in copies:
         copy.start()
     for copy in copies[:2]:
@@ -91,18 +87,20 @@
 
 
 def prepare_kernel(
-    block_of, at_ref, pattern_hbm, class_hbm, sharp_hbm, observed_hbm,
-    own_ref, sib_ref, observed_ref, pattern_ref, class_ref, sharp_ref, arrived,
+    block_of, at_ref, pattern_hbm, class_hbm, sharp_hbm, observed_ref,
+    own_ref, sib_ref, pattern_ref, class_ref, sharp_ref, arrived,
 ):
-    sources = (pattern_hbm, class_hbm, sharp_hbm, observed_hbm)
-    targets = (pattern_ref, class_ref, sharp_ref, observed_ref)
+    sources = (pattern_hbm, class_hbm, sharp_hbm)
+    targets = (pattern_ref, class_ref, sharp_ref)
     copies = [
         pltpu.make_async_copy(source, target, arrived.at[i])
         for i, (source, target) in enumerate(zip(sources, targets))
     ]
     for copy in copies:
         copy.start()
-    for copy in copies[:3]:
+    after_steps = own_ref.shape[0] - 2
+    own_ref[after_steps + 1 : after_steps + 2, :] = norms(observed_ref[...])
+    for copy in copies:
         copy.wait()
     tiles, devices = pattern_ref.shape
     tile = class_ref.shape[0] // tiles
@@ -115,10 +113,20 @@
                 jnp.where(pattern_ref[i, block] == 1, classes[:, i * tile : (i + 1) * tile], -1.0) for i in range(tiles)
             ]
             out_ref[step : step + 1, :] = jnp.concatenate(opened, axis=1)
-        out_ref[devices // 2 : devices // 2 + 1, :] = scale
-    copies[3].wait()
-    own_ref[devices // 2 + 1 : devices // 2 + 2, :] = norms(observed_ref[...])
-    sib_ref[devices // 2 + 1 : devices // 2 + 2, :] = scale
+        out_ref[after_steps : after_steps + 1, :] = scale
+    sib_ref[after_steps + 1 : after_steps + 2, :] = scale
+
+
+def choose_kernel(at_ref, first_ref, second_ref, out_ref):
+    core = at_ref[0] % 2
+
+    @pl.when(core == 0)
+    def _():
+        out_ref[...] = first_ref[...]
+
+    @pl.when(core == 1)
+    def _():
+        out_ref[...] = second_ref[...]
 
 
 def absorb_kernel(steps, count, first, observed_ref, aux_ref, *refs):
@@ -198,51 +206,45 @@
     core = [(i, i ^ 1) for i in range(devices)]
     at = lax.axis_index("blk").astype(jnp.int32).reshape(1)
 
-    packet = pl.pallas_call(
+    packet, observed_own = pl.pallas_call(
         pack_kernel,
-        out_shape=jax.ShapeDtypeStruct((count * size // LANES + META_ROWS, LANES), evolved.dtype),
-        in_specs=[hbm] * 3,
-        out_specs=vmem,
+        out_shape=(
+            jax.ShapeDtypeStruct((count * size // LANES + META_ROWS, LANES), evolved.dtype),
+            jax.ShapeDtypeStruct(observed.shape, observed.dtype),
+        ),
+        in_specs=[hbm] * 4,
+        out_specs=(vmem,) * 2,
         scratch_shapes=[
             pltpu.VMEM(sim_params.shape, sim_params.dtype),
             pltpu.VMEM(sim_class.shape, sim_class.dtype),
-            pltpu.SemaphoreType.DMA((size // LANES + 2,)),
+            pltpu.SemaphoreType.DMA((size // LANES + 3,)),
         ],
         compiler_params=compiler_params,
         name="pack",
-    )(*in_hbm(sim_params, sim_class, evolved))
-    packets = [packet]
-    moving = [packet, packet]
-
-    def send(step):
-        kind = step % 2
-        moving[kind] = lax.ppermute(moving[kind], "blk", pairs[kind])
-        packets.append(moving[kind])
-
-    send(0)
-    own_aux, sib_aux, observed_own = pl.pallas_call(
+    )(*in_hbm(sim_params, sim_class, evolved, observed))
+    forward = lax.ppermute(packet, "blk", pairs[0])
+    backward = lax.ppermute(packet, "blk", pairs[1])
+    observed_sib = lax.ppermute(observed_own, "blk", core)
+    own_aux, sib_aux = pl.pallas_call(
         functools.partial(prepare_kernel, block_of),
         out_shape=(
             jax.ShapeDtypeStruct((steps + 2, rows), f32),
             jax.ShapeDtypeStruct((steps + 2, rows), f32),
-            jax.ShapeDtypeStruct(observed.shape, observed.dtype),
         ),
-        in_specs=[smem] + [hbm] * 4,
-        out_specs=(vmem,) * 3,
+        in_specs=[smem] + [hbm] * 3 + [vmem],
+        out_specs=(vmem,) * 2,
         scratch_shapes=[
             pltpu.SMEM(pattern.shape, pattern.dtype),
             pltpu.VMEM(obs_class.shape, obs_class.dtype),
             pltpu.VMEM(sharpness.shape, sharpness.dtype),
-            pltpu.SemaphoreType.DMA((4,)),
+            pltpu.SemaphoreType.DMA((3,)),
         ],
         compiler_params=compiler_params,
         cost_estimate=pl.CostEstimate(flops=8 * rows * size, bytes_accessed=4 * rows * size, transcendentals=0),
         name="prepare",
-    )(after(at, packet), *in_hbm(pattern, obs_class, sharpness, observed))
-    observed_sib = lax.ppermute(observed, "blk", core)
+    )(at, *in_hbm(pattern, obs_class, sharpness), observed_own)
     sib_aux = lax.ppermute(sib_aux, "blk", core)
-    moving[1] = after(moving[1], own_aux)
-    send(1)
+    packets = [packet]
 
     def absorb(work, half, state):
         observed_half, aux = ((observed_own, own_aux), (observed_sib, sib_aux))[half]
@@ -261,27 +263,31 @@
             name="absorb",
         )(observed_half, aux, *(packets[i] for i in work), *before)
 
-    states = [None, None]
-    works = []
-    for first in range(0, steps, 2):
-        work = tuple(range(first, min(first + 2, steps)))
-        works += [(work, half) for half in ((0, 1) if first + 2 < steps else (1, 0))]
-    done = []
-    for step in range(steps - 1):
-        ahead = step + 2
-        if ahead < steps - 1:
-            if done:
-                moving[ahead % 2] = after(moving[ahead % 2], done[-1])
-            send(ahead)
-        if step < len(works):
-            work, half = works[step]
-            states[half] = absorb(work, half, states[half])
-            done.append(states[half])
-    for work, half in works[steps - 1 : -1]:
-        states[half] = absorb(work, half, states[half])
+    states = [absorb((0,), 0, None), None]
+    for step in range(1, steps - 1, 2):
+        arrived = (forward, backward)
+        packets += arrived
+        last = step + 2 == steps - 1
+        if last:
+            chosen = pl.pallas_call(
+                choose_kernel,
+                out_shape=jax.ShapeDtypeStruct(packet.shape, packet.dtype),
+                in_specs=[smem, vmem, vmem],
+                out_specs=vmem,
+                compiler_params=compiler_params,
+                name="choose",
+            )(at, *after(arrived, *(state for state in states if state is not None)))
+            packets_last = lax.ppermute(chosen, "blk", pairs[2])
+        else:
+            before = [state for state in states if state is not None]
+            forward = lax.ppermute(after(forward, *before), "blk", pairs[0])
+            backward = lax.ppermute(after(backward, *before), "blk", pairs[1])
+        states[0] = absorb((step, step + 1), 0, states[0])
+        states[1] = absorb((step, step + 1) if states[1] is not None else (0, step, step + 1), 1, states[1])
+    packets.append(after(packets_last, states[0]))
+    states[1] = absorb((steps - 1,), 1, states[1])
     other = lax.ppermute(states[1], "blk", core)
-    work, half = works[-1]
-    states[half] = absorb(work, half, states[half])
+    states[0] = absorb((steps - 1,), 0, states[0])
     mean, evidence = pl.pallas_call(
         functools.partial(finish_kernel, size),
         out_shape=(jax.ShapeDtypeStruct((sim_params.shape[0], rows), f32), jax.ShapeDtypeStruct((rows,), f32)),

time: 36.2 us -> 39.6 us (1.094)
  Pallas kernels: 12.6 us -> 16.9 us
  starting transfers between devices: 10.3 us -> 8.14 us
  waiting for transfers between devices: 12.4 us -> 13.7 us
    pallas_call x8 -> x9, Pallas kernels: 8.59 us -> 12.4 us  [absorb(): pl.pallas_call(functools.partial(absorb_kernel, work, count, state is Non...]
    ppermute x8, starting transfers between devices: 10.2 us -> 8.12 us  [the longest x2 3.17 us: on_device(): backward = lax.ppermute(after(backward, *before), 'blk', pairs[1])]
    pallas_call x1 -> x2, Pallas kernels: 0.99 us -> 2.42 us  [the longest x1 2.4 us: on_device(): pl.pallas_call(pack_kernel, out_shape=(jax.ShapeDtypeStruct((count * size...]
    ppermute x8, waiting for transfers between devices: 12.3 us -> 13.4 us  [the longest x2 5.07 us: on_device(): backward = lax.ppermute(after(backward, *before), 'blk', pairs[1])]
    pallas_call x1, Pallas kernels: 2.42 us -> 1.5 us  [on_device(): pl.pallas_call(functools.partial(prepare_kernel, block_of), out_shape=(ja...]
  transfers between devices with their start and end apart: 10 -> 10, of which waited for: 6 -> 6; matrix products, arithmetic and copies ran while one was open for 0% -> 0% of each run, Pallas kernels for 30% -> 33%
where the time goes in v4:
time: 39.6 us; the launch traced here: 39.4 us
  Pallas kernels  16.9 us (43%)
  waiting for transfers between devices  13.7 us (35%)
  starting transfers between devices  8.14 us (21%)
  between operations  0.68 us (2%)
    pallas_call x9, Pallas kernels, absorb(): pl.pallas_call(functools.partial(absorb_kernel, work, count, state is Non...  12.4 us
    ppermute x2, waiting for transfers between devices, on_device(): backward = lax.ppermute(after(backward, *before), 'blk', pairs[1])  5.07 us
    ppermute x1, waiting for transfers between devices, on_device(): backward = lax.ppermute(packet, 'blk', pairs[1])  3.9 us
    ppermute x1, waiting for transfers between devices, on_device(): packets_last = lax.ppermute(chosen, 'blk', pairs[2])  3.4 us
    ppermute x2, starting transfers between devices, on_device(): backward = lax.ppermute(after(backward, *before), 'blk', pairs[1])  3.17 us
    ppermute x1, starting transfers between devices, on_device(): backward = lax.ppermute(packet, 'blk', pairs[1])  2.58 us
    pallas_call x1, Pallas kernels, on_device(): pl.pallas_call(pack_kernel, out_shape=(jax.ShapeDtypeStruct((count * size...  2.4 us
    pallas_call x1, Pallas kernels, on_device(): pl.pallas_call(functools.partial(prepare_kernel, block_of), out_shape=(ja...  1.5 us
  transfers between devices with their start and end apart: 10, of which 6 were waited for; matrix products, arithmetic and copies ran while one was open for 0% of the time, Pallas kernels for 33%

profile of v4, /device:TPU:0, one launch (start us, length us, event | category | flops | bytes accessed | tf_op | source)
XLA Modules:
  0.0 39.4 jit_solution(9221340288315077245)
XLA Ops:
  0.6 2.4 %pack.1 = (bf16[1040,128]{1,0:T(8,128)(2,1)}, bf16[768,1024]{1,0:T(8,128)(2,1)S(1)}) custom-call(bf16[4,128]{1,0:T(4,128)(2,1)} %params_hbm.1, s32[128]{0:T(128)} %class_hbm.2, bf16[128,1024]{1,0:T(8,128)(2,1)} %evolved_hbm.1, bf16[768,1024]{1,0:T(8,128)(2,1)} %observed_hbm.1), custom_call_target="tpu_custom_call" | custom-call | tf_op jit(solution)/shard_map/pack/pallas_call | solution.py:209
  3.0 0.5 %collective-permute-start.3 = (bf16[768,1024]{1,0:T(8,128)(2,1)S(1)}, bf16[768,1024]{1,0:T(8,128)(2,1)S(1)}, u32[]{:S(2)}, u32[]{:S(2)}) collective-permute-start(bf16[768,1024]{1,0:T(8,128)(2,1)S(1)} %get-tuple-element.13.observed_ref), channel_id=1, source_target_pairs={{0,1},{1,0},{2,3},{3,2},{4,5},{5,4},{6,7},{7,6},{8,9},{9,8},{10,11... | collective-permute-start | bytes 4718600 | tf_op jit(solution)/shard_map/ppermute | solution.py:227
  3.6 2.6 %collective-permute-start.2 = (bf16[1040,128]{1,0:T(8,128)(2,1)}, bf16[1040,128]{1,0:T(8,128)(2,1)}, u32[]{:S(2)}, u32[]{:S(2)}) collective-permute-start(bf16[1040,128]{1,0:T(8,128)(2,1)} %get-tuple-element.15.refs_0_), channel_id=1, source_target_pairs={{0,2},{1,3},{2,6},{3,7},{4,0},{5,1},{6,10},{7,11},{8,4},{9,5},{10,... | collective-permute-start | bytes 798728 | tf_op jit(solution)/shard_map/ppermute | solution.py:226
  6.3 1.5 %prepare.1 = (f32[10,768]{1,0:T(8,128)S(1)}, f32[10,768]{1,0:T(8,128)S(1)}) custom-call(s32[1]{0:T(128)} %bitcast.at_ref, s32[6,16]{1,0:T(8,128)} %pattern_hbm.1, s32[768]{0:T(1024)} %class_hbm.3, f32[768]{0:T(1024)} %sharp_hbm.1, bf16[768,1024]{1,0:T(8,128)(2,1)S(1)} %get-tuple-element.13.observed_ref), custom_call_target="tpu_custom_call" | custom-call | flops 6291456 | bytes 3145728 | tf_op jit(solution)/shard_map/prepare/pallas_call | solution.py:228
  7.8 1.8 %absorb.9.refs_2_ = f32[8,768]{1,0:T(8,128)S(1)} custom-call(bf16[768,1024]{1,0:T(8,128)(2,1)S(1)} %get-tuple-element.13.observed_ref, f32[10,768]{1,0:T(8,128)S(1)} %get-tuple-element.14.aux_ref, bf16[1040,128]{1,0:T(8,128)(2,1)} %get-tuple-element.15.refs_0_), custom_call_target="tpu_custom_call" | custom-call | flops 201326592 | bytes 1835008 | tf_op jit(solution)/shard_map/absorb/pallas_call | solution.py:252
  9.6 3.9 %collective-permute-done.2.refs_1_.refs_2_ = bf16[1040,128]{1,0:T(8,128)(2,1)} collective-permute-done((bf16[1040,128]{1,0:T(8,128)(2,1)}, bf16[1040,128]{1,0:T(8,128)(2,1)}, u32[]{:S(2)}, u32[]{:S(2)}) %collective-permute-start.2) | collective-permute-done | bytes 266272 | tf_op jit(solution)/shard_map/ppermute | solution.py:226
  13.5 1.7 %collective-permute-start.6 = (bf16[1040,128]{1,0:T(8,128)(2,1)}, bf16[1040,128]{1,0:T(8,128)(2,1)S(1)}, u32[]{:S(2)}, u32[]{:S(2)}) collective-permute-start(bf16[1040,128]{1,0:T(8,128)(2,1)} %collective-permute-done.2.refs_1_.refs_2_), channel_id=1, source_target_pairs={{0,2},{1,3},{2,6},{3,7},{4,0},{5,1},{6,10},{7,11},{8,4},{9,5},{10,... | collective-permute-start | bytes 798728 | tf_op jit(solution)/shard_map/ppermute | solution.py:284
  15.2 0.3 collective-permute-start.1
  15.5 2.0 %absorb.10.refs_2_ = f32[8,768]{1,0:T(8,128)S(1)} custom-call(bf16[768,1024]{1,0:T(8,128)(2,1)S(1)} %get-tuple-element.13.observed_ref, f32[10,768]{1,0:T(8,128)S(1)} %get-tuple-element.14.aux_ref, bf16[1040,128]{1,0:T(8,128)(2,1)S(1)} %collective-permute-done.refs_0_.refs_1_, bf16[1040,128]{1,0:T(8,128)(2,1)} %collective-permute-done.2.refs_1_.refs_2_, ...), custom_call_target="tpu_custom_call" | custom-call | flops 402653184 | bytes 2097152 | tf_op jit(solution)/shard_map/absorb/pallas_call | solution.py:252
  17.6 2.2 %absorb.11.refs_2_ = f32[8,768]{1,0:T(8,128)S(1)} custom-call(bf16[768,1024]{1,0:T(8,128)(2,1)S(1)} %collective-permute-done.3.observed_ref, f32[10,768]{1,0:T(8,128)S(1)} %collective-permute-done.4.aux_ref, bf16[1040,128]{1,0:T(8,128)(2,1)} %get-tuple-element.15.refs_0_, bf16[1040,128]{1,0:T(8,128)(2,1)S(1)} %collective-permute-done.refs_0_.refs_1_, ...), custom_call_target="tpu_custom_call" | custom-call | flops 603979776 | bytes 2359296 | tf_op jit(solution)/shard_map/absorb/pallas_call | solution.py:252
  19.8 2.1 %collective-permute-done.6.refs_1_ = bf16[1040,128]{1,0:T(8,128)(2,1)S(1)} collective-permute-done((bf16[1040,128]{1,0:T(8,128)(2,1)}, bf16[1040,128]{1,0:T(8,128)(2,1)S(1)}, u32[]{:S(2)}, u32[]{:S(2)}) %collective-permute-start.6) | collective-permute-done | bytes 266272 | tf_op jit(solution)/shard_map/ppermute | solution.py:284
  21.9 1.5 %collective-permute-start.7 = (bf16[1040,128]{1,0:T(8,128)(2,1)S(1)}, bf16[1040,128]{1,0:T(8,128)(2,1)S(1)}, u32[]{:S(2)}, u32[]{:S(2)}) collective-permute-start(bf16[1040,128]{1,0:T(8,128)(2,1)S(1)} %collective-permute-done.6.refs_1_), channel_id=1, source_target_pairs={{0,2},{1,3},{2,6},{3,7},{4,0},{5,1},{6,10},{7,11},{8,4},{9,5},{10,... | collective-permute-start | bytes 798728 | tf_op jit(solution)/shard_map/ppermute | solution.py:284
  23.4 0.5 %collective-permute-start.5 = (bf16[1040,128]{1,0:T(8,128)(2,1)S(1)}, bf16[1040,128]{1,0:T(8,128)(2,1)S(1)}, u32[]{:S(2)}, u32[]{:S(2)}) collective-permute-start(bf16[1040,128]{1,0:T(8,128)(2,1)S(1)} %collective-permute-done.1.refs_0_), channel_id=1, source_target_pairs={{0,4},{1,5},{2,0},{3,1},{4,8},{5,9},{6,2},{7,3},{8,12},{9,13},{10,... | collective-permute-start | bytes 798728 | tf_op jit(solution)/shard_map/ppermute | solution.py:283
  23.9 1.1 %absorb.12.refs_2_ = f32[8,768]{1,0:T(8,128)S(1)} custom-call(bf16[768,1024]{1,0:T(8,128)(2,1)S(1)} %get-tuple-element.13.observed_ref, f32[10,768]{1,0:T(8,128)S(1)} %get-tuple-element.14.aux_ref, bf16[1040,128]{1,0:T(8,128)(2,1)S(1)} %collective-permute-done.1.refs_0_, bf16[1040,128]{1,0:T(8,128)(2,1)S(1)} %collective-permute-done.6.refs_1_, ...), custom_call_target="tpu_custom_call" | custom-call | flops 402653184 | bytes 2097152 | tf_op jit(solution)/shard_map/absorb/pallas_call | solution.py:252
  25.0 1.1 %absorb.13.refs_2_ = f32[8,768]{1,0:T(8,128)S(1)} custom-call(bf16[768,1024]{1,0:T(8,128)(2,1)S(1)} %collective-permute-done.3.observed_ref, f32[10,768]{1,0:T(8,128)S(1)} %collective-permute-done.4.aux_ref, bf16[1040,128]{1,0:T(8,128)(2,1)S(1)} %collective-permute-done.1.refs_0_, bf16[1040,128]{1,0:T(8,128)(2,1)S(1)} %collective-permute-done.6.refs_1_, ...), custom_call_target="tpu_custom_call" | custom-call | flops 402653184 | bytes 2097152 | tf_op jit(solution)/shard_map/absorb/pallas_call | solution.py:252
  26.2 3.0 %collective-permute-done.7.second_ref.refs_1_ = bf16[1040,128]{1,0:T(8,128)(2,1)S(1)} collective-permute-done((bf16[1040,128]{1,0:T(8,128)(2,1)S(1)}, bf16[1040,128]{1,0:T(8,128)(2,1)S(1)}, u32[]{:S(2)}, u32[]{:S(2)}) %collective-permute-start.7) | collective-permute-done | bytes 266272 | tf_op jit(solution)/shard_map/ppermute | solution.py:284
  29.2 1.0 %collective-permute-done.5.first_ref.refs_0_ = bf16[1040,128]{1,0:T(8,128)(2,1)S(1)} collective-permute-done((bf16[1040,128]{1,0:T(8,128)(2,1)S(1)}, bf16[1040,128]{1,0:T(8,128)(2,1)S(1)}, u32[]{:S(2)}, u32[]{:S(2)}) %collective-permute-start.5) | collective-permute-done | bytes 266272 | tf_op jit(solution)/shard_map/ppermute | solution.py:283
  30.2 0.8 %collective-permute-start.8 = (bf16[1040,128]{1,0:T(8,128)(2,1)S(1)}, bf16[1040,128]{1,0:T(8,128)(2,1)S(1)}, u32[]{:S(2)}, u32[]{:S(2)}) collective-permute-start(bf16[1040,128]{1,0:T(8,128)(2,1)S(1)} %choose.1), channel_id=1, source_target_pairs={{0,4},{1,3},{2,0},{3,7},{4,8},{5,1},{6,2},{7,11},{8,12},{9,5},{10,... | collective-permute-start | bytes 798728 | tf_op jit(solution)/shard_map/ppermute | solution.py:280
  31.0 1.1 %absorb.16.refs_1_ = f32[8,768]{1,0:T(8,128)S(1)} custom-call(bf16[768,1024]{1,0:T(8,128)(2,1)S(1)} %collective-permute-done.3.observed_ref, f32[10,768]{1,0:T(8,128)S(1)} %collective-permute-done.4.aux_ref, bf16[1040,128]{1,0:T(8,128)(2,1)S(1)} %collective-permute-done.5.first_ref.refs_0_, bf16[1040,128]{1,0:T(8,128)(2,1)S(1)} %collective-permute-done.7.second_ref.refs_1_, ...), custom_call_target="tpu_custom_call" | custom-call | flops 402653184 | bytes 2097152 | tf_op jit(solution)/shard_map/absorb/pallas_call | solution.py:252
  32.1 1.1 %absorb.14.refs_1_ = f32[8,768]{1,0:T(8,128)S(1)} custom-call(bf16[768,1024]{1,0:T(8,128)(2,1)S(1)} %get-tuple-element.13.observed_ref, f32[10,768]{1,0:T(8,128)S(1)} %get-tuple-element.14.aux_ref, bf16[1040,128]{1,0:T(8,128)(2,1)S(1)} %collective-permute-done.5.first_ref.refs_0_, bf16[1040,128]{1,0:T(8,128)(2,1)S(1)} %collective-permute-done.7.second_ref.refs_1_, ...), custom_call_target="tpu_custom_call" | custom-call | flops 402653184 | bytes 2097152 | tf_op jit(solution)/shard_map/absorb/pallas_call | solution.py:252
  33.3 3.4 %collective-permute-done.8.refs_0_ = bf16[1040,128]{1,0:T(8,128)(2,1)S(1)} collective-permute-done((bf16[1040,128]{1,0:T(8,128)(2,1)S(1)}, bf16[1040,128]{1,0:T(8,128)(2,1)S(1)}, u32[]{:S(2)}, u32[]{:S(2)}) %collective-permute-start.8) | collective-permute-done | bytes 266272 | tf_op jit(solution)/shard_map/ppermute | solution.py:280
  36.7 0.9 %absorb.17 = f32[8,768]{1,0:T(8,128)S(1)} custom-call(bf16[768,1024]{1,0:T(8,128)(2,1)S(1)} %collective-permute-done.3.observed_ref, f32[10,768]{1,0:T(8,128)S(1)} %collective-permute-done.4.aux_ref, bf16[1040,128]{1,0:T(8,128)(2,1)S(1)} %collective-permute-done.8.refs_0_, f32[8,768]{1,0:T(8,128)S(1)} %absorb.16.refs_1_), custom_call_target="tpu_custom_call" | custom-call | flops 201326592 | bytes 1835008 | tf_op jit(solution)/shard_map/absorb/pallas_call | solution.py:252
  37.6 0.9 %absorb.15.mine_ref = f32[8,768]{1,0:T(8,128)S(1)} custom-call(bf16[768,1024]{1,0:T(8,128)(2,1)S(1)} %get-tuple-element.13.observed_ref, f32[10,768]{1,0:T(8,128)S(1)} %get-tuple-element.14.aux_ref, bf16[1040,128]{1,0:T(8,128)(2,1)S(1)} %collective-permute-done.8.refs_0_, f32[8,768]{1,0:T(8,128)S(1)} %absorb.14.refs_1_), custom_call_target="tpu_custom_call" | custom-call | flops 201326592 | bytes 1835008 | tf_op jit(solution)/shard_map/absorb/pallas_call | solution.py:252
  38.7 0.6 %finish.1 = (f32[4,768]{1,0:T(4,128)}, f32[768]{0:T(1024)}) custom-call(f32[8,768]{1,0:T(8,128)S(1)} %absorb.15.mine_ref, f32[8,768]{1,0:T(8,128)S(1)} %collective-permute-done.9.other_ref, f32[10,768]{1,0:T(8,128)S(1)} %get-tuple-element.14.aux_ref), custom_call_target="tpu_custom_call" | custom-call | tf_op jit(solution)/shard_map/finish/pallas_call | solution.py:291
  (9 shorter events, 0.5 us)
Async XLA Ops:
  3.0 14.6 %collective-permute-start.3 = (bf16[768,1024]{1,0:T(8,128)(2,1)S(1)}, bf16[768,1024]{1,0:T(8,128)(2,1)S(1)}, u32[]{:S(2)}, u32[]{:S(2)}) collective-permute-start(bf16[768,1024]{1,0:T(8,128)(2,1)S(1)} %get-tuple-element.13.observed_ref), channel_id=1, source_target_pairs={{0,1},{1,0},{2,3},{3,2},{4,5},{5,4},{6,7},{7,6},{8,9},{9,8},{10,11... | collective-permute-start | bytes 4718600 | tf_op jit(solution)/shard_map/ppermute | solution.py:227
  3.6 10.0 %collective-permute-start.2 = (bf16[1040,128]{1,0:T(8,128)(2,1)}, bf16[1040,128]{1,0:T(8,128)(2,1)}, u32[]{:S(2)}, u32[]{:S(2)}) collective-permute-start(bf16[1040,128]{1,0:T(8,128)(2,1)} %get-tuple-element.15.refs_0_), channel_id=1, source_target_pairs={{0,2},{1,3},{2,6},{3,7},{4,0},{5,1},{6,10},{7,11},{8,4},{9,5},{10,... | collective-permute-start | bytes 798728 | tf_op jit(solution)/shard_map/ppermute | solution.py:226
  6.1 9.1 %collective-permute-start = (bf16[1040,128]{1,0:T(8,128)(2,1)}, bf16[1040,128]{1,0:T(8,128)(2,1)S(1)}, u32[]{:S(2)}, u32[]{:S(2)}) collective-permute-start(bf16[1040,128]{1,0:T(8,128)(2,1)} %get-tuple-element.15.refs_0_), channel_id=1, source_target_pairs={{0,4},{1,5},{2,0},{3,1},{4,8},{5,9},{6,2},{7,3},{8,12},{9,13},{10,... | collective-permute-start | bytes 798728 | tf_op jit(solution)/shard_map/ppermute | solution.py:225
  13.5 8.4 %collective-permute-start.6 = (bf16[1040,128]{1,0:T(8,128)(2,1)}, bf16[1040,128]{1,0:T(8,128)(2,1)S(1)}, u32[]{:S(2)}, u32[]{:S(2)}) collective-permute-start(bf16[1040,128]{1,0:T(8,128)(2,1)} %collective-permute-done.2.refs_1_.refs_2_), channel_id=1, source_target_pairs={{0,2},{1,3},{2,6},{3,7},{4,0},{5,1},{6,10},{7,11},{8,4},{9,5},{10,... | collective-permute-start | bytes 798728 | tf_op jit(solution)/shard_map/ppermute | solution.py:284
  15.2 8.2 %collective-permute-start.1 = (bf16[1040,128]{1,0:T(8,128)(2,1)S(1)}, bf16[1040,128]{1,0:T(8,128)(2,1)S(1)}, u32[]{:S(2)}, u32[]{:S(2)}) collective-permute-start(bf16[1040,128]{1,0:T(8,128)(2,1)S(1)} %collective-permute-done.refs_0_.refs_1_), channel_id=1, source_target_pairs={{0,4},{1,5},{2,0},{3,1},{4,8},{5,9},{6,2},{7,3},{8,12},{9,13},{10,... | collective-permute-start | bytes 798728 | tf_op jit(solution)/shard_map/ppermute | solution.py:283
  15.5 2.0 %collective-permute-start.4 = (f32[10,768]{1,0:T(8,128)S(1)}, f32[10,768]{1,0:T(8,128)S(1)}, u32[]{:S(2)}, u32[]{:S(2)}) collective-permute-start(f32[10,768]{1,0:T(8,128)S(1)} %get-tuple-element.17), channel_id=1, source_target_pairs={{0,1},{1,0},{2,3},{3,2},{4,5},{5,4},{6,7},{7,6},{8,9},{9,8},{10,11... | collective-permute-start | bytes 92168 | tf_op jit(solution)/shard_map/ppermute | solution.py:246
  21.9 7.3 %collective-permute-start.7 = (bf16[1040,128]{1,0:T(8,128)(2,1)S(1)}, bf16[1040,128]{1,0:T(8,128)(2,1)S(1)}, u32[]{:S(2)}, u32[]{:S(2)}) collective-permute-start(bf16[1040,128]{1,0:T(8,128)(2,1)S(1)} %collective-permute-done.6.refs_1_), channel_id=1, source_target_pairs={{0,2},{1,3},{2,6},{3,7},{4,0},{5,1},{6,10},{7,11},{8,4},{9,5},{10,... | collective-permute-start | bytes 798728 | tf_op jit(solution)/shard_map/ppermute | solution.py:284
  23.4 6.8 %collective-permute-start.5 = (bf16[1040,128]{1,0:T(8,128)(2,1)S(1)}, bf16[1040,128]{1,0:T(8,128)(2,1)S(1)}, u32[]{:S(2)}, u32[]{:S(2)}) collective-permute-start(bf16[1040,128]{1,0:T(8,128)(2,1)S(1)} %collective-permute-done.1.refs_0_), channel_id=1, source_target_pairs={{0,4},{1,5},{2,0},{3,1},{4,8},{5,9},{6,2},{7,3},{8,12},{9,13},{10,... | collective-permute-start | bytes 798728 | tf_op jit(solution)/shard_map/ppermute | solution.py:283
  30.2 6.5 %collective-permute-start.8 = (bf16[1040,128]{1,0:T(8,128)(2,1)S(1)}, bf16[1040,128]{1,0:T(8,128)(2,1)S(1)}, u32[]{:S(2)}, u32[]{:S(2)}) collective-permute-start(bf16[1040,128]{1,0:T(8,128)(2,1)S(1)} %choose.1), channel_id=1, source_target_pairs={{0,4},{1,3},{2,0},{3,7},{4,8},{5,1},{6,2},{7,11},{8,12},{9,5},{10,... | collective-permute-start | bytes 798728 | tf_op jit(solution)/shard_map/ppermute | solution.py:280
  37.5 1.2 %collective-permute-start.9 = (f32[8,768]{1,0:T(8,128)S(1)}, f32[8,768]{1,0:T(8,128)S(1)}, u32[]{:S(2)}, u32[]{:S(2)}) collective-permute-start(f32[8,768]{1,0:T(8,128)S(1)} %absorb.17), channel_id=1, source_target_pairs={{0,1},{1,0},{2,3},{3,2},{4,5},{5,4},{6,7},{7,6},{8,9},{9,8},{10,11... | collective-permute-start | bytes 73736 | tf_op jit(solution)/shard_map/ppermute | solution.py:289

commit v5 on v3

--- a/solution.py
+++ b/solution.py
@@ -31,19 +31,18 @@
         return jnp.where(chip % 2 == 0, chip // 2, chips - 1 - chip // 2)
 
     def beside(device, by):
-        return ring((place_of(device // 2) + by + chips) % chips) * 2 + device % 2
-
-    def way(device, kind):
-        return 1 - 2 * ((device + kind) % 2)
+        return ring((place_of(device // 2) + by + chips) % chips) * 2 + (device + by) % 2
 
     def block_of(device, step):
         if step == 0:
             return device
-        return beside(device, -way(device, (step - 1) % 2) * ((step + 1) // 2))
-
-    all_devices = np.arange(size)
+        stream, hop = (step - 1) % 2, (step - 1) // 2
+        way = 1 - 2 * ((device + 1 + stream + hop) % 2)
+        return beside(device, -way * (hop + 1))
+
+    devices = np.arange(size)
     with jax.ensure_compile_time_eval():
-        targets = [np.asarray(beside(all_devices, way(all_devices, kind))).tolist() for kind in range(2)]
+        targets = [np.asarray(beside(devices, 1 - 2 * ((devices + parity) % 2))).tolist() for parity in range(2)]
     return [list(enumerate(target)) for target in targets], block_of
 
 
@@ -216,7 +215,7 @@
 
     def send(step):
         kind = step % 2
-        moving[kind] = lax.ppermute(moving[kind], "blk", pairs[kind])
+        moving[kind] = lax.ppermute(moving[kind], "blk", pairs[(kind + step // 2) % 2])
         packets.append(moving[kind])
 
     send(0)

time: 36.2 us -> 32.2 us (0.89)
  waiting for transfers between devices: 12.4 us -> 4.96 us
  starting transfers between devices: 10.3 us -> 13.7 us
    ppermute x7, waiting for transfers between devices: 12.3 us -> 4.91 us  [send(): lax.ppermute(moving[kind], 'blk', pairs[(kind + step // 2) % 2])]
    ppermute x7, starting transfers between devices: 9.72 us -> 13.1 us  [send(): lax.ppermute(moving[kind], 'blk', pairs[(kind + step // 2) % 2])]
  transfers between devices with their start and end apart: 10 -> 10, of which waited for: 6 -> 6; matrix products, arithmetic and copies ran while one was open for 0% -> 0% of each run, Pallas kernels for 30% -> 34%
where the time goes in v5:
time: 32.2 us; the launch traced here: 32 us
  starting transfers between devices  13.7 us (43%)
  Pallas kernels  12.7 us (39%)
  waiting for transfers between devices  4.96 us (15%)
  between operations  0.67 us (2%)
    ppermute x7, starting transfers between devices, send(): lax.ppermute(moving[kind], 'blk', pairs[(kind + step // 2) % 2])  13.1 us
    pallas_call x8, Pallas kernels, absorb(): pl.pallas_call(functools.partial(absorb_kernel, work, count, state is Non...  8.6 us
    ppermute x7, waiting for transfers between devices, send(): lax.ppermute(moving[kind], 'blk', pairs[(kind + step // 2) % 2])  4.91 us
    pallas_call x1, Pallas kernels, on_device(): pl.pallas_call(functools.partial(prepare_kernel, block_of), out_shape=(ja...  2.42 us
    pallas_call x1, Pallas kernels, on_device(): pl.pallas_call(pack_kernel, out_shape=jax.ShapeDtypeStruct((count * size...  0.99 us
  transfers between devices with their start and end apart: 10, of which 6 were waited for; matrix products, arithmetic and copies ran while one was open for 0% of the time, Pallas kernels for 34%

profile of v5, /device:TPU:0, one launch (start us, length us, event | category | flops | bytes accessed | tf_op | source)
XLA Modules:
  0.0 32.0 jit_solution(16804179349744970052)
XLA Ops:
  0.6 0.5 %collective-permute-start.5 = (bf16[768,1024]{1,0:T(8,128)(2,1)}, bf16[768,1024]{1,0:T(8,128)(2,1)S(1)}, u32[]{:S(2)}, u32[]{:S(2)}) collective-permute-start(bf16[768,1024]{1,0:T(8,128)(2,1)} %observed_hbm.1), channel_id=1, source_target_pairs={{0,1},{1,0},{2,3},{3,2},{4,5},{5,4},{6,7},{7,6},{8,9},{9,8},{10,11... | collective-permute-start | bytes 4718600 | tf_op jit(solution)/shard_map/ppermute | solution.py:241
  1.1 1.0 %pack.1.refs_0_ = bf16[1040,128]{1,0:T(8,128)(2,1)S(1)} custom-call(bf16[4,128]{1,0:T(4,128)(2,1)} %params_hbm.1, s32[128]{0:T(128)} %class_hbm.2, bf16[128,1024]{1,0:T(8,128)(2,1)} %evolved_hbm.1), custom_call_target="tpu_custom_call" | custom-call | tf_op jit(solution)/shard_map/pack/pallas_call | solution.py:200
  2.1 2.8 %collective-permute-start.1 = (bf16[1040,128]{1,0:T(8,128)(2,1)S(1)}, bf16[1040,128]{1,0:T(8,128)(2,1)S(1)}, u32[]{:S(2)}, u32[]{:S(2)}) collective-permute-start(bf16[1040,128]{1,0:T(8,128)(2,1)S(1)} %pack.1.refs_0_), channel_id=1, source_target_pairs={{0,5},{1,2},{2,1},{3,6},{4,9},{5,0},{6,3},{7,10},{8,13},{9,4},{10,... | collective-permute-start | bytes 798728 | tf_op jit(solution)/shard_map/ppermute | solution.py:218
  4.9 2.4 %prepare.1 = (f32[10,768]{1,0:T(8,128)S(1)}, f32[10,768]{1,0:T(8,128)S(1)}, bf16[768,1024]{1,0:T(8,128)(2,1)S(1)}) custom-call(s32[1]{0:T(128)} %bitcast.at_ref, s32[6,16]{1,0:T(8,128)} %pattern_hbm.1, s32[768]{0:T(1024)} %class_hbm.3, f32[768]{0:T(1024)} %sharp_hbm.1, bf16[768,1024]{1,0:T(8,128)(2,1)} %observed_hbm.1), custom_call_target="tpu_custom_call" | custom-call | flops 6291456 | bytes 3145728 | tf_op jit(solution)/shard_map/prepare/pallas_call | solution.py:222
  7.3 1.2 %collective-permute-start = (bf16[1040,128]{1,0:T(8,128)(2,1)S(1)}, bf16[1040,128]{1,0:T(8,128)(2,1)S(1)}, u32[]{:S(2)}, u32[]{:S(2)}) collective-permute-start(bf16[1040,128]{1,0:T(8,128)(2,1)S(1)} %pack.1.refs_0_), channel_id=1, source_target_pairs={{0,3},{1,4},{2,7},{3,0},{4,1},{5,8},{6,11},{7,2},{8,5},{9,12},{10,... | collective-permute-start | bytes 798728 | tf_op jit(solution)/shard_map/ppermute | solution.py:218
  8.5 0.5 %collective-permute-done.1.refs_1_ = bf16[1040,128]{1,0:T(8,128)(2,1)S(1)} collective-permute-done((bf16[1040,128]{1,0:T(8,128)(2,1)S(1)}, bf16[1040,128]{1,0:T(8,128)(2,1)S(1)}, u32[]{:S(2)}, u32[]{:S(2)}) %collective-permute-start.1) | collective-permute-done | bytes 266272 | tf_op jit(solution)/shard_map/ppermute | solution.py:218
  9.0 1.7 %collective-permute-start.3 = (bf16[1040,128]{1,0:T(8,128)(2,1)S(1)}, bf16[1040,128]{1,0:T(8,128)(2,1)S(1)}, u32[]{:S(2)}, u32[]{:S(2)}) collective-permute-start(bf16[1040,128]{1,0:T(8,128)(2,1)S(1)} %collective-permute-done.1.refs_1_), channel_id=1, source_target_pairs={{0,3},{1,4},{2,7},{3,0},{4,1},{5,8},{6,11},{7,2},{8,5},{9,12},{10,... | collective-permute-start | bytes 798728 | tf_op jit(solution)/shard_map/ppermute | solution.py:218
  10.8 1.0 %absorb.8.refs_2_ = f32[8,768]{1,0:T(8,128)S(1)} custom-call(bf16[768,1024]{1,0:T(8,128)(2,1)S(1)} %get-tuple-element.12.observed_ref, f32[10,768]{1,0:T(8,128)S(1)} %get-tuple-element.13.aux_ref, bf16[1040,128]{1,0:T(8,128)(2,1)S(1)} %pack.1.refs_0_, bf16[1040,128]{1,0:T(8,128)(2,1)S(1)} %collective-permute-done.1.refs_1_), custom_call_target="tpu_custom_call" | custom-call | flops 402653184 | bytes 2097152 | tf_op jit(solution)/shard_map/absorb/pallas_call | solution.py:249
  11.7 1.5 %collective-permute-done.refs_0_ = bf16[1040,128]{1,0:T(8,128)(2,1)S(1)} collective-permute-done((bf16[1040,128]{1,0:T(8,128)(2,1)S(1)}, bf16[1040,128]{1,0:T(8,128)(2,1)S(1)}, u32[]{:S(2)}, u32[]{:S(2)}) %collective-permute-start) | collective-permute-done | bytes 266272 | tf_op jit(solution)/shard_map/ppermute | solution.py:218
  13.2 1.4 %collective-permute-start.2 = (bf16[1040,128]{1,0:T(8,128)(2,1)S(1)}, bf16[1040,128]{1,0:T(8,128)(2,1)S(1)}, u32[]{:S(2)}, u32[]{:S(2)}) collective-permute-start(bf16[1040,128]{1,0:T(8,128)(2,1)S(1)} %collective-permute-done.refs_0_), channel_id=1, source_target_pairs={{0,5},{1,2},{2,1},{3,6},{4,9},{5,0},{6,3},{7,10},{8,13},{9,4},{10,... | collective-permute-start | bytes 798728 | tf_op jit(solution)/shard_map/ppermute | solution.py:218
  14.7 0.9 %absorb.10.refs_2_ = f32[8,768]{1,0:T(8,128)S(1)} custom-call(bf16[768,1024]{1,0:T(8,128)(2,1)S(1)} %collective-permute-done.5.observed_ref, f32[10,768]{1,0:T(8,128)S(1)} %collective-permute-done.6.aux_ref, bf16[1040,128]{1,0:T(8,128)(2,1)S(1)} %pack.1.refs_0_, bf16[1040,128]{1,0:T(8,128)(2,1)S(1)} %collective-permute-done.1.refs_1_), custom_call_target="tpu_custom_call" | custom-call | flops 402653184 | bytes 2097152 | tf_op jit(solution)/shard_map/absorb/pallas_call | solution.py:249
  15.6 0.5 %collective-permute-done.3.refs_1_ = bf16[1040,128]{1,0:T(8,128)(2,1)S(1)} collective-permute-done((bf16[1040,128]{1,0:T(8,128)(2,1)S(1)}, bf16[1040,128]{1,0:T(8,128)(2,1)S(1)}, u32[]{:S(2)}, u32[]{:S(2)}) %collective-permute-start.3) | collective-permute-done | bytes 266272 | tf_op jit(solution)/shard_map/ppermute | solution.py:218
  16.1 1.3 %collective-permute-start.7 = (bf16[1040,128]{1,0:T(8,128)(2,1)S(1)}, bf16[1040,128]{1,0:T(8,128)(2,1)S(1)}, u32[]{:S(2)}, u32[]{:S(2)}) collective-permute-start(bf16[1040,128]{1,0:T(8,128)(2,1)S(1)} %collective-permute-done.3.refs_1_), channel_id=1, source_target_pairs={{0,5},{1,2},{2,1},{3,6},{4,9},{5,0},{6,3},{7,10},{8,13},{9,4},{10,... | collective-permute-start | bytes 798728 | tf_op jit(solution)/shard_map/ppermute | solution.py:218
  17.4 1.1 %absorb.9.refs_2_ = f32[8,768]{1,0:T(8,128)S(1)} custom-call(bf16[768,1024]{1,0:T(8,128)(2,1)S(1)} %get-tuple-element.12.observed_ref, f32[10,768]{1,0:T(8,128)S(1)} %get-tuple-element.13.aux_ref, bf16[1040,128]{1,0:T(8,128)(2,1)S(1)} %collective-permute-done.refs_0_, bf16[1040,128]{1,0:T(8,128)(2,1)S(1)} %collective-permute-done.3.refs_1_, ...), custom_call_target="tpu_custom_call" | custom-call | flops 402653184 | bytes 2097152 | tf_op jit(solution)/shard_map/absorb/pallas_call | solution.py:249
  18.5 0.6 %collective-permute-done.2.refs_0_ = bf16[1040,128]{1,0:T(8,128)(2,1)S(1)} collective-permute-done((bf16[1040,128]{1,0:T(8,128)(2,1)S(1)}, bf16[1040,128]{1,0:T(8,128)(2,1)S(1)}, u32[]{:S(2)}, u32[]{:S(2)}) %collective-permute-start.2) | collective-permute-done | bytes 266272 | tf_op jit(solution)/shard_map/ppermute | solution.py:218
  19.1 1.7 %collective-permute-start.4 = (bf16[1040,128]{1,0:T(8,128)(2,1)S(1)}, bf16[1040,128]{1,0:T(8,128)(2,1)S(1)}, u32[]{:S(2)}, u32[]{:S(2)}) collective-permute-start(bf16[1040,128]{1,0:T(8,128)(2,1)S(1)} %collective-permute-done.2.refs_0_), channel_id=1, source_target_pairs={{0,3},{1,4},{2,7},{3,0},{4,1},{5,8},{6,11},{7,2},{8,5},{9,12},{10,... | collective-permute-start | bytes 798728 | tf_op jit(solution)/shard_map/ppermute | solution.py:218
  20.8 1.1 %absorb.11.refs_2_ = f32[8,768]{1,0:T(8,128)S(1)} custom-call(bf16[768,1024]{1,0:T(8,128)(2,1)S(1)} %collective-permute-done.5.observed_ref, f32[10,768]{1,0:T(8,128)S(1)} %collective-permute-done.6.aux_ref, bf16[1040,128]{1,0:T(8,128)(2,1)S(1)} %collective-permute-done.refs_0_, bf16[1040,128]{1,0:T(8,128)(2,1)S(1)} %collective-permute-done.3.refs_1_, ...), custom_call_target="tpu_custom_call" | custom-call | flops 402653184 | bytes 2097152 | tf_op jit(solution)/shard_map/absorb/pallas_call | solution.py:249
  21.9 3.0 %collective-permute-start.8 = (bf16[1040,128]{1,0:T(8,128)(2,1)S(1)}, bf16[1040,128]{1,0:T(8,128)(2,1)S(1)}, u32[]{:S(2)}, u32[]{:S(2)}) collective-permute-start(bf16[1040,128]{1,0:T(8,128)(2,1)S(1)} %collective-permute-done.7.refs_1_), channel_id=1, source_target_pairs={{0,3},{1,4},{2,7},{3,0},{4,1},{5,8},{6,11},{7,2},{8,5},{9,12},{10,... | collective-permute-start | bytes 798728 | tf_op jit(solution)/shard_map/ppermute | solution.py:218
  25.0 1.1 %absorb.14.refs_2_ = f32[8,768]{1,0:T(8,128)S(1)} custom-call(bf16[768,1024]{1,0:T(8,128)(2,1)S(1)} %collective-permute-done.5.observed_ref, f32[10,768]{1,0:T(8,128)S(1)} %collective-permute-done.6.aux_ref, bf16[1040,128]{1,0:T(8,128)(2,1)S(1)} %collective-permute-done.2.refs_0_, bf16[1040,128]{1,0:T(8,128)(2,1)S(1)} %collective-permute-done.7.refs_1_, ...), custom_call_target="tpu_custom_call" | custom-call | flops 402653184 | bytes 2097152 | tf_op jit(solution)/shard_map/absorb/pallas_call | solution.py:249
  26.1 1.1 %absorb.12.refs_2_ = f32[8,768]{1,0:T(8,128)S(1)} custom-call(bf16[768,1024]{1,0:T(8,128)(2,1)S(1)} %get-tuple-element.12.observed_ref, f32[10,768]{1,0:T(8,128)S(1)} %get-tuple-element.13.aux_ref, bf16[1040,128]{1,0:T(8,128)(2,1)S(1)} %collective-permute-done.2.refs_0_, bf16[1040,128]{1,0:T(8,128)(2,1)S(1)} %collective-permute-done.7.refs_1_, ...), custom_call_target="tpu_custom_call" | custom-call | flops 402653184 | bytes 2097152 | tf_op jit(solution)/shard_map/absorb/pallas_call | solution.py:249
  27.2 1.9 %collective-permute-done.8.refs_1_ = bf16[1040,128]{1,0:T(8,128)(2,1)S(1)} collective-permute-done((bf16[1040,128]{1,0:T(8,128)(2,1)S(1)}, bf16[1040,128]{1,0:T(8,128)(2,1)S(1)}, u32[]{:S(2)}, u32[]{:S(2)}) %collective-permute-start.8) | collective-permute-done | bytes 266272 | tf_op jit(solution)/shard_map/ppermute | solution.py:218
  29.1 1.1 %absorb.15 = f32[8,768]{1,0:T(8,128)S(1)} custom-call(bf16[768,1024]{1,0:T(8,128)(2,1)S(1)} %collective-permute-done.5.observed_ref, f32[10,768]{1,0:T(8,128)S(1)} %collective-permute-done.6.aux_ref, bf16[1040,128]{1,0:T(8,128)(2,1)S(1)} %collective-permute-done.4.refs_0_, bf16[1040,128]{1,0:T(8,128)(2,1)S(1)} %collective-permute-done.8.refs_1_, ...), custom_call_target="tpu_custom_call" | custom-call | flops 402653184 | bytes 2097152 | tf_op jit(solution)/shard_map/absorb/pallas_call | solution.py:249
  30.2 1.1 %absorb.13.mine_ref = f32[8,768]{1,0:T(8,128)S(1)} custom-call(bf16[768,1024]{1,0:T(8,128)(2,1)S(1)} %get-tuple-element.12.observed_ref, f32[10,768]{1,0:T(8,128)S(1)} %get-tuple-element.13.aux_ref, bf16[1040,128]{1,0:T(8,128)(2,1)S(1)} %collective-permute-done.4.refs_0_, bf16[1040,128]{1,0:T(8,128)(2,1)S(1)} %collective-permute-done.8.refs_1_, ...), custom_call_target="tpu_custom_call" | custom-call | flops 402653184 | bytes 2097152 | tf_op jit(solution)/shard_map/absorb/pallas_call | solution.py:249
  31.4 0.6 %finish.1 = (f32[4,768]{1,0:T(4,128)}, f32[768]{0:T(1024)}) custom-call(f32[8,768]{1,0:T(8,128)S(1)} %absorb.13.mine_ref, f32[8,768]{1,0:T(8,128)S(1)} %collective-permute-done.9.other_ref, f32[10,768]{1,0:T(8,128)S(1)} %get-tuple-element.13.aux_ref), custom_call_target="tpu_custom_call" | custom-call | tf_op jit(solution)/shard_map/finish/pallas_call | solution.py:284
  (7 shorter events, 0.2 us)
Async XLA Ops:
  0.6 14.0 %collective-permute-start.5 = (bf16[768,1024]{1,0:T(8,128)(2,1)}, bf16[768,1024]{1,0:T(8,128)(2,1)S(1)}, u32[]{:S(2)}, u32[]{:S(2)}) collective-permute-start(bf16[768,1024]{1,0:T(8,128)(2,1)} %observed_hbm.1), channel_id=1, source_target_pairs={{0,1},{1,0},{2,3},{3,2},{4,5},{5,4},{6,7},{7,6},{8,9},{9,8},{10,11... | collective-permute-start | bytes 4718600 | tf_op jit(solution)/shard_map/ppermute | solution.py:241
  2.1 6.9 %collective-permute-start.1 = (bf16[1040,128]{1,0:T(8,128)(2,1)S(1)}, bf16[1040,128]{1,0:T(8,128)(2,1)S(1)}, u32[]{:S(2)}, u32[]{:S(2)}) collective-permute-start(bf16[1040,128]{1,0:T(8,128)(2,1)S(1)} %pack.1.refs_0_), channel_id=1, source_target_pairs={{0,5},{1,2},{2,1},{3,6},{4,9},{5,0},{6,3},{7,10},{8,13},{9,4},{10,... | collective-permute-start | bytes 798728 | tf_op jit(solution)/shard_map/ppermute | solution.py:218
  7.3 5.9 %collective-permute-start = (bf16[1040,128]{1,0:T(8,128)(2,1)S(1)}, bf16[1040,128]{1,0:T(8,128)(2,1)S(1)}, u32[]{:S(2)}, u32[]{:S(2)}) collective-permute-start(bf16[1040,128]{1,0:T(8,128)(2,1)S(1)} %pack.1.refs_0_), channel_id=1, source_target_pairs={{0,3},{1,4},{2,7},{3,0},{4,1},{5,8},{6,11},{7,2},{8,5},{9,12},{10,... | collective-permute-start | bytes 798728 | tf_op jit(solution)/shard_map/ppermute | solution.py:218
  9.0 7.1 %collective-permute-start.3 = (bf16[1040,128]{1,0:T(8,128)(2,1)S(1)}, bf16[1040,128]{1,0:T(8,128)(2,1)S(1)}, u32[]{:S(2)}, u32[]{:S(2)}) collective-permute-start(bf16[1040,128]{1,0:T(8,128)(2,1)S(1)} %collective-permute-done.1.refs_1_), channel_id=1, source_target_pairs={{0,3},{1,4},{2,7},{3,0},{4,1},{5,8},{6,11},{7,2},{8,5},{9,12},{10,... | collective-permute-start | bytes 798728 | tf_op jit(solution)/shard_map/ppermute | solution.py:218
  10.7 4.0 %collective-permute-start.6 = (f32[10,768]{1,0:T(8,128)S(1)}, f32[10,768]{1,0:T(8,128)S(1)}, u32[]{:S(2)}, u32[]{:S(2)}) collective-permute-start(f32[10,768]{1,0:T(8,128)S(1)} %get-tuple-element.17), channel_id=1, source_target_pairs={{0,1},{1,0},{2,3},{3,2},{4,5},{5,4},{6,7},{7,6},{8,9},{9,8},{10,11... | collective-permute-start | bytes 92168 | tf_op jit(solution)/shard_map/ppermute | solution.py:242
  13.2 5.8 %collective-permute-start.2 = (bf16[1040,128]{1,0:T(8,128)(2,1)S(1)}, bf16[1040,128]{1,0:T(8,128)(2,1)S(1)}, u32[]{:S(2)}, u32[]{:S(2)}) collective-permute-start(bf16[1040,128]{1,0:T(8,128)(2,1)S(1)} %collective-permute-done.refs_0_), channel_id=1, source_target_pairs={{0,5},{1,2},{2,1},{3,6},{4,9},{5,0},{6,3},{7,10},{8,13},{9,4},{10,... | collective-permute-start | bytes 798728 | tf_op jit(solution)/shard_map/ppermute | solution.py:218
  16.1 5.8 %collective-permute-start.7 = (bf16[1040,128]{1,0:T(8,128)(2,1)S(1)}, bf16[1040,128]{1,0:T(8,128)(2,1)S(1)}, u32[]{:S(2)}, u32[]{:S(2)}) collective-permute-start(bf16[1040,128]{1,0:T(8,128)(2,1)S(1)} %collective-permute-done.3.refs_1_), channel_id=1, source_target_pairs={{0,5},{1,2},{2,1},{3,6},{4,9},{5,0},{6,3},{7,10},{8,13},{9,4},{10,... | collective-permute-start | bytes 798728 | tf_op jit(solution)/shard_map/ppermute | solution.py:218
  19.1 8.1 %collective-permute-start.4 = (bf16[1040,128]{1,0:T(8,128)(2,1)S(1)}, bf16[1040,128]{1,0:T(8,128)(2,1)S(1)}, u32[]{:S(2)}, u32[]{:S(2)}) collective-permute-start(bf16[1040,128]{1,0:T(8,128)(2,1)S(1)} %collective-permute-done.2.refs_0_), channel_id=1, source_target_pairs={{0,3},{1,4},{2,7},{3,0},{4,1},{5,8},{6,11},{7,2},{8,5},{9,12},{10,... | collective-permute-start | bytes 798728 | tf_op jit(solution)/shard_map/ppermute | solution.py:218
  21.9 7.1 %collective-permute-start.8 = (bf16[1040,128]{1,0:T(8,128)(2,1)S(1)}, bf16[1040,128]{1,0:T(8,128)(2,1)S(1)}, u32[]{:S(2)}, u32[]{:S(2)}) collective-permute-start(bf16[1040,128]{1,0:T(8,128)(2,1)S(1)} %collective-permute-done.7.refs_1_), channel_id=1, source_target_pairs={{0,3},{1,4},{2,7},{3,0},{4,1},{5,8},{6,11},{7,2},{8,5},{9,12},{10,... | collective-permute-start | bytes 798728 | tf_op jit(solution)/shard_map/ppermute | solution.py:218
  30.2 1.2 %collective-permute-start.9 = (f32[8,768]{1,0:T(8,128)S(1)}, f32[8,768]{1,0:T(8,128)S(1)}, u32[]{:S(2)}, u32[]{:S(2)}) collective-permute-start(f32[8,768]{1,0:T(8,128)S(1)} %absorb.15), channel_id=1, source_target_pairs={{0,1},{1,0},{2,3},{3,2},{4,5},{5,4},{6,7},{7,6},{8,9},{9,8},{10,11... | collective-permute-start | bytes 73736 | tf_op jit(solution)/shard_map/ppermute | solution.py:281

commit v6 on v5

--- a/solution.py
+++ b/solution.py
@@ -54,7 +54,7 @@
     return values.reshape(1, values.shape[-1])
 
 
-def pack_kernel(params_hbm, class_hbm, evolved_hbm, packet_ref, params_ref, class_ref, arrived):
+def pack_kernel(params_hbm, class_hbm, evolved_hbm, packet_ref, meta_ref, params_ref, class_ref, arrived):
     rows, size = evolved_hbm.shape
     panels = size // LANES
     copies = [
@@ -72,9 +72,19 @@
     params = params_ref[...].astype(jnp.float32)
     classes = row(class_ref[...]).astype(jnp.float32)
     rest = jnp.broadcast_to(classes, (META_ROWS - params.shape[0], classes.shape[1]))
-    packet_ref[panels * rows :, :] = jnp.concatenate([params, rest], axis=0).astype(packet_ref.dtype)
+    meta = jnp.concatenate([params, rest], axis=0).astype(packet_ref.dtype)
+    packet_ref[panels * rows :, :] = meta
+    meta_ref[...] = meta
     for copy in copies[2:]:
         copy.wait()
+
+
+def join_kernel(block_ref, meta_ref, packet_ref):
+    rows, size = block_ref.shape
+    panels = size // LANES
+    for i in range(panels):
+        packet_ref[i * rows : (i + 1) * rows, :] = block_ref[:, i * LANES : (i + 1) * LANES]
+    packet_ref[panels * rows :, :] = meta_ref[...]
 
 
 def norms(observed):
@@ -184,6 +194,10 @@
     return [pltpu.with_memory_space_constraint(array, pltpu.HBM) for array in arrays]
 
 
+def cost(microseconds):
+    return pl.CostEstimate(flops=int(microseconds * 1.15e9), bytes_accessed=0, transcendentals=0)
+
+
 def on_device(pairs, block_of, observed, sharpness, obs_class, pattern, evolved, sim_params, sim_class):
     rows, size = observed.shape
     count = evolved.shape[0]
@@ -197,28 +211,25 @@
     core = [(i, i ^ 1) for i in range(devices)]
     at = lax.axis_index("blk").astype(jnp.int32).reshape(1)
 
-    packet = pl.pallas_call(
+    first = lax.ppermute(evolved, "blk", pairs[0])
+    packet, meta = pl.pallas_call(
         pack_kernel,
-        out_shape=jax.ShapeDtypeStruct((count * size // LANES + META_ROWS, LANES), evolved.dtype),
+        out_shape=(
+            jax.ShapeDtypeStruct((count * size // LANES + META_ROWS, LANES), evolved.dtype),
+            jax.ShapeDtypeStruct((META_ROWS, LANES), evolved.dtype),
+        ),
         in_specs=[hbm] * 3,
-        out_specs=vmem,
+        out_specs=(vmem,) * 2,
         scratch_shapes=[
             pltpu.VMEM(sim_params.shape, sim_params.dtype),
             pltpu.VMEM(sim_class.shape, sim_class.dtype),
             pltpu.SemaphoreType.DMA((size // LANES + 2,)),
         ],
         compiler_params=compiler_params,
+        cost_estimate=cost(0.05),
         name="pack",
     )(*in_hbm(sim_params, sim_class, evolved))
-    packets = [packet]
-    moving = [packet, packet]
-
-    def send(step):
-        kind = step % 2
-        moving[kind] = lax.ppermute(moving[kind], "blk", pairs[(kind + step // 2) % 2])
-        packets.append(moving[kind])
-
-    send(0)
+    first_meta = lax.ppermute(meta, "blk", pairs[0])
     own_aux, sib_aux, observed_own = pl.pallas_call(
         functools.partial(prepare_kernel, block_of),
         out_shape=(
@@ -235,12 +246,29 @@
             pltpu.SemaphoreType.DMA((4,)),
         ],
         compiler_params=compiler_params,
-        cost_estimate=pl.CostEstimate(flops=8 * rows * size, bytes_accessed=4 * rows * size, transcendentals=0),
+        cost_estimate=cost(0.05),
         name="prepare",
     )(after(at, packet), *in_hbm(pattern, obs_class, sharpness, observed))
     observed_sib = lax.ppermute(observed, "blk", core)
     sib_aux = lax.ppermute(sib_aux, "blk", core)
-    moving[1] = after(moving[1], own_aux)
+    packets = [packet]
+    moving = [None, after(packet, first_meta, own_aux)]
+
+    def send(step):
+        kind = step % 2
+        moving[kind] = lax.ppermute(moving[kind], "blk", pairs[(kind + step // 2) % 2])
+        packets.append(moving[kind])
+
+    moving[0] = pl.pallas_call(
+        join_kernel,
+        out_shape=jax.ShapeDtypeStruct(packet.shape, packet.dtype),
+        in_specs=[vmem] * 2,
+        out_specs=vmem,
+        compiler_params=compiler_params,
+        cost_estimate=cost(0.1),
+        name="join",
+    )(first, first_meta)
+    packets.append(moving[0])
     send(1)
 
     def absorb(work, half, state):
@@ -252,35 +280,34 @@
             in_specs=[vmem] * (2 + len(work) + len(before)),
             out_specs=vmem,
             compiler_params=compiler_params,
-            cost_estimate=pl.CostEstimate(
-                flops=2 * len(work) * rows * count * size,
-                bytes_accessed=2 * (rows + len(work) * count) * size,
-                transcendentals=len(work) * rows * count,
-            ),
+            cost_estimate=cost(0.1),
             name="absorb",
         )(observed_half, aux, *(packets[i] for i in work), *before)
 
+    works = [[] for _ in range(steps)]
+    waiting = ()
+    for block in range(1, steps - 2, 2):
+        works[block - 1] += [(waiting, 1)] if waiting else []
+        works[block - 1].append(((block - 1, block), 0))
+        waiting = (block - 1, block)
+    works[steps - 3] += [((*waiting, steps - 2), 1), ((steps - 2,), 0)]
+    works[steps - 2] += [((steps - 1,), 1), ((steps - 1,), 0)]
     states = [None, None]
-    works = []
-    for first in range(0, steps, 2):
-        work = tuple(range(first, min(first + 2, steps)))
-        works += [(work, half) for half in ((0, 1) if first + 2 < steps else (1, 0))]
     done = []
     for step in range(steps - 1):
         ahead = step + 2
         if ahead < steps - 1:
             if done:
-                moving[ahead % 2] = after(moving[ahead % 2], done[-1])
+                moving[ahead % 2] = after(moving[ahead % 2], *done[-2:])
             send(ahead)
-        if step < len(works):
-            work, half = works[step]
+        last = step == steps - 2
+        if last:
+            packets[-1] = after(packets[-1], states[0], states[1])
+        for work, half in works[step]:
             states[half] = absorb(work, half, states[half])
             done.append(states[half])
-    for work, half in works[steps - 1 : -1]:
-        states[half] = absorb(work, half, states[half])
-    other = lax.ppermute(states[1], "blk", core)
-    work, half = works[-1]
-    states[half] = absorb(work, half, states[half])
+            if last and half == 1:
+                other = lax.ppermute(states[1], "blk", core)
     mean, evidence = pl.pallas_call(
         functools.partial(finish_kernel, size),
         out_shape=(jax.ShapeDtypeStruct((sim_params.shape[0], rows), f32), jax.ShapeDtypeStruct((rows,), f32)),

time: 32.2 us -> 33.1 us (1.028)
  waiting for transfers between devices: 4.96 us -> 6.13 us
  starting transfers between devices: 13.7 us -> 12.6 us
  Pallas kernels: 12.7 us -> 13.5 us
    ppermute x7 -> x6, starting transfers between devices: 13.1 us -> 9.09 us  [send(): lax.ppermute(moving[kind], 'blk', pairs[(kind + step // 2) % 2])]
    ppermute x0 -> x2, starting transfers between devices: none -> 2.76 us  [the longest x1 2.69 us: on_device(): first = lax.ppermute(evolved, 'blk', pairs[0])]
    ppermute x0 -> x2, waiting for transfers between devices: none -> 0.79 us  [the longest x1 0.79 us: on_device(): first_meta = lax.ppermute(meta, 'blk', pairs[0])]
    pallas_call x8 -> x9, Pallas kernels: 8.6 us -> 9.39 us  [absorb(): pl.pallas_call(functools.partial(absorb_kernel, work, count, state is Non...]
    ppermute x7 -> x6, waiting for transfers between devices: 4.91 us -> 5.13 us  [send(): lax.ppermute(moving[kind], 'blk', pairs[(kind + step // 2) % 2])]
    pallas_call x1 -> x2, Pallas kernels: 0.99 us -> 1.04 us  [the longest x1 0.99 us: on_device(): pl.pallas_call(pack_kernel, out_shape=(jax.ShapeDtypeStruct((count * size...]
  transfers between devices with their start and end apart: 10 -> 11, of which waited for: 6 -> 6; matrix products, arithmetic and copies ran while one was open for 0% -> 0% of each run, Pallas kernels for 34% -> 36%
where the time goes in v6:
time: 33.1 us; the launch traced here: 32.9 us
  Pallas kernels  13.5 us (41%)
  starting transfers between devices  12.6 us (38%)
  waiting for transfers between devices  6.13 us (19%)
  between operations  0.68 us (2%)
    pallas_call x9, Pallas kernels, absorb(): pl.pallas_call(functools.partial(absorb_kernel, work, count, state is Non...  9.39 us
    ppermute x6, starting transfers between devices, send(): lax.ppermute(moving[kind], 'blk', pairs[(kind + step // 2) % 2])  9.09 us
    ppermute x6, waiting for transfers between devices, send(): lax.ppermute(moving[kind], 'blk', pairs[(kind + step // 2) % 2])  5.13 us
    ppermute x1, starting transfers between devices, on_device(): first = lax.ppermute(evolved, 'blk', pairs[0])  2.69 us
    pallas_call x1, Pallas kernels, on_device(): pl.pallas_call(functools.partial(prepare_kernel, block_of), out_shape=(ja...  2.43 us
    pallas_call x1, Pallas kernels, on_device(): pl.pallas_call(pack_kernel, out_shape=(jax.ShapeDtypeStruct((count * size...  0.99 us
    ppermute x1, waiting for transfers between devices, on_device(): first_meta = lax.ppermute(meta, 'blk', pairs[0])  0.79 us
  transfers between devices with their start and end apart: 11, of which 6 were waited for; matrix products, arithmetic and copies ran while one was open for 0% of the time, Pallas kernels for 36%

profile of v6, /device:TPU:0, one launch (start us, length us, event | category | flops | bytes accessed | tf_op | source)
XLA Modules:
  0.0 32.9 jit_solution(3519036260347095166)
XLA Ops:
  0.6 0.5 %collective-permute-start.4 = (bf16[768,1024]{1,0:T(8,128)(2,1)}, bf16[768,1024]{1,0:T(8,128)(2,1)S(1)}, u32[]{:S(2)}, u32[]{:S(2)}) collective-permute-start(bf16[768,1024]{1,0:T(8,128)(2,1)} %observed_hbm.1), channel_id=1, source_target_pairs={{0,1},{1,0},{2,3},{3,2},{4,5},{5,4},{6,7},{7,6},{8,9},{9,8},{10,11... | collective-permute-start | bytes 4718600 | tf_op jit(solution)/shard_map/ppermute | solution.py:252
  1.1 2.7 %collective-permute-start = (bf16[128,1024]{1,0:T(8,128)(2,1)}, bf16[128,1024]{1,0:T(8,128)(2,1)S(1)}, u32[]{:S(2)}, u32[]{:S(2)}) collective-permute-start(bf16[128,1024]{1,0:T(8,128)(2,1)} %evolved_hbm.1), channel_id=1, source_target_pairs={{0,5},{1,2},{2,1},{3,6},{4,9},{5,0},{6,3},{7,10},{8,13},{9,4},{10,... | collective-permute-start | bytes 786440 | tf_op jit(solution)/shard_map/ppermute | solution.py:214
  3.8 1.0 %pack.1 = (bf16[1040,128]{1,0:T(8,128)(2,1)S(1)}, bf16[16,128]{1,0:T(8,128)(2,1)S(1)}) custom-call(bf16[4,128]{1,0:T(4,128)(2,1)} %params_hbm.1, s32[128]{0:T(128)} %class_hbm.2, bf16[128,1024]{1,0:T(8,128)(2,1)} %evolved_hbm.1), custom_call_target="tpu_custom_call" | custom-call | flops 57500000 | tf_op jit(solution)/shard_map/pack/pallas_call | solution.py:215
  4.9 2.4 %prepare.1 = (f32[10,768]{1,0:T(8,128)S(1)}, f32[10,768]{1,0:T(8,128)S(1)}, bf16[768,1024]{1,0:T(8,128)(2,1)S(1)}) custom-call(s32[1]{0:T(128)} %bitcast.at_ref, s32[6,16]{1,0:T(8,128)} %pattern_hbm.1, s32[768]{0:T(1024)} %class_hbm.3, f32[768]{0:T(1024)} %sharp_hbm.1, bf16[768,1024]{1,0:T(8,128)(2,1)} %observed_hbm.1), custom_call_target="tpu_custom_call" | custom-call | flops 57500000 | tf_op jit(solution)/shard_map/prepare/pallas_call | solution.py:233
  7.4 0.8 %collective-permute-done.1.meta_ref = bf16[16,128]{1,0:T(8,128)(2,1)S(1)} collective-permute-done((bf16[16,128]{1,0:T(8,128)(2,1)S(1)}, bf16[16,128]{1,0:T(8,128)(2,1)S(1)}, u32[]{:S(2)}, u32[]{:S(2)}) %collective-permute-start.1) | collective-permute-done | bytes 4128 | tf_op jit(solution)/shard_map/ppermute | solution.py:232
  8.1 1.7 %collective-permute-start.6 = (bf16[1040,128]{1,0:T(8,128)(2,1)S(1)}, bf16[1040,128]{1,0:T(8,128)(2,1)S(1)}, u32[]{:S(2)}, u32[]{:S(2)}) collective-permute-start(bf16[1040,128]{1,0:T(8,128)(2,1)S(1)} %get-tuple-element.21.refs_0_), channel_id=1, source_target_pairs={{0,3},{1,4},{2,7},{3,0},{4,1},{5,8},{6,11},{7,2},{8,5},{9,12},{10,... | collective-permute-start | bytes 798728 | tf_op jit(solution)/shard_map/ppermute | solution.py:259
  10.0 1.0 %absorb.9.refs_2_ = f32[8,768]{1,0:T(8,128)S(1)} custom-call(bf16[768,1024]{1,0:T(8,128)(2,1)S(1)} %get-tuple-element.16.observed_ref, f32[10,768]{1,0:T(8,128)S(1)} %get-tuple-element.17.aux_ref, bf16[1040,128]{1,0:T(8,128)(2,1)S(1)} %get-tuple-element.21.refs_0_, bf16[1040,128]{1,0:T(8,128)(2,1)S(1)} %join.1.refs_1_), custom_call_target="tpu_custom_call" | custom-call | flops 115000000 | tf_op jit(solution)/shard_map/absorb/pallas_call | solution.py:277
  11.0 3.0 %collective-permute-done.6.refs_0_ = bf16[1040,128]{1,0:T(8,128)(2,1)S(1)} collective-permute-done((bf16[1040,128]{1,0:T(8,128)(2,1)S(1)}, bf16[1040,128]{1,0:T(8,128)(2,1)S(1)}, u32[]{:S(2)}, u32[]{:S(2)}) %collective-permute-start.6) | collective-permute-done | bytes 266272 | tf_op jit(solution)/shard_map/ppermute | solution.py:259
  14.0 2.0 %collective-permute-start.8 = (bf16[1040,128]{1,0:T(8,128)(2,1)S(1)}, bf16[1040,128]{1,0:T(8,128)(2,1)S(1)}, u32[]{:S(2)}, u32[]{:S(2)}) collective-permute-start(bf16[1040,128]{1,0:T(8,128)(2,1)S(1)} %collective-permute-done.6.refs_0_), channel_id=1, source_target_pairs={{0,5},{1,2},{2,1},{3,6},{4,9},{5,0},{6,3},{7,10},{8,13},{9,4},{10,... | collective-permute-start | bytes 798728 | tf_op jit(solution)/shard_map/ppermute | solution.py:259
  16.0 1.0 %collective-permute-done.2.refs_1_ = bf16[1040,128]{1,0:T(8,128)(2,1)S(1)} collective-permute-done((bf16[1040,128]{1,0:T(8,128)(2,1)S(1)}, bf16[1040,128]{1,0:T(8,128)(2,1)S(1)}, u32[]{:S(2)}, u32[]{:S(2)}) %collective-permute-start.2) | collective-permute-done | bytes 266272 | tf_op jit(solution)/shard_map/ppermute | solution.py:259
  17.0 2.1 %collective-permute-start.3 = (bf16[1040,128]{1,0:T(8,128)(2,1)S(1)}, bf16[1040,128]{1,0:T(8,128)(2,1)S(1)}, u32[]{:S(2)}, u32[]{:S(2)}) collective-permute-start(bf16[1040,128]{1,0:T(8,128)(2,1)S(1)} %collective-permute-done.2.refs_1_), channel_id=1, source_target_pairs={{0,5},{1,2},{2,1},{3,6},{4,9},{5,0},{6,3},{7,10},{8,13},{9,4},{10,... | collective-permute-start | bytes 798728 | tf_op jit(solution)/shard_map/ppermute | solution.py:259
  19.1 1.1 %absorb.11.refs_2_ = f32[8,768]{1,0:T(8,128)S(1)} custom-call(bf16[768,1024]{1,0:T(8,128)(2,1)S(1)} %get-tuple-element.16.observed_ref, f32[10,768]{1,0:T(8,128)S(1)} %get-tuple-element.17.aux_ref, bf16[1040,128]{1,0:T(8,128)(2,1)S(1)} %collective-permute-done.6.refs_0_, bf16[1040,128]{1,0:T(8,128)(2,1)S(1)} %collective-permute-done.2.refs_1_, ...), custom_call_target="tpu_custom_call" | custom-call | flops 115000000 | tf_op jit(solution)/shard_map/absorb/pallas_call | solution.py:277
  20.4 0.9 %absorb.10.refs_2_ = f32[8,768]{1,0:T(8,128)S(1)} custom-call(bf16[768,1024]{1,0:T(8,128)(2,1)S(1)} %collective-permute-done.4.observed_ref, f32[10,768]{1,0:T(8,128)S(1)} %collective-permute-done.5.aux_ref, bf16[1040,128]{1,0:T(8,128)(2,1)S(1)} %get-tuple-element.21.refs_0_, bf16[1040,128]{1,0:T(8,128)(2,1)S(1)} %join.1.refs_1_), custom_call_target="tpu_custom_call" | custom-call | flops 115000000 | tf_op jit(solution)/shard_map/absorb/pallas_call | solution.py:277
  21.3 0.8 %collective-permute-start.9 = (bf16[1040,128]{1,0:T(8,128)(2,1)S(1)}, bf16[1040,128]{1,0:T(8,128)(2,1)S(1)}, u32[]{:S(2)}, u32[]{:S(2)}) collective-permute-start(bf16[1040,128]{1,0:T(8,128)(2,1)S(1)} %collective-permute-done.8.refs_0_), channel_id=1, source_target_pairs={{0,3},{1,4},{2,7},{3,0},{4,1},{5,8},{6,11},{7,2},{8,5},{9,12},{10,... | collective-permute-start | bytes 798728 | tf_op jit(solution)/shard_map/ppermute | solution.py:259
  22.1 1.1 %collective-permute-done.3.refs_1_ = bf16[1040,128]{1,0:T(8,128)(2,1)S(1)} collective-permute-done((bf16[1040,128]{1,0:T(8,128)(2,1)S(1)}, bf16[1040,128]{1,0:T(8,128)(2,1)S(1)}, u32[]{:S(2)}, u32[]{:S(2)}) %collective-permute-start.3) | collective-permute-done | bytes 266272 | tf_op jit(solution)/shard_map/ppermute | solution.py:259
  23.2 2.3 %collective-permute-start.7 = (bf16[1040,128]{1,0:T(8,128)(2,1)S(1)}, bf16[1040,128]{1,0:T(8,128)(2,1)S(1)}, u32[]{:S(2)}, u32[]{:S(2)}) collective-permute-start(bf16[1040,128]{1,0:T(8,128)(2,1)S(1)} %collective-permute-done.3.refs_1_), channel_id=1, source_target_pairs={{0,3},{1,4},{2,7},{3,0},{4,1},{5,8},{6,11},{7,2},{8,5},{9,12},{10,... | collective-permute-start | bytes 798728 | tf_op jit(solution)/shard_map/ppermute | solution.py:259
  25.6 1.1 %absorb.12.refs_1_ = f32[8,768]{1,0:T(8,128)S(1)} custom-call(bf16[768,1024]{1,0:T(8,128)(2,1)S(1)} %get-tuple-element.16.observed_ref, f32[10,768]{1,0:T(8,128)S(1)} %get-tuple-element.17.aux_ref, bf16[1040,128]{1,0:T(8,128)(2,1)S(1)} %collective-permute-done.8.refs_0_, bf16[1040,128]{1,0:T(8,128)(2,1)S(1)} %collective-permute-done.3.refs_1_, ...), custom_call_target="tpu_custom_call" | custom-call | flops 115000000 | tf_op jit(solution)/shard_map/absorb/pallas_call | solution.py:277
  26.7 1.1 %absorb.14.refs_3_ = f32[8,768]{1,0:T(8,128)S(1)} custom-call(bf16[768,1024]{1,0:T(8,128)(2,1)S(1)} %collective-permute-done.4.observed_ref, f32[10,768]{1,0:T(8,128)S(1)} %collective-permute-done.5.aux_ref, bf16[1040,128]{1,0:T(8,128)(2,1)S(1)} %collective-permute-done.6.refs_0_, bf16[1040,128]{1,0:T(8,128)(2,1)S(1)} %collective-permute-done.2.refs_1_, ...), custom_call_target="tpu_custom_call" | custom-call | flops 115000000 | tf_op jit(solution)/shard_map/absorb/pallas_call | solution.py:277
  27.8 1.4 %absorb.15.refs_1_ = f32[8,768]{1,0:T(8,128)S(1)} custom-call(bf16[768,1024]{1,0:T(8,128)(2,1)S(1)} %collective-permute-done.4.observed_ref, f32[10,768]{1,0:T(8,128)S(1)} %collective-permute-done.5.aux_ref, bf16[1040,128]{1,0:T(8,128)(2,1)S(1)} %collective-permute-done.8.refs_0_, bf16[1040,128]{1,0:T(8,128)(2,1)S(1)} %collective-permute-done.3.refs_1_, ...), custom_call_target="tpu_custom_call" | custom-call | flops 115000000 | tf_op jit(solution)/shard_map/absorb/pallas_call | solution.py:277
  29.2 0.9 %absorb.13.refs_1_ = f32[8,768]{1,0:T(8,128)S(1)} custom-call(bf16[768,1024]{1,0:T(8,128)(2,1)S(1)} %get-tuple-element.16.observed_ref, f32[10,768]{1,0:T(8,128)S(1)} %get-tuple-element.17.aux_ref, bf16[1040,128]{1,0:T(8,128)(2,1)S(1)} %collective-permute-done.9.refs_0_.refs_2_, f32[8,768]{1,0:T(8,128)S(1)} %absorb.12.refs_1_), custom_call_target="tpu_custom_call" | custom-call | flops 115000000 | tf_op jit(solution)/shard_map/absorb/pallas_call | solution.py:277
  30.2 0.9 %absorb.17 = f32[8,768]{1,0:T(8,128)S(1)} custom-call(bf16[768,1024]{1,0:T(8,128)(2,1)S(1)} %collective-permute-done.4.observed_ref, f32[10,768]{1,0:T(8,128)S(1)} %collective-permute-done.5.aux_ref, bf16[1040,128]{1,0:T(8,128)(2,1)S(1)} %collective-permute-done.7.refs_0_, f32[8,768]{1,0:T(8,128)S(1)} %absorb.15.refs_1_), custom_call_target="tpu_custom_call" | custom-call | flops 115000000 | tf_op jit(solution)/shard_map/absorb/pallas_call | solution.py:277
  31.1 0.2 collective-permute-start.10
  31.3 0.9 %absorb.16.mine_ref = f32[8,768]{1,0:T(8,128)S(1)} custom-call(bf16[768,1024]{1,0:T(8,128)(2,1)S(1)} %get-tuple-element.16.observed_ref, f32[10,768]{1,0:T(8,128)S(1)} %get-tuple-element.17.aux_ref, bf16[1040,128]{1,0:T(8,128)(2,1)S(1)} %collective-permute-done.7.refs_0_, f32[8,768]{1,0:T(8,128)S(1)} %absorb.13.refs_1_), custom_call_target="tpu_custom_call" | custom-call | flops 115000000 | tf_op jit(solution)/shard_map/absorb/pallas_call | solution.py:277
  32.3 0.6 %finish.1 = (f32[4,768]{1,0:T(4,128)}, f32[768]{0:T(1024)}) custom-call(f32[8,768]{1,0:T(8,128)S(1)} %absorb.16.mine_ref, f32[8,768]{1,0:T(8,128)S(1)} %collective-permute-done.10.other_ref, f32[10,768]{1,0:T(8,128)S(1)} %get-tuple-element.17.aux_ref), custom_call_target="tpu_custom_call" | custom-call | tf_op jit(solution)/shard_map/finish/pallas_call | solution.py:311
  (11 shorter events, 0.5 us)
Async XLA Ops:
  0.6 19.7 %collective-permute-start.4 = (bf16[768,1024]{1,0:T(8,128)(2,1)}, bf16[768,1024]{1,0:T(8,128)(2,1)S(1)}, u32[]{:S(2)}, u32[]{:S(2)}) collective-permute-start(bf16[768,1024]{1,0:T(8,128)(2,1)} %observed_hbm.1), channel_id=1, source_target_pairs={{0,1},{1,0},{2,3},{3,2},{4,5},{5,4},{6,7},{7,6},{8,9},{9,8},{10,11... | collective-permute-start | bytes 4718600 | tf_op jit(solution)/shard_map/ppermute | solution.py:252
  1.1 8.7 %collective-permute-start = (bf16[128,1024]{1,0:T(8,128)(2,1)}, bf16[128,1024]{1,0:T(8,128)(2,1)S(1)}, u32[]{:S(2)}, u32[]{:S(2)}) collective-permute-start(bf16[128,1024]{1,0:T(8,128)(2,1)} %evolved_hbm.1), channel_id=1, source_target_pairs={{0,5},{1,2},{2,1},{3,6},{4,9},{5,0},{6,3},{7,10},{8,13},{9,4},{10,... | collective-permute-start | bytes 786440 | tf_op jit(solution)/shard_map/ppermute | solution.py:214
  4.8 3.3 %collective-permute-start.1 = (bf16[16,128]{1,0:T(8,128)(2,1)S(1)}, bf16[16,128]{1,0:T(8,128)(2,1)S(1)}, u32[]{:S(2)}, u32[]{:S(2)}) collective-permute-start(bf16[16,128]{1,0:T(8,128)(2,1)S(1)} %get-tuple-element.18), channel_id=1, source_target_pairs={{0,5},{1,2},{2,1},{3,6},{4,9},{5,0},{6,3},{7,10},{8,13},{9,4},{10,... | collective-permute-start | bytes 12296 | tf_op jit(solution)/shard_map/ppermute | solution.py:232
  8.1 5.8 %collective-permute-start.6 = (bf16[1040,128]{1,0:T(8,128)(2,1)S(1)}, bf16[1040,128]{1,0:T(8,128)(2,1)S(1)}, u32[]{:S(2)}, u32[]{:S(2)}) collective-permute-start(bf16[1040,128]{1,0:T(8,128)(2,1)S(1)} %get-tuple-element.21.refs_0_), channel_id=1, source_target_pairs={{0,3},{1,4},{2,7},{3,0},{4,1},{5,8},{6,11},{7,2},{8,5},{9,12},{10,... | collective-permute-start | bytes 798728 | tf_op jit(solution)/shard_map/ppermute | solution.py:259
  9.9 7.1 %collective-permute-start.2 = (bf16[1040,128]{1,0:T(8,128)(2,1)S(1)}, bf16[1040,128]{1,0:T(8,128)(2,1)S(1)}, u32[]{:S(2)}, u32[]{:S(2)}) collective-permute-start(bf16[1040,128]{1,0:T(8,128)(2,1)S(1)} %join.1.refs_1_), channel_id=1, source_target_pairs={{0,3},{1,4},{2,7},{3,0},{4,1},{5,8},{6,11},{7,2},{8,5},{9,12},{10,... | collective-permute-start | bytes 798728 | tf_op jit(solution)/shard_map/ppermute | solution.py:259
  14.0 7.3 %collective-permute-start.8 = (bf16[1040,128]{1,0:T(8,128)(2,1)S(1)}, bf16[1040,128]{1,0:T(8,128)(2,1)S(1)}, u32[]{:S(2)}, u32[]{:S(2)}) collective-permute-start(bf16[1040,128]{1,0:T(8,128)(2,1)S(1)} %collective-permute-done.6.refs_0_), channel_id=1, source_target_pairs={{0,5},{1,2},{2,1},{3,6},{4,9},{5,0},{6,3},{7,10},{8,13},{9,4},{10,... | collective-permute-start | bytes 798728 | tf_op jit(solution)/shard_map/ppermute | solution.py:259
  17.0 6.2 %collective-permute-start.3 = (bf16[1040,128]{1,0:T(8,128)(2,1)S(1)}, bf16[1040,128]{1,0:T(8,128)(2,1)S(1)}, u32[]{:S(2)}, u32[]{:S(2)}) collective-permute-start(bf16[1040,128]{1,0:T(8,128)(2,1)S(1)} %collective-permute-done.2.refs_1_), channel_id=1, source_target_pairs={{0,5},{1,2},{2,1},{3,6},{4,9},{5,0},{6,3},{7,10},{8,13},{9,4},{10,... | collective-permute-start | bytes 798728 | tf_op jit(solution)/shard_map/ppermute | solution.py:259
  19.1 1.2 %collective-permute-start.5 = (f32[10,768]{1,0:T(8,128)S(1)}, f32[10,768]{1,0:T(8,128)S(1)}, u32[]{:S(2)}, u32[]{:S(2)}) collective-permute-start(f32[10,768]{1,0:T(8,128)S(1)} %get-tuple-element.20), channel_id=1, source_target_pairs={{0,1},{1,0},{2,3},{3,2},{4,5},{5,4},{6,7},{7,6},{8,9},{9,8},{10,11... | collective-permute-start | bytes 92168 | tf_op jit(solution)/shard_map/ppermute | solution.py:253
  21.3 6.5 %collective-permute-start.9 = (bf16[1040,128]{1,0:T(8,128)(2,1)S(1)}, bf16[1040,128]{1,0:T(8,128)(2,1)S(1)}, u32[]{:S(2)}, u32[]{:S(2)}) collective-permute-start(bf16[1040,128]{1,0:T(8,128)(2,1)S(1)} %collective-permute-done.8.refs_0_), channel_id=1, source_target_pairs={{0,3},{1,4},{2,7},{3,0},{4,1},{5,8},{6,11},{7,2},{8,5},{9,12},{10,... | collective-permute-start | bytes 798728 | tf_op jit(solution)/shard_map/ppermute | solution.py:259
  23.2 7.0 %collective-permute-start.7 = (bf16[1040,128]{1,0:T(8,128)(2,1)S(1)}, bf16[1040,128]{1,0:T(8,128)(2,1)S(1)}, u32[]{:S(2)}, u32[]{:S(2)}) collective-permute-start(bf16[1040,128]{1,0:T(8,128)(2,1)S(1)} %collective-permute-done.3.refs_1_), channel_id=1, source_target_pairs={{0,3},{1,4},{2,7},{3,0},{4,1},{5,8},{6,11},{7,2},{8,5},{9,12},{10,... | collective-permute-start | bytes 798728 | tf_op jit(solution)/shard_map/ppermute | solution.py:259
  31.1 1.2 %collective-permute-start.10 = (f32[8,768]{1,0:T(8,128)S(1)}, f32[8,768]{1,0:T(8,128)S(1)}, u32[]{:S(2)}, u32[]{:S(2)}) collective-permute-start(f32[8,768]{1,0:T(8,128)S(1)} %absorb.17), channel_id=1, source_target_pairs={{0,1},{1,0},{2,3},{3,2},{4,5},{5,4},{6,7},{7,6},{8,9},{9,8},{10,11... | collective-permute-start | bytes 73736 | tf_op jit(solution)/shard_map/ppermute | solution.py:310

commit v7 on v5

--- a/solution.py
+++ b/solution.py
@@ -260,11 +260,13 @@
             name="absorb",
         )(observed_half, aux, *(packets[i] for i in work), *before)
 
+    works = [[] for _ in range(steps)]
+    for block in range(1, steps - 2, 2):
+        works[block - 1].append(((block - 1, block), 0))
+        works[block].append(((block - 1, block), 1))
+    works[steps - 3] += [((steps - 2,), 0), ((steps - 2,), 1)]
+    works[steps - 2] += [((steps - 1,), 1), ((steps - 1,), 0)]
     states = [None, None]
-    works = []
-    for first in range(0, steps, 2):
-        work = tuple(range(first, min(first + 2, steps)))
-        works += [(work, half) for half in ((0, 1) if first + 2 < steps else (1, 0))]
     done = []
     for step in range(steps - 1):
         ahead = step + 2
@@ -272,15 +274,14 @@
             if done:
                 moving[ahead % 2] = after(moving[ahead % 2], done[-1])
             send(ahead)
-        if step < len(works):
-            work, half = works[step]
+        last = step == steps - 2
+        if last:
+            packets[-1] = after(packets[-1], states[0], states[1])
+        for work, half in works[step]:
             states[half] = absorb(work, half, states[half])
             done.append(states[half])
-    for work, half in works[steps - 1 : -1]:
-        states[half] = absorb(work, half, states[half])
-    other = lax.ppermute(states[1], "blk", core)
-    work, half = works[-1]
-    states[half] = absorb(work, half, states[half])
+            if last and half == 1:
+                other = lax.ppermute(states[1], "blk", core)
     mean, evidence = pl.pallas_call(
         functools.partial(finish_kernel, size),
         out_shape=(jax.ShapeDtypeStruct((sim_params.shape[0], rows), f32), jax.ShapeDtypeStruct((rows,), f32)),

time: 32.2 us -> 32.3 us (level)
  Pallas kernels: 12.7 us -> 14 us
  starting transfers between devices: 13.7 us -> 13.1 us
  waiting for transfers between devices: 4.96 us -> 4.38 us
    ppermute x7, waiting for transfers between devices: 4.91 us -> 3.14 us  [send(): lax.ppermute(moving[kind], 'blk', pairs[(kind + step // 2) % 2])]
    pallas_call x8 -> x10, Pallas kernels: 8.6 us -> 9.92 us  [absorb(): pl.pallas_call(functools.partial(absorb_kernel, work, count, state is Non...]
    ppermute x1, waiting for transfers between devices: 0.01 us -> 1.23 us  [on_device(): sib_aux = lax.ppermute(sib_aux, 'blk', core)]
    ppermute x7, starting transfers between devices: 13.1 us -> 11.9 us  [send(): lax.ppermute(moving[kind], 'blk', pairs[(kind + step // 2) % 2])]
    ppermute x1, starting transfers between devices: 0.03 us -> 0.63 us  [on_device(): other = lax.ppermute(states[1], 'blk', core)]
  transfers between devices with their start and end apart: 10 -> 10, of which waited for: 6 -> 5; matrix products, arithmetic and copies ran while one was open for 0% -> 0% of each run, Pallas kernels for 34% -> 39%
where the time goes in v7:
time: 32.3 us; the launch traced here: 32.1 us
  Pallas kernels  14 us (43%)
  starting transfers between devices  13.1 us (41%)
  waiting for transfers between devices  4.38 us (14%)
  between operations  0.66 us (2%)
    ppermute x7, starting transfers between devices, send(): lax.ppermute(moving[kind], 'blk', pairs[(kind + step // 2) % 2])  11.9 us
    pallas_call x10, Pallas kernels, absorb(): pl.pallas_call(functools.partial(absorb_kernel, work, count, state is Non...  9.92 us
    ppermute x7, waiting for transfers between devices, send(): lax.ppermute(moving[kind], 'blk', pairs[(kind + step // 2) % 2])  3.14 us
    pallas_call x1, Pallas kernels, on_device(): pl.pallas_call(functools.partial(prepare_kernel, block_of), out_shape=(ja...  2.42 us
    ppermute x1, waiting for transfers between devices, on_device(): sib_aux = lax.ppermute(sib_aux, 'blk', core)  1.23 us
    pallas_call x1, Pallas kernels, on_device(): pl.pallas_call(pack_kernel, out_shape=jax.ShapeDtypeStruct((count * size...  0.99 us
  transfers between devices with their start and end apart: 10, of which 5 were waited for; matrix products, arithmetic and copies ran while one was open for 0% of the time, Pallas kernels for 39%

profile of v7, /device:TPU:0, one launch (start us, length us, event | category | flops | bytes accessed | tf_op | source)
XLA Modules:
  0.0 32.1 jit_solution(10358673590013396608)
XLA Ops:
  1.1 1.0 %pack.1.refs_0_ = bf16[1040,128]{1,0:T(8,128)(2,1)S(1)} custom-call(bf16[4,128]{1,0:T(4,128)(2,1)} %params_hbm.1, s32[128]{0:T(128)} %class_hbm.2, bf16[128,1024]{1,0:T(8,128)(2,1)} %evolved_hbm.1), custom_call_target="tpu_custom_call" | custom-call | tf_op jit(solution)/shard_map/pack/pallas_call | solution.py:200
  2.1 2.8 %collective-permute-start = (bf16[1040,128]{1,0:T(8,128)(2,1)S(1)}, bf16[1040,128]{1,0:T(8,128)(2,1)S(1)}, u32[]{:S(2)}, u32[]{:S(2)}) collective-permute-start(bf16[1040,128]{1,0:T(8,128)(2,1)S(1)} %pack.1.refs_0_), channel_id=1, source_target_pairs={{0,5},{1,2},{2,1},{3,6},{4,9},{5,0},{6,3},{7,10},{8,13},{9,4},{10,... | collective-permute-start | bytes 798728 | tf_op jit(solution)/shard_map/ppermute | solution.py:218
  4.9 2.4 %prepare.1 = (f32[10,768]{1,0:T(8,128)S(1)}, f32[10,768]{1,0:T(8,128)S(1)}, bf16[768,1024]{1,0:T(8,128)(2,1)S(1)}) custom-call(s32[1]{0:T(128)} %bitcast.at_ref, s32[6,16]{1,0:T(8,128)} %pattern_hbm.1, s32[768]{0:T(1024)} %class_hbm.3, f32[768]{0:T(1024)} %sharp_hbm.1, bf16[768,1024]{1,0:T(8,128)(2,1)} %observed_hbm.1), custom_call_target="tpu_custom_call" | custom-call | flops 6291456 | bytes 3145728 | tf_op jit(solution)/shard_map/prepare/pallas_call | solution.py:222
  7.3 1.2 %collective-permute-start.5 = (bf16[1040,128]{1,0:T(8,128)(2,1)S(1)}, bf16[1040,128]{1,0:T(8,128)(2,1)S(1)}, u32[]{:S(2)}, u32[]{:S(2)}) collective-permute-start(bf16[1040,128]{1,0:T(8,128)(2,1)S(1)} %pack.1.refs_0_), channel_id=1, source_target_pairs={{0,3},{1,4},{2,7},{3,0},{4,1},{5,8},{6,11},{7,2},{8,5},{9,12},{10,... | collective-permute-start | bytes 798728 | tf_op jit(solution)/shard_map/ppermute | solution.py:218
  9.0 1.7 %collective-permute-start.1 = (bf16[1040,128]{1,0:T(8,128)(2,1)S(1)}, bf16[1040,128]{1,0:T(8,128)(2,1)S(1)}, u32[]{:S(2)}, u32[]{:S(2)}) collective-permute-start(bf16[1040,128]{1,0:T(8,128)(2,1)S(1)} %collective-permute-done.refs_1_), channel_id=1, source_target_pairs={{0,3},{1,4},{2,7},{3,0},{4,1},{5,8},{6,11},{7,2},{8,5},{9,12},{10,... | collective-permute-start | bytes 798728 | tf_op jit(solution)/shard_map/ppermute | solution.py:218
  10.7 1.0 %absorb.12.refs_2_ = f32[8,768]{1,0:T(8,128)S(1)} custom-call(bf16[768,1024]{1,0:T(8,128)(2,1)S(1)} %get-tuple-element.13.observed_ref, f32[10,768]{1,0:T(8,128)S(1)} %get-tuple-element.14.aux_ref, bf16[1040,128]{1,0:T(8,128)(2,1)S(1)} %pack.1.refs_0_, bf16[1040,128]{1,0:T(8,128)(2,1)S(1)} %collective-permute-done.refs_1_), custom_call_target="tpu_custom_call" | custom-call | flops 402653184 | bytes 2097152 | tf_op jit(solution)/shard_map/absorb/pallas_call | solution.py:249
  11.6 1.6 %collective-permute-done.5.refs_0_ = bf16[1040,128]{1,0:T(8,128)(2,1)S(1)} collective-permute-done((bf16[1040,128]{1,0:T(8,128)(2,1)S(1)}, bf16[1040,128]{1,0:T(8,128)(2,1)S(1)}, u32[]{:S(2)}, u32[]{:S(2)}) %collective-permute-start.5) | collective-permute-done | bytes 266272 | tf_op jit(solution)/shard_map/ppermute | solution.py:218
  13.2 1.4 %collective-permute-start.7 = (bf16[1040,128]{1,0:T(8,128)(2,1)S(1)}, bf16[1040,128]{1,0:T(8,128)(2,1)S(1)}, u32[]{:S(2)}, u32[]{:S(2)}) collective-permute-start(bf16[1040,128]{1,0:T(8,128)(2,1)S(1)} %collective-permute-done.5.refs_0_), channel_id=1, source_target_pairs={{0,5},{1,2},{2,1},{3,6},{4,9},{5,0},{6,3},{7,10},{8,13},{9,4},{10,... | collective-permute-start | bytes 798728 | tf_op jit(solution)/shard_map/ppermute | solution.py:218
  14.7 1.2 %collective-permute-done.3.aux_ref = f32[10,768]{1,0:T(8,128)S(1)} collective-permute-done((f32[10,768]{1,0:T(8,128)S(1)}, f32[10,768]{1,0:T(8,128)S(1)}, u32[]{:S(2)}, u32[]{:S(2)}) %collective-permute-start.3) | collective-permute-done | bytes 30752 | tf_op jit(solution)/shard_map/ppermute | solution.py:242
  15.9 0.9 %absorb.10.refs_2_ = f32[8,768]{1,0:T(8,128)S(1)} custom-call(bf16[768,1024]{1,0:T(8,128)(2,1)S(1)} %collective-permute-done.2.observed_ref, f32[10,768]{1,0:T(8,128)S(1)} %collective-permute-done.3.aux_ref, bf16[1040,128]{1,0:T(8,128)(2,1)S(1)} %pack.1.refs_0_, bf16[1040,128]{1,0:T(8,128)(2,1)S(1)} %collective-permute-done.refs_1_), custom_call_target="tpu_custom_call" | custom-call | flops 402653184 | bytes 2097152 | tf_op jit(solution)/shard_map/absorb/pallas_call | solution.py:249
  16.8 1.3 %collective-permute-start.4 = (bf16[1040,128]{1,0:T(8,128)(2,1)S(1)}, bf16[1040,128]{1,0:T(8,128)(2,1)S(1)}, u32[]{:S(2)}, u32[]{:S(2)}) collective-permute-start(bf16[1040,128]{1,0:T(8,128)(2,1)S(1)} %collective-permute-done.1.refs_1_), channel_id=1, source_target_pairs={{0,5},{1,2},{2,1},{3,6},{4,9},{5,0},{6,3},{7,10},{8,13},{9,4},{10,... | collective-permute-start | bytes 798728 | tf_op jit(solution)/shard_map/ppermute | solution.py:218
  18.1 1.1 %absorb.13.refs_2_ = f32[8,768]{1,0:T(8,128)S(1)} custom-call(bf16[768,1024]{1,0:T(8,128)(2,1)S(1)} %get-tuple-element.13.observed_ref, f32[10,768]{1,0:T(8,128)S(1)} %get-tuple-element.14.aux_ref, bf16[1040,128]{1,0:T(8,128)(2,1)S(1)} %collective-permute-done.5.refs_0_, bf16[1040,128]{1,0:T(8,128)(2,1)S(1)} %collective-permute-done.1.refs_1_, ...), custom_call_target="tpu_custom_call" | custom-call | flops 402653184 | bytes 2097152 | tf_op jit(solution)/shard_map/absorb/pallas_call | solution.py:249
  19.3 1.5 %collective-permute-start.8 = (bf16[1040,128]{1,0:T(8,128)(2,1)S(1)}, bf16[1040,128]{1,0:T(8,128)(2,1)S(1)}, u32[]{:S(2)}, u32[]{:S(2)}) collective-permute-start(bf16[1040,128]{1,0:T(8,128)(2,1)S(1)} %collective-permute-done.7.refs_0_), channel_id=1, source_target_pairs={{0,3},{1,4},{2,7},{3,0},{4,1},{5,8},{6,11},{7,2},{8,5},{9,12},{10,... | collective-permute-start | bytes 798728 | tf_op jit(solution)/shard_map/ppermute | solution.py:218
  20.8 1.1 %absorb.11.refs_2_ = f32[8,768]{1,0:T(8,128)S(1)} custom-call(bf16[768,1024]{1,0:T(8,128)(2,1)S(1)} %collective-permute-done.2.observed_ref, f32[10,768]{1,0:T(8,128)S(1)} %collective-permute-done.3.aux_ref, bf16[1040,128]{1,0:T(8,128)(2,1)S(1)} %collective-permute-done.5.refs_0_, bf16[1040,128]{1,0:T(8,128)(2,1)S(1)} %collective-permute-done.1.refs_1_, ...), custom_call_target="tpu_custom_call" | custom-call | flops 402653184 | bytes 2097152 | tf_op jit(solution)/shard_map/absorb/pallas_call | solution.py:249
  21.9 1.0 %collective-permute-done.4.refs_1_ = bf16[1040,128]{1,0:T(8,128)(2,1)S(1)} collective-permute-done((bf16[1040,128]{1,0:T(8,128)(2,1)S(1)}, bf16[1040,128]{1,0:T(8,128)(2,1)S(1)}, u32[]{:S(2)}, u32[]{:S(2)}) %collective-permute-start.4) | collective-permute-done | bytes 266272 | tf_op jit(solution)/shard_map/ppermute | solution.py:218
  22.9 2.0 %collective-permute-start.6 = (bf16[1040,128]{1,0:T(8,128)(2,1)S(1)}, bf16[1040,128]{1,0:T(8,128)(2,1)S(1)}, u32[]{:S(2)}, u32[]{:S(2)}) collective-permute-start(bf16[1040,128]{1,0:T(8,128)(2,1)S(1)} %collective-permute-done.4.refs_1_), channel_id=1, source_target_pairs={{0,3},{1,4},{2,7},{3,0},{4,1},{5,8},{6,11},{7,2},{8,5},{9,12},{10,... | collective-permute-start | bytes 798728 | tf_op jit(solution)/shard_map/ppermute | solution.py:218
  25.0 1.1 %absorb.16.refs_1_ = f32[8,768]{1,0:T(8,128)S(1)} custom-call(bf16[768,1024]{1,0:T(8,128)(2,1)S(1)} %collective-permute-done.2.observed_ref, f32[10,768]{1,0:T(8,128)S(1)} %collective-permute-done.3.aux_ref, bf16[1040,128]{1,0:T(8,128)(2,1)S(1)} %collective-permute-done.7.refs_0_, bf16[1040,128]{1,0:T(8,128)(2,1)S(1)} %collective-permute-done.4.refs_1_, ...), custom_call_target="tpu_custom_call" | custom-call | flops 402653184 | bytes 2097152 | tf_op jit(solution)/shard_map/absorb/pallas_call | solution.py:249
  26.1 0.9 %absorb.17.refs_1_ = f32[8,768]{1,0:T(8,128)S(1)} custom-call(bf16[768,1024]{1,0:T(8,128)(2,1)S(1)} %collective-permute-done.2.observed_ref, f32[10,768]{1,0:T(8,128)S(1)} %collective-permute-done.3.aux_ref, bf16[1040,128]{1,0:T(8,128)(2,1)S(1)} %collective-permute-done.8.refs_0_, f32[8,768]{1,0:T(8,128)S(1)} %absorb.16.refs_1_), custom_call_target="tpu_custom_call" | custom-call | flops 201326592 | bytes 1835008 | tf_op jit(solution)/shard_map/absorb/pallas_call | solution.py:249
  27.0 1.1 %absorb.14.refs_1_ = f32[8,768]{1,0:T(8,128)S(1)} custom-call(bf16[768,1024]{1,0:T(8,128)(2,1)S(1)} %get-tuple-element.13.observed_ref, f32[10,768]{1,0:T(8,128)S(1)} %get-tuple-element.14.aux_ref, bf16[1040,128]{1,0:T(8,128)(2,1)S(1)} %collective-permute-done.7.refs_0_, bf16[1040,128]{1,0:T(8,128)(2,1)S(1)} %collective-permute-done.4.refs_1_, ...), custom_call_target="tpu_custom_call" | custom-call | flops 402653184 | bytes 2097152 | tf_op jit(solution)/shard_map/absorb/pallas_call | solution.py:249
  28.1 0.9 %absorb.15.refs_1_ = f32[8,768]{1,0:T(8,128)S(1)} custom-call(bf16[768,1024]{1,0:T(8,128)(2,1)S(1)} %get-tuple-element.13.observed_ref, f32[10,768]{1,0:T(8,128)S(1)} %get-tuple-element.14.aux_ref, bf16[1040,128]{1,0:T(8,128)(2,1)S(1)} %collective-permute-done.8.refs_0_, f32[8,768]{1,0:T(8,128)S(1)} %absorb.14.refs_1_), custom_call_target="tpu_custom_call" | custom-call | flops 201326592 | bytes 1835008 | tf_op jit(solution)/shard_map/absorb/pallas_call | solution.py:249
  29.1 0.9 %absorb.19 = f32[8,768]{1,0:T(8,128)S(1)} custom-call(bf16[768,1024]{1,0:T(8,128)(2,1)S(1)} %collective-permute-done.2.observed_ref, f32[10,768]{1,0:T(8,128)S(1)} %collective-permute-done.3.aux_ref, bf16[1040,128]{1,0:T(8,128)(2,1)S(1)} %collective-permute-done.6.refs_0_, f32[8,768]{1,0:T(8,128)S(1)} %absorb.17.refs_1_), custom_call_target="tpu_custom_call" | custom-call | flops 201326592 | bytes 1835008 | tf_op jit(solution)/shard_map/absorb/pallas_call | solution.py:249
  29.9 0.6 %collective-permute-start.9 = (f32[8,768]{1,0:T(8,128)S(1)}, f32[8,768]{1,0:T(8,128)S(1)}, u32[]{:S(2)}, u32[]{:S(2)}) collective-permute-start(f32[8,768]{1,0:T(8,128)S(1)} %absorb.19), channel_id=1, source_target_pairs={{0,1},{1,0},{2,3},{3,2},{4,5},{5,4},{6,7},{7,6},{8,9},{9,8},{10,11... | collective-permute-start | bytes 73736 | tf_op jit(solution)/shard_map/ppermute | solution.py:284
  30.6 0.9 %absorb.18.mine_ref = f32[8,768]{1,0:T(8,128)S(1)} custom-call(bf16[768,1024]{1,0:T(8,128)(2,1)S(1)} %get-tuple-element.13.observed_ref, f32[10,768]{1,0:T(8,128)S(1)} %get-tuple-element.14.aux_ref, bf16[1040,128]{1,0:T(8,128)(2,1)S(1)} %collective-permute-done.6.refs_0_, f32[8,768]{1,0:T(8,128)S(1)} %absorb.15.refs_1_), custom_call_target="tpu_custom_call" | custom-call | flops 201326592 | bytes 1835008 | tf_op jit(solution)/shard_map/absorb/pallas_call | solution.py:249
  31.5 0.6 %finish.1 = (f32[4,768]{1,0:T(4,128)}, f32[768]{0:T(1024)}) custom-call(f32[8,768]{1,0:T(8,128)S(1)} %absorb.18.mine_ref, f32[8,768]{1,0:T(8,128)S(1)} %collective-permute-done.9.other_ref, f32[10,768]{1,0:T(8,128)S(1)} %get-tuple-element.14.aux_ref), custom_call_target="tpu_custom_call" | custom-call | tf_op jit(solution)/shard_map/finish/pallas_call | solution.py:285
  (9 shorter events, 1.1 us)
Async XLA Ops:
  0.6 15.3 %collective-permute-start.2 = (bf16[768,1024]{1,0:T(8,128)(2,1)}, bf16[768,1024]{1,0:T(8,128)(2,1)S(1)}, u32[]{:S(2)}, u32[]{:S(2)}) collective-permute-start(bf16[768,1024]{1,0:T(8,128)(2,1)} %observed_hbm.1), channel_id=1, source_target_pairs={{0,1},{1,0},{2,3},{3,2},{4,5},{5,4},{6,7},{7,6},{8,9},{9,8},{10,11... | collective-permute-start | bytes 4718600 | tf_op jit(solution)/shard_map/ppermute | solution.py:241
  2.1 6.9 %collective-permute-start = (bf16[1040,128]{1,0:T(8,128)(2,1)S(1)}, bf16[1040,128]{1,0:T(8,128)(2,1)S(1)}, u32[]{:S(2)}, u32[]{:S(2)}) collective-permute-start(bf16[1040,128]{1,0:T(8,128)(2,1)S(1)} %pack.1.refs_0_), channel_id=1, source_target_pairs={{0,5},{1,2},{2,1},{3,6},{4,9},{5,0},{6,3},{7,10},{8,13},{9,4},{10,... | collective-permute-start | bytes 798728 | tf_op jit(solution)/shard_map/ppermute | solution.py:218
  7.3 5.9 %collective-permute-start.5 = (bf16[1040,128]{1,0:T(8,128)(2,1)S(1)}, bf16[1040,128]{1,0:T(8,128)(2,1)S(1)}, u32[]{:S(2)}, u32[]{:S(2)}) collective-permute-start(bf16[1040,128]{1,0:T(8,128)(2,1)S(1)} %pack.1.refs_0_), channel_id=1, source_target_pairs={{0,3},{1,4},{2,7},{3,0},{4,1},{5,8},{6,11},{7,2},{8,5},{9,12},{10,... | collective-permute-start | bytes 798728 | tf_op jit(solution)/shard_map/ppermute | solution.py:218
  9.0 7.8 %collective-permute-start.1 = (bf16[1040,128]{1,0:T(8,128)(2,1)S(1)}, bf16[1040,128]{1,0:T(8,128)(2,1)S(1)}, u32[]{:S(2)}, u32[]{:S(2)}) collective-permute-start(bf16[1040,128]{1,0:T(8,128)(2,1)S(1)} %collective-permute-done.refs_1_), channel_id=1, source_target_pairs={{0,3},{1,4},{2,7},{3,0},{4,1},{5,8},{6,11},{7,2},{8,5},{9,12},{10,... | collective-permute-start | bytes 798728 | tf_op jit(solution)/shard_map/ppermute | solution.py:218
  13.2 6.0 %collective-permute-start.7 = (bf16[1040,128]{1,0:T(8,128)(2,1)S(1)}, bf16[1040,128]{1,0:T(8,128)(2,1)S(1)}, u32[]{:S(2)}, u32[]{:S(2)}) collective-permute-start(bf16[1040,128]{1,0:T(8,128)(2,1)S(1)} %collective-permute-done.5.refs_0_), channel_id=1, source_target_pairs={{0,5},{1,2},{2,1},{3,6},{4,9},{5,0},{6,3},{7,10},{8,13},{9,4},{10,... | collective-permute-start | bytes 798728 | tf_op jit(solution)/shard_map/ppermute | solution.py:218
  14.7 1.2 %collective-permute-start.3 = (f32[10,768]{1,0:T(8,128)S(1)}, f32[10,768]{1,0:T(8,128)S(1)}, u32[]{:S(2)}, u32[]{:S(2)}) collective-permute-start(f32[10,768]{1,0:T(8,128)S(1)} %get-tuple-element.15), channel_id=1, source_target_pairs={{0,1},{1,0},{2,3},{3,2},{4,5},{5,4},{6,7},{7,6},{8,9},{9,8},{10,11... | collective-permute-start | bytes 92168 | tf_op jit(solution)/shard_map/ppermute | solution.py:242
  16.8 6.1 %collective-permute-start.4 = (bf16[1040,128]{1,0:T(8,128)(2,1)S(1)}, bf16[1040,128]{1,0:T(8,128)(2,1)S(1)}, u32[]{:S(2)}, u32[]{:S(2)}) collective-permute-start(bf16[1040,128]{1,0:T(8,128)(2,1)S(1)} %collective-permute-done.1.refs_1_), channel_id=1, source_target_pairs={{0,5},{1,2},{2,1},{3,6},{4,9},{5,0},{6,3},{7,10},{8,13},{9,4},{10,... | collective-permute-start | bytes 798728 | tf_op jit(solution)/shard_map/ppermute | solution.py:218
  19.3 6.8 %collective-permute-start.8 = (bf16[1040,128]{1,0:T(8,128)(2,1)S(1)}, bf16[1040,128]{1,0:T(8,128)(2,1)S(1)}, u32[]{:S(2)}, u32[]{:S(2)}) collective-permute-start(bf16[1040,128]{1,0:T(8,128)(2,1)S(1)} %collective-permute-done.7.refs_0_), channel_id=1, source_target_pairs={{0,3},{1,4},{2,7},{3,0},{4,1},{5,8},{6,11},{7,2},{8,5},{9,12},{10,... | collective-permute-start | bytes 798728 | tf_op jit(solution)/shard_map/ppermute | solution.py:218
  22.9 6.1 %collective-permute-start.6 = (bf16[1040,128]{1,0:T(8,128)(2,1)S(1)}, bf16[1040,128]{1,0:T(8,128)(2,1)S(1)}, u32[]{:S(2)}, u32[]{:S(2)}) collective-permute-start(bf16[1040,128]{1,0:T(8,128)(2,1)S(1)} %collective-permute-done.4.refs_1_), channel_id=1, source_target_pairs={{0,3},{1,4},{2,7},{3,0},{4,1},{5,8},{6,11},{7,2},{8,5},{9,12},{10,... | collective-permute-start | bytes 798728 | tf_op jit(solution)/shard_map/ppermute | solution.py:218
  29.9 1.5 %collective-permute-start.9 = (f32[8,768]{1,0:T(8,128)S(1)}, f32[8,768]{1,0:T(8,128)S(1)}, u32[]{:S(2)}, u32[]{:S(2)}) collective-permute-start(f32[8,768]{1,0:T(8,128)S(1)} %absorb.19), channel_id=1, source_target_pairs={{0,1},{1,0},{2,3},{3,2},{4,5},{5,4},{6,7},{7,6},{8,9},{9,8},{10,11... | collective-permute-start | bytes 73736 | tf_op jit(solution)/shard_map/ppermute | solution.py:284

commit v8 on v7

--- a/solution.py
+++ b/solution.py
@@ -244,7 +244,7 @@
     send(1)
 
     def absorb(work, half, state):
-        observed_half, aux = ((observed_own, own_aux), (observed_sib, sib_aux))[half]
+        observed_half, aux = (observed_sib, sib_aux) if half else (observed_own, own_aux)
         before = () if state is None else (state,)
         return pl.pallas_call(
             functools.partial(absorb_kernel, work, count, state is None),
@@ -277,6 +277,8 @@
         last = step == steps - 2
         if last:
             packets[-1] = after(packets[-1], states[0], states[1])
+        if step == 0:
+            own_aux = after(own_aux, sib_aux)
         for work, half in works[step]:
             states[half] = absorb(work, half, states[half])
             done.append(states[half])

time: 32.3 us -> 31.6 us (0.978)
  waiting for transfers between devices: 4.38 us -> 3.1 us
    ppermute x7, waiting for transfers between devices: 3.14 us -> 1.94 us  [send(): lax.ppermute(moving[kind], 'blk', pairs[(kind + step // 2) % 2])]
    ppermute x7, starting transfers between devices: 11.9 us -> 12.4 us  [send(): lax.ppermute(moving[kind], 'blk', pairs[(kind + step // 2) % 2])]
  transfers between devices with their start and end apart: 10 -> 10, of which waited for: 5 -> 6; matrix products, arithmetic and copies ran while one was open for 0% -> 0% of each run, Pallas kernels for 39% -> 40%
where the time goes in v8:
time: 31.6 us; the launch traced here: 31.1 us
  Pallas kernels  14 us (44%)
  starting transfers between devices  13.4 us (42%)
  waiting for transfers between devices  3.1 us (10%)
  between operations  0.66 us (2%)
    ppermute x7, starting transfers between devices, send(): lax.ppermute(moving[kind], 'blk', pairs[(kind + step // 2) % 2])  12.4 us
    pallas_call x10, Pallas kernels, absorb(): pl.pallas_call(functools.partial(absorb_kernel, work, count, state is Non...  9.94 us
    pallas_call x1, Pallas kernels, on_device(): pl.pallas_call(functools.partial(prepare_kernel, block_of), out_shape=(ja...  2.42 us
    ppermute x7, waiting for transfers between devices, send(): lax.ppermute(moving[kind], 'blk', pairs[(kind + step // 2) % 2])  1.94 us
    ppermute x1, waiting for transfers between devices, on_device(): sib_aux = lax.ppermute(sib_aux, 'blk', core)  1.16 us
    pallas_call x1, Pallas kernels, on_device(): pl.pallas_call(pack_kernel, out_shape=jax.ShapeDtypeStruct((count * size...  0.99 us
    pallas_call x1, Pallas kernels, on_device(): pl.pallas_call(functools.partial(finish_kernel, size), out_shape=(jax.Sha...  0.64 us
  transfers between devices with their start and end apart: 10, of which 6 were waited for; matrix products, arithmetic and copies ran while one was open for 0% of the time, Pallas kernels for 40%

profile of v8, /device:TPU:0, one launch (start us, length us, event | category | flops | bytes accessed | tf_op | source)
XLA Modules:
  0.0 31.1 jit_solution(11059887525020371325)
XLA Ops:
  0.6 0.5 %collective-permute-start.3 = (bf16[768,1024]{1,0:T(8,128)(2,1)}, bf16[768,1024]{1,0:T(8,128)(2,1)S(1)}, u32[]{:S(2)}, u32[]{:S(2)}) collective-permute-start(bf16[768,1024]{1,0:T(8,128)(2,1)} %observed_hbm.1), channel_id=1, source_target_pairs={{0,1},{1,0},{2,3},{3,2},{4,5},{5,4},{6,7},{7,6},{8,9},{9,8},{10,11... | collective-permute-start | bytes 4718600 | tf_op jit(solution)/shard_map/ppermute | solution.py:241
  1.1 1.0 %pack.1.refs_0_ = bf16[1040,128]{1,0:T(8,128)(2,1)S(1)} custom-call(bf16[4,128]{1,0:T(4,128)(2,1)} %params_hbm.1, s32[128]{0:T(128)} %class_hbm.2, bf16[128,1024]{1,0:T(8,128)(2,1)} %evolved_hbm.1), custom_call_target="tpu_custom_call" | custom-call | tf_op jit(solution)/shard_map/pack/pallas_call | solution.py:200
  2.1 2.8 %collective-permute-start.1 = (bf16[1040,128]{1,0:T(8,128)(2,1)S(1)}, bf16[1040,128]{1,0:T(8,128)(2,1)S(1)}, u32[]{:S(2)}, u32[]{:S(2)}) collective-permute-start(bf16[1040,128]{1,0:T(8,128)(2,1)S(1)} %pack.1.refs_0_), channel_id=1, source_target_pairs={{0,5},{1,2},{2,1},{3,6},{4,9},{5,0},{6,3},{7,10},{8,13},{9,4},{10,... | collective-permute-start | bytes 798728 | tf_op jit(solution)/shard_map/ppermute | solution.py:218
  4.9 2.4 %prepare.1 = (f32[10,768]{1,0:T(8,128)S(1)}, f32[10,768]{1,0:T(8,128)S(1)}, bf16[768,1024]{1,0:T(8,128)(2,1)S(1)}) custom-call(s32[1]{0:T(128)} %bitcast.at_ref, s32[6,16]{1,0:T(8,128)} %pattern_hbm.1, s32[768]{0:T(1024)} %class_hbm.3, f32[768]{0:T(1024)} %sharp_hbm.1, bf16[768,1024]{1,0:T(8,128)(2,1)} %observed_hbm.1), custom_call_target="tpu_custom_call" | custom-call | flops 6291456 | bytes 3145728 | tf_op jit(solution)/shard_map/prepare/pallas_call | solution.py:222
  7.3 1.2 %collective-permute-start.5 = (bf16[1040,128]{1,0:T(8,128)(2,1)S(1)}, bf16[1040,128]{1,0:T(8,128)(2,1)S(1)}, u32[]{:S(2)}, u32[]{:S(2)}) collective-permute-start(bf16[1040,128]{1,0:T(8,128)(2,1)S(1)} %pack.1.refs_0_), channel_id=1, source_target_pairs={{0,3},{1,4},{2,7},{3,0},{4,1},{5,8},{6,11},{7,2},{8,5},{9,12},{10,... | collective-permute-start | bytes 798728 | tf_op jit(solution)/shard_map/ppermute | solution.py:218
  9.0 1.7 %collective-permute-start.2 = (bf16[1040,128]{1,0:T(8,128)(2,1)S(1)}, bf16[1040,128]{1,0:T(8,128)(2,1)S(1)}, u32[]{:S(2)}, u32[]{:S(2)}) collective-permute-start(bf16[1040,128]{1,0:T(8,128)(2,1)S(1)} %collective-permute-done.1.refs_1_), channel_id=1, source_target_pairs={{0,3},{1,4},{2,7},{3,0},{4,1},{5,8},{6,11},{7,2},{8,5},{9,12},{10,... | collective-permute-start | bytes 798728 | tf_op jit(solution)/shard_map/ppermute | solution.py:218
  10.8 1.2 %collective-permute-done.aux_ref = f32[10,768]{1,0:T(8,128)S(1)} collective-permute-done((f32[10,768]{1,0:T(8,128)S(1)}, f32[10,768]{1,0:T(8,128)S(1)}, u32[]{:S(2)}, u32[]{:S(2)}) %collective-permute-start) | collective-permute-done | bytes 30752 | tf_op jit(solution)/shard_map/ppermute | solution.py:242
  11.9 1.0 %absorb.12.refs_2_ = f32[8,768]{1,0:T(8,128)S(1)} custom-call(bf16[768,1024]{1,0:T(8,128)(2,1)S(1)} %get-tuple-element.14.observed_ref, f32[10,768]{1,0:T(8,128)S(1)} %get-tuple-element.17.aux_ref, bf16[1040,128]{1,0:T(8,128)(2,1)S(1)} %pack.1.refs_0_, bf16[1040,128]{1,0:T(8,128)(2,1)S(1)} %collective-permute-done.1.refs_1_), custom_call_target="tpu_custom_call" | custom-call | flops 402653184 | bytes 2097152 | tf_op jit(solution)/shard_map/absorb/pallas_call | solution.py:249
  13.2 1.4 %collective-permute-start.7 = (bf16[1040,128]{1,0:T(8,128)(2,1)S(1)}, bf16[1040,128]{1,0:T(8,128)(2,1)S(1)}, u32[]{:S(2)}, u32[]{:S(2)}) collective-permute-start(bf16[1040,128]{1,0:T(8,128)(2,1)S(1)} %collective-permute-done.5.refs_0_), channel_id=1, source_target_pairs={{0,5},{1,2},{2,1},{3,6},{4,9},{5,0},{6,3},{7,10},{8,13},{9,4},{10,... | collective-permute-start | bytes 798728 | tf_op jit(solution)/shard_map/ppermute | solution.py:218
  14.7 0.9 %absorb.10.refs_2_ = f32[8,768]{1,0:T(8,128)S(1)} custom-call(bf16[768,1024]{1,0:T(8,128)(2,1)S(1)} %collective-permute-done.3.observed_ref, f32[10,768]{1,0:T(8,128)S(1)} %collective-permute-done.aux_ref, bf16[1040,128]{1,0:T(8,128)(2,1)S(1)} %pack.1.refs_0_, bf16[1040,128]{1,0:T(8,128)(2,1)S(1)} %collective-permute-done.1.refs_1_), custom_call_target="tpu_custom_call" | custom-call | flops 402653184 | bytes 2097152 | tf_op jit(solution)/shard_map/absorb/pallas_call | solution.py:249
  15.6 0.5 %collective-permute-done.2.refs_1_ = bf16[1040,128]{1,0:T(8,128)(2,1)S(1)} collective-permute-done((bf16[1040,128]{1,0:T(8,128)(2,1)S(1)}, bf16[1040,128]{1,0:T(8,128)(2,1)S(1)}, u32[]{:S(2)}, u32[]{:S(2)}) %collective-permute-start.2) | collective-permute-done | bytes 266272 | tf_op jit(solution)/shard_map/ppermute | solution.py:218
  16.1 1.3 %collective-permute-start.4 = (bf16[1040,128]{1,0:T(8,128)(2,1)S(1)}, bf16[1040,128]{1,0:T(8,128)(2,1)S(1)}, u32[]{:S(2)}, u32[]{:S(2)}) collective-permute-start(bf16[1040,128]{1,0:T(8,128)(2,1)S(1)} %collective-permute-done.2.refs_1_), channel_id=1, source_target_pairs={{0,5},{1,2},{2,1},{3,6},{4,9},{5,0},{6,3},{7,10},{8,13},{9,4},{10,... | collective-permute-start | bytes 798728 | tf_op jit(solution)/shard_map/ppermute | solution.py:218
  17.4 1.1 %absorb.13.refs_2_ = f32[8,768]{1,0:T(8,128)S(1)} custom-call(bf16[768,1024]{1,0:T(8,128)(2,1)S(1)} %get-tuple-element.14.observed_ref, f32[10,768]{1,0:T(8,128)S(1)} %get-tuple-element.17.aux_ref, bf16[1040,128]{1,0:T(8,128)(2,1)S(1)} %collective-permute-done.5.refs_0_, bf16[1040,128]{1,0:T(8,128)(2,1)S(1)} %collective-permute-done.2.refs_1_, ...), custom_call_target="tpu_custom_call" | custom-call | flops 402653184 | bytes 2097152 | tf_op jit(solution)/shard_map/absorb/pallas_call | solution.py:249
  18.5 0.6 %collective-permute-done.7.refs_0_ = bf16[1040,128]{1,0:T(8,128)(2,1)S(1)} collective-permute-done((bf16[1040,128]{1,0:T(8,128)(2,1)S(1)}, bf16[1040,128]{1,0:T(8,128)(2,1)S(1)}, u32[]{:S(2)}, u32[]{:S(2)}) %collective-permute-start.7) | collective-permute-done | bytes 266272 | tf_op jit(solution)/shard_map/ppermute | solution.py:218
  19.1 1.8 %collective-permute-start.8 = (bf16[1040,128]{1,0:T(8,128)(2,1)S(1)}, bf16[1040,128]{1,0:T(8,128)(2,1)S(1)}, u32[]{:S(2)}, u32[]{:S(2)}) collective-permute-start(bf16[1040,128]{1,0:T(8,128)(2,1)S(1)} %collective-permute-done.7.refs_0_), channel_id=1, source_target_pairs={{0,3},{1,4},{2,7},{3,0},{4,1},{5,8},{6,11},{7,2},{8,5},{9,12},{10,... | collective-permute-start | bytes 798728 | tf_op jit(solution)/shard_map/ppermute | solution.py:218
  20.9 1.1 %absorb.11.refs_2_ = f32[8,768]{1,0:T(8,128)S(1)} custom-call(bf16[768,1024]{1,0:T(8,128)(2,1)S(1)} %collective-permute-done.3.observed_ref, f32[10,768]{1,0:T(8,128)S(1)} %collective-permute-done.aux_ref, bf16[1040,128]{1,0:T(8,128)(2,1)S(1)} %collective-permute-done.5.refs_0_, bf16[1040,128]{1,0:T(8,128)(2,1)S(1)} %collective-permute-done.2.refs_1_, ...), custom_call_target="tpu_custom_call" | custom-call | flops 402653184 | bytes 2097152 | tf_op jit(solution)/shard_map/absorb/pallas_call | solution.py:249
  22.0 2.2 %collective-permute-start.6 = (bf16[1040,128]{1,0:T(8,128)(2,1)S(1)}, bf16[1040,128]{1,0:T(8,128)(2,1)S(1)}, u32[]{:S(2)}, u32[]{:S(2)}) collective-permute-start(bf16[1040,128]{1,0:T(8,128)(2,1)S(1)} %collective-permute-done.4.refs_1_), channel_id=1, source_target_pairs={{0,3},{1,4},{2,7},{3,0},{4,1},{5,8},{6,11},{7,2},{8,5},{9,12},{10,... | collective-permute-start | bytes 798728 | tf_op jit(solution)/shard_map/ppermute | solution.py:218
  24.2 1.1 %absorb.16.refs_1_ = f32[8,768]{1,0:T(8,128)S(1)} custom-call(bf16[768,1024]{1,0:T(8,128)(2,1)S(1)} %collective-permute-done.3.observed_ref, f32[10,768]{1,0:T(8,128)S(1)} %collective-permute-done.aux_ref, bf16[1040,128]{1,0:T(8,128)(2,1)S(1)} %collective-permute-done.7.refs_0_, bf16[1040,128]{1,0:T(8,128)(2,1)S(1)} %collective-permute-done.4.refs_1_, ...), custom_call_target="tpu_custom_call" | custom-call | flops 402653184 | bytes 2097152 | tf_op jit(solution)/shard_map/absorb/pallas_call | solution.py:249
  25.3 0.9 %absorb.17.refs_1_ = f32[8,768]{1,0:T(8,128)S(1)} custom-call(bf16[768,1024]{1,0:T(8,128)(2,1)S(1)} %collective-permute-done.3.observed_ref, f32[10,768]{1,0:T(8,128)S(1)} %collective-permute-done.aux_ref, bf16[1040,128]{1,0:T(8,128)(2,1)S(1)} %collective-permute-done.8.refs_0_, f32[8,768]{1,0:T(8,128)S(1)} %absorb.16.refs_1_), custom_call_target="tpu_custom_call" | custom-call | flops 201326592 | bytes 1835008 | tf_op jit(solution)/shard_map/absorb/pallas_call | solution.py:249
  26.2 1.1 %absorb.14.refs_1_ = f32[8,768]{1,0:T(8,128)S(1)} custom-call(bf16[768,1024]{1,0:T(8,128)(2,1)S(1)} %get-tuple-element.14.observed_ref, f32[10,768]{1,0:T(8,128)S(1)} %get-tuple-element.17.aux_ref, bf16[1040,128]{1,0:T(8,128)(2,1)S(1)} %collective-permute-done.7.refs_0_, bf16[1040,128]{1,0:T(8,128)(2,1)S(1)} %collective-permute-done.4.refs_1_, ...), custom_call_target="tpu_custom_call" | custom-call | flops 402653184 | bytes 2097152 | tf_op jit(solution)/shard_map/absorb/pallas_call | solution.py:249
  27.4 0.9 %absorb.15.refs_1_ = f32[8,768]{1,0:T(8,128)S(1)} custom-call(bf16[768,1024]{1,0:T(8,128)(2,1)S(1)} %get-tuple-element.14.observed_ref, f32[10,768]{1,0:T(8,128)S(1)} %get-tuple-element.17.aux_ref, bf16[1040,128]{1,0:T(8,128)(2,1)S(1)} %collective-permute-done.8.refs_0_, f32[8,768]{1,0:T(8,128)S(1)} %absorb.14.refs_1_), custom_call_target="tpu_custom_call" | custom-call | flops 201326592 | bytes 1835008 | tf_op jit(solution)/shard_map/absorb/pallas_call | solution.py:249
  28.3 0.9 %absorb.19 = f32[8,768]{1,0:T(8,128)S(1)} custom-call(bf16[768,1024]{1,0:T(8,128)(2,1)S(1)} %collective-permute-done.3.observed_ref, f32[10,768]{1,0:T(8,128)S(1)} %collective-permute-done.aux_ref, bf16[1040,128]{1,0:T(8,128)(2,1)S(1)} %collective-permute-done.6.refs_0_, f32[8,768]{1,0:T(8,128)S(1)} %absorb.17.refs_1_), custom_call_target="tpu_custom_call" | custom-call | flops 201326592 | bytes 1835008 | tf_op jit(solution)/shard_map/absorb/pallas_call | solution.py:249
  29.6 0.9 %absorb.18.mine_ref = f32[8,768]{1,0:T(8,128)S(1)} custom-call(bf16[768,1024]{1,0:T(8,128)(2,1)S(1)} %get-tuple-element.14.observed_ref, f32[10,768]{1,0:T(8,128)S(1)} %get-tuple-element.17.aux_ref, bf16[1040,128]{1,0:T(8,128)(2,1)S(1)} %collective-permute-done.6.refs_0_, f32[8,768]{1,0:T(8,128)S(1)} %absorb.15.refs_1_), custom_call_target="tpu_custom_call" | custom-call | flops 201326592 | bytes 1835008 | tf_op jit(solution)/shard_map/absorb/pallas_call | solution.py:249
  30.5 0.6 %finish.1 = (f32[4,768]{1,0:T(4,128)}, f32[768]{0:T(1024)}) custom-call(f32[8,768]{1,0:T(8,128)S(1)} %absorb.18.mine_ref, f32[8,768]{1,0:T(8,128)S(1)} %collective-permute-done.9.other_ref, f32[10,768]{1,0:T(8,128)S(1)} %get-tuple-element.17.aux_ref), custom_call_target="tpu_custom_call" | custom-call | tf_op jit(solution)/shard_map/finish/pallas_call | solution.py:287
  (9 shorter events, 1.3 us)
Async XLA Ops:
  0.6 14.0 %collective-permute-start.3 = (bf16[768,1024]{1,0:T(8,128)(2,1)}, bf16[768,1024]{1,0:T(8,128)(2,1)S(1)}, u32[]{:S(2)}, u32[]{:S(2)}) collective-permute-start(bf16[768,1024]{1,0:T(8,128)(2,1)} %observed_hbm.1), channel_id=1, source_target_pairs={{0,1},{1,0},{2,3},{3,2},{4,5},{5,4},{6,7},{7,6},{8,9},{9,8},{10,11... | collective-permute-start | bytes 4718600 | tf_op jit(solution)/shard_map/ppermute | solution.py:241
  2.1 6.9 %collective-permute-start.1 = (bf16[1040,128]{1,0:T(8,128)(2,1)S(1)}, bf16[1040,128]{1,0:T(8,128)(2,1)S(1)}, u32[]{:S(2)}, u32[]{:S(2)}) collective-permute-start(bf16[1040,128]{1,0:T(8,128)(2,1)S(1)} %pack.1.refs_0_), channel_id=1, source_target_pairs={{0,5},{1,2},{2,1},{3,6},{4,9},{5,0},{6,3},{7,10},{8,13},{9,4},{10,... | collective-permute-start | bytes 798728 | tf_op jit(solution)/shard_map/ppermute | solution.py:218
  7.3 5.9 %collective-permute-start.5 = (bf16[1040,128]{1,0:T(8,128)(2,1)S(1)}, bf16[1040,128]{1,0:T(8,128)(2,1)S(1)}, u32[]{:S(2)}, u32[]{:S(2)}) collective-permute-start(bf16[1040,128]{1,0:T(8,128)(2,1)S(1)} %pack.1.refs_0_), channel_id=1, source_target_pairs={{0,3},{1,4},{2,7},{3,0},{4,1},{5,8},{6,11},{7,2},{8,5},{9,12},{10,... | collective-permute-start | bytes 798728 | tf_op jit(solution)/shard_map/ppermute | solution.py:218
  9.0 7.1 %collective-permute-start.2 = (bf16[1040,128]{1,0:T(8,128)(2,1)S(1)}, bf16[1040,128]{1,0:T(8,128)(2,1)S(1)}, u32[]{:S(2)}, u32[]{:S(2)}) collective-permute-start(bf16[1040,128]{1,0:T(8,128)(2,1)S(1)} %collective-permute-done.1.refs_1_), channel_id=1, source_target_pairs={{0,3},{1,4},{2,7},{3,0},{4,1},{5,8},{6,11},{7,2},{8,5},{9,12},{10,... | collective-permute-start | bytes 798728 | tf_op jit(solution)/shard_map/ppermute | solution.py:218
  10.7 1.2 %collective-permute-start = (f32[10,768]{1,0:T(8,128)S(1)}, f32[10,768]{1,0:T(8,128)S(1)}, u32[]{:S(2)}, u32[]{:S(2)}) collective-permute-start(f32[10,768]{1,0:T(8,128)S(1)} %get-tuple-element.16), channel_id=1, source_target_pairs={{0,1},{1,0},{2,3},{3,2},{4,5},{5,4},{6,7},{7,6},{8,9},{9,8},{10,11... | collective-permute-start | bytes 92168 | tf_op jit(solution)/shard_map/ppermute | solution.py:242
  13.2 5.8 %collective-permute-start.7 = (bf16[1040,128]{1,0:T(8,128)(2,1)S(1)}, bf16[1040,128]{1,0:T(8,128)(2,1)S(1)}, u32[]{:S(2)}, u32[]{:S(2)}) collective-permute-start(bf16[1040,128]{1,0:T(8,128)(2,1)S(1)} %collective-permute-done.5.refs_0_), channel_id=1, source_target_pairs={{0,5},{1,2},{2,1},{3,6},{4,9},{5,0},{6,3},{7,10},{8,13},{9,4},{10,... | collective-permute-start | bytes 798728 | tf_op jit(solution)/shard_map/ppermute | solution.py:218
  16.1 5.9 %collective-permute-start.4 = (bf16[1040,128]{1,0:T(8,128)(2,1)S(1)}, bf16[1040,128]{1,0:T(8,128)(2,1)S(1)}, u32[]{:S(2)}, u32[]{:S(2)}) collective-permute-start(bf16[1040,128]{1,0:T(8,128)(2,1)S(1)} %collective-permute-done.2.refs_1_), channel_id=1, source_target_pairs={{0,5},{1,2},{2,1},{3,6},{4,9},{5,0},{6,3},{7,10},{8,13},{9,4},{10,... | collective-permute-start | bytes 798728 | tf_op jit(solution)/shard_map/ppermute | solution.py:218
  19.1 6.3 %collective-permute-start.8 = (bf16[1040,128]{1,0:T(8,128)(2,1)S(1)}, bf16[1040,128]{1,0:T(8,128)(2,1)S(1)}, u32[]{:S(2)}, u32[]{:S(2)}) collective-permute-start(bf16[1040,128]{1,0:T(8,128)(2,1)S(1)} %collective-permute-done.7.refs_0_), channel_id=1, source_target_pairs={{0,3},{1,4},{2,7},{3,0},{4,1},{5,8},{6,11},{7,2},{8,5},{9,12},{10,... | collective-permute-start | bytes 798728 | tf_op jit(solution)/shard_map/ppermute | solution.py:218
  22.0 6.3 %collective-permute-start.6 = (bf16[1040,128]{1,0:T(8,128)(2,1)S(1)}, bf16[1040,128]{1,0:T(8,128)(2,1)S(1)}, u32[]{:S(2)}, u32[]{:S(2)}) collective-permute-start(bf16[1040,128]{1,0:T(8,128)(2,1)S(1)} %collective-permute-done.4.refs_1_), channel_id=1, source_target_pairs={{0,3},{1,4},{2,7},{3,0},{4,1},{5,8},{6,11},{7,2},{8,5},{9,12},{10,... | collective-permute-start | bytes 798728 | tf_op jit(solution)/shard_map/ppermute | solution.py:218
  29.2 1.3 %collective-permute-start.9 = (f32[8,768]{1,0:T(8,128)S(1)}, f32[8,768]{1,0:T(8,128)S(1)}, u32[]{:S(2)}, u32[]{:S(2)}) collective-permute-start(f32[8,768]{1,0:T(8,128)S(1)} %absorb.19), channel_id=1, source_target_pairs={{0,1},{1,0},{2,3},{3,2},{4,5},{5,4},{6,7},{7,6},{8,9},{9,8},{10,11... | collective-permute-start | bytes 73736 | tf_op jit(solution)/shard_map/ppermute | solution.py:286

commit v9 on v8

--- a/solution.py
+++ b/solution.py
@@ -54,7 +54,7 @@
     return values.reshape(1, values.shape[-1])
 
 
-def pack_kernel(params_hbm, class_hbm, evolved_hbm, packet_ref, params_ref, class_ref, arrived):
+def pack_kernel(params_hbm, class_hbm, evolved_hbm, upper_ref, lower_ref, params_ref, class_ref, arrived):
     rows, size = evolved_hbm.shape
     panels = size // LANES
     copies = [
@@ -62,7 +62,8 @@
         pltpu.make_async_copy(class_hbm, class_ref, arrived.at[1]),
     ]
     for i in range(panels):
-        panel = packet_ref.at[pl.ds(i * rows, rows), :]
+        half = panels // 2
+        panel = (upper_ref if i < half else lower_ref).at[pl.ds(i % half * rows, rows), :]
         source = evolved_hbm.at[:, pl.ds(i * LANES, LANES)]
         copies.append(pltpu.make_async_copy(source, panel, arrived.at[i + 2]))
     for copy in copies:
@@ -72,21 +73,18 @@
     params = params_ref[...].astype(jnp.float32)
     classes = row(class_ref[...]).astype(jnp.float32)
     rest = jnp.broadcast_to(classes, (META_ROWS - params.shape[0], classes.shape[1]))
-    packet_ref[panels * rows :, :] = jnp.concatenate([params, rest], axis=0).astype(packet_ref.dtype)
+    upper_ref[panels // 2 * rows :, :] = jnp.concatenate([params, rest], axis=0).astype(upper_ref.dtype)
     for copy in copies[2:]:
         copy.wait()
 
 
 def norms(observed):
-    wide = observed.astype(jnp.float32)
-    square = wide * wide
-    high = square.astype(jnp.bfloat16)
-    low = (square - high.astype(jnp.float32)).astype(jnp.bfloat16)
-    ones = jnp.ones((SUBLANES, observed.shape[1]), jnp.bfloat16)
-    return sum(
-        lax.dot_general(ones, part, (((1,), (1,)), ((), ())), preferred_element_type=jnp.float32)[0:1]
-        for part in (high, low)
-    )
+    rows, size = observed.shape
+    sums = jnp.zeros((rows, LANES), jnp.float32)
+    for i in range(size // LANES):
+        panel = observed[:, i * LANES : (i + 1) * LANES].astype(jnp.float32)
+        sums += panel * panel
+    return jnp.sum(sums.T, axis=0, keepdims=True)
 
 
 def prepare_kernel(
@@ -121,19 +119,24 @@
 
 
 def absorb_kernel(steps, count, first, observed_ref, aux_ref, *refs):
-    packet_refs, out_ref = refs[: len(steps)], refs[-1]
+    count_refs = 2 * len(steps)
+    packet_refs, out_ref = list(zip(refs[:count_refs:2], refs[1:count_refs:2])), refs[-1]
     panels = observed_ref.shape[1] // LANES
-    blocks = [jnp.concatenate([ref[i * count : (i + 1) * count, :] for i in range(panels)], axis=1) for ref in packet_refs]
+    half = panels // 2
+    blocks = [
+        jnp.concatenate([ref[i * count : (i + 1) * count, :] for ref in both for i in range(half)], axis=1)
+        for both in packet_refs
+    ]
     inner = lax.dot_general(
         joined(blocks, 0), observed_ref[...], (((1,), (1,)), ((), ())), preferred_element_type=jnp.float32
     )
-    metas = [ref[panels * count :, :] for ref in packet_refs]
+    metas = [upper[half * count :, :] for upper, _ in packet_refs]
     after_steps = aux_ref.shape[0] - 2
     scale = aux_ref[after_steps : after_steps + 1, :]
     if first:
         top = jnp.full(scale.shape, NEG_START, jnp.float32)
     else:
-        state_ref = refs[len(steps)]
+        state_ref = refs[count_refs]
         top = old = state_ref[0:1, :]
     scores = []
     for i, (step, block, meta) in enumerate(zip(steps, blocks, metas)):
@@ -199,9 +202,11 @@
 
     packet = pl.pallas_call(
         pack_kernel,
-        out_shape=jax.ShapeDtypeStruct((count * size // LANES + META_ROWS, LANES), evolved.dtype),
+        out_shape=[
+            jax.ShapeDtypeStruct((count * size // LANES // 2 + rest, LANES), evolved.dtype) for rest in (META_ROWS, 0)
+        ],
         in_specs=[hbm] * 3,
-        out_specs=vmem,
+        out_specs=[vmem] * 2,
         scratch_shapes=[
             pltpu.VMEM(sim_params.shape, sim_params.dtype),
             pltpu.VMEM(sim_class.shape, sim_class.dtype),
@@ -215,7 +220,7 @@
 
     def send(step):
         kind = step % 2
-        moving[kind] = lax.ppermute(moving[kind], "blk", pairs[(kind + step // 2) % 2])
+        moving[kind] = [lax.ppermute(part, "blk", pairs[(kind + step // 2) % 2]) for part in moving[kind]]
         packets.append(moving[kind])
 
     send(0)
@@ -249,7 +254,7 @@
         return pl.pallas_call(
             functools.partial(absorb_kernel, work, count, state is None),
             out_shape=jax.ShapeDtypeStruct((SUBLANES, rows), f32),
-            in_specs=[vmem] * (2 + len(work) + len(before)),
+            in_specs=[vmem] * (2 + 2 * len(work) + len(before)),
             out_specs=vmem,
             compiler_params=compiler_params,
             cost_estimate=pl.CostEstimate(
@@ -258,12 +263,13 @@
                 transcendentals=len(work) * rows * count,
             ),
             name="absorb",
-        )(observed_half, aux, *(packets[i] for i in work), *before)
+        )(observed_half, aux, *(part for i in work for part in packets[i]), *before)
 
     works = [[] for _ in range(steps)]
     for block in range(1, steps - 2, 2):
-        works[block - 1].append(((block - 1, block), 0))
-        works[block].append(((block - 1, block), 1))
+        pair = (block - 1, block)
+        works[block - 1].append((pair, 0))
+        works[block if block < steps - 3 else block - 1].append((pair, 1))
     works[steps - 3] += [((steps - 2,), 0), ((steps - 2,), 1)]
     works[steps - 2] += [((steps - 1,), 1), ((steps - 1,), 0)]
     states = [None, None]
@@ -272,13 +278,11 @@
         ahead = step + 2
         if ahead < steps - 1:
             if done:
-                moving[ahead % 2] = after(moving[ahead % 2], done[-1])
+                moving[ahead % 2] = [after(part, done[-1]) for part in moving[ahead % 2]]
             send(ahead)
         last = step == steps - 2
-        if last:
-            packets[-1] = after(packets[-1], states[0], states[1])
-        if step == 0:
-            own_aux = after(own_aux, sib_aux)
+        if step >= steps - 3:
+            packets[step + 1] = after(packets[step + 1], states[0], states[1])
         for work, half in works[step]:
             states[half] = absorb(work, half, states[half])
             done.append(states[half])

time: 31.6 us -> 31.1 us (0.984)
  starting transfers between devices: 13.4 us -> 14.9 us
  waiting for transfers between devices: 3.1 us -> 1.88 us
  Pallas kernels: 14 us -> 13.4 us
    ppermute x7 -> x14, starting transfers between devices: 12.4 us -> 14.1 us  [send(): lax.ppermute(part, 'blk', pairs[(kind + step // 2) % 2])]
    ppermute x1, waiting for transfers between devices: 1.16 us -> 0.01 us  [on_device(): sib_aux = lax.ppermute(sib_aux, 'blk', core)]
    pallas_call x1, Pallas kernels: 2.42 us -> 1.85 us  [on_device(): pl.pallas_call(functools.partial(prepare_kernel, block_of), out_shape=(ja...]
    ppermute x7 -> x14, waiting for transfers between devices: 1.94 us -> 1.68 us  [send(): lax.ppermute(part, 'blk', pairs[(kind + step // 2) % 2])]
  transfers between devices with their start and end apart: 10 -> 17, of which waited for: 6 -> 5; matrix products, arithmetic and copies ran while one was open for 0% -> 0% of each run, Pallas kernels for 40% -> 39%
where the time goes in v9:
time: 31.1 us; the launch traced here: 30.8 us
  starting transfers between devices  14.9 us (48%)
  Pallas kernels  13.4 us (43%)
  waiting for transfers between devices  1.88 us (6%)
  between operations  0.68 us (2%)
    ppermute x14, starting transfers between devices, send(): lax.ppermute(part, 'blk', pairs[(kind + step // 2) % 2])  14.1 us
    pallas_call x10, Pallas kernels, absorb(): pl.pallas_call(functools.partial(absorb_kernel, work, count, state is Non...  9.94 us
    pallas_call x1, Pallas kernels, on_device(): pl.pallas_call(functools.partial(prepare_kernel, block_of), out_shape=(ja...  1.85 us
    ppermute x14, waiting for transfers between devices, send(): lax.ppermute(part, 'blk', pairs[(kind + step // 2) % 2])  1.68 us
    pallas_call x1, Pallas kernels, on_device(): pl.pallas_call(pack_kernel, out_shape=[jax.ShapeDtypeStruct((count * size...  0.99 us
    pallas_call x1, Pallas kernels, on_device(): pl.pallas_call(functools.partial(finish_kernel, size), out_shape=(jax.Sha...  0.63 us
  transfers between devices with their start and end apart: 17, of which 5 were waited for; matrix products, arithmetic and copies ran while one was open for 0% of the time, Pallas kernels for 39%

profile of v9, /device:TPU:0, one launch (start us, length us, event | category | flops | bytes accessed | tf_op | source)
XLA Modules:
  0.0 30.8 jit_solution(9171351851232971512)
XLA Ops:
  0.6 0.5 %collective-permute-start.2 = (bf16[768,1024]{1,0:T(8,128)(2,1)}, bf16[768,1024]{1,0:T(8,128)(2,1)S(1)}, u32[]{:S(2)}, u32[]{:S(2)}) collective-permute-start(bf16[768,1024]{1,0:T(8,128)(2,1)} %observed_hbm.1), channel_id=1, source_target_pairs={{0,1},{1,0},{2,3},{3,2},{4,5},{5,4},{6,7},{7,6},{8,9},{9,8},{10,11... | collective-permute-start | bytes 4718600 | tf_op jit(solution)/shard_map/ppermute | solution.py:246
  1.1 1.0 %pack.1 = (bf16[528,128]{1,0:T(8,128)(2,1)S(1)}, bf16[512,128]{1,0:T(8,128)(2,1)S(1)}) custom-call(bf16[4,128]{1,0:T(4,128)(2,1)} %params_hbm.1, s32[128]{0:T(128)} %class_hbm.2, bf16[128,1024]{1,0:T(8,128)(2,1)} %evolved_hbm.1), custom_call_target="tpu_custom_call" | custom-call | tf_op jit(solution)/shard_map/pack/pallas_call | solution.py:203
  2.1 2.8 %collective-permute-start = (bf16[528,128]{1,0:T(8,128)(2,1)S(1)}, bf16[528,128]{1,0:T(8,128)(2,1)S(1)}, u32[]{:S(2)}, u32[]{:S(2)}) collective-permute-start(bf16[528,128]{1,0:T(8,128)(2,1)S(1)} %get-tuple-element.29.refs_0_), channel_id=1, source_target_pairs={{0,5},{1,2},{2,1},{3,6},{4,9},{5,0},{6,3},{7,10},{8,13},{9,4},{10,... | collective-permute-start | bytes 405512 | tf_op jit(solution)/shard_map/ppermute | solution.py:223
  5.0 1.8 %prepare.1 = (f32[10,768]{1,0:T(8,128)S(1)}, f32[10,768]{1,0:T(8,128)S(1)}, bf16[768,1024]{1,0:T(8,128)(2,1)S(1)}) custom-call(s32[1]{0:T(128)} %bitcast.at_ref, s32[6,16]{1,0:T(8,128)} %pattern_hbm.1, s32[768]{0:T(1024)} %class_hbm.3, f32[768]{0:T(1024)} %sharp_hbm.1, bf16[768,1024]{1,0:T(8,128)(2,1)} %observed_hbm.1), custom_call_target="tpu_custom_call" | custom-call | flops 6291456 | bytes 3145728 | tf_op jit(solution)/shard_map/prepare/pallas_call | solution.py:227
  6.8 1.7 %collective-permute-start.7 = (bf16[512,128]{1,0:T(8,128)(2,1)S(1)}, bf16[512,128]{1,0:T(8,128)(2,1)S(1)}, u32[]{:S(2)}, u32[]{:S(2)}) collective-permute-start(bf16[512,128]{1,0:T(8,128)(2,1)S(1)} %get-tuple-element.30.refs_1_), channel_id=1, source_target_pairs={{0,3},{1,4},{2,7},{3,0},{4,1},{5,8},{6,11},{7,2},{8,5},{9,12},{10,... | collective-permute-start | bytes 393224 | tf_op jit(solution)/shard_map/ppermute | solution.py:223
  8.7 1.6 %collective-permute-start.1 = (bf16[528,128]{1,0:T(8,128)(2,1)S(1)}, bf16[528,128]{1,0:T(8,128)(2,1)S(1)}, u32[]{:S(2)}, u32[]{:S(2)}) collective-permute-start(bf16[528,128]{1,0:T(8,128)(2,1)S(1)} %collective-permute-done.refs_2_), channel_id=1, source_target_pairs={{0,3},{1,4},{2,7},{3,0},{4,1},{5,8},{6,11},{7,2},{8,5},{9,12},{10,... | collective-permute-start | bytes 405512 | tf_op jit(solution)/shard_map/ppermute | solution.py:223
  10.3 0.4 %collective-permute-start.8 = (bf16[512,128]{1,0:T(8,128)(2,1)S(1)}, bf16[512,128]{1,0:T(8,128)(2,1)S(1)}, u32[]{:S(2)}, u32[]{:S(2)}) collective-permute-start(bf16[512,128]{1,0:T(8,128)(2,1)S(1)} %collective-permute-done.4.refs_3_), channel_id=1, source_target_pairs={{0,3},{1,4},{2,7},{3,0},{4,1},{5,8},{6,11},{7,2},{8,5},{9,12},{10,... | collective-permute-start | bytes 393224 | tf_op jit(solution)/shard_map/ppermute | solution.py:223
  10.7 0.6 %collective-permute-done.7.refs_1_ = bf16[512,128]{1,0:T(8,128)(2,1)S(1)} collective-permute-done((bf16[512,128]{1,0:T(8,128)(2,1)S(1)}, bf16[512,128]{1,0:T(8,128)(2,1)S(1)}, u32[]{:S(2)}, u32[]{:S(2)}) %collective-permute-start.7) | collective-permute-done | bytes 131104 | tf_op jit(solution)/shard_map/ppermute | solution.py:223
  11.4 1.0 %absorb.12.refs_4_ = f32[8,768]{1,0:T(8,128)S(1)} custom-call(bf16[768,1024]{1,0:T(8,128)(2,1)S(1)} %get-tuple-element.25.observed_ref, f32[10,768]{1,0:T(8,128)S(1)} %get-tuple-element.26.aux_ref, bf16[528,128]{1,0:T(8,128)(2,1)S(1)} %get-tuple-element.29.refs_0_, bf16[512,128]{1,0:T(8,128)(2,1)S(1)} %get-tuple-element.30.refs_1_, ...), custom_call_target="tpu_custom_call" | custom-call | flops 402653184 | bytes 2097152 | tf_op jit(solution)/shard_map/absorb/pallas_call | solution.py:254
  12.4 0.6 %collective-permute-done.6.refs_0_ = bf16[528,128]{1,0:T(8,128)(2,1)S(1)} collective-permute-done((bf16[528,128]{1,0:T(8,128)(2,1)S(1)}, bf16[528,128]{1,0:T(8,128)(2,1)S(1)}, u32[]{:S(2)}, u32[]{:S(2)}) %collective-permute-start.6) | collective-permute-done | bytes 135200 | tf_op jit(solution)/shard_map/ppermute | solution.py:223
  12.9 1.8 %collective-permute-start.12 = (bf16[528,128]{1,0:T(8,128)(2,1)S(1)}, bf16[528,128]{1,0:T(8,128)(2,1)S(1)}, u32[]{:S(2)}, u32[]{:S(2)}) collective-permute-start(bf16[528,128]{1,0:T(8,128)(2,1)S(1)} %collective-permute-done.6.refs_0_), channel_id=1, source_target_pairs={{0,5},{1,2},{2,1},{3,6},{4,9},{5,0},{6,3},{7,10},{8,13},{9,4},{10,... | collective-permute-start | bytes 405512 | tf_op jit(solution)/shard_map/ppermute | solution.py:223
  14.7 1.0 %absorb.10.refs_4_ = f32[8,768]{1,0:T(8,128)S(1)} custom-call(bf16[768,1024]{1,0:T(8,128)(2,1)S(1)} %collective-permute-done.2.observed_ref, f32[10,768]{1,0:T(8,128)S(1)} %collective-permute-done.3.aux_ref, bf16[528,128]{1,0:T(8,128)(2,1)S(1)} %get-tuple-element.29.refs_0_, bf16[512,128]{1,0:T(8,128)(2,1)S(1)} %get-tuple-element.30.refs_1_, ...), custom_call_target="tpu_custom_call" | custom-call | flops 402653184 | bytes 2097152 | tf_op jit(solution)/shard_map/absorb/pallas_call | solution.py:254
  15.7 1.7 %collective-permute-start.5 = (bf16[528,128]{1,0:T(8,128)(2,1)S(1)}, bf16[528,128]{1,0:T(8,128)(2,1)S(1)}, u32[]{:S(2)}, u32[]{:S(2)}) collective-permute-start(bf16[528,128]{1,0:T(8,128)(2,1)S(1)} %collective-permute-done.1.refs_2_), channel_id=1, source_target_pairs={{0,5},{1,2},{2,1},{3,6},{4,9},{5,0},{6,3},{7,10},{8,13},{9,4},{10,... | collective-permute-start | bytes 405512 | tf_op jit(solution)/shard_map/ppermute | solution.py:223
  17.7 1.1 %absorb.13.refs_4_ = f32[8,768]{1,0:T(8,128)S(1)} custom-call(bf16[768,1024]{1,0:T(8,128)(2,1)S(1)} %get-tuple-element.25.observed_ref, f32[10,768]{1,0:T(8,128)S(1)} %get-tuple-element.26.aux_ref, bf16[528,128]{1,0:T(8,128)(2,1)S(1)} %collective-permute-done.6.refs_0_, bf16[512,128]{1,0:T(8,128)(2,1)S(1)} %collective-permute-done.7.refs_1_, ...), custom_call_target="tpu_custom_call" | custom-call | flops 402653184 | bytes 2097152 | tf_op jit(solution)/shard_map/absorb/pallas_call | solution.py:254
  19.1 1.7 %collective-permute-start.13 = (bf16[528,128]{1,0:T(8,128)(2,1)S(1)}, bf16[528,128]{1,0:T(8,128)(2,1)S(1)}, u32[]{:S(2)}, u32[]{:S(2)}) collective-permute-start(bf16[528,128]{1,0:T(8,128)(2,1)S(1)} %collective-permute-done.12.refs_0_), channel_id=1, source_target_pairs={{0,3},{1,4},{2,7},{3,0},{4,1},{5,8},{6,11},{7,2},{8,5},{9,12},{10,... | collective-permute-start | bytes 405512 | tf_op jit(solution)/shard_map/ppermute | solution.py:223
  20.9 1.1 %absorb.11.refs_4_ = f32[8,768]{1,0:T(8,128)S(1)} custom-call(bf16[768,1024]{1,0:T(8,128)(2,1)S(1)} %collective-permute-done.2.observed_ref, f32[10,768]{1,0:T(8,128)S(1)} %collective-permute-done.3.aux_ref, bf16[528,128]{1,0:T(8,128)(2,1)S(1)} %collective-permute-done.6.refs_0_, bf16[512,128]{1,0:T(8,128)(2,1)S(1)} %collective-permute-done.7.refs_1_, ...), custom_call_target="tpu_custom_call" | custom-call | flops 402653184 | bytes 2097152 | tf_op jit(solution)/shard_map/absorb/pallas_call | solution.py:254
  22.0 1.7 %collective-permute-start.9 = (bf16[528,128]{1,0:T(8,128)(2,1)S(1)}, bf16[528,128]{1,0:T(8,128)(2,1)S(1)}, u32[]{:S(2)}, u32[]{:S(2)}) collective-permute-start(bf16[528,128]{1,0:T(8,128)(2,1)S(1)} %collective-permute-done.5.refs_2_), channel_id=1, source_target_pairs={{0,3},{1,4},{2,7},{3,0},{4,1},{5,8},{6,11},{7,2},{8,5},{9,12},{10,... | collective-permute-start | bytes 405512 | tf_op jit(solution)/shard_map/ppermute | solution.py:223
  23.9 1.1 %absorb.15.refs_2_ = f32[8,768]{1,0:T(8,128)S(1)} custom-call(bf16[768,1024]{1,0:T(8,128)(2,1)S(1)} %collective-permute-done.2.observed_ref, f32[10,768]{1,0:T(8,128)S(1)} %collective-permute-done.3.aux_ref, bf16[528,128]{1,0:T(8,128)(2,1)S(1)} %collective-permute-done.12.refs_0_, bf16[512,128]{1,0:T(8,128)(2,1)S(1)} %collective-permute-done.14.refs_1_, ...), custom_call_target="tpu_custom_call" | custom-call | flops 402653184 | bytes 2097152 | tf_op jit(solution)/shard_map/absorb/pallas_call | solution.py:254
  25.0 1.1 %absorb.14.refs_2_ = f32[8,768]{1,0:T(8,128)S(1)} custom-call(bf16[768,1024]{1,0:T(8,128)(2,1)S(1)} %get-tuple-element.25.observed_ref, f32[10,768]{1,0:T(8,128)S(1)} %get-tuple-element.26.aux_ref, bf16[528,128]{1,0:T(8,128)(2,1)S(1)} %collective-permute-done.12.refs_0_, bf16[512,128]{1,0:T(8,128)(2,1)S(1)} %collective-permute-done.14.refs_1_, ...), custom_call_target="tpu_custom_call" | custom-call | flops 402653184 | bytes 2097152 | tf_op jit(solution)/shard_map/absorb/pallas_call | solution.py:254
  26.1 0.9 %absorb.16.refs_2_ = f32[8,768]{1,0:T(8,128)S(1)} custom-call(bf16[768,1024]{1,0:T(8,128)(2,1)S(1)} %get-tuple-element.25.observed_ref, f32[10,768]{1,0:T(8,128)S(1)} %get-tuple-element.26.aux_ref, bf16[528,128]{1,0:T(8,128)(2,1)S(1)} %collective-permute-done.13.refs_0_, bf16[512,128]{1,0:T(8,128)(2,1)S(1)} %collective-permute-done.15.refs_1_, ...), custom_call_target="tpu_custom_call" | custom-call | flops 201326592 | bytes 1835008 | tf_op jit(solution)/shard_map/absorb/pallas_call | solution.py:254
  27.0 0.9 %absorb.17.refs_2_ = f32[8,768]{1,0:T(8,128)S(1)} custom-call(bf16[768,1024]{1,0:T(8,128)(2,1)S(1)} %collective-permute-done.2.observed_ref, f32[10,768]{1,0:T(8,128)S(1)} %collective-permute-done.3.aux_ref, bf16[528,128]{1,0:T(8,128)(2,1)S(1)} %collective-permute-done.13.refs_0_, bf16[512,128]{1,0:T(8,128)(2,1)S(1)} %collective-permute-done.15.refs_1_, ...), custom_call_target="tpu_custom_call" | custom-call | flops 201326592 | bytes 1835008 | tf_op jit(solution)/shard_map/absorb/pallas_call | solution.py:254
  28.1 0.9 %absorb.19 = f32[8,768]{1,0:T(8,128)S(1)} custom-call(bf16[768,1024]{1,0:T(8,128)(2,1)S(1)} %collective-permute-done.2.observed_ref, f32[10,768]{1,0:T(8,128)S(1)} %collective-permute-done.3.aux_ref, bf16[528,128]{1,0:T(8,128)(2,1)S(1)} %collective-permute-done.9.refs_0_, bf16[512,128]{1,0:T(8,128)(2,1)S(1)} %collective-permute-done.11.refs_1_, ...), custom_call_target="tpu_custom_call" | custom-call | flops 201326592 | bytes 1835008 | tf_op jit(solution)/shard_map/absorb/pallas_call | solution.py:254
  29.1 0.9 %absorb.18.mine_ref = f32[8,768]{1,0:T(8,128)S(1)} custom-call(bf16[768,1024]{1,0:T(8,128)(2,1)S(1)} %get-tuple-element.25.observed_ref, f32[10,768]{1,0:T(8,128)S(1)} %get-tuple-element.26.aux_ref, bf16[528,128]{1,0:T(8,128)(2,1)S(1)} %collective-permute-done.9.refs_0_, bf16[512,128]{1,0:T(8,128)(2,1)S(1)} %collective-permute-done.11.refs_1_, ...), custom_call_target="tpu_custom_call" | custom-call | flops 201326592 | bytes 1835008 | tf_op jit(solution)/shard_map/absorb/pallas_call | solution.py:254
  30.2 0.6 %finish.1 = (f32[4,768]{1,0:T(4,128)}, f32[768]{0:T(1024)}) custom-call(f32[8,768]{1,0:T(8,128)S(1)} %absorb.18.mine_ref, f32[8,768]{1,0:T(8,128)S(1)} %collective-permute-done.16.other_ref, f32[10,768]{1,0:T(8,128)S(1)} %get-tuple-element.26.aux_ref), custom_call_target="tpu_custom_call" | custom-call | tf_op jit(solution)/shard_map/finish/pallas_call | solution.py:291
  (23 shorter events, 1.7 us)
Async XLA Ops:
  0.6 14.1 %collective-permute-start.2 = (bf16[768,1024]{1,0:T(8,128)(2,1)}, bf16[768,1024]{1,0:T(8,128)(2,1)S(1)}, u32[]{:S(2)}, u32[]{:S(2)}) collective-permute-start(bf16[768,1024]{1,0:T(8,128)(2,1)} %observed_hbm.1), channel_id=1, source_target_pairs={{0,1},{1,0},{2,3},{3,2},{4,5},{5,4},{6,7},{7,6},{8,9},{9,8},{10,11... | collective-permute-start | bytes 4718600 | tf_op jit(solution)/shard_map/ppermute | solution.py:246
  2.1 6.5 %collective-permute-start = (bf16[528,128]{1,0:T(8,128)(2,1)S(1)}, bf16[528,128]{1,0:T(8,128)(2,1)S(1)}, u32[]{:S(2)}, u32[]{:S(2)}) collective-permute-start(bf16[528,128]{1,0:T(8,128)(2,1)S(1)} %get-tuple-element.29.refs_0_), channel_id=1, source_target_pairs={{0,5},{1,2},{2,1},{3,6},{4,9},{5,0},{6,3},{7,10},{8,13},{9,4},{10,... | collective-permute-start | bytes 405512 | tf_op jit(solution)/shard_map/ppermute | solution.py:223
  4.9 5.4 %collective-permute-start.4 = (bf16[512,128]{1,0:T(8,128)(2,1)S(1)}, bf16[512,128]{1,0:T(8,128)(2,1)S(1)}, u32[]{:S(2)}, u32[]{:S(2)}) collective-permute-start(bf16[512,128]{1,0:T(8,128)(2,1)S(1)} %get-tuple-element.30.refs_1_), channel_id=1, source_target_pairs={{0,5},{1,2},{2,1},{3,6},{4,9},{5,0},{6,3},{7,10},{8,13},{9,4},{10,... | collective-permute-start | bytes 393224 | tf_op jit(solution)/shard_map/ppermute | solution.py:223
  6.8 4.5 %collective-permute-start.7 = (bf16[512,128]{1,0:T(8,128)(2,1)S(1)}, bf16[512,128]{1,0:T(8,128)(2,1)S(1)}, u32[]{:S(2)}, u32[]{:S(2)}) collective-permute-start(bf16[512,128]{1,0:T(8,128)(2,1)S(1)} %get-tuple-element.30.refs_1_), channel_id=1, source_target_pairs={{0,3},{1,4},{2,7},{3,0},{4,1},{5,8},{6,11},{7,2},{8,5},{9,12},{10,... | collective-permute-start | bytes 393224 | tf_op jit(solution)/shard_map/ppermute | solution.py:223
  8.5 4.4 %collective-permute-start.6 = (bf16[528,128]{1,0:T(8,128)(2,1)S(1)}, bf16[528,128]{1,0:T(8,128)(2,1)S(1)}, u32[]{:S(2)}, u32[]{:S(2)}) collective-permute-start(bf16[528,128]{1,0:T(8,128)(2,1)S(1)} %get-tuple-element.29.refs_0_), channel_id=1, source_target_pairs={{0,3},{1,4},{2,7},{3,0},{4,1},{5,8},{6,11},{7,2},{8,5},{9,12},{10,... | collective-permute-start | bytes 405512 | tf_op jit(solution)/shard_map/ppermute | solution.py:223
  8.7 7.0 %collective-permute-start.1 = (bf16[528,128]{1,0:T(8,128)(2,1)S(1)}, bf16[528,128]{1,0:T(8,128)(2,1)S(1)}, u32[]{:S(2)}, u32[]{:S(2)}) collective-permute-start(bf16[528,128]{1,0:T(8,128)(2,1)S(1)} %collective-permute-done.refs_2_), channel_id=1, source_target_pairs={{0,3},{1,4},{2,7},{3,0},{4,1},{5,8},{6,11},{7,2},{8,5},{9,12},{10,... | collective-permute-start | bytes 405512 | tf_op jit(solution)/shard_map/ppermute | solution.py:223
  10.3 7.2 %collective-permute-start.8 = (bf16[512,128]{1,0:T(8,128)(2,1)S(1)}, bf16[512,128]{1,0:T(8,128)(2,1)S(1)}, u32[]{:S(2)}, u32[]{:S(2)}) collective-permute-start(bf16[512,128]{1,0:T(8,128)(2,1)S(1)} %collective-permute-done.4.refs_3_), channel_id=1, source_target_pairs={{0,3},{1,4},{2,7},{3,0},{4,1},{5,8},{6,11},{7,2},{8,5},{9,12},{10,... | collective-permute-start | bytes 393224 | tf_op jit(solution)/shard_map/ppermute | solution.py:223
  11.3 3.4 %collective-permute-start.3 = (f32[10,768]{1,0:T(8,128)S(1)}, f32[10,768]{1,0:T(8,128)S(1)}, u32[]{:S(2)}, u32[]{:S(2)}) collective-permute-start(f32[10,768]{1,0:T(8,128)S(1)} %get-tuple-element.27), channel_id=1, source_target_pairs={{0,1},{1,0},{2,3},{3,2},{4,5},{5,4},{6,7},{7,6},{8,9},{9,8},{10,11... | collective-permute-start | bytes 92168 | tf_op jit(solution)/shard_map/ppermute | solution.py:247
  12.9 6.2 %collective-permute-start.12 = (bf16[528,128]{1,0:T(8,128)(2,1)S(1)}, bf16[528,128]{1,0:T(8,128)(2,1)S(1)}, u32[]{:S(2)}, u32[]{:S(2)}) collective-permute-start(bf16[528,128]{1,0:T(8,128)(2,1)S(1)} %collective-permute-done.6.refs_0_), channel_id=1, source_target_pairs={{0,5},{1,2},{2,1},{3,6},{4,9},{5,0},{6,3},{7,10},{8,13},{9,4},{10,... | collective-permute-start | bytes 405512 | tf_op jit(solution)/shard_map/ppermute | solution.py:223
  14.7 4.4 %collective-permute-start.14 = (bf16[512,128]{1,0:T(8,128)(2,1)S(1)}, bf16[512,128]{1,0:T(8,128)(2,1)S(1)}, u32[]{:S(2)}, u32[]{:S(2)}) collective-permute-start(bf16[512,128]{1,0:T(8,128)(2,1)S(1)} %collective-permute-done.7.refs_1_), channel_id=1, source_target_pairs={{0,5},{1,2},{2,1},{3,6},{4,9},{5,0},{6,3},{7,10},{8,13},{9,4},{10,... | collective-permute-start | bytes 393224 | tf_op jit(solution)/shard_map/ppermute | solution.py:223
  15.7 6.3 %collective-permute-start.5 = (bf16[528,128]{1,0:T(8,128)(2,1)S(1)}, bf16[528,128]{1,0:T(8,128)(2,1)S(1)}, u32[]{:S(2)}, u32[]{:S(2)}) collective-permute-start(bf16[528,128]{1,0:T(8,128)(2,1)S(1)} %collective-permute-done.1.refs_2_), channel_id=1, source_target_pairs={{0,5},{1,2},{2,1},{3,6},{4,9},{5,0},{6,3},{7,10},{8,13},{9,4},{10,... | collective-permute-start | bytes 405512 | tf_op jit(solution)/shard_map/ppermute | solution.py:223
  17.4 6.3 %collective-permute-start.10 = (bf16[512,128]{1,0:T(8,128)(2,1)S(1)}, bf16[512,128]{1,0:T(8,128)(2,1)S(1)}, u32[]{:S(2)}, u32[]{:S(2)}) collective-permute-start(bf16[512,128]{1,0:T(8,128)(2,1)S(1)} %collective-permute-done.8.refs_3_), channel_id=1, source_target_pairs={{0,5},{1,2},{2,1},{3,6},{4,9},{5,0},{6,3},{7,10},{8,13},{9,4},{10,... | collective-permute-start | bytes 393224 | tf_op jit(solution)/shard_map/ppermute | solution.py:223
  19.1 7.0 %collective-permute-start.13 = (bf16[528,128]{1,0:T(8,128)(2,1)S(1)}, bf16[528,128]{1,0:T(8,128)(2,1)S(1)}, u32[]{:S(2)}, u32[]{:S(2)}) collective-permute-start(bf16[528,128]{1,0:T(8,128)(2,1)S(1)} %collective-permute-done.12.refs_0_), channel_id=1, source_target_pairs={{0,3},{1,4},{2,7},{3,0},{4,1},{5,8},{6,11},{7,2},{8,5},{9,12},{10,... | collective-permute-start | bytes 405512 | tf_op jit(solution)/shard_map/ppermute | solution.py:223
  20.8 5.3 %collective-permute-start.15 = (bf16[512,128]{1,0:T(8,128)(2,1)S(1)}, bf16[512,128]{1,0:T(8,128)(2,1)S(1)}, u32[]{:S(2)}, u32[]{:S(2)}) collective-permute-start(bf16[512,128]{1,0:T(8,128)(2,1)S(1)} %collective-permute-done.14.refs_1_), channel_id=1, source_target_pairs={{0,3},{1,4},{2,7},{3,0},{4,1},{5,8},{6,11},{7,2},{8,5},{9,12},{10,... | collective-permute-start | bytes 393224 | tf_op jit(solution)/shard_map/ppermute | solution.py:223
  22.0 6.1 %collective-permute-start.9 = (bf16[528,128]{1,0:T(8,128)(2,1)S(1)}, bf16[528,128]{1,0:T(8,128)(2,1)S(1)}, u32[]{:S(2)}, u32[]{:S(2)}) collective-permute-start(bf16[528,128]{1,0:T(8,128)(2,1)S(1)} %collective-permute-done.5.refs_2_), channel_id=1, source_target_pairs={{0,3},{1,4},{2,7},{3,0},{4,1},{5,8},{6,11},{7,2},{8,5},{9,12},{10,... | collective-permute-start | bytes 405512 | tf_op jit(solution)/shard_map/ppermute | solution.py:223
  23.7 4.4 %collective-permute-start.11 = (bf16[512,128]{1,0:T(8,128)(2,1)S(1)}, bf16[512,128]{1,0:T(8,128)(2,1)S(1)}, u32[]{:S(2)}, u32[]{:S(2)}) collective-permute-start(bf16[512,128]{1,0:T(8,128)(2,1)S(1)} %collective-permute-done.10.refs_3_), channel_id=1, source_target_pairs={{0,3},{1,4},{2,7},{3,0},{4,1},{5,8},{6,11},{7,2},{8,5},{9,12},{10,... | collective-permute-start | bytes 393224 | tf_op jit(solution)/shard_map/ppermute | solution.py:223
  29.0 1.2 %collective-permute-start.16 = (f32[8,768]{1,0:T(8,128)S(1)}, f32[8,768]{1,0:T(8,128)S(1)}, u32[]{:S(2)}, u32[]{:S(2)}) collective-permute-start(f32[8,768]{1,0:T(8,128)S(1)} %absorb.19), channel_id=1, source_target_pairs={{0,1},{1,0},{2,3},{3,2},{4,5},{5,4},{6,7},{7,6},{8,9},{9,8},{10,11... | collective-permute-start | bytes 73736 | tf_op jit(solution)/shard_map/ppermute | solution.py:290

commit v10 on v9

--- a/solution.py
+++ b/solution.py
@@ -114,11 +114,9 @@
             out_ref[step : step + 1, :] = jnp.concatenate(opened, axis=1)
         out_ref[devices // 2 : devices // 2 + 1, :] = scale
     copies[3].wait()
-    own_ref[devices // 2 + 1 : devices // 2 + 2, :] = norms(observed_ref[...])
-    sib_ref[devices // 2 + 1 : devices // 2 + 2, :] = scale
-
-
-def absorb_kernel(steps, count, first, observed_ref, aux_ref, *refs):
+
+
+def absorb_kernel(steps, count, first, with_norms, observed_ref, aux_ref, *refs):
     count_refs = 2 * len(steps)
     packet_refs, out_ref = list(zip(refs[:count_refs:2], refs[1:count_refs:2])), refs[-1]
     panels = observed_ref.shape[1] // LANES
@@ -131,7 +129,7 @@
         joined(blocks, 0), observed_ref[...], (((1,), (1,)), ((), ())), preferred_element_type=jnp.float32
     )
     metas = [upper[half * count :, :] for upper, _ in packet_refs]
-    after_steps = aux_ref.shape[0] - 2
+    after_steps = aux_ref.shape[0] - 1
     scale = aux_ref[after_steps : after_steps + 1, :]
     if first:
         top = jnp.full(scale.shape, NEG_START, jnp.float32)
@@ -142,7 +140,7 @@
     for i, (step, block, meta) in enumerate(zip(steps, blocks, metas)):
         wide = block.astype(jnp.float32)
         half_square = 0.5 * jnp.sum(wide * wide, axis=1, keepdims=True)
-        classes = meta[META_ROWS // 2 :].astype(jnp.float32)
+        classes = meta.astype(jnp.float32)[META_ROWS // 2 :]
         column = jnp.concatenate([classes] * (count // SUBLANES), axis=0).T[:, 0:1]
         active = column == aux_ref[step : step + 1, :]
         score = jnp.where(active, inner[i * count : (i + 1) * count] - half_square, -jnp.inf)
@@ -161,11 +159,14 @@
     out_ref[0:1, :] = top
     out_ref[1:2, :] = total
     out_ref[2:6, :] = sums
-    out_ref[6:8, :] = jnp.zeros_like(out_ref[6:8, :])
+    if with_norms:
+        out_ref[6:8, :] = jnp.broadcast_to(norms(observed_ref[...]), out_ref[6:8, :].shape)
+    else:
+        out_ref[6:8, :] = jnp.zeros_like(out_ref[6:8, :]) if first else state_ref[6:8, :]
 
 
 def finish_kernel(size, mine_ref, other_ref, aux_ref, mean_ref, evidence_ref):
-    after_steps = aux_ref.shape[0] - 2
+    after_steps = aux_ref.shape[0] - 1
     scale = aux_ref[after_steps : after_steps + 1, :]
     top_a, top_b = mine_ref[0:1, :], other_ref[0:1, :]
     top = jnp.maximum(top_a, top_b)
@@ -175,7 +176,7 @@
     sums = mine_ref[2:6, :] * factor_a + other_ref[2:6, :] * factor_b
     mean_ref[...] = sums / total
     sharp = scale * (0.5 / LOG2E)
-    evidence = sharp * (2.0 * size - aux_ref[after_steps + 1 : after_steps + 2, :] + 2.0 * top) + jnp.log(total)
+    evidence = sharp * (2.0 * size - mine_ref[6:7, :] + 2.0 * top) + jnp.log(total)
     evidence_ref[...] = evidence.reshape(evidence_ref.shape)
 
 
@@ -227,8 +228,8 @@
     own_aux, sib_aux, observed_own = pl.pallas_call(
         functools.partial(prepare_kernel, block_of),
         out_shape=(
-            jax.ShapeDtypeStruct((steps + 2, rows), f32),
-            jax.ShapeDtypeStruct((steps + 2, rows), f32),
+            jax.ShapeDtypeStruct((steps + 1, rows), f32),
+            jax.ShapeDtypeStruct((steps + 1, rows), f32),
             jax.ShapeDtypeStruct(observed.shape, observed.dtype),
         ),
         in_specs=[smem] + [hbm] * 4,
@@ -252,7 +253,7 @@
         observed_half, aux = (observed_sib, sib_aux) if half else (observed_own, own_aux)
         before = () if state is None else (state,)
         return pl.pallas_call(
-            functools.partial(absorb_kernel, work, count, state is None),
+            functools.partial(absorb_kernel, work, count, state is None, half == 0 and work == (steps - 2,)),
             out_shape=jax.ShapeDtypeStruct((SUBLANES, rows), f32),
             in_specs=[vmem] * (2 + 2 * len(work) + len(before)),
             out_specs=vmem,
@@ -269,8 +270,9 @@
     for block in range(1, steps - 2, 2):
         pair = (block - 1, block)
         works[block - 1].append((pair, 0))
-        works[block if block < steps - 3 else block - 1].append((pair, 1))
-    works[steps - 3] += [((steps - 2,), 0), ((steps - 2,), 1)]
+        if block < steps - 3:
+            works[block].append((pair, 1))
+    works[steps - 3] += [((steps - 2,), 0), ((*pair, steps - 2), 1)]
     works[steps - 2] += [((steps - 1,), 1), ((steps - 1,), 0)]
     states = [None, None]
     done = []

time: 31.1 us -> 30.5 us (0.981)
  starting transfers between devices: 14.9 us -> 16.2 us
  waiting for transfers between devices: 1.88 us -> 0.77 us
  Pallas kernels: 13.4 us -> 12.6 us
    ppermute x14, starting transfers between devices: 14.1 us -> 15.6 us  [send(): lax.ppermute(part, 'blk', pairs[(kind + step // 2) % 2])]
    ppermute x14, waiting for transfers between devices: 1.68 us -> 0.5 us  [send(): lax.ppermute(part, 'blk', pairs[(kind + step // 2) % 2])]
    pallas_call x10 -> x9, Pallas kernels: 9.94 us -> 9.51 us  [absorb(): pl.pallas_call(functools.partial(absorb_kernel, work, count, state is Non...]
    pallas_call x1, Pallas kernels: 1.85 us -> 1.47 us  [on_device(): pl.pallas_call(functools.partial(prepare_kernel, block_of), out_shape=(ja...]
  transfers between devices with their start and end apart: 17 -> 17, of which waited for: 5 -> 2; matrix products, arithmetic and copies ran while one was open for 0% -> 0% of each run, Pallas kernels for 39% -> 37%
where the time goes in v10:
time: 30.5 us; the launch traced here: 30.3 us
  starting transfers between devices  16.2 us (53%)
  Pallas kernels  12.6 us (41%)
  waiting for transfers between devices  0.77 us (3%)
  between operations  0.7 us (2%)
    ppermute x14, starting transfers between devices, send(): lax.ppermute(part, 'blk', pairs[(kind + step // 2) % 2])  15.6 us
    pallas_call x9, Pallas kernels, absorb(): pl.pallas_call(functools.partial(absorb_kernel, work, count, state is Non...  9.51 us
    pallas_call x1, Pallas kernels, on_device(): pl.pallas_call(functools.partial(prepare_kernel, block_of), out_shape=(ja...  1.47 us
    pallas_call x1, Pallas kernels, on_device(): pl.pallas_call(pack_kernel, out_shape=[jax.ShapeDtypeStruct((count * size...  0.99 us
    pallas_call x1, Pallas kernels, on_device(): pl.pallas_call(functools.partial(finish_kernel, size), out_shape=(jax.Sha...  0.63 us
  transfers between devices with their start and end apart: 17, of which 2 were waited for; matrix products, arithmetic and copies ran while one was open for 0% of the time, Pallas kernels for 37%

profile of v10, /device:TPU:0, one launch (start us, length us, event | category | flops | bytes accessed | tf_op | source)
XLA Modules:
  0.0 30.3 jit_solution(10711365466858447406)
XLA Ops:
  0.6 0.5 %collective-permute-start.2 = (bf16[768,1024]{1,0:T(8,128)(2,1)}, bf16[768,1024]{1,0:T(8,128)(2,1)S(1)}, u32[]{:S(2)}, u32[]{:S(2)}) collective-permute-start(bf16[768,1024]{1,0:T(8,128)(2,1)} %observed_hbm.1), channel_id=1, source_target_pairs={{0,1},{1,0},{2,3},{3,2},{4,5},{5,4},{6,7},{7,6},{8,9},{9,8},{10,11... | collective-permute-start | bytes 4718600 | tf_op jit(solution)/shard_map/ppermute | solution.py:247
  1.1 1.0 %pack.1 = (bf16[528,128]{1,0:T(8,128)(2,1)S(1)}, bf16[512,128]{1,0:T(8,128)(2,1)S(1)}) custom-call(bf16[4,128]{1,0:T(4,128)(2,1)} %params_hbm.1, s32[128]{0:T(128)} %class_hbm.2, bf16[128,1024]{1,0:T(8,128)(2,1)} %evolved_hbm.1), custom_call_target="tpu_custom_call" | custom-call | tf_op jit(solution)/shard_map/pack/pallas_call | solution.py:204
  2.1 2.8 %collective-permute-start = (bf16[528,128]{1,0:T(8,128)(2,1)S(1)}, bf16[528,128]{1,0:T(8,128)(2,1)S(1)}, u32[]{:S(2)}, u32[]{:S(2)}) collective-permute-start(bf16[528,128]{1,0:T(8,128)(2,1)S(1)} %get-tuple-element.29.refs_0_), channel_id=1, source_target_pairs={{0,5},{1,2},{2,1},{3,6},{4,9},{5,0},{6,3},{7,10},{8,13},{9,4},{10,... | collective-permute-start | bytes 405512 | tf_op jit(solution)/shard_map/ppermute | solution.py:224
  5.0 1.5 %prepare.1 = (f32[9,768]{1,0:T(8,128)S(1)}, f32[9,768]{1,0:T(8,128)S(1)}, bf16[768,1024]{1,0:T(8,128)(2,1)S(1)}) custom-call(s32[1]{0:T(128)} %bitcast.at_ref, s32[6,16]{1,0:T(8,128)} %pattern_hbm.1, s32[768]{0:T(1024)} %class_hbm.3, f32[768]{0:T(1024)} %sharp_hbm.1, bf16[768,1024]{1,0:T(8,128)(2,1)} %observed_hbm.1), custom_call_target="tpu_custom_call" | custom-call | flops 6291456 | bytes 3145728 | tf_op jit(solution)/shard_map/prepare/pallas_call | solution.py:228
  6.5 1.7 %collective-permute-start.6 = (bf16[528,128]{1,0:T(8,128)(2,1)S(1)}, bf16[528,128]{1,0:T(8,128)(2,1)S(1)}, u32[]{:S(2)}, u32[]{:S(2)}) collective-permute-start(bf16[528,128]{1,0:T(8,128)(2,1)S(1)} %get-tuple-element.29.refs_0_), channel_id=1, source_target_pairs={{0,3},{1,4},{2,7},{3,0},{4,1},{5,8},{6,11},{7,2},{8,5},{9,12},{10,... | collective-permute-start | bytes 405512 | tf_op jit(solution)/shard_map/ppermute | solution.py:224
  8.3 1.6 %collective-permute-start.1 = (bf16[528,128]{1,0:T(8,128)(2,1)S(1)}, bf16[528,128]{1,0:T(8,128)(2,1)S(1)}, u32[]{:S(2)}, u32[]{:S(2)}) collective-permute-start(bf16[528,128]{1,0:T(8,128)(2,1)S(1)} %collective-permute-done.refs_2_), channel_id=1, source_target_pairs={{0,3},{1,4},{2,7},{3,0},{4,1},{5,8},{6,11},{7,2},{8,5},{9,12},{10,... | collective-permute-start | bytes 405512 | tf_op jit(solution)/shard_map/ppermute | solution.py:224
  9.9 1.3 %collective-permute-start.8 = (bf16[512,128]{1,0:T(8,128)(2,1)S(1)}, bf16[512,128]{1,0:T(8,128)(2,1)S(1)}, u32[]{:S(2)}, u32[]{:S(2)}) collective-permute-start(bf16[512,128]{1,0:T(8,128)(2,1)S(1)} %collective-permute-done.4.refs_3_), channel_id=1, source_target_pairs={{0,3},{1,4},{2,7},{3,0},{4,1},{5,8},{6,11},{7,2},{8,5},{9,12},{10,... | collective-permute-start | bytes 393224 | tf_op jit(solution)/shard_map/ppermute | solution.py:224
  11.2 1.0 %absorb.11.refs_4_ = f32[8,768]{1,0:T(8,128)S(1)} custom-call(bf16[768,1024]{1,0:T(8,128)(2,1)S(1)} %get-tuple-element.25.observed_ref, f32[9,768]{1,0:T(8,128)S(1)} %get-tuple-element.26.aux_ref, bf16[528,128]{1,0:T(8,128)(2,1)S(1)} %get-tuple-element.29.refs_0_, bf16[512,128]{1,0:T(8,128)(2,1)S(1)} %get-tuple-element.30.refs_1_, ...), custom_call_target="tpu_custom_call" | custom-call | flops 402653184 | bytes 2097152 | tf_op jit(solution)/shard_map/absorb/pallas_call | solution.py:255
  12.1 0.4 %collective-permute-done.7.refs_1_ = bf16[512,128]{1,0:T(8,128)(2,1)S(1)} collective-permute-done((bf16[512,128]{1,0:T(8,128)(2,1)S(1)}, bf16[512,128]{1,0:T(8,128)(2,1)S(1)}, u32[]{:S(2)}, u32[]{:S(2)}) %collective-permute-start.7) | collective-permute-done | bytes 131104 | tf_op jit(solution)/shard_map/ppermute | solution.py:224
  12.5 1.8 %collective-permute-start.12 = (bf16[528,128]{1,0:T(8,128)(2,1)S(1)}, bf16[528,128]{1,0:T(8,128)(2,1)S(1)}, u32[]{:S(2)}, u32[]{:S(2)}) collective-permute-start(bf16[528,128]{1,0:T(8,128)(2,1)S(1)} %collective-permute-done.6.refs_0_), channel_id=1, source_target_pairs={{0,5},{1,2},{2,1},{3,6},{4,9},{5,0},{6,3},{7,10},{8,13},{9,4},{10,... | collective-permute-start | bytes 405512 | tf_op jit(solution)/shard_map/ppermute | solution.py:224
  14.4 1.0 %absorb.9.refs_4_ = f32[8,768]{1,0:T(8,128)S(1)} custom-call(bf16[768,1024]{1,0:T(8,128)(2,1)S(1)} %collective-permute-done.2.observed_ref, f32[9,768]{1,0:T(8,128)S(1)} %collective-permute-done.3.aux_ref, bf16[528,128]{1,0:T(8,128)(2,1)S(1)} %get-tuple-element.29.refs_0_, bf16[512,128]{1,0:T(8,128)(2,1)S(1)} %get-tuple-element.30.refs_1_, ...), custom_call_target="tpu_custom_call" | custom-call | flops 402653184 | bytes 2097152 | tf_op jit(solution)/shard_map/absorb/pallas_call | solution.py:255
  15.3 1.7 %collective-permute-start.5 = (bf16[528,128]{1,0:T(8,128)(2,1)S(1)}, bf16[528,128]{1,0:T(8,128)(2,1)S(1)}, u32[]{:S(2)}, u32[]{:S(2)}) collective-permute-start(bf16[528,128]{1,0:T(8,128)(2,1)S(1)} %collective-permute-done.1.refs_2_), channel_id=1, source_target_pairs={{0,5},{1,2},{2,1},{3,6},{4,9},{5,0},{6,3},{7,10},{8,13},{9,4},{10,... | collective-permute-start | bytes 405512 | tf_op jit(solution)/shard_map/ppermute | solution.py:224
  17.3 1.1 %absorb.12.refs_4_ = f32[8,768]{1,0:T(8,128)S(1)} custom-call(bf16[768,1024]{1,0:T(8,128)(2,1)S(1)} %get-tuple-element.25.observed_ref, f32[9,768]{1,0:T(8,128)S(1)} %get-tuple-element.26.aux_ref, bf16[528,128]{1,0:T(8,128)(2,1)S(1)} %collective-permute-done.6.refs_0_, bf16[512,128]{1,0:T(8,128)(2,1)S(1)} %collective-permute-done.7.refs_1_, ...), custom_call_target="tpu_custom_call" | custom-call | flops 402653184 | bytes 2097152 | tf_op jit(solution)/shard_map/absorb/pallas_call | solution.py:255
  18.4 1.5 %collective-permute-start.13 = (bf16[528,128]{1,0:T(8,128)(2,1)S(1)}, bf16[528,128]{1,0:T(8,128)(2,1)S(1)}, u32[]{:S(2)}, u32[]{:S(2)}) collective-permute-start(bf16[528,128]{1,0:T(8,128)(2,1)S(1)} %collective-permute-done.12.refs_0_), channel_id=1, source_target_pairs={{0,3},{1,4},{2,7},{3,0},{4,1},{5,8},{6,11},{7,2},{8,5},{9,12},{10,... | collective-permute-start | bytes 405512 | tf_op jit(solution)/shard_map/ppermute | solution.py:224
  19.9 0.5 %collective-permute-start.15 = (bf16[512,128]{1,0:T(8,128)(2,1)S(1)}, bf16[512,128]{1,0:T(8,128)(2,1)S(1)}, u32[]{:S(2)}, u32[]{:S(2)}) collective-permute-start(bf16[512,128]{1,0:T(8,128)(2,1)S(1)} %collective-permute-done.14.refs_1_), channel_id=1, source_target_pairs={{0,3},{1,4},{2,7},{3,0},{4,1},{5,8},{6,11},{7,2},{8,5},{9,12},{10,... | collective-permute-start | bytes 393224 | tf_op jit(solution)/shard_map/ppermute | solution.py:224
  20.4 1.1 %absorb.10.refs_6_ = f32[8,768]{1,0:T(8,128)S(1)} custom-call(bf16[768,1024]{1,0:T(8,128)(2,1)S(1)} %collective-permute-done.2.observed_ref, f32[9,768]{1,0:T(8,128)S(1)} %collective-permute-done.3.aux_ref, bf16[528,128]{1,0:T(8,128)(2,1)S(1)} %collective-permute-done.6.refs_0_, bf16[512,128]{1,0:T(8,128)(2,1)S(1)} %collective-permute-done.7.refs_1_, ...), custom_call_target="tpu_custom_call" | custom-call | flops 402653184 | bytes 2097152 | tf_op jit(solution)/shard_map/absorb/pallas_call | solution.py:255
  21.5 1.3 %collective-permute-start.9 = (bf16[528,128]{1,0:T(8,128)(2,1)S(1)}, bf16[528,128]{1,0:T(8,128)(2,1)S(1)}, u32[]{:S(2)}, u32[]{:S(2)}) collective-permute-start(bf16[528,128]{1,0:T(8,128)(2,1)S(1)} %collective-permute-done.5.refs_2_), channel_id=1, source_target_pairs={{0,3},{1,4},{2,7},{3,0},{4,1},{5,8},{6,11},{7,2},{8,5},{9,12},{10,... | collective-permute-start | bytes 405512 | tf_op jit(solution)/shard_map/ppermute | solution.py:224
  22.8 1.0 %collective-permute-start.11 = (bf16[512,128]{1,0:T(8,128)(2,1)S(1)}, bf16[512,128]{1,0:T(8,128)(2,1)S(1)}, u32[]{:S(2)}, u32[]{:S(2)}) collective-permute-start(bf16[512,128]{1,0:T(8,128)(2,1)S(1)} %collective-permute-done.10.refs_3_), channel_id=1, source_target_pairs={{0,3},{1,4},{2,7},{3,0},{4,1},{5,8},{6,11},{7,2},{8,5},{9,12},{10,... | collective-permute-start | bytes 393224 | tf_op jit(solution)/shard_map/ppermute | solution.py:224
  23.9 1.1 %absorb.13.refs_2_ = f32[8,768]{1,0:T(8,128)S(1)} custom-call(bf16[768,1024]{1,0:T(8,128)(2,1)S(1)} %get-tuple-element.25.observed_ref, f32[9,768]{1,0:T(8,128)S(1)} %get-tuple-element.26.aux_ref, bf16[528,128]{1,0:T(8,128)(2,1)S(1)} %collective-permute-done.12.refs_0_, bf16[512,128]{1,0:T(8,128)(2,1)S(1)} %collective-permute-done.14.refs_1_, ...), custom_call_target="tpu_custom_call" | custom-call | flops 402653184 | bytes 2097152 | tf_op jit(solution)/shard_map/absorb/pallas_call | solution.py:255
  25.0 1.1 %absorb.14.refs_2_ = f32[8,768]{1,0:T(8,128)S(1)} custom-call(bf16[768,1024]{1,0:T(8,128)(2,1)S(1)} %get-tuple-element.25.observed_ref, f32[9,768]{1,0:T(8,128)S(1)} %get-tuple-element.26.aux_ref, bf16[528,128]{1,0:T(8,128)(2,1)S(1)} %collective-permute-done.13.refs_0_.refs_4_, bf16[512,128]{1,0:T(8,128)(2,1)S(1)} %collective-permute-done.15.refs_1_.refs_5_, ...), custom_call_target="tpu_custom_call" | custom-call | flops 201326592 | bytes 1835008 | tf_op jit(solution)/shard_map/absorb/pallas_call | solution.py:255
  26.1 1.4 %absorb.15.refs_2_ = f32[8,768]{1,0:T(8,128)S(1)} custom-call(bf16[768,1024]{1,0:T(8,128)(2,1)S(1)} %collective-permute-done.2.observed_ref, f32[9,768]{1,0:T(8,128)S(1)} %collective-permute-done.3.aux_ref, bf16[528,128]{1,0:T(8,128)(2,1)S(1)} %collective-permute-done.12.refs_0_, bf16[512,128]{1,0:T(8,128)(2,1)S(1)} %collective-permute-done.14.refs_1_, ...), custom_call_target="tpu_custom_call" | custom-call | flops 603979776 | bytes 2359296 | tf_op jit(solution)/shard_map/absorb/pallas_call | solution.py:255
  27.6 0.9 %absorb.17 = f32[8,768]{1,0:T(8,128)S(1)} custom-call(bf16[768,1024]{1,0:T(8,128)(2,1)S(1)} %collective-permute-done.2.observed_ref, f32[9,768]{1,0:T(8,128)S(1)} %collective-permute-done.3.aux_ref, bf16[528,128]{1,0:T(8,128)(2,1)S(1)} %collective-permute-done.9.refs_0_, bf16[512,128]{1,0:T(8,128)(2,1)S(1)} %collective-permute-done.11.refs_1_, ...), custom_call_target="tpu_custom_call" | custom-call | flops 201326592 | bytes 1835008 | tf_op jit(solution)/shard_map/absorb/pallas_call | solution.py:255
  28.5 0.9 %absorb.16.mine_ref = f32[8,768]{1,0:T(8,128)S(1)} custom-call(bf16[768,1024]{1,0:T(8,128)(2,1)S(1)} %get-tuple-element.25.observed_ref, f32[9,768]{1,0:T(8,128)S(1)} %get-tuple-element.26.aux_ref, bf16[528,128]{1,0:T(8,128)(2,1)S(1)} %collective-permute-done.9.refs_0_, bf16[512,128]{1,0:T(8,128)(2,1)S(1)} %collective-permute-done.11.refs_1_, ...), custom_call_target="tpu_custom_call" | custom-call | flops 201326592 | bytes 1835008 | tf_op jit(solution)/shard_map/absorb/pallas_call | solution.py:255
  29.7 0.6 %finish.1 = (f32[4,768]{1,0:T(4,128)}, f32[768]{0:T(1024)}) custom-call(f32[8,768]{1,0:T(8,128)S(1)} %absorb.16.mine_ref, f32[8,768]{1,0:T(8,128)S(1)} %collective-permute-done.16.other_ref, f32[9,768]{1,0:T(8,128)S(1)} %get-tuple-element.26.aux_ref), custom_call_target="tpu_custom_call" | custom-call | tf_op jit(solution)/shard_map/finish/pallas_call | solution.py:293
  (22 shorter events, 0.9 us)
Async XLA Ops:
  0.6 13.7 %collective-permute-start.2 = (bf16[768,1024]{1,0:T(8,128)(2,1)}, bf16[768,1024]{1,0:T(8,128)(2,1)S(1)}, u32[]{:S(2)}, u32[]{:S(2)}) collective-permute-start(bf16[768,1024]{1,0:T(8,128)(2,1)} %observed_hbm.1), channel_id=1, source_target_pairs={{0,1},{1,0},{2,3},{3,2},{4,5},{5,4},{6,7},{7,6},{8,9},{9,8},{10,11... | collective-permute-start | bytes 4718600 | tf_op jit(solution)/shard_map/ppermute | solution.py:247
  2.1 6.1 %collective-permute-start = (bf16[528,128]{1,0:T(8,128)(2,1)S(1)}, bf16[528,128]{1,0:T(8,128)(2,1)S(1)}, u32[]{:S(2)}, u32[]{:S(2)}) collective-permute-start(bf16[528,128]{1,0:T(8,128)(2,1)S(1)} %get-tuple-element.29.refs_0_), channel_id=1, source_target_pairs={{0,5},{1,2},{2,1},{3,6},{4,9},{5,0},{6,3},{7,10},{8,13},{9,4},{10,... | collective-permute-start | bytes 405512 | tf_op jit(solution)/shard_map/ppermute | solution.py:224
  4.9 5.0 %collective-permute-start.4 = (bf16[512,128]{1,0:T(8,128)(2,1)S(1)}, bf16[512,128]{1,0:T(8,128)(2,1)S(1)}, u32[]{:S(2)}, u32[]{:S(2)}) collective-permute-start(bf16[512,128]{1,0:T(8,128)(2,1)S(1)} %get-tuple-element.30.refs_1_), channel_id=1, source_target_pairs={{0,5},{1,2},{2,1},{3,6},{4,9},{5,0},{6,3},{7,10},{8,13},{9,4},{10,... | collective-permute-start | bytes 393224 | tf_op jit(solution)/shard_map/ppermute | solution.py:224
  6.5 4.7 %collective-permute-start.6 = (bf16[528,128]{1,0:T(8,128)(2,1)S(1)}, bf16[528,128]{1,0:T(8,128)(2,1)S(1)}, u32[]{:S(2)}, u32[]{:S(2)}) collective-permute-start(bf16[528,128]{1,0:T(8,128)(2,1)S(1)} %get-tuple-element.29.refs_0_), channel_id=1, source_target_pairs={{0,3},{1,4},{2,7},{3,0},{4,1},{5,8},{6,11},{7,2},{8,5},{9,12},{10,... | collective-permute-start | bytes 405512 | tf_op jit(solution)/shard_map/ppermute | solution.py:224
  8.1 4.4 %collective-permute-start.7 = (bf16[512,128]{1,0:T(8,128)(2,1)S(1)}, bf16[512,128]{1,0:T(8,128)(2,1)S(1)}, u32[]{:S(2)}, u32[]{:S(2)}) collective-permute-start(bf16[512,128]{1,0:T(8,128)(2,1)S(1)} %get-tuple-element.30.refs_1_), channel_id=1, source_target_pairs={{0,3},{1,4},{2,7},{3,0},{4,1},{5,8},{6,11},{7,2},{8,5},{9,12},{10,... | collective-permute-start | bytes 393224 | tf_op jit(solution)/shard_map/ppermute | solution.py:224
  8.3 7.1 %collective-permute-start.1 = (bf16[528,128]{1,0:T(8,128)(2,1)S(1)}, bf16[528,128]{1,0:T(8,128)(2,1)S(1)}, u32[]{:S(2)}, u32[]{:S(2)}) collective-permute-start(bf16[528,128]{1,0:T(8,128)(2,1)S(1)} %collective-permute-done.refs_2_), channel_id=1, source_target_pairs={{0,3},{1,4},{2,7},{3,0},{4,1},{5,8},{6,11},{7,2},{8,5},{9,12},{10,... | collective-permute-start | bytes 405512 | tf_op jit(solution)/shard_map/ppermute | solution.py:224
  9.9 7.2 %collective-permute-start.8 = (bf16[512,128]{1,0:T(8,128)(2,1)S(1)}, bf16[512,128]{1,0:T(8,128)(2,1)S(1)}, u32[]{:S(2)}, u32[]{:S(2)}) collective-permute-start(bf16[512,128]{1,0:T(8,128)(2,1)S(1)} %collective-permute-done.4.refs_3_), channel_id=1, source_target_pairs={{0,3},{1,4},{2,7},{3,0},{4,1},{5,8},{6,11},{7,2},{8,5},{9,12},{10,... | collective-permute-start | bytes 393224 | tf_op jit(solution)/shard_map/ppermute | solution.py:224
  11.1 3.2 %collective-permute-start.3 = (f32[9,768]{1,0:T(8,128)S(1)}, f32[9,768]{1,0:T(8,128)S(1)}, u32[]{:S(2)}, u32[]{:S(2)}) collective-permute-start(f32[9,768]{1,0:T(8,128)S(1)} %get-tuple-element.27), channel_id=1, source_target_pairs={{0,1},{1,0},{2,3},{3,2},{4,5},{5,4},{6,7},{7,6},{8,9},{9,8},{10,11... | collective-permute-start | bytes 82952 | tf_op jit(solution)/shard_map/ppermute | solution.py:248
  12.5 5.9 %collective-permute-start.12 = (bf16[528,128]{1,0:T(8,128)(2,1)S(1)}, bf16[528,128]{1,0:T(8,128)(2,1)S(1)}, u32[]{:S(2)}, u32[]{:S(2)}) collective-permute-start(bf16[528,128]{1,0:T(8,128)(2,1)S(1)} %collective-permute-done.6.refs_0_), channel_id=1, source_target_pairs={{0,5},{1,2},{2,1},{3,6},{4,9},{5,0},{6,3},{7,10},{8,13},{9,4},{10,... | collective-permute-start | bytes 405512 | tf_op jit(solution)/shard_map/ppermute | solution.py:224
  14.3 5.6 %collective-permute-start.14 = (bf16[512,128]{1,0:T(8,128)(2,1)S(1)}, bf16[512,128]{1,0:T(8,128)(2,1)S(1)}, u32[]{:S(2)}, u32[]{:S(2)}) collective-permute-start(bf16[512,128]{1,0:T(8,128)(2,1)S(1)} %collective-permute-done.7.refs_1_), channel_id=1, source_target_pairs={{0,5},{1,2},{2,1},{3,6},{4,9},{5,0},{6,3},{7,10},{8,13},{9,4},{10,... | collective-permute-start | bytes 393224 | tf_op jit(solution)/shard_map/ppermute | solution.py:224
  15.3 6.2 %collective-permute-start.5 = (bf16[528,128]{1,0:T(8,128)(2,1)S(1)}, bf16[528,128]{1,0:T(8,128)(2,1)S(1)}, u32[]{:S(2)}, u32[]{:S(2)}) collective-permute-start(bf16[528,128]{1,0:T(8,128)(2,1)S(1)} %collective-permute-done.1.refs_2_), channel_id=1, source_target_pairs={{0,5},{1,2},{2,1},{3,6},{4,9},{5,0},{6,3},{7,10},{8,13},{9,4},{10,... | collective-permute-start | bytes 405512 | tf_op jit(solution)/shard_map/ppermute | solution.py:224
  17.1 5.8 %collective-permute-start.10 = (bf16[512,128]{1,0:T(8,128)(2,1)S(1)}, bf16[512,128]{1,0:T(8,128)(2,1)S(1)}, u32[]{:S(2)}, u32[]{:S(2)}) collective-permute-start(bf16[512,128]{1,0:T(8,128)(2,1)S(1)} %collective-permute-done.8.refs_3_), channel_id=1, source_target_pairs={{0,5},{1,2},{2,1},{3,6},{4,9},{5,0},{6,3},{7,10},{8,13},{9,4},{10,... | collective-permute-start | bytes 393224 | tf_op jit(solution)/shard_map/ppermute | solution.py:224
  18.4 6.6 %collective-permute-start.13 = (bf16[528,128]{1,0:T(8,128)(2,1)S(1)}, bf16[528,128]{1,0:T(8,128)(2,1)S(1)}, u32[]{:S(2)}, u32[]{:S(2)}) collective-permute-start(bf16[528,128]{1,0:T(8,128)(2,1)S(1)} %collective-permute-done.12.refs_0_), channel_id=1, source_target_pairs={{0,3},{1,4},{2,7},{3,0},{4,1},{5,8},{6,11},{7,2},{8,5},{9,12},{10,... | collective-permute-start | bytes 405512 | tf_op jit(solution)/shard_map/ppermute | solution.py:224
  19.9 5.1 %collective-permute-start.15 = (bf16[512,128]{1,0:T(8,128)(2,1)S(1)}, bf16[512,128]{1,0:T(8,128)(2,1)S(1)}, u32[]{:S(2)}, u32[]{:S(2)}) collective-permute-start(bf16[512,128]{1,0:T(8,128)(2,1)S(1)} %collective-permute-done.14.refs_1_), channel_id=1, source_target_pairs={{0,3},{1,4},{2,7},{3,0},{4,1},{5,8},{6,11},{7,2},{8,5},{9,12},{10,... | collective-permute-start | bytes 393224 | tf_op jit(solution)/shard_map/ppermute | solution.py:224
  21.5 6.0 %collective-permute-start.9 = (bf16[528,128]{1,0:T(8,128)(2,1)S(1)}, bf16[528,128]{1,0:T(8,128)(2,1)S(1)}, u32[]{:S(2)}, u32[]{:S(2)}) collective-permute-start(bf16[528,128]{1,0:T(8,128)(2,1)S(1)} %collective-permute-done.5.refs_2_), channel_id=1, source_target_pairs={{0,3},{1,4},{2,7},{3,0},{4,1},{5,8},{6,11},{7,2},{8,5},{9,12},{10,... | collective-permute-start | bytes 405512 | tf_op jit(solution)/shard_map/ppermute | solution.py:224
  22.8 4.7 %collective-permute-start.11 = (bf16[512,128]{1,0:T(8,128)(2,1)S(1)}, bf16[512,128]{1,0:T(8,128)(2,1)S(1)}, u32[]{:S(2)}, u32[]{:S(2)}) collective-permute-start(bf16[512,128]{1,0:T(8,128)(2,1)S(1)} %collective-permute-done.10.refs_3_), channel_id=1, source_target_pairs={{0,3},{1,4},{2,7},{3,0},{4,1},{5,8},{6,11},{7,2},{8,5},{9,12},{10,... | collective-permute-start | bytes 393224 | tf_op jit(solution)/shard_map/ppermute | solution.py:224
  28.4 1.2 %collective-permute-start.16 = (f32[8,768]{1,0:T(8,128)S(1)}, f32[8,768]{1,0:T(8,128)S(1)}, u32[]{:S(2)}, u32[]{:S(2)}) collective-permute-start(f32[8,768]{1,0:T(8,128)S(1)} %absorb.17), channel_id=1, source_target_pairs={{0,1},{1,0},{2,3},{3,2},{4,5},{5,4},{6,7},{7,6},{8,9},{9,8},{10,11... | collective-permute-start | bytes 73736 | tf_op jit(solution)/shard_map/ppermute | solution.py:292

commit v11 on v10

--- a/solution.py
+++ b/solution.py
@@ -244,7 +244,7 @@
         cost_estimate=pl.CostEstimate(flops=8 * rows * size, bytes_accessed=4 * rows * size, transcendentals=0),
         name="prepare",
     )(after(at, packet), *in_hbm(pattern, obs_class, sharpness, observed))
-    observed_sib = lax.ppermute(observed, "blk", core)
+    observed_sib = lax.ppermute(after(observed, packet[0]), "blk", core)
     sib_aux = lax.ppermute(sib_aux, "blk", core)
     moving[1] = after(moving[1], own_aux)
     send(1)
@@ -280,7 +280,7 @@
         ahead = step + 2
         if ahead < steps - 1:
             if done:
-                moving[ahead % 2] = [after(part, done[-1]) for part in moving[ahead % 2]]
+                moving[ahead % 2] = [after(part, done[-2 if ahead == steps - 2 and i == 0 else -1]) for i, part in enumerate(moving[ahead % 2])]
             send(ahead)
         last = step == steps - 2
         if step >= steps - 3:

time: 30.5 us -> 30.4 us (level)
  transfers between devices with their start and end apart: 17 -> 17, of which waited for: 2 -> 2; matrix products, arithmetic and copies ran while one was open for 0% -> 0% of each run, Pallas kernels for 37% -> 33%
where the time goes in v11:
time: 30.4 us; the launch traced here: 30.2 us
  starting transfers between devices  16.3 us (54%)
  Pallas kernels  12.6 us (41%)
  between operations  0.7 us (2%)
  waiting for transfers between devices  0.57 us (2%)
    ppermute x14, starting transfers between devices, send(): lax.ppermute(part, 'blk', pairs[(kind + step // 2) % 2])  15.5 us
    pallas_call x9, Pallas kernels, absorb(): pl.pallas_call(functools.partial(absorb_kernel, work, count, state is Non...  9.5 us
    pallas_call x1, Pallas kernels, on_device(): pl.pallas_call(functools.partial(prepare_kernel, block_of), out_shape=(ja...  1.47 us
    pallas_call x1, Pallas kernels, on_device(): pl.pallas_call(pack_kernel, out_shape=[jax.ShapeDtypeStruct((count * size...  0.99 us
    pallas_call x1, Pallas kernels, on_device(): pl.pallas_call(functools.partial(finish_kernel, size), out_shape=(jax.Sha...  0.63 us
  transfers between devices with their start and end apart: 17, of which 2 were waited for; matrix products, arithmetic and copies ran while one was open for 0% of the time, Pallas kernels for 33%

profile of v11, /device:TPU:0, one launch (start us, length us, event | category | flops | bytes accessed | tf_op | source)
XLA Modules:
  0.0 30.2 jit_solution(16645578995511326978)
XLA Ops:
  0.6 1.0 %pack.1 = (bf16[528,128]{1,0:T(8,128)(2,1)S(1)}, bf16[512,128]{1,0:T(8,128)(2,1)S(1)}) custom-call(bf16[4,128]{1,0:T(4,128)(2,1)} %params_hbm.1, s32[128]{0:T(128)} %class_hbm.2, bf16[128,1024]{1,0:T(8,128)(2,1)} %evolved_hbm.1), custom_call_target="tpu_custom_call" | custom-call | tf_op jit(solution)/shard_map/pack/pallas_call | solution.py:204
  1.6 0.5 %collective-permute-start.2 = (bf16[768,1024]{1,0:T(8,128)(2,1)}, bf16[768,1024]{1,0:T(8,128)(2,1)S(1)}, u32[]{:S(2)}, u32[]{:S(2)}) collective-permute-start(bf16[768,1024]{1,0:T(8,128)(2,1)} %observed_hbm.1), channel_id=1, source_target_pairs={{0,1},{1,0},{2,3},{3,2},{4,5},{5,4},{6,7},{7,6},{8,9},{9,8},{10,11... | collective-permute-start | bytes 4718600 | tf_op jit(solution)/shard_map/ppermute | solution.py:247
  2.1 2.7 %collective-permute-start = (bf16[528,128]{1,0:T(8,128)(2,1)S(1)}, bf16[528,128]{1,0:T(8,128)(2,1)S(1)}, u32[]{:S(2)}, u32[]{:S(2)}) collective-permute-start(bf16[528,128]{1,0:T(8,128)(2,1)S(1)} %get-tuple-element.31.refs_0_), channel_id=1, source_target_pairs={{0,5},{1,2},{2,1},{3,6},{4,9},{5,0},{6,3},{7,10},{8,13},{9,4},{10,... | collective-permute-start | bytes 405512 | tf_op jit(solution)/shard_map/ppermute | solution.py:224
  4.9 1.5 %prepare.1 = (f32[9,768]{1,0:T(8,128)S(1)}, f32[9,768]{1,0:T(8,128)S(1)}, bf16[768,1024]{1,0:T(8,128)(2,1)S(1)}) custom-call(s32[1]{0:T(128)} %bitcast.at_ref, s32[6,16]{1,0:T(8,128)} %pattern_hbm.1, s32[768]{0:T(1024)} %class_hbm.3, f32[768]{0:T(1024)} %sharp_hbm.1, bf16[768,1024]{1,0:T(8,128)(2,1)} %observed_hbm.1), custom_call_target="tpu_custom_call" | custom-call | flops 6291456 | bytes 3145728 | tf_op jit(solution)/shard_map/prepare/pallas_call | solution.py:228
  6.4 1.7 %collective-permute-start.6 = (bf16[528,128]{1,0:T(8,128)(2,1)S(1)}, bf16[528,128]{1,0:T(8,128)(2,1)S(1)}, u32[]{:S(2)}, u32[]{:S(2)}) collective-permute-start(bf16[528,128]{1,0:T(8,128)(2,1)S(1)} %get-tuple-element.31.refs_0_), channel_id=1, source_target_pairs={{0,3},{1,4},{2,7},{3,0},{4,1},{5,8},{6,11},{7,2},{8,5},{9,12},{10,... | collective-permute-start | bytes 405512 | tf_op jit(solution)/shard_map/ppermute | solution.py:224
  8.2 1.7 %collective-permute-start.1 = (bf16[528,128]{1,0:T(8,128)(2,1)S(1)}, bf16[528,128]{1,0:T(8,128)(2,1)S(1)}, u32[]{:S(2)}, u32[]{:S(2)}) collective-permute-start(bf16[528,128]{1,0:T(8,128)(2,1)S(1)} %collective-permute-done.refs_2_), channel_id=1, source_target_pairs={{0,3},{1,4},{2,7},{3,0},{4,1},{5,8},{6,11},{7,2},{8,5},{9,12},{10,... | collective-permute-start | bytes 405512 | tf_op jit(solution)/shard_map/ppermute | solution.py:224
  9.8 1.2 %collective-permute-start.8 = (bf16[512,128]{1,0:T(8,128)(2,1)S(1)}, bf16[512,128]{1,0:T(8,128)(2,1)S(1)}, u32[]{:S(2)}, u32[]{:S(2)}) collective-permute-start(bf16[512,128]{1,0:T(8,128)(2,1)S(1)} %collective-permute-done.4.refs_3_), channel_id=1, source_target_pairs={{0,3},{1,4},{2,7},{3,0},{4,1},{5,8},{6,11},{7,2},{8,5},{9,12},{10,... | collective-permute-start | bytes 393224 | tf_op jit(solution)/shard_map/ppermute | solution.py:224
  11.2 1.0 %absorb.10.refs_4_ = f32[8,768]{1,0:T(8,128)S(1)} custom-call(bf16[768,1024]{1,0:T(8,128)(2,1)S(1)} %get-tuple-element.26.observed_ref, f32[9,768]{1,0:T(8,128)S(1)} %get-tuple-element.27.aux_ref, bf16[528,128]{1,0:T(8,128)(2,1)S(1)} %get-tuple-element.31.refs_0_, bf16[512,128]{1,0:T(8,128)(2,1)S(1)} %get-tuple-element.32.refs_1_, ...), custom_call_target="tpu_custom_call" | custom-call | flops 402653184 | bytes 2097152 | tf_op jit(solution)/shard_map/absorb/pallas_call | solution.py:255
  12.2 0.3 collective-permute-done.7.refs_1_
  12.5 1.8 %collective-permute-start.12 = (bf16[528,128]{1,0:T(8,128)(2,1)S(1)}, bf16[528,128]{1,0:T(8,128)(2,1)S(1)}, u32[]{:S(2)}, u32[]{:S(2)}) collective-permute-start(bf16[528,128]{1,0:T(8,128)(2,1)S(1)} %collective-permute-done.6.refs_0_), channel_id=1, source_target_pairs={{0,5},{1,2},{2,1},{3,6},{4,9},{5,0},{6,3},{7,10},{8,13},{9,4},{10,... | collective-permute-start | bytes 405512 | tf_op jit(solution)/shard_map/ppermute | solution.py:224
  14.3 1.0 %absorb.9.refs_4_ = f32[8,768]{1,0:T(8,128)S(1)} custom-call(bf16[768,1024]{1,0:T(8,128)(2,1)S(1)} %collective-permute-done.2.observed_ref, f32[9,768]{1,0:T(8,128)S(1)} %collective-permute-done.3.aux_ref, bf16[528,128]{1,0:T(8,128)(2,1)S(1)} %get-tuple-element.31.refs_0_, bf16[512,128]{1,0:T(8,128)(2,1)S(1)} %get-tuple-element.32.refs_1_, ...), custom_call_target="tpu_custom_call" | custom-call | flops 402653184 | bytes 2097152 | tf_op jit(solution)/shard_map/absorb/pallas_call | solution.py:255
  15.3 1.7 %collective-permute-start.5 = (bf16[528,128]{1,0:T(8,128)(2,1)S(1)}, bf16[528,128]{1,0:T(8,128)(2,1)S(1)}, u32[]{:S(2)}, u32[]{:S(2)}) collective-permute-start(bf16[528,128]{1,0:T(8,128)(2,1)S(1)} %collective-permute-done.1.refs_2_), channel_id=1, source_target_pairs={{0,5},{1,2},{2,1},{3,6},{4,9},{5,0},{6,3},{7,10},{8,13},{9,4},{10,... | collective-permute-start | bytes 405512 | tf_op jit(solution)/shard_map/ppermute | solution.py:224
  17.2 1.1 %absorb.11.refs_4_ = f32[8,768]{1,0:T(8,128)S(1)} custom-call(bf16[768,1024]{1,0:T(8,128)(2,1)S(1)} %get-tuple-element.26.observed_ref, f32[9,768]{1,0:T(8,128)S(1)} %get-tuple-element.27.aux_ref, bf16[528,128]{1,0:T(8,128)(2,1)S(1)} %collective-permute-done.6.refs_0_, bf16[512,128]{1,0:T(8,128)(2,1)S(1)} %collective-permute-done.7.refs_1_, ...), custom_call_target="tpu_custom_call" | custom-call | flops 402653184 | bytes 2097152 | tf_op jit(solution)/shard_map/absorb/pallas_call | solution.py:255
  18.4 1.5 %collective-permute-start.13 = (bf16[528,128]{1,0:T(8,128)(2,1)S(1)}, bf16[528,128]{1,0:T(8,128)(2,1)S(1)}, u32[]{:S(2)}, u32[]{:S(2)}) collective-permute-start(bf16[528,128]{1,0:T(8,128)(2,1)S(1)} %collective-permute-done.12.refs_0_), channel_id=1, source_target_pairs={{0,3},{1,4},{2,7},{3,0},{4,1},{5,8},{6,11},{7,2},{8,5},{9,12},{10,... | collective-permute-start | bytes 405512 | tf_op jit(solution)/shard_map/ppermute | solution.py:224
  19.9 0.5 %collective-permute-start.15 = (bf16[512,128]{1,0:T(8,128)(2,1)S(1)}, bf16[512,128]{1,0:T(8,128)(2,1)S(1)}, u32[]{:S(2)}, u32[]{:S(2)}) collective-permute-start(bf16[512,128]{1,0:T(8,128)(2,1)S(1)} %collective-permute-done.14.refs_1_), channel_id=1, source_target_pairs={{0,3},{1,4},{2,7},{3,0},{4,1},{5,8},{6,11},{7,2},{8,5},{9,12},{10,... | collective-permute-start | bytes 393224 | tf_op jit(solution)/shard_map/ppermute | solution.py:224
  20.4 1.4 %collective-permute-start.9 = (bf16[528,128]{1,0:T(8,128)(2,1)S(1)}, bf16[528,128]{1,0:T(8,128)(2,1)S(1)}, u32[]{:S(2)}, u32[]{:S(2)}) collective-permute-start(bf16[528,128]{1,0:T(8,128)(2,1)S(1)} %collective-permute-done.5.refs_2_), channel_id=1, source_target_pairs={{0,3},{1,4},{2,7},{3,0},{4,1},{5,8},{6,11},{7,2},{8,5},{9,12},{10,... | collective-permute-start | bytes 405512 | tf_op jit(solution)/shard_map/ppermute | solution.py:224
  21.8 1.1 %absorb.12.refs_6_ = f32[8,768]{1,0:T(8,128)S(1)} custom-call(bf16[768,1024]{1,0:T(8,128)(2,1)S(1)} %collective-permute-done.2.observed_ref, f32[9,768]{1,0:T(8,128)S(1)} %collective-permute-done.3.aux_ref, bf16[528,128]{1,0:T(8,128)(2,1)S(1)} %collective-permute-done.6.refs_0_, bf16[512,128]{1,0:T(8,128)(2,1)S(1)} %collective-permute-done.7.refs_1_, ...), custom_call_target="tpu_custom_call" | custom-call | flops 402653184 | bytes 2097152 | tf_op jit(solution)/shard_map/absorb/pallas_call | solution.py:255
  22.9 0.9 %collective-permute-start.11 = (bf16[512,128]{1,0:T(8,128)(2,1)S(1)}, bf16[512,128]{1,0:T(8,128)(2,1)S(1)}, u32[]{:S(2)}, u32[]{:S(2)}) collective-permute-start(bf16[512,128]{1,0:T(8,128)(2,1)S(1)} %collective-permute-done.10.refs_3_), channel_id=1, source_target_pairs={{0,3},{1,4},{2,7},{3,0},{4,1},{5,8},{6,11},{7,2},{8,5},{9,12},{10,... | collective-permute-start | bytes 393224 | tf_op jit(solution)/shard_map/ppermute | solution.py:224
  23.8 1.1 %absorb.13.refs_2_ = f32[8,768]{1,0:T(8,128)S(1)} custom-call(bf16[768,1024]{1,0:T(8,128)(2,1)S(1)} %get-tuple-element.26.observed_ref, f32[9,768]{1,0:T(8,128)S(1)} %get-tuple-element.27.aux_ref, bf16[528,128]{1,0:T(8,128)(2,1)S(1)} %collective-permute-done.12.refs_0_, bf16[512,128]{1,0:T(8,128)(2,1)S(1)} %collective-permute-done.14.refs_1_, ...), custom_call_target="tpu_custom_call" | custom-call | flops 402653184 | bytes 2097152 | tf_op jit(solution)/shard_map/absorb/pallas_call | solution.py:255
  24.9 1.1 %absorb.14.refs_2_ = f32[8,768]{1,0:T(8,128)S(1)} custom-call(bf16[768,1024]{1,0:T(8,128)(2,1)S(1)} %get-tuple-element.26.observed_ref, f32[9,768]{1,0:T(8,128)S(1)} %get-tuple-element.27.aux_ref, bf16[528,128]{1,0:T(8,128)(2,1)S(1)} %collective-permute-done.13.refs_0_.refs_4_, bf16[512,128]{1,0:T(8,128)(2,1)S(1)} %collective-permute-done.15.refs_1_.refs_5_, ...), custom_call_target="tpu_custom_call" | custom-call | flops 201326592 | bytes 1835008 | tf_op jit(solution)/shard_map/absorb/pallas_call | solution.py:255
  26.0 1.4 %absorb.15.refs_2_ = f32[8,768]{1,0:T(8,128)S(1)} custom-call(bf16[768,1024]{1,0:T(8,128)(2,1)S(1)} %collective-permute-done.2.observed_ref, f32[9,768]{1,0:T(8,128)S(1)} %collective-permute-done.3.aux_ref, bf16[528,128]{1,0:T(8,128)(2,1)S(1)} %collective-permute-done.12.refs_0_, bf16[512,128]{1,0:T(8,128)(2,1)S(1)} %collective-permute-done.14.refs_1_, ...), custom_call_target="tpu_custom_call" | custom-call | flops 603979776 | bytes 2359296 | tf_op jit(solution)/shard_map/absorb/pallas_call | solution.py:255
  27.5 0.9 %absorb.17 = f32[8,768]{1,0:T(8,128)S(1)} custom-call(bf16[768,1024]{1,0:T(8,128)(2,1)S(1)} %collective-permute-done.2.observed_ref, f32[9,768]{1,0:T(8,128)S(1)} %collective-permute-done.3.aux_ref, bf16[528,128]{1,0:T(8,128)(2,1)S(1)} %collective-permute-done.9.refs_0_, bf16[512,128]{1,0:T(8,128)(2,1)S(1)} %collective-permute-done.11.refs_1_, ...), custom_call_target="tpu_custom_call" | custom-call | flops 201326592 | bytes 1835008 | tf_op jit(solution)/shard_map/absorb/pallas_call | solution.py:255
  28.5 0.9 %absorb.16.mine_ref = f32[8,768]{1,0:T(8,128)S(1)} custom-call(bf16[768,1024]{1,0:T(8,128)(2,1)S(1)} %get-tuple-element.26.observed_ref, f32[9,768]{1,0:T(8,128)S(1)} %get-tuple-element.27.aux_ref, bf16[528,128]{1,0:T(8,128)(2,1)S(1)} %collective-permute-done.9.refs_0_, bf16[512,128]{1,0:T(8,128)(2,1)S(1)} %collective-permute-done.11.refs_1_, ...), custom_call_target="tpu_custom_call" | custom-call | flops 201326592 | bytes 1835008 | tf_op jit(solution)/shard_map/absorb/pallas_call | solution.py:255
  29.6 0.6 %finish.1 = (f32[4,768]{1,0:T(4,128)}, f32[768]{0:T(1024)}) custom-call(f32[8,768]{1,0:T(8,128)S(1)} %absorb.16.mine_ref, f32[8,768]{1,0:T(8,128)S(1)} %collective-permute-done.16.other_ref, f32[9,768]{1,0:T(8,128)S(1)} %get-tuple-element.27.aux_ref), custom_call_target="tpu_custom_call" | custom-call | tf_op jit(solution)/shard_map/finish/pallas_call | solution.py:293
  (22 shorter events, 1.0 us)
Async XLA Ops:
  1.6 12.7 %collective-permute-start.2 = (bf16[768,1024]{1,0:T(8,128)(2,1)}, bf16[768,1024]{1,0:T(8,128)(2,1)S(1)}, u32[]{:S(2)}, u32[]{:S(2)}) collective-permute-start(bf16[768,1024]{1,0:T(8,128)(2,1)} %observed_hbm.1), channel_id=1, source_target_pairs={{0,1},{1,0},{2,3},{3,2},{4,5},{5,4},{6,7},{7,6},{8,9},{9,8},{10,11... | collective-permute-start | bytes 4718600 | tf_op jit(solution)/shard_map/ppermute | solution.py:247
  2.1 6.0 %collective-permute-start = (bf16[528,128]{1,0:T(8,128)(2,1)S(1)}, bf16[528,128]{1,0:T(8,128)(2,1)S(1)}, u32[]{:S(2)}, u32[]{:S(2)}) collective-permute-start(bf16[528,128]{1,0:T(8,128)(2,1)S(1)} %get-tuple-element.31.refs_0_), channel_id=1, source_target_pairs={{0,5},{1,2},{2,1},{3,6},{4,9},{5,0},{6,3},{7,10},{8,13},{9,4},{10,... | collective-permute-start | bytes 405512 | tf_op jit(solution)/shard_map/ppermute | solution.py:224
  4.8 5.0 %collective-permute-start.4 = (bf16[512,128]{1,0:T(8,128)(2,1)S(1)}, bf16[512,128]{1,0:T(8,128)(2,1)S(1)}, u32[]{:S(2)}, u32[]{:S(2)}) collective-permute-start(bf16[512,128]{1,0:T(8,128)(2,1)S(1)} %get-tuple-element.32.refs_1_), channel_id=1, source_target_pairs={{0,5},{1,2},{2,1},{3,6},{4,9},{5,0},{6,3},{7,10},{8,13},{9,4},{10,... | collective-permute-start | bytes 393224 | tf_op jit(solution)/shard_map/ppermute | solution.py:224
  6.4 4.7 %collective-permute-start.6 = (bf16[528,128]{1,0:T(8,128)(2,1)S(1)}, bf16[528,128]{1,0:T(8,128)(2,1)S(1)}, u32[]{:S(2)}, u32[]{:S(2)}) collective-permute-start(bf16[528,128]{1,0:T(8,128)(2,1)S(1)} %get-tuple-element.31.refs_0_), channel_id=1, source_target_pairs={{0,3},{1,4},{2,7},{3,0},{4,1},{5,8},{6,11},{7,2},{8,5},{9,12},{10,... | collective-permute-start | bytes 405512 | tf_op jit(solution)/shard_map/ppermute | solution.py:224
  8.1 4.4 %collective-permute-start.7 = (bf16[512,128]{1,0:T(8,128)(2,1)S(1)}, bf16[512,128]{1,0:T(8,128)(2,1)S(1)}, u32[]{:S(2)}, u32[]{:S(2)}) collective-permute-start(bf16[512,128]{1,0:T(8,128)(2,1)S(1)} %get-tuple-element.32.refs_1_), channel_id=1, source_target_pairs={{0,3},{1,4},{2,7},{3,0},{4,1},{5,8},{6,11},{7,2},{8,5},{9,12},{10,... | collective-permute-start | bytes 393224 | tf_op jit(solution)/shard_map/ppermute | solution.py:224
  8.2 7.1 %collective-permute-start.1 = (bf16[528,128]{1,0:T(8,128)(2,1)S(1)}, bf16[528,128]{1,0:T(8,128)(2,1)S(1)}, u32[]{:S(2)}, u32[]{:S(2)}) collective-permute-start(bf16[528,128]{1,0:T(8,128)(2,1)S(1)} %collective-permute-done.refs_2_), channel_id=1, source_target_pairs={{0,3},{1,4},{2,7},{3,0},{4,1},{5,8},{6,11},{7,2},{8,5},{9,12},{10,... | collective-permute-start | bytes 405512 | tf_op jit(solution)/shard_map/ppermute | solution.py:224
  9.8 7.2 %collective-permute-start.8 = (bf16[512,128]{1,0:T(8,128)(2,1)S(1)}, bf16[512,128]{1,0:T(8,128)(2,1)S(1)}, u32[]{:S(2)}, u32[]{:S(2)}) collective-permute-start(bf16[512,128]{1,0:T(8,128)(2,1)S(1)} %collective-permute-done.4.refs_3_), channel_id=1, source_target_pairs={{0,3},{1,4},{2,7},{3,0},{4,1},{5,8},{6,11},{7,2},{8,5},{9,12},{10,... | collective-permute-start | bytes 393224 | tf_op jit(solution)/shard_map/ppermute | solution.py:224
  11.0 3.3 %collective-permute-start.3 = (f32[9,768]{1,0:T(8,128)S(1)}, f32[9,768]{1,0:T(8,128)S(1)}, u32[]{:S(2)}, u32[]{:S(2)}) collective-permute-start(f32[9,768]{1,0:T(8,128)S(1)} %get-tuple-element.29), channel_id=1, source_target_pairs={{0,1},{1,0},{2,3},{3,2},{4,5},{5,4},{6,7},{7,6},{8,9},{9,8},{10,11... | collective-permute-start | bytes 82952 | tf_op jit(solution)/shard_map/ppermute | solution.py:248
  12.5 5.9 %collective-permute-start.12 = (bf16[528,128]{1,0:T(8,128)(2,1)S(1)}, bf16[528,128]{1,0:T(8,128)(2,1)S(1)}, u32[]{:S(2)}, u32[]{:S(2)}) collective-permute-start(bf16[528,128]{1,0:T(8,128)(2,1)S(1)} %collective-permute-done.6.refs_0_), channel_id=1, source_target_pairs={{0,5},{1,2},{2,1},{3,6},{4,9},{5,0},{6,3},{7,10},{8,13},{9,4},{10,... | collective-permute-start | bytes 405512 | tf_op jit(solution)/shard_map/ppermute | solution.py:224
  14.3 5.6 %collective-permute-start.14 = (bf16[512,128]{1,0:T(8,128)(2,1)S(1)}, bf16[512,128]{1,0:T(8,128)(2,1)S(1)}, u32[]{:S(2)}, u32[]{:S(2)}) collective-permute-start(bf16[512,128]{1,0:T(8,128)(2,1)S(1)} %collective-permute-done.7.refs_1_), channel_id=1, source_target_pairs={{0,5},{1,2},{2,1},{3,6},{4,9},{5,0},{6,3},{7,10},{8,13},{9,4},{10,... | collective-permute-start | bytes 393224 | tf_op jit(solution)/shard_map/ppermute | solution.py:224
  15.3 5.1 %collective-permute-start.5 = (bf16[528,128]{1,0:T(8,128)(2,1)S(1)}, bf16[528,128]{1,0:T(8,128)(2,1)S(1)}, u32[]{:S(2)}, u32[]{:S(2)}) collective-permute-start(bf16[528,128]{1,0:T(8,128)(2,1)S(1)} %collective-permute-done.1.refs_2_), channel_id=1, source_target_pairs={{0,5},{1,2},{2,1},{3,6},{4,9},{5,0},{6,3},{7,10},{8,13},{9,4},{10,... | collective-permute-start | bytes 405512 | tf_op jit(solution)/shard_map/ppermute | solution.py:224
  17.0 5.9 %collective-permute-start.10 = (bf16[512,128]{1,0:T(8,128)(2,1)S(1)}, bf16[512,128]{1,0:T(8,128)(2,1)S(1)}, u32[]{:S(2)}, u32[]{:S(2)}) collective-permute-start(bf16[512,128]{1,0:T(8,128)(2,1)S(1)} %collective-permute-done.8.refs_3_), channel_id=1, source_target_pairs={{0,5},{1,2},{2,1},{3,6},{4,9},{5,0},{6,3},{7,10},{8,13},{9,4},{10,... | collective-permute-start | bytes 393224 | tf_op jit(solution)/shard_map/ppermute | solution.py:224
  18.4 6.6 %collective-permute-start.13 = (bf16[528,128]{1,0:T(8,128)(2,1)S(1)}, bf16[528,128]{1,0:T(8,128)(2,1)S(1)}, u32[]{:S(2)}, u32[]{:S(2)}) collective-permute-start(bf16[528,128]{1,0:T(8,128)(2,1)S(1)} %collective-permute-done.12.refs_0_), channel_id=1, source_target_pairs={{0,3},{1,4},{2,7},{3,0},{4,1},{5,8},{6,11},{7,2},{8,5},{9,12},{10,... | collective-permute-start | bytes 405512 | tf_op jit(solution)/shard_map/ppermute | solution.py:224
  19.9 5.1 %collective-permute-start.15 = (bf16[512,128]{1,0:T(8,128)(2,1)S(1)}, bf16[512,128]{1,0:T(8,128)(2,1)S(1)}, u32[]{:S(2)}, u32[]{:S(2)}) collective-permute-start(bf16[512,128]{1,0:T(8,128)(2,1)S(1)} %collective-permute-done.14.refs_1_), channel_id=1, source_target_pairs={{0,3},{1,4},{2,7},{3,0},{4,1},{5,8},{6,11},{7,2},{8,5},{9,12},{10,... | collective-permute-start | bytes 393224 | tf_op jit(solution)/shard_map/ppermute | solution.py:224
  20.4 7.1 %collective-permute-start.9 = (bf16[528,128]{1,0:T(8,128)(2,1)S(1)}, bf16[528,128]{1,0:T(8,128)(2,1)S(1)}, u32[]{:S(2)}, u32[]{:S(2)}) collective-permute-start(bf16[528,128]{1,0:T(8,128)(2,1)S(1)} %collective-permute-done.5.refs_2_), channel_id=1, source_target_pairs={{0,3},{1,4},{2,7},{3,0},{4,1},{5,8},{6,11},{7,2},{8,5},{9,12},{10,... | collective-permute-start | bytes 405512 | tf_op jit(solution)/shard_map/ppermute | solution.py:224
  22.9 4.6 %collective-permute-start.11 = (bf16[512,128]{1,0:T(8,128)(2,1)S(1)}, bf16[512,128]{1,0:T(8,128)(2,1)S(1)}, u32[]{:S(2)}, u32[]{:S(2)}) collective-permute-start(bf16[512,128]{1,0:T(8,128)(2,1)S(1)} %collective-permute-done.10.refs_3_), channel_id=1, source_target_pairs={{0,3},{1,4},{2,7},{3,0},{4,1},{5,8},{6,11},{7,2},{8,5},{9,12},{10,... | collective-permute-start | bytes 393224 | tf_op jit(solution)/shard_map/ppermute | solution.py:224
  28.4 1.2 %collective-permute-start.16 = (f32[8,768]{1,0:T(8,128)S(1)}, f32[8,768]{1,0:T(8,128)S(1)}, u32[]{:S(2)}, u32[]{:S(2)}) collective-permute-start(f32[8,768]{1,0:T(8,128)S(1)} %absorb.17), channel_id=1, source_target_pairs={{0,1},{1,0},{2,3},{3,2},{4,5},{5,4},{6,7},{7,6},{8,9},{9,8},{10,11... | collective-permute-start | bytes 73736 | tf_op jit(solution)/shard_map/ppermute | solution.py:292

commit v12 on v11

--- a/solution.py
+++ b/solution.py
@@ -97,7 +97,7 @@
         pltpu.make_async_copy(source, target, arrived.at[i])
         for i, (source, target) in enumerate(zip(sources, targets))
     ]
-    for copy in copies:
+    for copy in reversed(copies):
         copy.start()
     for copy in copies[:3]:
         copy.wait()

time: 30.4 us -> 30.5 us (level)
  transfers between devices with their start and end apart: 17 -> 17, of which waited for: 2 -> 2; matrix products, arithmetic and copies ran while one was open for 0% -> 0% of each run, Pallas kernels for 33% -> 34%
where the time goes in v12:
time: 30.5 us; the launch traced here: 30.3 us
  starting transfers between devices  16.3 us (53%)
  Pallas kernels  12.7 us (42%)
  between operations  0.7 us (2%)
  waiting for transfers between devices  0.58 us (2%)
    ppermute x14, starting transfers between devices, send(): lax.ppermute(part, 'blk', pairs[(kind + step // 2) % 2])  15.4 us
    pallas_call x9, Pallas kernels, absorb(): pl.pallas_call(functools.partial(absorb_kernel, work, count, state is Non...  9.52 us
    pallas_call x1, Pallas kernels, on_device(): pl.pallas_call(functools.partial(prepare_kernel, block_of), out_shape=(ja...  1.55 us
    pallas_call x1, Pallas kernels, on_device(): pl.pallas_call(pack_kernel, out_shape=[jax.ShapeDtypeStruct((count * size...  0.99 us
    pallas_call x1, Pallas kernels, on_device(): pl.pallas_call(functools.partial(finish_kernel, size), out_shape=(jax.Sha...  0.63 us
  transfers between devices with their start and end apart: 17, of which 2 were waited for; matrix products, arithmetic and copies ran while one was open for 0% of the time, Pallas kernels for 34%

profile of v12, /device:TPU:0, one launch (start us, length us, event | category | flops | bytes accessed | tf_op | source)
XLA Modules:
  0.0 30.3 jit_solution(3431383996556303848)
XLA Ops:
  0.6 1.0 %pack.1 = (bf16[528,128]{1,0:T(8,128)(2,1)S(1)}, bf16[512,128]{1,0:T(8,128)(2,1)S(1)}) custom-call(bf16[4,128]{1,0:T(4,128)(2,1)} %params_hbm.1, s32[128]{0:T(128)} %class_hbm.2, bf16[128,1024]{1,0:T(8,128)(2,1)} %evolved_hbm.1), custom_call_target="tpu_custom_call" | custom-call | tf_op jit(solution)/shard_map/pack/pallas_call | solution.py:204
  1.6 0.5 %collective-permute-start.2 = (bf16[768,1024]{1,0:T(8,128)(2,1)}, bf16[768,1024]{1,0:T(8,128)(2,1)S(1)}, u32[]{:S(2)}, u32[]{:S(2)}) collective-permute-start(bf16[768,1024]{1,0:T(8,128)(2,1)} %observed_hbm.1), channel_id=1, source_target_pairs={{0,1},{1,0},{2,3},{3,2},{4,5},{5,4},{6,7},{7,6},{8,9},{9,8},{10,11... | collective-permute-start | bytes 4718600 | tf_op jit(solution)/shard_map/ppermute | solution.py:247
  2.1 2.7 %collective-permute-start = (bf16[528,128]{1,0:T(8,128)(2,1)S(1)}, bf16[528,128]{1,0:T(8,128)(2,1)S(1)}, u32[]{:S(2)}, u32[]{:S(2)}) collective-permute-start(bf16[528,128]{1,0:T(8,128)(2,1)S(1)} %get-tuple-element.31.refs_0_), channel_id=1, source_target_pairs={{0,5},{1,2},{2,1},{3,6},{4,9},{5,0},{6,3},{7,10},{8,13},{9,4},{10,... | collective-permute-start | bytes 405512 | tf_op jit(solution)/shard_map/ppermute | solution.py:224
  4.9 1.5 %prepare.1 = (f32[9,768]{1,0:T(8,128)S(1)}, f32[9,768]{1,0:T(8,128)S(1)}, bf16[768,1024]{1,0:T(8,128)(2,1)S(1)}) custom-call(s32[1]{0:T(128)} %bitcast.at_ref, s32[6,16]{1,0:T(8,128)} %pattern_hbm.1, s32[768]{0:T(1024)} %class_hbm.3, f32[768]{0:T(1024)} %sharp_hbm.1, bf16[768,1024]{1,0:T(8,128)(2,1)} %observed_hbm.1), custom_call_target="tpu_custom_call" | custom-call | flops 6291456 | bytes 3145728 | tf_op jit(solution)/shard_map/prepare/pallas_call | solution.py:228
  6.4 1.7 %collective-permute-start.6 = (bf16[528,128]{1,0:T(8,128)(2,1)S(1)}, bf16[528,128]{1,0:T(8,128)(2,1)S(1)}, u32[]{:S(2)}, u32[]{:S(2)}) collective-permute-start(bf16[528,128]{1,0:T(8,128)(2,1)S(1)} %get-tuple-element.31.refs_0_), channel_id=1, source_target_pairs={{0,3},{1,4},{2,7},{3,0},{4,1},{5,8},{6,11},{7,2},{8,5},{9,12},{10,... | collective-permute-start | bytes 405512 | tf_op jit(solution)/shard_map/ppermute | solution.py:224
  8.2 1.7 %collective-permute-start.1 = (bf16[528,128]{1,0:T(8,128)(2,1)S(1)}, bf16[528,128]{1,0:T(8,128)(2,1)S(1)}, u32[]{:S(2)}, u32[]{:S(2)}) collective-permute-start(bf16[528,128]{1,0:T(8,128)(2,1)S(1)} %collective-permute-done.refs_2_), channel_id=1, source_target_pairs={{0,3},{1,4},{2,7},{3,0},{4,1},{5,8},{6,11},{7,2},{8,5},{9,12},{10,... | collective-permute-start | bytes 405512 | tf_op jit(solution)/shard_map/ppermute | solution.py:224
  9.9 1.0 %collective-permute-start.8 = (bf16[512,128]{1,0:T(8,128)(2,1)S(1)}, bf16[512,128]{1,0:T(8,128)(2,1)S(1)}, u32[]{:S(2)}, u32[]{:S(2)}) collective-permute-start(bf16[512,128]{1,0:T(8,128)(2,1)S(1)} %collective-permute-done.4.refs_3_), channel_id=1, source_target_pairs={{0,3},{1,4},{2,7},{3,0},{4,1},{5,8},{6,11},{7,2},{8,5},{9,12},{10,... | collective-permute-start | bytes 393224 | tf_op jit(solution)/shard_map/ppermute | solution.py:224
  10.9 0.3 %collective-permute-start.3 = (f32[9,768]{1,0:T(8,128)S(1)}, f32[9,768]{1,0:T(8,128)S(1)}, u32[]{:S(2)}, u32[]{:S(2)}) collective-permute-start(f32[9,768]{1,0:T(8,128)S(1)} %get-tuple-element.29), channel_id=1, source_target_pairs={{0,1},{1,0},{2,3},{3,2},{4,5},{5,4},{6,7},{7,6},{8,9},{9,8},{10,11... | collective-permute-start | bytes 82952 | tf_op jit(solution)/shard_map/ppermute | solution.py:248
  11.3 1.0 %absorb.10.refs_4_ = f32[8,768]{1,0:T(8,128)S(1)} custom-call(bf16[768,1024]{1,0:T(8,128)(2,1)S(1)} %get-tuple-element.26.observed_ref, f32[9,768]{1,0:T(8,128)S(1)} %get-tuple-element.27.aux_ref, bf16[528,128]{1,0:T(8,128)(2,1)S(1)} %get-tuple-element.31.refs_0_, bf16[512,128]{1,0:T(8,128)(2,1)S(1)} %get-tuple-element.32.refs_1_, ...), custom_call_target="tpu_custom_call" | custom-call | flops 402653184 | bytes 2097152 | tf_op jit(solution)/shard_map/absorb/pallas_call | solution.py:255
  12.5 1.8 %collective-permute-start.12 = (bf16[528,128]{1,0:T(8,128)(2,1)S(1)}, bf16[528,128]{1,0:T(8,128)(2,1)S(1)}, u32[]{:S(2)}, u32[]{:S(2)}) collective-permute-start(bf16[528,128]{1,0:T(8,128)(2,1)S(1)} %collective-permute-done.6.refs_0_), channel_id=1, source_target_pairs={{0,5},{1,2},{2,1},{3,6},{4,9},{5,0},{6,3},{7,10},{8,13},{9,4},{10,... | collective-permute-start | bytes 405512 | tf_op jit(solution)/shard_map/ppermute | solution.py:224
  14.4 1.0 %absorb.9.refs_4_ = f32[8,768]{1,0:T(8,128)S(1)} custom-call(bf16[768,1024]{1,0:T(8,128)(2,1)S(1)} %collective-permute-done.2.observed_ref, f32[9,768]{1,0:T(8,128)S(1)} %collective-permute-done.3.aux_ref, bf16[528,128]{1,0:T(8,128)(2,1)S(1)} %get-tuple-element.31.refs_0_, bf16[512,128]{1,0:T(8,128)(2,1)S(1)} %get-tuple-element.32.refs_1_, ...), custom_call_target="tpu_custom_call" | custom-call | flops 402653184 | bytes 2097152 | tf_op jit(solution)/shard_map/absorb/pallas_call | solution.py:255
  15.3 1.7 %collective-permute-start.5 = (bf16[528,128]{1,0:T(8,128)(2,1)S(1)}, bf16[528,128]{1,0:T(8,128)(2,1)S(1)}, u32[]{:S(2)}, u32[]{:S(2)}) collective-permute-start(bf16[528,128]{1,0:T(8,128)(2,1)S(1)} %collective-permute-done.1.refs_2_), channel_id=1, source_target_pairs={{0,5},{1,2},{2,1},{3,6},{4,9},{5,0},{6,3},{7,10},{8,13},{9,4},{10,... | collective-permute-start | bytes 405512 | tf_op jit(solution)/shard_map/ppermute | solution.py:224
  17.3 1.1 %absorb.11.refs_4_ = f32[8,768]{1,0:T(8,128)S(1)} custom-call(bf16[768,1024]{1,0:T(8,128)(2,1)S(1)} %get-tuple-element.26.observed_ref, f32[9,768]{1,0:T(8,128)S(1)} %get-tuple-element.27.aux_ref, bf16[528,128]{1,0:T(8,128)(2,1)S(1)} %collective-permute-done.6.refs_0_, bf16[512,128]{1,0:T(8,128)(2,1)S(1)} %collective-permute-done.7.refs_1_, ...), custom_call_target="tpu_custom_call" | custom-call | flops 402653184 | bytes 2097152 | tf_op jit(solution)/shard_map/absorb/pallas_call | solution.py:255
  18.4 1.5 %collective-permute-start.13 = (bf16[528,128]{1,0:T(8,128)(2,1)S(1)}, bf16[528,128]{1,0:T(8,128)(2,1)S(1)}, u32[]{:S(2)}, u32[]{:S(2)}) collective-permute-start(bf16[528,128]{1,0:T(8,128)(2,1)S(1)} %collective-permute-done.12.refs_0_), channel_id=1, source_target_pairs={{0,3},{1,4},{2,7},{3,0},{4,1},{5,8},{6,11},{7,2},{8,5},{9,12},{10,... | collective-permute-start | bytes 405512 | tf_op jit(solution)/shard_map/ppermute | solution.py:224
  19.9 0.5 %collective-permute-start.15 = (bf16[512,128]{1,0:T(8,128)(2,1)S(1)}, bf16[512,128]{1,0:T(8,128)(2,1)S(1)}, u32[]{:S(2)}, u32[]{:S(2)}) collective-permute-start(bf16[512,128]{1,0:T(8,128)(2,1)S(1)} %collective-permute-done.14.refs_1_), channel_id=1, source_target_pairs={{0,3},{1,4},{2,7},{3,0},{4,1},{5,8},{6,11},{7,2},{8,5},{9,12},{10,... | collective-permute-start | bytes 393224 | tf_op jit(solution)/shard_map/ppermute | solution.py:224
  20.4 1.4 %collective-permute-start.9 = (bf16[528,128]{1,0:T(8,128)(2,1)S(1)}, bf16[528,128]{1,0:T(8,128)(2,1)S(1)}, u32[]{:S(2)}, u32[]{:S(2)}) collective-permute-start(bf16[528,128]{1,0:T(8,128)(2,1)S(1)} %collective-permute-done.5.refs_2_), channel_id=1, source_target_pairs={{0,3},{1,4},{2,7},{3,0},{4,1},{5,8},{6,11},{7,2},{8,5},{9,12},{10,... | collective-permute-start | bytes 405512 | tf_op jit(solution)/shard_map/ppermute | solution.py:224
  21.9 1.1 %absorb.12.refs_6_ = f32[8,768]{1,0:T(8,128)S(1)} custom-call(bf16[768,1024]{1,0:T(8,128)(2,1)S(1)} %collective-permute-done.2.observed_ref, f32[9,768]{1,0:T(8,128)S(1)} %collective-permute-done.3.aux_ref, bf16[528,128]{1,0:T(8,128)(2,1)S(1)} %collective-permute-done.6.refs_0_, bf16[512,128]{1,0:T(8,128)(2,1)S(1)} %collective-permute-done.7.refs_1_, ...), custom_call_target="tpu_custom_call" | custom-call | flops 402653184 | bytes 2097152 | tf_op jit(solution)/shard_map/absorb/pallas_call | solution.py:255
  23.0 0.9 %collective-permute-start.11 = (bf16[512,128]{1,0:T(8,128)(2,1)S(1)}, bf16[512,128]{1,0:T(8,128)(2,1)S(1)}, u32[]{:S(2)}, u32[]{:S(2)}) collective-permute-start(bf16[512,128]{1,0:T(8,128)(2,1)S(1)} %collective-permute-done.10.refs_3_), channel_id=1, source_target_pairs={{0,3},{1,4},{2,7},{3,0},{4,1},{5,8},{6,11},{7,2},{8,5},{9,12},{10,... | collective-permute-start | bytes 393224 | tf_op jit(solution)/shard_map/ppermute | solution.py:224
  23.9 1.1 %absorb.13.refs_2_ = f32[8,768]{1,0:T(8,128)S(1)} custom-call(bf16[768,1024]{1,0:T(8,128)(2,1)S(1)} %get-tuple-element.26.observed_ref, f32[9,768]{1,0:T(8,128)S(1)} %get-tuple-element.27.aux_ref, bf16[528,128]{1,0:T(8,128)(2,1)S(1)} %collective-permute-done.12.refs_0_, bf16[512,128]{1,0:T(8,128)(2,1)S(1)} %collective-permute-done.14.refs_1_, ...), custom_call_target="tpu_custom_call" | custom-call | flops 402653184 | bytes 2097152 | tf_op jit(solution)/shard_map/absorb/pallas_call | solution.py:255
  25.0 1.1 %absorb.14.refs_2_ = f32[8,768]{1,0:T(8,128)S(1)} custom-call(bf16[768,1024]{1,0:T(8,128)(2,1)S(1)} %get-tuple-element.26.observed_ref, f32[9,768]{1,0:T(8,128)S(1)} %get-tuple-element.27.aux_ref, bf16[528,128]{1,0:T(8,128)(2,1)S(1)} %collective-permute-done.13.refs_0_.refs_4_, bf16[512,128]{1,0:T(8,128)(2,1)S(1)} %collective-permute-done.15.refs_1_.refs_5_, ...), custom_call_target="tpu_custom_call" | custom-call | flops 201326592 | bytes 1835008 | tf_op jit(solution)/shard_map/absorb/pallas_call | solution.py:255
  26.1 1.4 %absorb.15.refs_2_ = f32[8,768]{1,0:T(8,128)S(1)} custom-call(bf16[768,1024]{1,0:T(8,128)(2,1)S(1)} %collective-permute-done.2.observed_ref, f32[9,768]{1,0:T(8,128)S(1)} %collective-permute-done.3.aux_ref, bf16[528,128]{1,0:T(8,128)(2,1)S(1)} %collective-permute-done.12.refs_0_, bf16[512,128]{1,0:T(8,128)(2,1)S(1)} %collective-permute-done.14.refs_1_, ...), custom_call_target="tpu_custom_call" | custom-call | flops 603979776 | bytes 2359296 | tf_op jit(solution)/shard_map/absorb/pallas_call | solution.py:255
  27.6 0.9 %absorb.17 = f32[8,768]{1,0:T(8,128)S(1)} custom-call(bf16[768,1024]{1,0:T(8,128)(2,1)S(1)} %collective-permute-done.2.observed_ref, f32[9,768]{1,0:T(8,128)S(1)} %collective-permute-done.3.aux_ref, bf16[528,128]{1,0:T(8,128)(2,1)S(1)} %collective-permute-done.9.refs_0_, bf16[512,128]{1,0:T(8,128)(2,1)S(1)} %collective-permute-done.11.refs_1_, ...), custom_call_target="tpu_custom_call" | custom-call | flops 201326592 | bytes 1835008 | tf_op jit(solution)/shard_map/absorb/pallas_call | solution.py:255
  28.6 0.9 %absorb.16.mine_ref = f32[8,768]{1,0:T(8,128)S(1)} custom-call(bf16[768,1024]{1,0:T(8,128)(2,1)S(1)} %get-tuple-element.26.observed_ref, f32[9,768]{1,0:T(8,128)S(1)} %get-tuple-element.27.aux_ref, bf16[528,128]{1,0:T(8,128)(2,1)S(1)} %collective-permute-done.9.refs_0_, bf16[512,128]{1,0:T(8,128)(2,1)S(1)} %collective-permute-done.11.refs_1_, ...), custom_call_target="tpu_custom_call" | custom-call | flops 201326592 | bytes 1835008 | tf_op jit(solution)/shard_map/absorb/pallas_call | solution.py:255
  29.7 0.6 %finish.1 = (f32[4,768]{1,0:T(4,128)}, f32[768]{0:T(1024)}) custom-call(f32[8,768]{1,0:T(8,128)S(1)} %absorb.16.mine_ref, f32[8,768]{1,0:T(8,128)S(1)} %collective-permute-done.16.other_ref, f32[9,768]{1,0:T(8,128)S(1)} %get-tuple-element.27.aux_ref), custom_call_target="tpu_custom_call" | custom-call | tf_op jit(solution)/shard_map/finish/pallas_call | solution.py:293
  (22 shorter events, 1.1 us)
Async XLA Ops:
  1.6 12.7 %collective-permute-start.2 = (bf16[768,1024]{1,0:T(8,128)(2,1)}, bf16[768,1024]{1,0:T(8,128)(2,1)S(1)}, u32[]{:S(2)}, u32[]{:S(2)}) collective-permute-start(bf16[768,1024]{1,0:T(8,128)(2,1)} %observed_hbm.1), channel_id=1, source_target_pairs={{0,1},{1,0},{2,3},{3,2},{4,5},{5,4},{6,7},{7,6},{8,9},{9,8},{10,11... | collective-permute-start | bytes 4718600 | tf_op jit(solution)/shard_map/ppermute | solution.py:247
  2.1 6.1 %collective-permute-start = (bf16[528,128]{1,0:T(8,128)(2,1)S(1)}, bf16[528,128]{1,0:T(8,128)(2,1)S(1)}, u32[]{:S(2)}, u32[]{:S(2)}) collective-permute-start(bf16[528,128]{1,0:T(8,128)(2,1)S(1)} %get-tuple-element.31.refs_0_), channel_id=1, source_target_pairs={{0,5},{1,2},{2,1},{3,6},{4,9},{5,0},{6,3},{7,10},{8,13},{9,4},{10,... | collective-permute-start | bytes 405512 | tf_op jit(solution)/shard_map/ppermute | solution.py:224
  4.8 5.1 %collective-permute-start.4 = (bf16[512,128]{1,0:T(8,128)(2,1)S(1)}, bf16[512,128]{1,0:T(8,128)(2,1)S(1)}, u32[]{:S(2)}, u32[]{:S(2)}) collective-permute-start(bf16[512,128]{1,0:T(8,128)(2,1)S(1)} %get-tuple-element.32.refs_1_), channel_id=1, source_target_pairs={{0,5},{1,2},{2,1},{3,6},{4,9},{5,0},{6,3},{7,10},{8,13},{9,4},{10,... | collective-permute-start | bytes 393224 | tf_op jit(solution)/shard_map/ppermute | solution.py:224
  6.4 4.5 %collective-permute-start.6 = (bf16[528,128]{1,0:T(8,128)(2,1)S(1)}, bf16[528,128]{1,0:T(8,128)(2,1)S(1)}, u32[]{:S(2)}, u32[]{:S(2)}) collective-permute-start(bf16[528,128]{1,0:T(8,128)(2,1)S(1)} %get-tuple-element.31.refs_0_), channel_id=1, source_target_pairs={{0,3},{1,4},{2,7},{3,0},{4,1},{5,8},{6,11},{7,2},{8,5},{9,12},{10,... | collective-permute-start | bytes 405512 | tf_op jit(solution)/shard_map/ppermute | solution.py:224
  8.1 4.4 %collective-permute-start.7 = (bf16[512,128]{1,0:T(8,128)(2,1)S(1)}, bf16[512,128]{1,0:T(8,128)(2,1)S(1)}, u32[]{:S(2)}, u32[]{:S(2)}) collective-permute-start(bf16[512,128]{1,0:T(8,128)(2,1)S(1)} %get-tuple-element.32.refs_1_), channel_id=1, source_target_pairs={{0,3},{1,4},{2,7},{3,0},{4,1},{5,8},{6,11},{7,2},{8,5},{9,12},{10,... | collective-permute-start | bytes 393224 | tf_op jit(solution)/shard_map/ppermute | solution.py:224
  8.2 7.1 %collective-permute-start.1 = (bf16[528,128]{1,0:T(8,128)(2,1)S(1)}, bf16[528,128]{1,0:T(8,128)(2,1)S(1)}, u32[]{:S(2)}, u32[]{:S(2)}) collective-permute-start(bf16[528,128]{1,0:T(8,128)(2,1)S(1)} %collective-permute-done.refs_2_), channel_id=1, source_target_pairs={{0,3},{1,4},{2,7},{3,0},{4,1},{5,8},{6,11},{7,2},{8,5},{9,12},{10,... | collective-permute-start | bytes 405512 | tf_op jit(solution)/shard_map/ppermute | solution.py:224
  9.9 7.2 %collective-permute-start.8 = (bf16[512,128]{1,0:T(8,128)(2,1)S(1)}, bf16[512,128]{1,0:T(8,128)(2,1)S(1)}, u32[]{:S(2)}, u32[]{:S(2)}) collective-permute-start(bf16[512,128]{1,0:T(8,128)(2,1)S(1)} %collective-permute-done.4.refs_3_), channel_id=1, source_target_pairs={{0,3},{1,4},{2,7},{3,0},{4,1},{5,8},{6,11},{7,2},{8,5},{9,12},{10,... | collective-permute-start | bytes 393224 | tf_op jit(solution)/shard_map/ppermute | solution.py:224
  10.9 3.4 %collective-permute-start.3 = (f32[9,768]{1,0:T(8,128)S(1)}, f32[9,768]{1,0:T(8,128)S(1)}, u32[]{:S(2)}, u32[]{:S(2)}) collective-permute-start(f32[9,768]{1,0:T(8,128)S(1)} %get-tuple-element.29), channel_id=1, source_target_pairs={{0,1},{1,0},{2,3},{3,2},{4,5},{5,4},{6,7},{7,6},{8,9},{9,8},{10,11... | collective-permute-start | bytes 82952 | tf_op jit(solution)/shard_map/ppermute | solution.py:248
  12.5 5.9 %collective-permute-start.12 = (bf16[528,128]{1,0:T(8,128)(2,1)S(1)}, bf16[528,128]{1,0:T(8,128)(2,1)S(1)}, u32[]{:S(2)}, u32[]{:S(2)}) collective-permute-start(bf16[528,128]{1,0:T(8,128)(2,1)S(1)} %collective-permute-done.6.refs_0_), channel_id=1, source_target_pairs={{0,5},{1,2},{2,1},{3,6},{4,9},{5,0},{6,3},{7,10},{8,13},{9,4},{10,... | collective-permute-start | bytes 405512 | tf_op jit(solution)/shard_map/ppermute | solution.py:224
  14.3 5.6 %collective-permute-start.14 = (bf16[512,128]{1,0:T(8,128)(2,1)S(1)}, bf16[512,128]{1,0:T(8,128)(2,1)S(1)}, u32[]{:S(2)}, u32[]{:S(2)}) collective-permute-start(bf16[512,128]{1,0:T(8,128)(2,1)S(1)} %collective-permute-done.7.refs_1_), channel_id=1, source_target_pairs={{0,5},{1,2},{2,1},{3,6},{4,9},{5,0},{6,3},{7,10},{8,13},{9,4},{10,... | collective-permute-start | bytes 393224 | tf_op jit(solution)/shard_map/ppermute | solution.py:224
  15.3 5.1 %collective-permute-start.5 = (bf16[528,128]{1,0:T(8,128)(2,1)S(1)}, bf16[528,128]{1,0:T(8,128)(2,1)S(1)}, u32[]{:S(2)}, u32[]{:S(2)}) collective-permute-start(bf16[528,128]{1,0:T(8,128)(2,1)S(1)} %collective-permute-done.1.refs_2_), channel_id=1, source_target_pairs={{0,5},{1,2},{2,1},{3,6},{4,9},{5,0},{6,3},{7,10},{8,13},{9,4},{10,... | collective-permute-start | bytes 405512 | tf_op jit(solution)/shard_map/ppermute | solution.py:224
  17.1 5.9 %collective-permute-start.10 = (bf16[512,128]{1,0:T(8,128)(2,1)S(1)}, bf16[512,128]{1,0:T(8,128)(2,1)S(1)}, u32[]{:S(2)}, u32[]{:S(2)}) collective-permute-start(bf16[512,128]{1,0:T(8,128)(2,1)S(1)} %collective-permute-done.8.refs_3_), channel_id=1, source_target_pairs={{0,5},{1,2},{2,1},{3,6},{4,9},{5,0},{6,3},{7,10},{8,13},{9,4},{10,... | collective-permute-start | bytes 393224 | tf_op jit(solution)/shard_map/ppermute | solution.py:224
  18.4 6.6 %collective-permute-start.13 = (bf16[528,128]{1,0:T(8,128)(2,1)S(1)}, bf16[528,128]{1,0:T(8,128)(2,1)S(1)}, u32[]{:S(2)}, u32[]{:S(2)}) collective-permute-start(bf16[528,128]{1,0:T(8,128)(2,1)S(1)} %collective-permute-done.12.refs_0_), channel_id=1, source_target_pairs={{0,3},{1,4},{2,7},{3,0},{4,1},{5,8},{6,11},{7,2},{8,5},{9,12},{10,... | collective-permute-start | bytes 405512 | tf_op jit(solution)/shard_map/ppermute | solution.py:224
  19.9 5.1 %collective-permute-start.15 = (bf16[512,128]{1,0:T(8,128)(2,1)S(1)}, bf16[512,128]{1,0:T(8,128)(2,1)S(1)}, u32[]{:S(2)}, u32[]{:S(2)}) collective-permute-start(bf16[512,128]{1,0:T(8,128)(2,1)S(1)} %collective-permute-done.14.refs_1_), channel_id=1, source_target_pairs={{0,3},{1,4},{2,7},{3,0},{4,1},{5,8},{6,11},{7,2},{8,5},{9,12},{10,... | collective-permute-start | bytes 393224 | tf_op jit(solution)/shard_map/ppermute | solution.py:224
  20.4 7.1 %collective-permute-start.9 = (bf16[528,128]{1,0:T(8,128)(2,1)S(1)}, bf16[528,128]{1,0:T(8,128)(2,1)S(1)}, u32[]{:S(2)}, u32[]{:S(2)}) collective-permute-start(bf16[528,128]{1,0:T(8,128)(2,1)S(1)} %collective-permute-done.5.refs_2_), channel_id=1, source_target_pairs={{0,3},{1,4},{2,7},{3,0},{4,1},{5,8},{6,11},{7,2},{8,5},{9,12},{10,... | collective-permute-start | bytes 405512 | tf_op jit(solution)/shard_map/ppermute | solution.py:224
  23.0 4.6 %collective-permute-start.11 = (bf16[512,128]{1,0:T(8,128)(2,1)S(1)}, bf16[512,128]{1,0:T(8,128)(2,1)S(1)}, u32[]{:S(2)}, u32[]{:S(2)}) collective-permute-start(bf16[512,128]{1,0:T(8,128)(2,1)S(1)} %collective-permute-done.10.refs_3_), channel_id=1, source_target_pairs={{0,3},{1,4},{2,7},{3,0},{4,1},{5,8},{6,11},{7,2},{8,5},{9,12},{10,... | collective-permute-start | bytes 393224 | tf_op jit(solution)/shard_map/ppermute | solution.py:224
  28.5 1.2 %collective-permute-start.16 = (f32[8,768]{1,0:T(8,128)S(1)}, f32[8,768]{1,0:T(8,128)S(1)}, u32[]{:S(2)}, u32[]{:S(2)}) collective-permute-start(f32[8,768]{1,0:T(8,128)S(1)} %absorb.17), channel_id=1, source_target_pairs={{0,1},{1,0},{2,3},{3,2},{4,5},{5,4},{6,7},{7,6},{8,9},{9,8},{10,11... | collective-permute-start | bytes 73736 | tf_op jit(solution)/shard_map/ppermute | solution.py:292
